TPU v7x, 32 devices: a whole 2x2x4 slice. The times are simulated.
32 devices in a mesh: grp: 2 (over y), head: 4 (over z), tm: 4 (over x, core).
Axes of the slice: x: 2, y: 2, z: 4, core: 2. Of those that a mesh axis runs over, the one named last changes fastest.
Arguments:
- query_rows: bfloat16 [32, 64, 3072], P(('grp', 'tm'), 'head'), parts along dimension 0, may hold values from -180 to 180
- key_rows: bfloat16 [32, 64, 3072], P(('grp', 'tm'), 'head'), parts along dimension 0, may hold values from -6 to 6
- value_rows: bfloat16 [32, 64, 3072], P(('grp', 'tm'), 'head'), parts along dimension 0, may hold values from -6 to 6
- pair_list: int32 [32, 32], P('grp'), parts along dimension 0, may hold values from 0 to 15, as said below
- block_tokens: int32 [32], P('grp'), parts along dimension 0, may hold values from 1 to 64, 768 in all
Outputs:
- attended: bfloat16 [32, 64, 3072], P(('grp', 'tm'), 'head'), parts along dimension 0
There are 2 independent parts, one for each index of `grp`. A program takes and returns all parts, laid end to end along the dimension named above; each array names one. Nothing has to cross between parts.
Inputs may be any that keep to these rules, and one draw needn't show every extreme that they name: `pair_list`: row q names q in column 0 and q xor 1 in column 1; a block may be named twice in a row. The query blocks of one time shard name at most 2 different blocks of a time shard beside it and at most 1 of a time shard two or more away; both bounds are reached.
All inputs are finite; a program needn't handle non-finite values.
Results may differ from a plain program's by a relative error of at most 0.0012.
The roundings to bfloat16 on the way count: a program that leaves them out, or rounds other values in their place, can miss the bound.
Values may be sent and summed in bfloat16 or wider, within the bound.
No kernel may reach another device: no remote copies, remote signals or barrier semaphores. Data moves between devices by JAX's collectives and lax.ppermute only.
A program may use at most 128 MiB of HBM per device.

v0:
```python
import functools
import math

import jax
import jax.numpy as jnp
from jax import lax
from jax.experimental import pallas as pl
from jax.experimental.pallas import tpu as pltpu
from jax.sharding import PartitionSpec as P

HD = 128
BLK = 64
NEAR_CAP = 2
FAR_CAP = 1
NEG = -1e30
ROTATE_SCALE = 1.0 / math.sqrt(HD)
SCORE_SCALE = 1.0 / math.sqrt(HD)
VMEM = 24 * 1024 * 1024
WIDE_VMEM = 60 * 1024 * 1024
TOKEN = jax.ShapeDtypeStruct((8, 128), jnp.float32)
NO_COST = pl.CostEstimate(flops=0, bytes_accessed=0, transcendentals=0)
HIGH_COST = pl.CostEstimate(flops=10**11, bytes_accessed=0, transcendentals=0)
LOG2E = math.log2(math.e)


def sign_matrix():
    common = lax.broadcasted_iota(jnp.int32, (HD, HD), 0) & lax.broadcasted_iota(
        jnp.int32, (HD, HD), 1
    )
    bits = HD.bit_length() - 1
    parity = common
    for bit in range(1, bits):
        parity = parity ^ (common >> bit)
    return jnp.where((parity & 1) == 0, 1.0, -1.0).astype(jnp.bfloat16)


def rows_of(block):
    rows, width = math.prod(block.shape[:-1]), block.shape[-1]
    if block.shape[-2] % 16 == 0:
        return block.reshape(rows, width)
    return block.astype(jnp.float32).reshape(rows, width).astype(block.dtype)


def fields_of(message):
    at, fields = 0, []
    for source, start, size in message:
        fields.append((source, start, size, at))
        at += size
    return fields, at


def rotate_kernel(message, sources, count_head, skipped, *refs):
    fields, total = fields_of(message)
    ins = dict(zip(sources, refs))
    outs, (token, buffer, sems) = refs[len(sources) + skipped : -3], refs[-3:]
    token[...] = jnp.zeros_like(token)
    blocks, tokens, width = refs[0].shape
    width_here = width // count_head
    me = lax.axis_index("head")
    order = list(range(1, count_head)) + [0]
    copies = {}
    for s in order:
        goal = lax.rem(me + s, count_head)
        for f, (source, start, size, at) in enumerate(fields):
            column = pl.multiple_of(goal * width_here + start, HD)
            copies[s, f] = pltpu.make_async_copy(
                ins[source].at[:, :, pl.ds(column, size)],
                buffer.at[s, :, :, pl.ds(at, size)],
                sems.at[s, f],
            )
            copies[s, f].start()
    sign = sign_matrix()
    for s in order:
        for f, (_, _, size, start) in enumerate(fields):
            copies[s, f].wait()
            flat = rows_of(buffer[s, :, :, start : start + size])
            heads = [flat[:, at : at + HD] for at in range(0, size, HD)]
            turned = jnp.dot(
                jnp.concatenate(heads, axis=0), sign, preferred_element_type=jnp.float32
            )
            turned = (turned * ROTATE_SCALE).reshape(size // HD, blocks, tokens, HD)
            for h in range(size // HD):
                at = start + h * HD
                outs[s][:, :, at : at + HD] = turned[h].astype(jnp.bfloat16)


def rotate_pieces(arrays, message, count_head, after=(), limit=VMEM):
    blocks, tokens, _ = arrays[0].shape
    fields, total = fields_of(message)
    sources = sorted({source for source, _, _ in message})
    one = (blocks, tokens, total)
    *pieces, token = pl.pallas_call(
        functools.partial(rotate_kernel, message, sources, count_head, len(after)),
        in_specs=[pl.BlockSpec(memory_space=pltpu.HBM)] * len(sources)
        + [pl.BlockSpec(memory_space=pl.ANY)] * len(after),
        out_specs=[pl.BlockSpec(memory_space=pltpu.VMEM)] * (count_head + 1),
        out_shape=[jax.ShapeDtypeStruct(one, jnp.bfloat16)] * count_head + [TOKEN],
        scratch_shapes=[
            pltpu.VMEM((count_head,) + one, jnp.bfloat16),
            pltpu.SemaphoreType.DMA((count_head, len(fields))),
        ],
        cost_estimate=NO_COST,
        compiler_params=pltpu.CompilerParams(vmem_limit_bytes=limit),
    )(*[arrays[source] for source in sources], *after)
    return pieces, token


def slots_at(distance, count_tm):
    return NEAR_CAP if distance in (1, count_tm - 1) else FAR_CAP


def pick_kernel(count_head, count_tm, lanes, skipped, picks_ref, *refs):
    pieces, outs = refs[:count_head], refs[count_head + skipped :]
    shard = lax.axis_index("tm")
    for distance, out in enumerate(outs, 1):
        goal = lax.rem(shard + distance, count_tm)
        for k in range(slots_at(distance, count_tm)):
            pick = picks_ref[NEAR_CAP * goal + k]
            for s in range(count_head):
                out[k, s] = pieces[s][pick, :, lanes[0] : lanes[1]]


def pick_blocks(picks, pieces, lanes, count_tm, after):
    count_head = len(pieces)
    one = (count_head, pieces[0].shape[1], lanes[1] - lanes[0])
    vmem = pl.BlockSpec(memory_space=pltpu.VMEM)
    return pl.pallas_call(
        functools.partial(pick_kernel, count_head, count_tm, lanes, len(after)),
        in_specs=[pl.BlockSpec(memory_space=pltpu.SMEM)]
        + [vmem] * count_head
        + [pl.BlockSpec(memory_space=pl.ANY)] * len(after),
        out_specs=[vmem] * (count_tm - 1),
        out_shape=[
            jax.ShapeDtypeStruct((slots_at(distance, count_tm),) + one, jnp.bfloat16)
            for distance in range(1, count_tm)
        ],
        cost_estimate=HIGH_COST,
        compiler_params=pltpu.CompilerParams(vmem_limit_bytes=VMEM),
    )(picks, *pieces, *after)


def remote_rows(count_tm):
    return [
        (distance, k)
        for distance in range(1, count_tm)
        for k in range(slots_at(distance, count_tm))
    ]


def split(value, by):
    if by & (by - 1) == 0:
        return value >> (by.bit_length() - 1), value & (by - 1)
    return lax.div(value, by), lax.rem(value, by)


def plan_kernel(count_head, count_tm, blocks, pair_ref, tokens_ref, _, picks_ref, bias_ref, named_ref, table_ref, sem):
    total_blocks, columns = pair_ref.shape
    pairs = pair_ref[...]
    lane = lax.broadcasted_iota(jnp.int32, named_ref.shape, 1)
    named = jnp.zeros(named_ref.shape, jnp.int32)
    for c in range(columns):
        named = jnp.where(pairs[:, c : c + 1] == lane, 1, named)
    named_ref[...] = named
    copy = pltpu.make_async_copy(named_ref, table_ref, sem)
    copy.start()
    copy.wait()
    shard = lax.axis_index("tm")
    place = lax.axis_index("head")
    mine = shard * blocks

    def two_picks(wanted):
        picks = [jnp.int32(0)] * NEAR_CAP
        count = jnp.int32(0)
        for j in range(blocks):
            for k in range(NEAR_CAP):
                picks[k] = jnp.where((wanted[j] > 0) & (count == k), j, picks[k])
            count = count + wanted[j]
        return picks, count

    def named_by(rows, column):
        found = table_ref[rows, column]
        for i in range(1, blocks):
            found = found | table_ref[rows + i, column]
        return found

    for d in range(count_tm):
        picks, _ = two_picks([named_by(d * blocks, mine + j) for j in range(blocks)])
        for k in range(NEAR_CAP):
            picks_ref[NEAR_CAP * d + k] = picks[k]

    kept = [[table_ref[mine + i, mine + j] * tokens_ref[mine + j] for j in range(blocks)] for i in range(blocks)]
    arrivals = {}
    for distance, k in remote_rows(count_tm):
        first = lax.rem(shard - distance + count_tm, count_tm) * blocks
        if k == 0:
            arrivals[distance] = two_picks([named_by(mine, first + j) for j in range(blocks)])
        picks, count = arrivals[distance]
        there = first + picks[k]
        live = jnp.where(count > k, tokens_ref[there], 0)
        for i in range(blocks):
            kept[i].append(table_ref[mine + i, there] * live)

    total = bias_ref.shape[1]
    piece_rows = BLK // count_head
    at = lax.broadcasted_iota(jnp.int32, (blocks, total), 1)
    query = lax.broadcasted_iota(jnp.int32, (blocks, total), 0)
    own = at < blocks * BLK
    group, token = split(at, piece_rows)
    own_piece, own_block = split(group, blocks)
    far_row, far_group = split(group, count_head)
    row = jnp.where(own, own_block, far_row)
    piece = jnp.where(own, own_piece, far_group)
    source = jnp.where(piece > place, place - piece + count_head, place - piece)
    position = source * piece_rows + token
    limit = jnp.zeros((blocks, total), jnp.int32)
    for r in range(len(kept[0])):
        value = jnp.zeros((blocks, total), jnp.int32)
        for i in range(blocks):
            value = jnp.where(query == i, kept[i][r], value)
        limit = jnp.where(row == r, value, limit)
    bias_ref[...] = jnp.where(position < limit, 0.0, NEG)


def plan(pair_list, block_tokens, after, blocks, count_head, count_tm):
    total_blocks = pair_list.shape[0]
    lanes = -(-total_blocks // 128) * 128
    total = (blocks + len(remote_rows(count_tm))) * BLK
    return pl.pallas_call(
        functools.partial(plan_kernel, count_head, count_tm, blocks),
        in_specs=[
            pl.BlockSpec(memory_space=pltpu.VMEM),
            pl.BlockSpec(memory_space=pltpu.SMEM),
            pl.BlockSpec(memory_space=pl.ANY),
        ],
        out_specs=[pl.BlockSpec(memory_space=pltpu.SMEM), pl.BlockSpec(memory_space=pltpu.VMEM)],
        out_shape=[
            jax.ShapeDtypeStruct((NEAR_CAP * count_tm,), jnp.int32),
            jax.ShapeDtypeStruct((blocks, total), jnp.float32),
        ],
        scratch_shapes=[
            pltpu.VMEM((total_blocks, lanes), jnp.int32),
            pltpu.SMEM((total_blocks, lanes), jnp.int32),
            pltpu.SemaphoreType.DMA,
        ],
        cost_estimate=NO_COST,
        compiler_params=pltpu.CompilerParams(vmem_limit_bytes=VMEM),
    )(pair_list, block_tokens, after)


def attend_kernel(counts, at, size, tokens_ref, bias_ref, *refs):
    count_head, count_tm, skipped = counts
    query_at, key_at = at
    queries, owns = refs[:count_head], refs[count_head : 2 * count_head]
    slots = refs[2 * count_head : 2 * count_head + count_tm - 1]
    outs = refs[2 * count_head + count_tm - 1 + skipped :]
    blocks, tokens, _ = owns[0].shape
    shard = lax.axis_index("tm")
    me = lax.axis_index("head")
    sign = sign_matrix()
    for h in range(size // HD):
        lanes = slice(h * HD, (h + 1) * HD)
        query_lanes = slice(query_at + h * HD, query_at + (h + 1) * HD)
        query = jnp.concatenate(
            [rows_of(queries[s][i, :, query_lanes]) for i in range(blocks) for s in range(count_head)],
            axis=0,
        )

        def gathered(kind):
            first = kind * size + h * HD
            own_lanes = slice(key_at + first, key_at + first + HD)
            pieces = [rows_of(own[:, :, own_lanes]) for own in owns]
            pieces += [
                rows_of(slots[distance - 1][k, :, :, first : first + HD])
                for distance, k in remote_rows(count_tm)
            ]
            return jnp.concatenate(pieces, axis=0)

        keys, values = gathered(0), gathered(1)
        total = keys.shape[0]
        dots = lax.dot_general(
            query, keys, (((1,), (1,)), ((), ())), preferred_element_type=jnp.float32
        )
        dots = dots.reshape(blocks, BLK, total) + bias_ref[...][:, None, :]
        peak = jnp.max(dots, axis=-1, keepdims=True)
        weights = jnp.exp2((dots - peak) * (SCORE_SCALE * LOG2E))
        denominator = jnp.sum(weights, axis=-1, keepdims=True).reshape(blocks * BLK, 1)
        weights_half = weights.astype(jnp.bfloat16).reshape(blocks * BLK, total)
        mixed = jnp.dot(weights_half, values, preferred_element_type=jnp.float32) / denominator
        turned = jnp.zeros_like(mixed)
        rest = mixed
        for _ in range(3):
            piece = rest.astype(jnp.bfloat16)
            turned = turned + jnp.dot(piece, sign, preferred_element_type=jnp.float32)
            rest = rest - piece.astype(jnp.float32)
        turned = (turned * ROTATE_SCALE).reshape(blocks, count_head, tokens, HD)
        token = lax.broadcasted_iota(jnp.int32, (tokens, HD), 0)
        for s in range(count_head):
            position = lax.rem(me - s + count_head, count_head) * tokens + token
            for i in range(blocks):
                outs[s][i, :, lanes] = jnp.where(
                    position < tokens_ref[shard * blocks + i], turned[i, s], 0.0
                ).astype(jnp.bfloat16)


def attend(block_tokens, bias, queries, query_at, owns, key_at, slots, size, after, cost):
    count_head, count_tm = len(owns), len(slots) + 1
    blocks, tokens, _ = owns[0].shape
    vmem = pl.BlockSpec(memory_space=pltpu.VMEM)
    return pl.pallas_call(
        functools.partial(
            attend_kernel, (count_head, count_tm, len(after)), (query_at, key_at), size
        ),
        in_specs=[pl.BlockSpec(memory_space=pltpu.SMEM)]
        + [vmem] * (2 * count_head + count_tm)
        + [pl.BlockSpec(memory_space=pl.ANY)] * len(after),
        out_specs=[vmem] * count_head,
        out_shape=[jax.ShapeDtypeStruct((blocks, tokens, size), jnp.bfloat16)] * count_head,
        cost_estimate=cost,
        compiler_params=pltpu.CompilerParams(vmem_limit_bytes=VMEM),
    )(block_tokens, bias, *queries, *owns, *slots, *after)


def place_kernel(count_head, starts, width_here, *refs):
    pieces, out_ref, sems = refs[:-2], refs[-2], refs[-1]
    me = lax.axis_index("head")
    copies = []
    for at, piece in enumerate(pieces):
        part, s = at // count_head, at % count_head
        column = lax.rem(me + s, count_head) * width_here + starts[part]
        copies.append(
            pltpu.make_async_copy(
                piece,
                out_ref.at[:, :, pl.ds(pl.multiple_of(column, HD), piece.shape[-1])],
                sems.at[at],
            )
        )
        copies[-1].start()
    for copy in copies:
        copy.wait()


def place_pieces(parts, starts, width_here):
    count_head = len(parts[0])
    pieces = [piece for part in parts for piece in part]
    blocks, tokens, _ = pieces[0].shape
    return pl.pallas_call(
        functools.partial(place_kernel, count_head, starts, width_here),
        in_specs=[pl.BlockSpec(memory_space=pl.ANY)] * len(pieces),
        out_specs=pl.BlockSpec(memory_space=pltpu.HBM),
        out_shape=jax.ShapeDtypeStruct((blocks, tokens, count_head * width_here), jnp.bfloat16),
        scratch_shapes=[pltpu.SemaphoreType.DMA((len(pieces),))],
        compiler_params=pltpu.CompilerParams(vmem_limit_bytes=VMEM),
    )(*pieces)


def shifted(array, axis, distance):
    count = lax.axis_size(axis)
    return lax.ppermute(array, axis, [(i, (i + distance) % count) for i in range(count)])


def exchange(pieces, direction):
    return [pieces[0]] + [
        shifted(piece, "head", direction * s) for s, piece in enumerate(pieces[1:], 1)
    ]


def forward(sent):
    return [shifted(block, "tm", distance) for distance, block in enumerate(sent, 1)]


def shards(query_rows, key_rows, value_rows, pair_list, block_tokens):
    count_head = lax.axis_size("head")
    count_tm = lax.axis_size("tm")
    blocks, tokens, width = query_rows.shape
    width_here = width // count_head
    heads = width_here // HD
    cut = (heads + 1) // 2 * HD
    parts = [(0, cut), (cut, width_here - cut)] if heads > 1 else [(0, width_here)]
    arrays = [query_rows, key_rows, value_rows]
    messages = []
    for at, part in enumerate(parts):
        message = [(1,) + part, (2,) + part]
        messages.append(message + ([(0,) + parts[at - 1]] if at else []))
    messages.append([(0,) + parts[-1]])
    key_at = [0] * len(parts)
    query_at = [2 * size for _, size in parts[1:]] + [0]

    pieces, token = rotate_pieces(arrays, messages[0], count_head, limit=WIDE_VMEM)
    packed = [pieces]
    picks, bias = plan(pair_list, block_tokens, token, blocks, count_head, count_tm)
    after = (bias,)
    for message in messages[1:-1]:
        pieces, token = rotate_pieces(arrays, message, count_head, after)
        packed.append(pieces)
        after = (token,)
    received = [exchange(pieces, 1) for pieces in packed]
    sent, after = [], ()
    for at, (_, size) in enumerate(parts):
        lanes = (key_at[at], key_at[at] + 2 * size)
        sent.append(pick_blocks(picks, received[at], lanes, count_tm, after))
        after = (sent[-1][0],)
        if not at:
            pieces, _ = rotate_pieces(arrays, messages[-1], count_head, after)
    received.append(exchange(pieces, 1))
    returned, after = [], ()
    for at, (_, size) in enumerate(parts):
        cost = NO_COST if at == len(parts) - 1 else HIGH_COST
        attended = attend(
            block_tokens, bias, received[at + 1], query_at[at], received[at], key_at[at],
            forward(sent[at]), size, after, cost,
        )
        after = (attended[0],)
        returned.append(exchange(attended, -1))
    return place_pieces(returned, [start for start, _ in parts], width_here)


def solution(mesh):
    placed = (
        P(("grp", "tm"), "head", None),
        P(("grp", "tm"), "head", None),
        P(("grp", "tm"), "head", None),
        P("grp", None),
        P("grp"),
    )
    return jax.shard_map(
        shards,
        mesh=mesh,
        in_specs=placed,
        out_specs=P(("grp", "tm"), "head", None),
        check_vma=False,
    )
```

profile of v0, /device:TPU:0, one launch (start us, length us, event | category | flops | bytes accessed | tf_op | source)
XLA Modules:
  0.0 58.1 jit_solution(17314947335976256703)
XLA Ops:
  0.0 2.9 %shard_map.55 = (bf16[4,16,768]{2,1,0:T(8,128)(2,1)}, bf16[4,16,768]{2,1,0:T(8,128)(2,1)}, bf16[4,16,768]{2,1,0:T(8,128)(2,1)}, bf16[4,16,768]{2,1,0:T(8,128)(2,1)}, f32[8,128]{1,0:T(8,128)}) custom-call(bf16[4,16,3072]{2,1,0:T(8,128)(2,1)} %refs_1_.3, bf16[4,16,3072]{2,1,0:T(8,128)(2,1)} %refs_2_.1), custom_call_target="tpu_custom_call" | custom-call | tf_op jit(solution)/shard_map/pallas_call | solution.py:92
  2.9 0.0 copy-start.7
  2.9 3.1 %collective-permute-start.3 = (bf16[4,16,768]{2,1,0:T(8,128)(2,1)}, bf16[4,16,768]{2,1,0:T(8,128)(2,1)S(1)}, u32[]{:S(2)}, u32[]{:S(2)}) collective-permute-start(bf16[4,16,768]{2,1,0:T(8,128)(2,1)} %get-tuple-element.41), channel_id=1, source_target_pairs={{0,4},{4,8},{8,12},{12,0},{1,5},{5,9},{9,13},{13,1},{2,6},{6,10},{... | collective-permute-start | bytes 294920 | tf_op jit(solution)/shard_map/ppermute | solution.py:358
  6.0 2.6 %collective-permute-start.4 = (bf16[4,16,768]{2,1,0:T(8,128)(2,1)}, bf16[4,16,768]{2,1,0:T(8,128)(2,1)S(1)}, u32[]{:S(2)}, u32[]{:S(2)}) collective-permute-start(bf16[4,16,768]{2,1,0:T(8,128)(2,1)} %get-tuple-element.42), channel_id=1, source_target_pairs={{0,8},{4,12},{8,0},{12,4},{1,9},{5,13},{9,1},{13,5},{2,10},{6,14},... | collective-permute-start | bytes 294920 | tf_op jit(solution)/shard_map/ppermute | solution.py:358
  8.6 1.3 %collective-permute-start.5 = (bf16[4,16,768]{2,1,0:T(8,128)(2,1)}, bf16[4,16,768]{2,1,0:T(8,128)(2,1)S(1)}, u32[]{:S(2)}, u32[]{:S(2)}) collective-permute-start(bf16[4,16,768]{2,1,0:T(8,128)(2,1)} %get-tuple-element.43), channel_id=1, source_target_pairs={{0,12},{4,0},{8,4},{12,8},{1,13},{5,1},{9,5},{13,9},{2,14},{6,2},{... | collective-permute-start | bytes 294920 | tf_op jit(solution)/shard_map/ppermute | solution.py:358
  9.9 0.0 copy-done.7
  9.9 0.0 copy-done.8
  9.9 0.7 %copy-done.6 = s32[16,32]{1,0:T(8,128)S(1)} copy-done((s32[16,32]{1,0:T(8,128)S(1)}, s32[16,32]{1,0:T(8,128)}, u32[]{:S(2)}) %copy-start.6) | copy-done | bytes 2072
  10.6 2.3 %shard_map.56 = (s32[8]{0:T(128)S(1)}, f32[4,576]{1,0:T(4,128)S(1)}) custom-call(s32[16,32]{1,0:T(8,128)S(1)} %copy-done.6, s32[16]{0:T(128)S(1)} %copy-done.8, f32[8,128]{1,0:T(8,128)S(1)} %copy-done.7), custom_call_target="tpu_custom_call" | custom-call | tf_op jit(solution)/shard_map/pallas_call | solution.py:228
  12.9 0.0 copy-start.4
  12.9 0.0 copy-done
  12.9 0.0 copy-start.2
  12.9 1.0 %copy-done.2 = bf16[4,16,3072]{2,1,0:T(8,128)(2,1)S(1)} copy-done((bf16[4,16,3072]{2,1,0:T(8,128)(2,1)S(1)}, bf16[4,16,3072]{2,1,0:T(8,128)(2,1)}, u32[]{:S(2)}) %copy-start.2) | copy-done | bytes 393240
  13.9 2.6 %shard_map.57 = (bf16[4,16,1152]{2,1,0:T(8,128)(2,1)S(1)}, bf16[4,16,1152]{2,1,0:T(8,128)(2,1)S(1)}, bf16[4,16,1152]{2,1,0:T(8,128)(2,1)S(1)}, bf16[4,16,1152]{2,1,0:T(8,128)(2,1)S(1)}, f32[8,128]{1,0:T(8,128)}) custom-call(bf16[4,16,3072]{2,1,0:T(8,128)(2,1)S(1)} %copy-done.2, bf16[4,16,3072]{2,1,0:T(8,128)(2,1)S(1)} %copy-done, ...), custom_call_target="tpu_custom_call" | custom-call | tf_op jit(solution)/shard_map/pallas_call | solution.py:92
  16.5 0.0 copy-done.4
  16.5 0.7 %collective-permute-start = (bf16[4,16,1152]{2,1,0:T(8,128)(2,1)S(1)}, bf16[4,16,1152]{2,1,0:T(8,128)(2,1)S(1)}, u32[]{:S(2)}, u32[]{:S(2)}) collective-permute-start(bf16[4,16,1152]{2,1,0:T(8,128)(2,1)S(1)} %get-tuple-element.37), channel_id=1, source_target_pairs={{0,4},{4,8},{8,12},{12,0},{1,5},{5,9},{9,13},{13,1},{2,6},{6,10},{... | collective-permute-start | bytes 442376 | tf_op jit(solution)/shard_map/ppermute | solution.py:358
  17.2 0.5 collective-permute-start.1
  17.8 0.0 collective-permute-done.3.refs_1_.refs_5_
  17.8 2.6 %collective-permute-start.2 = (bf16[4,16,1152]{2,1,0:T(8,128)(2,1)S(1)}, bf16[4,16,1152]{2,1,0:T(8,128)(2,1)S(1)}, u32[]{:S(2)}, u32[]{:S(2)}) collective-permute-start(bf16[4,16,1152]{2,1,0:T(8,128)(2,1)S(1)} %get-tuple-element.39), channel_id=1, source_target_pairs={{0,12},{4,0},{8,4},{12,8},{1,13},{5,1},{9,5},{13,9},{2,14},{6,2},{... | collective-permute-start | bytes 442376 | tf_op jit(solution)/shard_map/ppermute | solution.py:358
  20.4 0.0 collective-permute-done.4.refs_2_.refs_6_
  20.4 0.0 collective-permute-done.5.refs_3_.refs_7_
  20.4 0.0 copy-start.3
  20.4 0.6 %shard_map.58 = (bf16[2,4,16,768]{3,2,1,0:T(8,128)(2,1)S(1)}, bf16[1,4,16,768]{3,2,1,0:T(8,128)(2,1)S(1)}, bf16[2,4,16,768]{3,2,1,0:T(8,128)(2,1)S(1)}) custom-call(s32[8]{0:T(128)S(1)} %get-tuple-element.44.picks_ref, bf16[4,16,768]{2,1,0:T(8,128)(2,1)S(1)} %copy-done.10, bf16[4,16,768]{2,1,0:T(8,128)(2,1)S(1)} %collective-permute-done.3.refs_1_.refs_5_, ...), custom_call_target="tpu_custom_call" | custom-call | flops 99999997952 | tf_op jit(solution)/shard_map/pallas_call | solution.py:127
  21.0 0.1 collective-permute-start.6
  21.1 0.3 copy-done.3
  21.4 1.2 %shard_map.60 = (bf16[4,16,384]{2,1,0:T(8,128)(2,1)S(1)}, bf16[4,16,384]{2,1,0:T(8,128)(2,1)S(1)}, bf16[4,16,384]{2,1,0:T(8,128)(2,1)}, bf16[4,16,384]{2,1,0:T(8,128)(2,1)S(1)}, f32[8,128]{1,0:T(8,128)}) custom-call(bf16[4,16,3072]{2,1,0:T(8,128)(2,1)S(1)} %copy-done.3, bf16[2,4,16,768]{3,2,1,0:T(8,128)(2,1)S(1)} %get-tuple-element.45.refs_1_.refs_4_), custom_call_target="tpu_custom_call" | custom-call | tf_op jit(solution)/shard_map/pallas_call | solution.py:92
  22.6 1.6 %collective-permute-start.7 = (bf16[1,4,16,768]{3,2,1,0:T(8,128)(2,1)S(1)}, bf16[1,4,16,768]{3,2,1,0:T(8,128)(2,1)S(1)}, u32[]{:S(2)}, u32[]{:S(2)}) collective-permute-start(bf16[1,4,16,768]{3,2,1,0:T(8,128)(2,1)S(1)} %get-tuple-element.46), channel_id=1, source_target_pairs={{0,2},{1,3},{2,0},{3,1},{4,6},{5,7},{6,4},{7,5},{8,10},{9,11},{10,... | collective-permute-start | bytes 294920 | tf_op jit(solution)/shard_map/ppermute | solution.py:358
  24.2 1.0 %collective-permute-done.refs_1_.refs_5_ = bf16[4,16,1152]{2,1,0:T(8,128)(2,1)S(1)} collective-permute-done((bf16[4,16,1152]{2,1,0:T(8,128)(2,1)S(1)}, bf16[4,16,1152]{2,1,0:T(8,128)(2,1)S(1)}, u32[]{:S(2)}, u32[]{:S(2)}) %collective-permute-start) | collective-permute-done | bytes 147488 | tf_op jit(solution)/shard_map/ppermute | solution.py:358
  25.2 0.1 collective-permute-start.8
  25.3 4.3 %collective-permute-done.1.refs_2_.refs_6_ = bf16[4,16,1152]{2,1,0:T(8,128)(2,1)S(1)} collective-permute-done((bf16[4,16,1152]{2,1,0:T(8,128)(2,1)S(1)}, bf16[4,16,1152]{2,1,0:T(8,128)(2,1)S(1)}, u32[]{:S(2)}, u32[]{:S(2)}) %collective-permute-start.1) | collective-permute-done | bytes 147488 | tf_op jit(solution)/shard_map/ppermute | solution.py:358
  29.6 0.0 collective-permute-start.12
  29.6 0.0 collective-permute-done.2.refs_3_.refs_7_
  29.6 3.2 %collective-permute-start.13 = (bf16[4,16,384]{2,1,0:T(8,128)(2,1)}, bf16[4,16,384]{2,1,0:T(8,128)(2,1)}, u32[]{:S(2)}, u32[]{:S(2)}) collective-permute-start(bf16[4,16,384]{2,1,0:T(8,128)(2,1)} %get-tuple-element.54), channel_id=1, source_target_pairs={{0,8},{4,12},{8,0},{12,4},{1,9},{5,13},{9,1},{13,5},{2,10},{6,14},... | collective-permute-start | bytes 147464 | tf_op jit(solution)/shard_map/ppermute | solution.py:358
  32.8 0.6 %shard_map.61 = (bf16[2,4,16,768]{3,2,1,0:T(8,128)(2,1)S(1)}, bf16[1,4,16,768]{3,2,1,0:T(8,128)(2,1)S(1)}, bf16[2,4,16,768]{3,2,1,0:T(8,128)(2,1)S(1)}) custom-call(s32[8]{0:T(128)S(1)} %get-tuple-element.44.picks_ref, bf16[4,16,1152]{2,1,0:T(8,128)(2,1)S(1)} %get-tuple-element.36.refs_0_.refs_4_, ...), custom_call_target="tpu_custom_call" | custom-call | flops 99999997952 | tf_op jit(solution)/shard_map/pallas_call | solution.py:127
  33.4 2.4 %collective-permute-done.12.refs_1_ = bf16[4,16,384]{2,1,0:T(8,128)(2,1)S(1)} collective-permute-done((bf16[4,16,384]{2,1,0:T(8,128)(2,1)S(1)}, bf16[4,16,384]{2,1,0:T(8,128)(2,1)S(1)}, u32[]{:S(2)}, u32[]{:S(2)}) %collective-permute-start.12) | collective-permute-done | bytes 49184 | tf_op jit(solution)/shard_map/ppermute | solution.py:358
  35.8 0.9 %collective-permute-start.14 = (bf16[4,16,384]{2,1,0:T(8,128)(2,1)S(1)}, bf16[4,16,384]{2,1,0:T(8,128)(2,1)S(1)}, u32[]{:S(2)}, u32[]{:S(2)}) collective-permute-start(bf16[4,16,384]{2,1,0:T(8,128)(2,1)S(1)} %get-tuple-element.55), channel_id=1, source_target_pairs={{0,12},{4,0},{8,4},{12,8},{1,13},{5,1},{9,5},{13,9},{2,14},{6,2},{... | collective-permute-start | bytes 147464 | tf_op jit(solution)/shard_map/ppermute | solution.py:358
  36.7 0.0 collective-permute-done.7.refs_9_
  36.7 0.0 collective-permute-start.15
  36.7 0.0 collective-permute-done.6.refs_8_
  36.7 0.0 copy-start.9
  36.7 1.6 %collective-permute-start.16 = (bf16[1,4,16,768]{3,2,1,0:T(8,128)(2,1)S(1)}, bf16[1,4,16,768]{3,2,1,0:T(8,128)(2,1)S(1)}, u32[]{:S(2)}, u32[]{:S(2)}) collective-permute-start(bf16[1,4,16,768]{3,2,1,0:T(8,128)(2,1)S(1)} %get-tuple-element.57), channel_id=1, source_target_pairs={{0,2},{1,3},{2,0},{3,1},{4,6},{5,7},{6,4},{7,5},{8,10},{9,11},{10,... | collective-permute-start | bytes 294920 | tf_op jit(solution)/shard_map/ppermute | solution.py:358
  38.3 0.0 collective-permute-done.8.refs_10_
  38.3 1.4 %collective-permute-start.17 = (bf16[2,4,16,768]{3,2,1,0:T(8,128)(2,1)S(1)}, bf16[2,4,16,768]{3,2,1,0:T(8,128)(2,1)S(1)}, u32[]{:S(2)}, u32[]{:S(2)}) collective-permute-start(bf16[2,4,16,768]{3,2,1,0:T(8,128)(2,1)S(1)} %get-tuple-element.58), channel_id=1, source_target_pairs={{0,3},{1,0},{2,1},{3,2},{4,7},{5,4},{6,5},{7,6},{8,11},{9,8},{10,9... | collective-permute-start | bytes 589832 | tf_op jit(solution)/shard_map/ppermute | solution.py:358
  39.7 0.0 copy-done.9
  39.7 2.4 %shard_map.59 = (bf16[4,16,384]{2,1,0:T(8,128)(2,1)S(1)}, bf16[4,16,384]{2,1,0:T(8,128)(2,1)S(1)}, bf16[4,16,384]{2,1,0:T(8,128)(2,1)S(1)}, bf16[4,16,384]{2,1,0:T(8,128)(2,1)S(1)}) custom-call(s32[16]{0:T(128)S(1)} %copy-done.9, f32[4,576]{1,0:T(4,128)S(1)} %copy-done.5, bf16[4,16,1152]{2,1,0:T(8,128)(2,1)S(1)} %get-tuple-element.36.refs_0_.refs_4_, ...), custom_call_target="tpu_custom_call" | custom-call | flops 99999997952 | tf_op jit(solution)/shard_map/pallas_call | solution.py:309
  42.1 0.0 collective-permute-done.13.refs_2_
  42.1 0.1 collective-permute-start.9
  42.2 0.0 collective-permute-done.14.refs_3_
  42.2 2.6 %collective-permute-start.10 = (bf16[4,16,384]{2,1,0:T(8,128)(2,1)S(1)}, bf16[4,16,384]{2,1,0:T(8,128)(2,1)S(1)}, u32[]{:S(2)}, u32[]{:S(2)}) collective-permute-start(bf16[4,16,384]{2,1,0:T(8,128)(2,1)S(1)} %get-tuple-element.50), channel_id=1, source_target_pairs={{0,8},{4,12},{8,0},{12,4},{1,9},{5,13},{9,1},{13,5},{2,10},{6,14},... | collective-permute-start | bytes 147464 | tf_op jit(solution)/shard_map/ppermute | solution.py:358
  44.8 0.0 collective-permute-done.16.refs_9_
  44.8 0.0 collective-permute-start.11
  44.8 0.0 collective-permute-done.15.refs_8_
  44.8 0.2 collective-permute-done.17.refs_10_
  45.0 2.7 %shard_map.62 = (bf16[4,16,384]{2,1,0:T(8,128)(2,1)S(1)}, bf16[4,16,384]{2,1,0:T(8,128)(2,1)S(1)}, bf16[4,16,384]{2,1,0:T(8,128)(2,1)S(1)}, bf16[4,16,384]{2,1,0:T(8,128)(2,1)S(1)}) custom-call(s32[16]{0:T(128)S(1)} %copy-done.9, f32[4,576]{1,0:T(4,128)S(1)} %copy-done.5, bf16[4,16,384]{2,1,0:T(8,128)(2,1)S(1)} %get-tuple-element.52.refs_0_, ...), custom_call_target="tpu_custom_call" | custom-call | tf_op jit(solution)/shard_map/pallas_call | solution.py:309
  47.7 3.7 %collective-permute-start.18 = (bf16[4,16,384]{2,1,0:T(8,128)(2,1)S(1)}, bf16[4,16,384]{2,1,0:T(8,128)(2,1)S(1)}, u32[]{:S(2)}, u32[]{:S(2)}) collective-permute-start(bf16[4,16,384]{2,1,0:T(8,128)(2,1)S(1)} %get-tuple-element.60), channel_id=1, source_target_pairs={{0,12},{4,0},{8,4},{12,8},{1,13},{5,1},{9,5},{13,9},{2,14},{6,2},{... | collective-permute-start | bytes 147464 | tf_op jit(solution)/shard_map/ppermute | solution.py:358
  51.4 0.0 collective-permute-start.19
  51.4 0.0 collective-permute-done.9.refs_1_
  51.4 0.6 %collective-permute-start.20 = (bf16[4,16,384]{2,1,0:T(8,128)(2,1)S(1)}, bf16[4,16,384]{2,1,0:T(8,128)(2,1)S(1)}, u32[]{:S(2)}, u32[]{:S(2)}) collective-permute-start(bf16[4,16,384]{2,1,0:T(8,128)(2,1)S(1)} %get-tuple-element.62), channel_id=1, source_target_pairs={{0,4},{4,8},{8,12},{12,0},{1,5},{5,9},{9,13},{13,1},{2,6},{6,10},{... | collective-permute-start | bytes 147464 | tf_op jit(solution)/shard_map/ppermute | solution.py:358
  52.1 0.0 collective-permute-done.10.refs_2_
  52.1 0.0 collective-permute-done.11.refs_3_
  52.1 1.5 %collective-permute-done.18.refs_5_ = bf16[4,16,384]{2,1,0:T(8,128)(2,1)S(1)} collective-permute-done((bf16[4,16,384]{2,1,0:T(8,128)(2,1)S(1)}, bf16[4,16,384]{2,1,0:T(8,128)(2,1)S(1)}, u32[]{:S(2)}, u32[]{:S(2)}) %collective-permute-start.18) | collective-permute-done | bytes 49184 | tf_op jit(solution)/shard_map/ppermute | solution.py:358
  53.5 3.1 %collective-permute-done.19.refs_6_ = bf16[4,16,384]{2,1,0:T(8,128)(2,1)S(1)} collective-permute-done((bf16[4,16,384]{2,1,0:T(8,128)(2,1)S(1)}, bf16[4,16,384]{2,1,0:T(8,128)(2,1)S(1)}, u32[]{:S(2)}, u32[]{:S(2)}) %collective-permute-start.19) | collective-permute-done | bytes 49184 | tf_op jit(solution)/shard_map/ppermute | solution.py:358
  56.7 0.6 %collective-permute-done.20.refs_7_ = bf16[4,16,384]{2,1,0:T(8,128)(2,1)S(1)} collective-permute-done((bf16[4,16,384]{2,1,0:T(8,128)(2,1)S(1)}, bf16[4,16,384]{2,1,0:T(8,128)(2,1)S(1)}, u32[]{:S(2)}, u32[]{:S(2)}) %collective-permute-start.20) | collective-permute-done | bytes 49184 | tf_op jit(solution)/shard_map/ppermute | solution.py:358
  57.3 0.8 %shard_map.63 = bf16[4,16,3072]{2,1,0:T(8,128)(2,1)} custom-call(bf16[4,16,384]{2,1,0:T(8,128)(2,1)S(1)} %get-tuple-element.48.refs_11_.refs_0_, bf16[4,16,384]{2,1,0:T(8,128)(2,1)S(1)} %collective-permute-done.9.refs_1_, bf16[4,16,384]{2,1,0:T(8,128)(2,1)S(1)} %collective-permute-done.10.refs_2_, bf16[4,16,384]{2,1,0:T(8,128)(2,1)S(1)} %collective-permute-done.11.refs_3_, ...), custom_call_target="tpu_custom_call" | custom-call | tf_op jit(solution)/shard_map/pallas_call | solution.py:346
  (9 shorter events, 0.0 us)
Async XLA Ops:
  0.0 12.9 %copy-start = (bf16[4,16,3072]{2,1,0:T(8,128)(2,1)S(1)}, bf16[4,16,3072]{2,1,0:T(8,128)(2,1)}, u32[]{:S(2)}) copy-start(bf16[4,16,3072]{2,1,0:T(8,128)(2,1)} %refs_1_.3) | copy-start | bytes 1179652
  0.0 12.9 %copy-start.1 = (bf16[4,16,3072]{2,1,0:T(8,128)(2,1)S(1)}, bf16[4,16,3072]{2,1,0:T(8,128)(2,1)}, u32[]{:S(2)}) copy-start(bf16[4,16,3072]{2,1,0:T(8,128)(2,1)} %refs_2_.1) | copy-start | bytes 1179652
  2.9 7.0 %copy-start.7 = (f32[8,128]{1,0:T(8,128)S(1)}, f32[8,128]{1,0:T(8,128)}, u32[]{:S(2)}) copy-start(f32[8,128]{1,0:T(8,128)} %get-tuple-element.34._) | copy-start | bytes 12292
  2.9 14.9 %collective-permute-start.3 = (bf16[4,16,768]{2,1,0:T(8,128)(2,1)}, bf16[4,16,768]{2,1,0:T(8,128)(2,1)S(1)}, u32[]{:S(2)}, u32[]{:S(2)}) collective-permute-start(bf16[4,16,768]{2,1,0:T(8,128)(2,1)} %get-tuple-element.41), channel_id=1, source_target_pairs={{0,4},{4,8},{8,12},{12,0},{1,5},{5,9},{9,13},{13,1},{2,6},{6,10},{... | collective-permute-start | bytes 294920 | tf_op jit(solution)/shard_map/ppermute | solution.py:358
  6.0 14.4 %collective-permute-start.4 = (bf16[4,16,768]{2,1,0:T(8,128)(2,1)}, bf16[4,16,768]{2,1,0:T(8,128)(2,1)S(1)}, u32[]{:S(2)}, u32[]{:S(2)}) collective-permute-start(bf16[4,16,768]{2,1,0:T(8,128)(2,1)} %get-tuple-element.42), channel_id=1, source_target_pairs={{0,8},{4,12},{8,0},{12,4},{1,9},{5,13},{9,1},{13,5},{2,10},{6,14},... | collective-permute-start | bytes 294920 | tf_op jit(solution)/shard_map/ppermute | solution.py:358
  8.5 1.4 %copy-start.8 = (s32[16]{0:T(128)S(1)}, s32[16]{0:T(128)}, u32[]{:S(2)}) copy-start(s32[16]{0:T(128)} %tokens_ref.5) | copy-start | bytes 196
  8.6 11.8 %collective-permute-start.5 = (bf16[4,16,768]{2,1,0:T(8,128)(2,1)}, bf16[4,16,768]{2,1,0:T(8,128)(2,1)S(1)}, u32[]{:S(2)}, u32[]{:S(2)}) collective-permute-start(bf16[4,16,768]{2,1,0:T(8,128)(2,1)} %get-tuple-element.43), channel_id=1, source_target_pairs={{0,12},{4,0},{8,4},{12,8},{1,13},{5,1},{9,5},{13,9},{2,14},{6,2},{... | collective-permute-start | bytes 294920 | tf_op jit(solution)/shard_map/ppermute | solution.py:358
  9.9 0.7 %copy-start.6 = (s32[16,32]{1,0:T(8,128)S(1)}, s32[16,32]{1,0:T(8,128)}, u32[]{:S(2)}) copy-start(s32[16,32]{1,0:T(8,128)} %pair_ref.1) | copy-start | bytes 6148
  12.9 3.6 %copy-start.4 = (f32[4,576]{1,0:T(4,128)}, f32[4,576]{1,0:T(4,128)S(1)}, u32[]{:S(2)}) copy-start(f32[4,576]{1,0:T(4,128)S(1)} %get-tuple-element.35.refs_3_.bias_ref) | copy-start | bytes 27652
  12.9 1.0 %copy-start.2 = (bf16[4,16,3072]{2,1,0:T(8,128)(2,1)S(1)}, bf16[4,16,3072]{2,1,0:T(8,128)(2,1)}, u32[]{:S(2)}) copy-start(bf16[4,16,3072]{2,1,0:T(8,128)(2,1)} %refs_0_.5) | copy-start | bytes 1179652
  13.9 6.5 %copy-start.10 = (bf16[4,16,768]{2,1,0:T(8,128)(2,1)S(1)}, bf16[4,16,768]{2,1,0:T(8,128)(2,1)}, u32[]{:S(2)}) copy-start(bf16[4,16,768]{2,1,0:T(8,128)(2,1)} %get-tuple-element.40.refs_0_.refs_4_) | copy-start | bytes 294916
  16.5 8.7 %collective-permute-start = (bf16[4,16,1152]{2,1,0:T(8,128)(2,1)S(1)}, bf16[4,16,1152]{2,1,0:T(8,128)(2,1)S(1)}, u32[]{:S(2)}, u32[]{:S(2)}) collective-permute-start(bf16[4,16,1152]{2,1,0:T(8,128)(2,1)S(1)} %get-tuple-element.37), channel_id=1, source_target_pairs={{0,4},{4,8},{8,12},{12,0},{1,5},{5,9},{9,13},{13,1},{2,6},{6,10},{... | collective-permute-start | bytes 442376 | tf_op jit(solution)/shard_map/ppermute | solution.py:358
  17.2 12.3 %collective-permute-start.1 = (bf16[4,16,1152]{2,1,0:T(8,128)(2,1)S(1)}, bf16[4,16,1152]{2,1,0:T(8,128)(2,1)S(1)}, u32[]{:S(2)}, u32[]{:S(2)}) collective-permute-start(bf16[4,16,1152]{2,1,0:T(8,128)(2,1)S(1)} %get-tuple-element.38), channel_id=1, source_target_pairs={{0,8},{4,12},{8,0},{12,4},{1,9},{5,13},{9,1},{13,5},{2,10},{6,14},... | collective-permute-start | bytes 442376 | tf_op jit(solution)/shard_map/ppermute | solution.py:358
  17.8 11.8 %collective-permute-start.2 = (bf16[4,16,1152]{2,1,0:T(8,128)(2,1)S(1)}, bf16[4,16,1152]{2,1,0:T(8,128)(2,1)S(1)}, u32[]{:S(2)}, u32[]{:S(2)}) collective-permute-start(bf16[4,16,1152]{2,1,0:T(8,128)(2,1)S(1)} %get-tuple-element.39), channel_id=1, source_target_pairs={{0,12},{4,0},{8,4},{12,8},{1,13},{5,1},{9,5},{13,9},{2,14},{6,2},{... | collective-permute-start | bytes 442376 | tf_op jit(solution)/shard_map/ppermute | solution.py:358
  20.4 1.0 %copy-start.3 = (bf16[4,16,3072]{2,1,0:T(8,128)(2,1)S(1)}, bf16[4,16,3072]{2,1,0:T(8,128)(2,1)}, u32[]{:S(2)}) copy-start(bf16[4,16,3072]{2,1,0:T(8,128)(2,1)} %refs_0_.5) | copy-start | bytes 1179652
  21.0 15.7 %collective-permute-start.6 = (bf16[2,4,16,768]{3,2,1,0:T(8,128)(2,1)S(1)}, bf16[2,4,16,768]{3,2,1,0:T(8,128)(2,1)S(1)}, u32[]{:S(2)}, u32[]{:S(2)}) collective-permute-start(bf16[2,4,16,768]{3,2,1,0:T(8,128)(2,1)S(1)} %get-tuple-element.45.refs_1_.refs_4_), channel_id=1, source_target_pairs={{0,1},{1,2},{2,3},{3,0},{4,5},{5,6},{6,7},{7,4},{8,9},{9,10},{10,1... | collective-permute-start | bytes 589832 | tf_op jit(solution)/shard_map/ppermute | solution.py:358
  22.6 14.1 %collective-permute-start.7 = (bf16[1,4,16,768]{3,2,1,0:T(8,128)(2,1)S(1)}, bf16[1,4,16,768]{3,2,1,0:T(8,128)(2,1)S(1)}, u32[]{:S(2)}, u32[]{:S(2)}) collective-permute-start(bf16[1,4,16,768]{3,2,1,0:T(8,128)(2,1)S(1)} %get-tuple-element.46), channel_id=1, source_target_pairs={{0,2},{1,3},{2,0},{3,1},{4,6},{5,7},{6,4},{7,5},{8,10},{9,11},{10,... | collective-permute-start | bytes 294920 | tf_op jit(solution)/shard_map/ppermute | solution.py:358
  25.2 13.1 %collective-permute-start.8 = (bf16[2,4,16,768]{3,2,1,0:T(8,128)(2,1)S(1)}, bf16[2,4,16,768]{3,2,1,0:T(8,128)(2,1)S(1)}, u32[]{:S(2)}, u32[]{:S(2)}) collective-permute-start(bf16[2,4,16,768]{3,2,1,0:T(8,128)(2,1)S(1)} %get-tuple-element.47), channel_id=1, source_target_pairs={{0,3},{1,0},{2,1},{3,2},{4,7},{5,4},{6,5},{7,6},{8,11},{9,8},{10,9... | collective-permute-start | bytes 589832 | tf_op jit(solution)/shard_map/ppermute | solution.py:358
  29.6 6.2 %collective-permute-start.12 = (bf16[4,16,384]{2,1,0:T(8,128)(2,1)S(1)}, bf16[4,16,384]{2,1,0:T(8,128)(2,1)S(1)}, u32[]{:S(2)}, u32[]{:S(2)}) collective-permute-start(bf16[4,16,384]{2,1,0:T(8,128)(2,1)S(1)} %get-tuple-element.53), channel_id=1, source_target_pairs={{0,4},{4,8},{8,12},{12,0},{1,5},{5,9},{9,13},{13,1},{2,6},{6,10},{... | collective-permute-start | bytes 147464 | tf_op jit(solution)/shard_map/ppermute | solution.py:358
  29.6 12.5 %collective-permute-start.13 = (bf16[4,16,384]{2,1,0:T(8,128)(2,1)}, bf16[4,16,384]{2,1,0:T(8,128)(2,1)}, u32[]{:S(2)}, u32[]{:S(2)}) collective-permute-start(bf16[4,16,384]{2,1,0:T(8,128)(2,1)} %get-tuple-element.54), channel_id=1, source_target_pairs={{0,8},{4,12},{8,0},{12,4},{1,9},{5,13},{9,1},{13,5},{2,10},{6,14},... | collective-permute-start | bytes 147464 | tf_op jit(solution)/shard_map/ppermute | solution.py:358
  32.8 6.8 %copy-start.5 = (f32[4,576]{1,0:T(4,128)S(1)}, f32[4,576]{1,0:T(4,128)}, u32[]{:S(2)}) copy-start(f32[4,576]{1,0:T(4,128)} %copy-done.4) | copy-start | bytes 27652
  35.8 6.4 %collective-permute-start.14 = (bf16[4,16,384]{2,1,0:T(8,128)(2,1)S(1)}, bf16[4,16,384]{2,1,0:T(8,128)(2,1)S(1)}, u32[]{:S(2)}, u32[]{:S(2)}) collective-permute-start(bf16[4,16,384]{2,1,0:T(8,128)(2,1)S(1)} %get-tuple-element.55), channel_id=1, source_target_pairs={{0,12},{4,0},{8,4},{12,8},{1,13},{5,1},{9,5},{13,9},{2,14},{6,2},{... | collective-permute-start | bytes 147464 | tf_op jit(solution)/shard_map/ppermute | solution.py:358
  36.7 8.1 %collective-permute-start.15 = (bf16[2,4,16,768]{3,2,1,0:T(8,128)(2,1)S(1)}, bf16[2,4,16,768]{3,2,1,0:T(8,128)(2,1)S(1)}, u32[]{:S(2)}, u32[]{:S(2)}) collective-permute-start(bf16[2,4,16,768]{3,2,1,0:T(8,128)(2,1)S(1)} %get-tuple-element.56), channel_id=1, source_target_pairs={{0,1},{1,2},{2,3},{3,0},{4,5},{5,6},{6,7},{7,4},{8,9},{9,10},{10,1... | collective-permute-start | bytes 589832 | tf_op jit(solution)/shard_map/ppermute | solution.py:358
  36.7 3.0 %copy-start.9 = (s32[16]{0:T(128)S(1)}, s32[16]{0:T(128)}, u32[]{:S(2)}) copy-start(s32[16]{0:T(128)} %tokens_ref.5) | copy-start | bytes 196
  36.7 8.1 %collective-permute-start.16 = (bf16[1,4,16,768]{3,2,1,0:T(8,128)(2,1)S(1)}, bf16[1,4,16,768]{3,2,1,0:T(8,128)(2,1)S(1)}, u32[]{:S(2)}, u32[]{:S(2)}) collective-permute-start(bf16[1,4,16,768]{3,2,1,0:T(8,128)(2,1)S(1)} %get-tuple-element.57), channel_id=1, source_target_pairs={{0,2},{1,3},{2,0},{3,1},{4,6},{5,7},{6,4},{7,5},{8,10},{9,11},{10,... | collective-permute-start | bytes 294920 | tf_op jit(solution)/shard_map/ppermute | solution.py:358
  38.3 6.7 %collective-permute-start.17 = (bf16[2,4,16,768]{3,2,1,0:T(8,128)(2,1)S(1)}, bf16[2,4,16,768]{3,2,1,0:T(8,128)(2,1)S(1)}, u32[]{:S(2)}, u32[]{:S(2)}) collective-permute-start(bf16[2,4,16,768]{3,2,1,0:T(8,128)(2,1)S(1)} %get-tuple-element.58), channel_id=1, source_target_pairs={{0,3},{1,0},{2,1},{3,2},{4,7},{5,4},{6,5},{7,6},{8,11},{9,8},{10,9... | collective-permute-start | bytes 589832 | tf_op jit(solution)/shard_map/ppermute | solution.py:358
  42.1 9.3 %collective-permute-start.9 = (bf16[4,16,384]{2,1,0:T(8,128)(2,1)S(1)}, bf16[4,16,384]{2,1,0:T(8,128)(2,1)S(1)}, u32[]{:S(2)}, u32[]{:S(2)}) collective-permute-start(bf16[4,16,384]{2,1,0:T(8,128)(2,1)S(1)} %get-tuple-element.49), channel_id=1, source_target_pairs={{0,12},{4,0},{8,4},{12,8},{1,13},{5,1},{9,5},{13,9},{2,14},{6,2},{... | collective-permute-start | bytes 147464 | tf_op jit(solution)/shard_map/ppermute | solution.py:358
  42.2 9.9 %collective-permute-start.10 = (bf16[4,16,384]{2,1,0:T(8,128)(2,1)S(1)}, bf16[4,16,384]{2,1,0:T(8,128)(2,1)S(1)}, u32[]{:S(2)}, u32[]{:S(2)}) collective-permute-start(bf16[4,16,384]{2,1,0:T(8,128)(2,1)S(1)} %get-tuple-element.50), channel_id=1, source_target_pairs={{0,8},{4,12},{8,0},{12,4},{1,9},{5,13},{9,1},{13,5},{2,10},{6,14},... | collective-permute-start | bytes 147464 | tf_op jit(solution)/shard_map/ppermute | solution.py:358
  44.8 7.3 %collective-permute-start.11 = (bf16[4,16,384]{2,1,0:T(8,128)(2,1)S(1)}, bf16[4,16,384]{2,1,0:T(8,128)(2,1)S(1)}, u32[]{:S(2)}, u32[]{:S(2)}) collective-permute-start(bf16[4,16,384]{2,1,0:T(8,128)(2,1)S(1)} %get-tuple-element.51), channel_id=1, source_target_pairs={{0,4},{4,8},{8,12},{12,0},{1,5},{5,9},{9,13},{13,1},{2,6},{6,10},{... | collective-permute-start | bytes 147464 | tf_op jit(solution)/shard_map/ppermute | solution.py:358
  47.7 5.8 %collective-permute-start.18 = (bf16[4,16,384]{2,1,0:T(8,128)(2,1)S(1)}, bf16[4,16,384]{2,1,0:T(8,128)(2,1)S(1)}, u32[]{:S(2)}, u32[]{:S(2)}) collective-permute-start(bf16[4,16,384]{2,1,0:T(8,128)(2,1)S(1)} %get-tuple-element.60), channel_id=1, source_target_pairs={{0,12},{4,0},{8,4},{12,8},{1,13},{5,1},{9,5},{13,9},{2,14},{6,2},{... | collective-permute-start | bytes 147464 | tf_op jit(solution)/shard_map/ppermute | solution.py:358
  51.4 5.3 %collective-permute-start.19 = (bf16[4,16,384]{2,1,0:T(8,128)(2,1)S(1)}, bf16[4,16,384]{2,1,0:T(8,128)(2,1)S(1)}, u32[]{:S(2)}, u32[]{:S(2)}) collective-permute-start(bf16[4,16,384]{2,1,0:T(8,128)(2,1)S(1)} %get-tuple-element.61), channel_id=1, source_target_pairs={{0,8},{4,12},{8,0},{12,4},{1,9},{5,13},{9,1},{13,5},{2,10},{6,14},... | collective-permute-start | bytes 147464 | tf_op jit(solution)/shard_map/ppermute | solution.py:358
  51.4 5.9 %collective-permute-start.20 = (bf16[4,16,384]{2,1,0:T(8,128)(2,1)S(1)}, bf16[4,16,384]{2,1,0:T(8,128)(2,1)S(1)}, u32[]{:S(2)}, u32[]{:S(2)}) collective-permute-start(bf16[4,16,384]{2,1,0:T(8,128)(2,1)S(1)} %get-tuple-element.62), channel_id=1, source_target_pairs={{0,4},{4,8},{8,12},{12,0},{1,5},{5,9},{9,13},{13,1},{2,6},{6,10},{... | collective-permute-start | bytes 147464 | tf_op jit(solution)/shard_map/ppermute | solution.py:358
where the time goes:
time: 58.4 us; the launch traced here: 58.1 us
  starting transfers between devices  26.7 us (46%)
  Pallas kernels  16 us (27%)
  waiting for transfers between devices  13.1 us (22%)
  local copies, waits for them, and re-layouts  2.05 us (4%)
    ppermute x21, starting transfers between devices, shifted(): lax.ppermute(array, axis, [(i, (i + distance) % count) for i in range(cou...  26.7 us
    ppermute x21, waiting for transfers between devices, shifted(): lax.ppermute(array, axis, [(i, (i + distance) % count) for i in range(cou...  13.1 us
    pallas_call x3, Pallas kernels, rotate_pieces(): pl.pallas_call(functools.partial(rotate_kernel, message, sources, count_h...  6.67 us
    pallas_call x2, Pallas kernels, attend(): pl.pallas_call(functools.partial(attend_kernel, (count_head, count_tm, le...  5.15 us
    pallas_call x1, Pallas kernels, plan(): pl.pallas_call(functools.partial(plan_kernel, count_head, count_tm, block...  2.25 us
    unnamed x22, local copies, waits for them, and re-layouts  2.05 us
    pallas_call x2, Pallas kernels, pick_blocks(): pl.pallas_call(functools.partial(pick_kernel, count_head, count_tm, lanes...  1.18 us
  transfers between devices with their start and end apart: 21, of which 7 were waited for; matrix products, arithmetic and copies ran while one was open for 0% of the time, Pallas kernels for 21%

commit v1 on v0

--- a/solution.py
+++ b/solution.py
@@ -49,10 +49,18 @@
     return fields, at
 
 
+def by_distance(refs, count, direction):
+    if len(refs) > 1:
+        return list(refs)
+    me = lax.axis_index("head")
+    return [refs[0].at[lax.rem(me + direction * s + count, count)] for s in range(count)]
+
+
 def rotate_kernel(message, sources, count_head, skipped, *refs):
     fields, total = fields_of(message)
     ins = dict(zip(sources, refs))
-    outs, (token, buffer, sems) = refs[len(sources) + skipped : -3], refs[-3:]
+    outs = by_distance(refs[len(sources) + skipped : -3], count_head, 1)
+    token, buffer, sems = refs[-3:]
     token[...] = jnp.zeros_like(token)
     blocks, tokens, width = refs[0].shape
     width_here = width // count_head
@@ -84,17 +92,18 @@
                 outs[s][:, :, at : at + HD] = turned[h].astype(jnp.bfloat16)
 
 
-def rotate_pieces(arrays, message, count_head, after=(), limit=VMEM):
+def rotate_pieces(arrays, message, count_head, after=(), limit=VMEM, stacked=False):
     blocks, tokens, _ = arrays[0].shape
     fields, total = fields_of(message)
     sources = sorted({source for source, _, _ in message})
     one = (blocks, tokens, total)
+    shapes = [(count_head,) + one] if stacked else [one] * count_head
     *pieces, token = pl.pallas_call(
         functools.partial(rotate_kernel, message, sources, count_head, len(after)),
         in_specs=[pl.BlockSpec(memory_space=pltpu.HBM)] * len(sources)
         + [pl.BlockSpec(memory_space=pl.ANY)] * len(after),
-        out_specs=[pl.BlockSpec(memory_space=pltpu.VMEM)] * (count_head + 1),
-        out_shape=[jax.ShapeDtypeStruct(one, jnp.bfloat16)] * count_head + [TOKEN],
+        out_specs=[pl.BlockSpec(memory_space=pltpu.VMEM)] * (len(shapes) + 1),
+        out_shape=[jax.ShapeDtypeStruct(shape, jnp.bfloat16) for shape in shapes] + [TOKEN],
         scratch_shapes=[
             pltpu.VMEM((count_head,) + one, jnp.bfloat16),
             pltpu.SemaphoreType.DMA((count_head, len(fields))),
@@ -248,11 +257,11 @@
 
 
 def attend_kernel(counts, at, size, tokens_ref, bias_ref, *refs):
-    count_head, count_tm, skipped = counts
+    count_head, count_tm, query_count, skipped = counts
     query_at, key_at = at
-    queries, owns = refs[:count_head], refs[count_head : 2 * count_head]
-    slots = refs[2 * count_head : 2 * count_head + count_tm - 1]
-    outs = refs[2 * count_head + count_tm - 1 + skipped :]
+    queries, refs = by_distance(refs[:query_count], count_head, -1), refs[query_count:]
+    owns, slots = refs[:count_head], refs[count_head : count_head + count_tm - 1]
+    outs = refs[count_head + count_tm - 1 + skipped :]
     blocks, tokens, _ = owns[0].shape
     shard = lax.axis_index("tm")
     me = lax.axis_index("head")
@@ -308,10 +317,13 @@
     vmem = pl.BlockSpec(memory_space=pltpu.VMEM)
     return pl.pallas_call(
         functools.partial(
-            attend_kernel, (count_head, count_tm, len(after)), (query_at, key_at), size
+            attend_kernel,
+            (count_head, count_tm, len(queries), len(after)),
+            (query_at, key_at),
+            size,
         ),
         in_specs=[pl.BlockSpec(memory_space=pltpu.SMEM)]
-        + [vmem] * (2 * count_head + count_tm)
+        + [vmem] * (len(queries) + count_head + count_tm)
         + [pl.BlockSpec(memory_space=pl.ANY)] * len(after),
         out_specs=[vmem] * count_head,
         out_shape=[jax.ShapeDtypeStruct((blocks, tokens, size), jnp.bfloat16)] * count_head,
@@ -377,37 +389,28 @@
     cut = (heads + 1) // 2 * HD
     parts = [(0, cut), (cut, width_here - cut)] if heads > 1 else [(0, width_here)]
     arrays = [query_rows, key_rows, value_rows]
-    messages = []
-    for at, part in enumerate(parts):
-        message = [(1,) + part, (2,) + part]
-        messages.append(message + ([(0,) + parts[at - 1]] if at else []))
-    messages.append([(0,) + parts[-1]])
-    key_at = [0] * len(parts)
-    query_at = [2 * size for _, size in parts[1:]] + [0]
-
+    messages = [[(1,) + part, (2,) + part] for part in parts]
     pieces, token = rotate_pieces(arrays, messages[0], count_head, limit=WIDE_VMEM)
     packed = [pieces]
     picks, bias = plan(pair_list, block_tokens, token, blocks, count_head, count_tm)
     after = (bias,)
-    for message in messages[1:-1]:
+    for message in messages[1:]:
         pieces, token = rotate_pieces(arrays, message, count_head, after)
         packed.append(pieces)
         after = (token,)
     received = [exchange(pieces, 1) for pieces in packed]
     sent, after = [], ()
-    for at, (_, size) in enumerate(parts):
-        lanes = (key_at[at], key_at[at] + 2 * size)
-        sent.append(pick_blocks(picks, received[at], lanes, count_tm, after))
+    for owns, (_, size) in zip(received, parts):
+        sent.append(pick_blocks(picks, owns, (0, 2 * size), count_tm, after))
         after = (sent[-1][0],)
-        if not at:
-            pieces, _ = rotate_pieces(arrays, messages[-1], count_head, after)
-    received.append(exchange(pieces, 1))
+    message = [(0, 0, width_here)]
+    (query,), _ = rotate_pieces(arrays, message, count_head, (sent[0][0],), stacked=True)
+    query = lax.all_to_all(query, "head", split_axis=0, concat_axis=0, tiled=True)
     returned, after = [], ()
-    for at, (_, size) in enumerate(parts):
+    for at, (start, size) in enumerate(parts):
         cost = NO_COST if at == len(parts) - 1 else HIGH_COST
         attended = attend(
-            block_tokens, bias, received[at + 1], query_at[at], received[at], key_at[at],
-            forward(sent[at]), size, after, cost,
+            block_tokens, bias, [query], start, received[at], 0, forward(sent[at]), size, after, cost
         )
         after = (attended[0],)
         returned.append(exchange(attended, -1))

time: 58.4 us -> 56 us (0.959)
  starting transfers between devices: 26.7 us -> 25.1 us
  local copies, waits for them, and re-layouts: 2.05 us -> 1.06 us
  waiting for transfers between devices: 13.1 us -> 13.9 us
    ppermute x21 -> x18, starting transfers between devices: 26.7 us -> 21.6 us  [shifted(): lax.ppermute(array, axis, [(i, (i + distance) % count) for i in range(cou...]
    all_to_all x0 -> x1, waiting for transfers between devices: none -> 4.83 us  [shards(): lax.all_to_all(query, 'head', split_axis=0, concat_axis=0, tiled=True)]
    ppermute x21 -> x18, waiting for transfers between devices: 13.1 us -> 9.04 us  [shifted(): lax.ppermute(array, axis, [(i, (i + distance) % count) for i in range(cou...]
    all_to_all x0 -> x1, starting transfers between devices: none -> 3.47 us  [shards(): lax.all_to_all(query, 'head', split_axis=0, concat_axis=0, tiled=True)]
    unnamed x22 -> x20, local copies, waits for them, and re-layouts: 2.05 us -> 1.06 us
  transfers between devices with their start and end apart: 21 -> 19, of which waited for: 7 -> 6; matrix products, arithmetic and copies ran while one was open for 0% -> 0% of each run, Pallas kernels for 21% -> 21%
where the time goes in v1:
time: 56 us; the launch traced here: 55.7 us
  starting transfers between devices  25.1 us (45%)
  Pallas kernels  15.5 us (28%)
  waiting for transfers between devices  13.9 us (25%)
  local copies, waits for them, and re-layouts  1.06 us (2%)
    ppermute x18, starting transfers between devices, shifted(): lax.ppermute(array, axis, [(i, (i + distance) % count) for i in range(cou...  21.6 us
    ppermute x18, waiting for transfers between devices, shifted(): lax.ppermute(array, axis, [(i, (i + distance) % count) for i in range(cou...  9.04 us
    pallas_call x3, Pallas kernels, rotate_pieces(): pl.pallas_call(functools.partial(rotate_kernel, message, sources, count_h...  6.39 us
    pallas_call x2, Pallas kernels, attend(): pl.pallas_call(functools.partial(attend_kernel, (count_head, count_tm, le...  4.86 us
    all_to_all x1, waiting for transfers between devices, shards(): lax.all_to_all(query, 'head', split_axis=0, concat_axis=0, tiled=True)  4.83 us
    all_to_all x1, starting transfers between devices, shards(): lax.all_to_all(query, 'head', split_axis=0, concat_axis=0, tiled=True)  3.47 us
    pallas_call x1, Pallas kernels, plan(): pl.pallas_call(functools.partial(plan_kernel, count_head, count_tm, block...  2.25 us
    pallas_call x2, Pallas kernels, pick_blocks(): pl.pallas_call(functools.partial(pick_kernel, count_head, count_tm, lanes...  1.18 us
  transfers between devices with their start and end apart: 19, of which 6 were waited for; matrix products, arithmetic and copies ran while one was open for 0% of the time, Pallas kernels for 21%

profile of v1, /device:TPU:0, one launch (start us, length us, event | category | flops | bytes accessed | tf_op | source)
XLA Modules:
  0.0 55.7 jit_solution(16404041266382097266)
XLA Ops:
  0.0 0.0 copy-start
  0.0 0.0 copy-start.1
  0.0 2.9 %shard_map.55 = (bf16[4,16,768]{2,1,0:T(8,128)(2,1)}, bf16[4,16,768]{2,1,0:T(8,128)(2,1)}, bf16[4,16,768]{2,1,0:T(8,128)(2,1)}, bf16[4,16,768]{2,1,0:T(8,128)(2,1)}, f32[8,128]{1,0:T(8,128)}) custom-call(bf16[4,16,3072]{2,1,0:T(8,128)(2,1)} %refs_0_.5, bf16[4,16,3072]{2,1,0:T(8,128)(2,1)} %refs_1_.3), custom_call_target="tpu_custom_call" | custom-call | tf_op jit(solution)/shard_map/pallas_call | solution.py:101
  2.9 0.0 copy-start.6
  2.9 3.1 %collective-permute-start = (bf16[4,16,768]{2,1,0:T(8,128)(2,1)}, bf16[4,16,768]{2,1,0:T(8,128)(2,1)S(1)}, u32[]{:S(2)}, u32[]{:S(2)}) collective-permute-start(bf16[4,16,768]{2,1,0:T(8,128)(2,1)} %get-tuple-element.35), channel_id=1, source_target_pairs={{0,4},{4,8},{8,12},{12,0},{1,5},{5,9},{9,13},{13,1},{2,6},{6,10},{... | collective-permute-start | bytes 294920 | tf_op jit(solution)/shard_map/ppermute | solution.py:370
  6.0 2.6 %collective-permute-start.1 = (bf16[4,16,768]{2,1,0:T(8,128)(2,1)}, bf16[4,16,768]{2,1,0:T(8,128)(2,1)S(1)}, u32[]{:S(2)}, u32[]{:S(2)}) collective-permute-start(bf16[4,16,768]{2,1,0:T(8,128)(2,1)} %get-tuple-element.36), channel_id=1, source_target_pairs={{0,8},{4,12},{8,0},{12,4},{1,9},{5,13},{9,1},{13,5},{2,10},{6,14},... | collective-permute-start | bytes 294920 | tf_op jit(solution)/shard_map/ppermute | solution.py:370
  8.6 1.3 %collective-permute-start.2 = (bf16[4,16,768]{2,1,0:T(8,128)(2,1)}, bf16[4,16,768]{2,1,0:T(8,128)(2,1)S(1)}, u32[]{:S(2)}, u32[]{:S(2)}) collective-permute-start(bf16[4,16,768]{2,1,0:T(8,128)(2,1)} %get-tuple-element.37), channel_id=1, source_target_pairs={{0,12},{4,0},{8,4},{12,8},{1,13},{5,1},{9,5},{13,9},{2,14},{6,2},{... | collective-permute-start | bytes 294920 | tf_op jit(solution)/shard_map/ppermute | solution.py:370
  9.9 0.0 copy-done.6
  9.9 0.0 copy-done.7
  9.9 0.7 %copy-done.5 = s32[16,32]{1,0:T(8,128)S(1)} copy-done((s32[16,32]{1,0:T(8,128)S(1)}, s32[16,32]{1,0:T(8,128)}, u32[]{:S(2)}) %copy-start.5) | copy-done | bytes 2072
  10.6 2.3 %shard_map.56 = (s32[8]{0:T(128)S(1)}, f32[4,576]{1,0:T(4,128)S(1)}) custom-call(s32[16,32]{1,0:T(8,128)S(1)} %copy-done.5, s32[16]{0:T(128)S(1)} %copy-done.7, f32[8,128]{1,0:T(8,128)S(1)} %copy-done.6), custom_call_target="tpu_custom_call" | custom-call | tf_op jit(solution)/shard_map/pallas_call | solution.py:237
  12.9 0.0 copy-start.3
  12.9 0.0 copy-done
  12.9 0.0 copy-done.1
  12.9 0.0 copy-start.9
  12.9 1.9 %shard_map.60 = (bf16[4,16,768]{2,1,0:T(8,128)(2,1)S(1)}, bf16[4,16,768]{2,1,0:T(8,128)(2,1)S(1)}, bf16[4,16,768]{2,1,0:T(8,128)(2,1)S(1)}, bf16[4,16,768]{2,1,0:T(8,128)(2,1)S(1)}, f32[8,128]{1,0:T(8,128)}) custom-call(bf16[4,16,3072]{2,1,0:T(8,128)(2,1)S(1)} %copy-done, bf16[4,16,3072]{2,1,0:T(8,128)(2,1)S(1)} %copy-done.1, ...), custom_call_target="tpu_custom_call" | custom-call | tf_op jit(solution)/shard_map/pallas_call | solution.py:101
  14.8 0.0 copy-done.3
  14.8 0.7 %collective-permute-start.9 = (bf16[4,16,768]{2,1,0:T(8,128)(2,1)S(1)}, bf16[4,16,768]{2,1,0:T(8,128)(2,1)S(1)}, u32[]{:S(2)}, u32[]{:S(2)}) collective-permute-start(bf16[4,16,768]{2,1,0:T(8,128)(2,1)S(1)} %get-tuple-element.47), channel_id=1, source_target_pairs={{0,4},{4,8},{8,12},{12,0},{1,5},{5,9},{9,13},{13,1},{2,6},{6,10},{... | collective-permute-start | bytes 294920 | tf_op jit(solution)/shard_map/ppermute | solution.py:370
  15.6 0.5 collective-permute-start.10
  16.1 0.0 collective-permute-done.refs_1_.refs_2_
  16.1 2.6 %collective-permute-start.11 = (bf16[4,16,768]{2,1,0:T(8,128)(2,1)S(1)}, bf16[4,16,768]{2,1,0:T(8,128)(2,1)S(1)}, u32[]{:S(2)}, u32[]{:S(2)}) collective-permute-start(bf16[4,16,768]{2,1,0:T(8,128)(2,1)S(1)} %get-tuple-element.49), channel_id=1, source_target_pairs={{0,12},{4,0},{8,4},{12,8},{1,13},{5,1},{9,5},{13,9},{2,14},{6,2},{... | collective-permute-start | bytes 294920 | tf_op jit(solution)/shard_map/ppermute | solution.py:370
  18.7 0.0 collective-permute-done.1.refs_2_.refs_3_
  18.7 0.0 collective-permute-done.2.refs_3_.refs_4_
  18.7 0.0 copy-done.9
  18.7 0.0 copy-start.2
  18.7 0.6 %shard_map.57 = (bf16[2,4,16,768]{3,2,1,0:T(8,128)(2,1)S(1)}, bf16[1,4,16,768]{3,2,1,0:T(8,128)(2,1)S(1)}, bf16[2,4,16,768]{3,2,1,0:T(8,128)(2,1)S(1)}) custom-call(s32[8]{0:T(128)S(1)} %get-tuple-element.33.picks_ref, bf16[4,16,768]{2,1,0:T(8,128)(2,1)S(1)} %copy-done.9, bf16[4,16,768]{2,1,0:T(8,128)(2,1)S(1)} %collective-permute-done.refs_1_.refs_2_, ...), custom_call_target="tpu_custom_call" | custom-call | flops 99999997952 | tf_op jit(solution)/shard_map/pallas_call | solution.py:136
  19.3 0.1 collective-permute-start.3
  19.4 0.3 copy-done.2
  19.7 1.6 %shard_map.58 = (bf16[4,4,16,768]{3,2,1,0:T(8,128)(2,1)}, f32[8,128]{1,0:T(8,128)}) custom-call(bf16[4,16,3072]{2,1,0:T(8,128)(2,1)S(1)} %copy-done.2, bf16[2,4,16,768]{3,2,1,0:T(8,128)(2,1)S(1)} %get-tuple-element.38.refs_1_.refs_4_), custom_call_target="tpu_custom_call" | custom-call | tf_op jit(solution)/shard_map/pallas_call | solution.py:101
  21.4 3.5 %all-to-all-start = ((bf16[4,4,16,768]{3,2,1,0:T(8,128)(2,1)}), bf16[4,4,16,768]{3,2,1,0:T(8,128)(2,1)S(1)}, u32[]{:S(2)}, u32[]{:S(2)}) async-start(bf16[4,4,16,768]{3,2,1,0:T(8,128)(2,1)} %get-tuple-element.39), calls=%async_computation | async-start | bytes 786432 | tf_op jit(solution)/shard_map/all_to_all | solution.py:408
  24.8 1.6 %collective-permute-start.4 = (bf16[1,4,16,768]{3,2,1,0:T(8,128)(2,1)S(1)}, bf16[1,4,16,768]{3,2,1,0:T(8,128)(2,1)S(1)}, u32[]{:S(2)}, u32[]{:S(2)}) collective-permute-start(bf16[1,4,16,768]{3,2,1,0:T(8,128)(2,1)S(1)} %get-tuple-element.40), channel_id=1, source_target_pairs={{0,2},{1,3},{2,0},{3,1},{4,6},{5,7},{6,4},{7,5},{8,10},{9,11},{10,... | collective-permute-start | bytes 294920 | tf_op jit(solution)/shard_map/ppermute | solution.py:370
  26.4 0.0 collective-permute-done.9.refs_1_.refs_2_
  26.4 1.1 %collective-permute-start.5 = (bf16[2,4,16,768]{3,2,1,0:T(8,128)(2,1)S(1)}, bf16[2,4,16,768]{3,2,1,0:T(8,128)(2,1)S(1)}, u32[]{:S(2)}, u32[]{:S(2)}) collective-permute-start(bf16[2,4,16,768]{3,2,1,0:T(8,128)(2,1)S(1)} %get-tuple-element.41), channel_id=1, source_target_pairs={{0,3},{1,0},{2,1},{3,2},{4,7},{5,4},{6,5},{7,6},{8,11},{9,8},{10,9... | collective-permute-start | bytes 589832 | tf_op jit(solution)/shard_map/ppermute | solution.py:370
  27.5 0.0 collective-permute-done.10.refs_2_.refs_3_
  27.5 0.0 collective-permute-done.11.refs_3_.refs_4_
  27.5 0.6 %shard_map.61 = (bf16[2,4,16,768]{3,2,1,0:T(8,128)(2,1)S(1)}, bf16[1,4,16,768]{3,2,1,0:T(8,128)(2,1)S(1)}, bf16[2,4,16,768]{3,2,1,0:T(8,128)(2,1)S(1)}) custom-call(s32[8]{0:T(128)S(1)} %get-tuple-element.33.picks_ref, bf16[4,16,768]{2,1,0:T(8,128)(2,1)S(1)} %get-tuple-element.46.refs_0_.refs_1_, ...), custom_call_target="tpu_custom_call" | custom-call | flops 99999997952 | tf_op jit(solution)/shard_map/pallas_call | solution.py:136
  28.1 0.1 collective-permute-start.12
  28.2 0.0 copy-start.8
  28.2 0.6 %collective-permute-start.13 = (bf16[1,4,16,768]{3,2,1,0:T(8,128)(2,1)S(1)}, bf16[1,4,16,768]{3,2,1,0:T(8,128)(2,1)S(1)}, u32[]{:S(2)}, u32[]{:S(2)}) collective-permute-start(bf16[1,4,16,768]{3,2,1,0:T(8,128)(2,1)S(1)} %get-tuple-element.51), channel_id=1, source_target_pairs={{0,2},{1,3},{2,0},{3,1},{4,6},{5,7},{6,4},{7,5},{8,10},{9,11},{10,... | collective-permute-start | bytes 294920 | tf_op jit(solution)/shard_map/ppermute | solution.py:370
  28.8 1.5 %collective-permute-done.4.refs_6_ = bf16[1,4,16,768]{3,2,1,0:T(8,128)(2,1)S(1)} collective-permute-done((bf16[1,4,16,768]{3,2,1,0:T(8,128)(2,1)S(1)}, bf16[1,4,16,768]{3,2,1,0:T(8,128)(2,1)S(1)}, u32[]{:S(2)}, u32[]{:S(2)}) %collective-permute-start.4) | collective-permute-done | bytes 98336 | tf_op jit(solution)/shard_map/ppermute | solution.py:370
  30.3 0.2 collective-permute-start.14
  30.5 0.0 collective-permute-done.3.refs_5_
  30.5 2.2 %collective-permute-done.5.refs_7_ = bf16[2,4,16,768]{3,2,1,0:T(8,128)(2,1)S(1)} collective-permute-done((bf16[2,4,16,768]{3,2,1,0:T(8,128)(2,1)S(1)}, bf16[2,4,16,768]{3,2,1,0:T(8,128)(2,1)S(1)}, u32[]{:S(2)}, u32[]{:S(2)}) %collective-permute-start.5) | collective-permute-done | bytes 196640 | tf_op jit(solution)/shard_map/ppermute | solution.py:370
  32.8 4.8 %all-to-all-done.refs_0_ = bf16[4,4,16,768]{3,2,1,0:T(8,128)(2,1)S(1)} async-done(((bf16[4,4,16,768]{3,2,1,0:T(8,128)(2,1)}), bf16[4,4,16,768]{3,2,1,0:T(8,128)(2,1)S(1)}, u32[]{:S(2)}, u32[]{:S(2)}) %all-to-all-start) | async-done | bytes 393248 | tf_op jit(solution)/shard_map/all_to_all | solution.py:408
  37.6 0.0 copy-done.4
  37.6 0.0 copy-done.8
  37.6 2.4 %shard_map.59 = (bf16[4,16,384]{2,1,0:T(8,128)(2,1)S(1)}, bf16[4,16,384]{2,1,0:T(8,128)(2,1)S(1)}, bf16[4,16,384]{2,1,0:T(8,128)(2,1)S(1)}, bf16[4,16,384]{2,1,0:T(8,128)(2,1)S(1)}) custom-call(s32[16]{0:T(128)S(1)} %copy-done.8, f32[4,576]{1,0:T(4,128)S(1)} %copy-done.4, bf16[4,4,16,768]{3,2,1,0:T(8,128)(2,1)S(1)} %all-to-all-done.refs_0_, ...), custom_call_target="tpu_custom_call" | custom-call | flops 99999997952 | tf_op jit(solution)/shard_map/pallas_call | solution.py:318
  40.0 1.5 %collective-permute-start.6 = (bf16[4,16,384]{2,1,0:T(8,128)(2,1)S(1)}, bf16[4,16,384]{2,1,0:T(8,128)(2,1)S(1)}, u32[]{:S(2)}, u32[]{:S(2)}) collective-permute-start(bf16[4,16,384]{2,1,0:T(8,128)(2,1)S(1)} %get-tuple-element.43), channel_id=1, source_target_pairs={{0,12},{4,0},{8,4},{12,8},{1,13},{5,1},{9,5},{13,9},{2,14},{6,2},{... | collective-permute-start | bytes 147464 | tf_op jit(solution)/shard_map/ppermute | solution.py:370
  41.6 0.0 collective-permute-start.7
  41.6 0.0 collective-permute-done.13.refs_6_
  41.6 0.6 %collective-permute-start.8 = (bf16[4,16,384]{2,1,0:T(8,128)(2,1)S(1)}, bf16[4,16,384]{2,1,0:T(8,128)(2,1)S(1)}, u32[]{:S(2)}, u32[]{:S(2)}) collective-permute-start(bf16[4,16,384]{2,1,0:T(8,128)(2,1)S(1)} %get-tuple-element.45), channel_id=1, source_target_pairs={{0,4},{4,8},{8,12},{12,0},{1,5},{5,9},{9,13},{13,1},{2,6},{6,10},{... | collective-permute-start | bytes 147464 | tf_op jit(solution)/shard_map/ppermute | solution.py:370
  42.2 0.0 collective-permute-done.12.refs_5_
  42.2 0.0 collective-permute-done.14.refs_7_
  42.2 2.4 %shard_map.62 = (bf16[4,16,384]{2,1,0:T(8,128)(2,1)S(1)}, bf16[4,16,384]{2,1,0:T(8,128)(2,1)S(1)}, bf16[4,16,384]{2,1,0:T(8,128)(2,1)S(1)}, bf16[4,16,384]{2,1,0:T(8,128)(2,1)S(1)}) custom-call(s32[16]{0:T(128)S(1)} %copy-done.8, f32[4,576]{1,0:T(4,128)S(1)} %copy-done.4, bf16[4,4,16,768]{3,2,1,0:T(8,128)(2,1)S(1)} %all-to-all-done.refs_0_, ...), custom_call_target="tpu_custom_call" | custom-call | tf_op jit(solution)/shard_map/pallas_call | solution.py:318
  44.6 3.2 %collective-permute-start.15 = (bf16[4,16,384]{2,1,0:T(8,128)(2,1)S(1)}, bf16[4,16,384]{2,1,0:T(8,128)(2,1)S(1)}, u32[]{:S(2)}, u32[]{:S(2)}) collective-permute-start(bf16[4,16,384]{2,1,0:T(8,128)(2,1)S(1)} %get-tuple-element.54), channel_id=1, source_target_pairs={{0,12},{4,0},{8,4},{12,8},{1,13},{5,1},{9,5},{13,9},{2,14},{6,2},{... | collective-permute-start | bytes 147464 | tf_op jit(solution)/shard_map/ppermute | solution.py:370
  47.9 1.1 %collective-permute-start.16 = (bf16[4,16,384]{2,1,0:T(8,128)(2,1)S(1)}, bf16[4,16,384]{2,1,0:T(8,128)(2,1)S(1)}, u32[]{:S(2)}, u32[]{:S(2)}) collective-permute-start(bf16[4,16,384]{2,1,0:T(8,128)(2,1)S(1)} %get-tuple-element.55), channel_id=1, source_target_pairs={{0,8},{4,12},{8,0},{12,4},{1,9},{5,13},{9,1},{13,5},{2,10},{6,14},... | collective-permute-start | bytes 147464 | tf_op jit(solution)/shard_map/ppermute | solution.py:370
  49.0 0.0 collective-permute-done.6.refs_1_
  49.0 0.6 %collective-permute-start.17 = (bf16[4,16,384]{2,1,0:T(8,128)(2,1)S(1)}, bf16[4,16,384]{2,1,0:T(8,128)(2,1)S(1)}, u32[]{:S(2)}, u32[]{:S(2)}) collective-permute-start(bf16[4,16,384]{2,1,0:T(8,128)(2,1)S(1)} %get-tuple-element.56), channel_id=1, source_target_pairs={{0,4},{4,8},{8,12},{12,0},{1,5},{5,9},{9,13},{13,1},{2,6},{6,10},{... | collective-permute-start | bytes 147464 | tf_op jit(solution)/shard_map/ppermute | solution.py:370
  49.6 0.0 collective-permute-done.7.refs_2_
  49.6 0.0 collective-permute-done.8.refs_3_
  49.6 0.1 collective-permute-done.15.refs_5_
  49.7 3.5 %collective-permute-done.16.refs_6_ = bf16[4,16,384]{2,1,0:T(8,128)(2,1)S(1)} collective-permute-done((bf16[4,16,384]{2,1,0:T(8,128)(2,1)S(1)}, bf16[4,16,384]{2,1,0:T(8,128)(2,1)S(1)}, u32[]{:S(2)}, u32[]{:S(2)}) %collective-permute-start.16) | collective-permute-done | bytes 49184 | tf_op jit(solution)/shard_map/ppermute | solution.py:370
  53.2 1.7 %collective-permute-done.17.refs_7_ = bf16[4,16,384]{2,1,0:T(8,128)(2,1)S(1)} collective-permute-done((bf16[4,16,384]{2,1,0:T(8,128)(2,1)S(1)}, bf16[4,16,384]{2,1,0:T(8,128)(2,1)S(1)}, u32[]{:S(2)}, u32[]{:S(2)}) %collective-permute-start.17) | collective-permute-done | bytes 49184 | tf_op jit(solution)/shard_map/ppermute | solution.py:370
  54.9 0.8 %shard_map.63 = bf16[4,16,3072]{2,1,0:T(8,128)(2,1)} custom-call(bf16[4,16,384]{2,1,0:T(8,128)(2,1)S(1)} %get-tuple-element.42.refs_8_.refs_0_, bf16[4,16,384]{2,1,0:T(8,128)(2,1)S(1)} %collective-permute-done.6.refs_1_, bf16[4,16,384]{2,1,0:T(8,128)(2,1)S(1)} %collective-permute-done.7.refs_2_, bf16[4,16,384]{2,1,0:T(8,128)(2,1)S(1)} %collective-permute-done.8.refs_3_, ...), custom_call_target="tpu_custom_call" | custom-call | tf_op jit(solution)/shard_map/pallas_call | solution.py:358
  (3 shorter events, 0.0 us)
Async XLA Ops:
  0.0 12.9 %copy-start = (bf16[4,16,3072]{2,1,0:T(8,128)(2,1)S(1)}, bf16[4,16,3072]{2,1,0:T(8,128)(2,1)}, u32[]{:S(2)}) copy-start(bf16[4,16,3072]{2,1,0:T(8,128)(2,1)} %refs_0_.5) | copy-start | bytes 1179652
  0.0 12.9 %copy-start.1 = (bf16[4,16,3072]{2,1,0:T(8,128)(2,1)S(1)}, bf16[4,16,3072]{2,1,0:T(8,128)(2,1)}, u32[]{:S(2)}) copy-start(bf16[4,16,3072]{2,1,0:T(8,128)(2,1)} %refs_1_.3) | copy-start | bytes 1179652
  2.9 7.0 %copy-start.6 = (f32[8,128]{1,0:T(8,128)S(1)}, f32[8,128]{1,0:T(8,128)}, u32[]{:S(2)}) copy-start(f32[8,128]{1,0:T(8,128)} %get-tuple-element.31._) | copy-start | bytes 12292
  2.9 13.2 %collective-permute-start = (bf16[4,16,768]{2,1,0:T(8,128)(2,1)}, bf16[4,16,768]{2,1,0:T(8,128)(2,1)S(1)}, u32[]{:S(2)}, u32[]{:S(2)}) collective-permute-start(bf16[4,16,768]{2,1,0:T(8,128)(2,1)} %get-tuple-element.35), channel_id=1, source_target_pairs={{0,4},{4,8},{8,12},{12,0},{1,5},{5,9},{9,13},{13,1},{2,6},{6,10},{... | collective-permute-start | bytes 294920 | tf_op jit(solution)/shard_map/ppermute | solution.py:370
  6.0 12.8 %collective-permute-start.1 = (bf16[4,16,768]{2,1,0:T(8,128)(2,1)}, bf16[4,16,768]{2,1,0:T(8,128)(2,1)S(1)}, u32[]{:S(2)}, u32[]{:S(2)}) collective-permute-start(bf16[4,16,768]{2,1,0:T(8,128)(2,1)} %get-tuple-element.36), channel_id=1, source_target_pairs={{0,8},{4,12},{8,0},{12,4},{1,9},{5,13},{9,1},{13,5},{2,10},{6,14},... | collective-permute-start | bytes 294920 | tf_op jit(solution)/shard_map/ppermute | solution.py:370
  8.5 1.4 %copy-start.7 = (s32[16]{0:T(128)S(1)}, s32[16]{0:T(128)}, u32[]{:S(2)}) copy-start(s32[16]{0:T(128)} %tokens_ref.5) | copy-start | bytes 196
  8.6 10.2 %collective-permute-start.2 = (bf16[4,16,768]{2,1,0:T(8,128)(2,1)}, bf16[4,16,768]{2,1,0:T(8,128)(2,1)S(1)}, u32[]{:S(2)}, u32[]{:S(2)}) collective-permute-start(bf16[4,16,768]{2,1,0:T(8,128)(2,1)} %get-tuple-element.37), channel_id=1, source_target_pairs={{0,12},{4,0},{8,4},{12,8},{1,13},{5,1},{9,5},{13,9},{2,14},{6,2},{... | collective-permute-start | bytes 294920 | tf_op jit(solution)/shard_map/ppermute | solution.py:370
  9.9 0.7 %copy-start.5 = (s32[16,32]{1,0:T(8,128)S(1)}, s32[16,32]{1,0:T(8,128)}, u32[]{:S(2)}) copy-start(s32[16,32]{1,0:T(8,128)} %pair_ref.1) | copy-start | bytes 6148
  12.9 2.0 %copy-start.3 = (f32[4,576]{1,0:T(4,128)}, f32[4,576]{1,0:T(4,128)S(1)}, u32[]{:S(2)}) copy-start(f32[4,576]{1,0:T(4,128)S(1)} %get-tuple-element.32.bias_ref.refs_2_) | copy-start | bytes 27652
  12.9 5.8 %copy-start.9 = (bf16[4,16,768]{2,1,0:T(8,128)(2,1)S(1)}, bf16[4,16,768]{2,1,0:T(8,128)(2,1)}, u32[]{:S(2)}) copy-start(bf16[4,16,768]{2,1,0:T(8,128)(2,1)} %get-tuple-element.34.refs_0_.refs_1_) | copy-start | bytes 294916
  14.8 11.6 %collective-permute-start.9 = (bf16[4,16,768]{2,1,0:T(8,128)(2,1)S(1)}, bf16[4,16,768]{2,1,0:T(8,128)(2,1)S(1)}, u32[]{:S(2)}, u32[]{:S(2)}) collective-permute-start(bf16[4,16,768]{2,1,0:T(8,128)(2,1)S(1)} %get-tuple-element.47), channel_id=1, source_target_pairs={{0,4},{4,8},{8,12},{12,0},{1,5},{5,9},{9,13},{13,1},{2,6},{6,10},{... | collective-permute-start | bytes 294920 | tf_op jit(solution)/shard_map/ppermute | solution.py:370
  15.6 12.0 %collective-permute-start.10 = (bf16[4,16,768]{2,1,0:T(8,128)(2,1)S(1)}, bf16[4,16,768]{2,1,0:T(8,128)(2,1)S(1)}, u32[]{:S(2)}, u32[]{:S(2)}) collective-permute-start(bf16[4,16,768]{2,1,0:T(8,128)(2,1)S(1)} %get-tuple-element.48), channel_id=1, source_target_pairs={{0,8},{4,12},{8,0},{12,4},{1,9},{5,13},{9,1},{13,5},{2,10},{6,14},... | collective-permute-start | bytes 294920 | tf_op jit(solution)/shard_map/ppermute | solution.py:370
  16.1 11.4 %collective-permute-start.11 = (bf16[4,16,768]{2,1,0:T(8,128)(2,1)S(1)}, bf16[4,16,768]{2,1,0:T(8,128)(2,1)S(1)}, u32[]{:S(2)}, u32[]{:S(2)}) collective-permute-start(bf16[4,16,768]{2,1,0:T(8,128)(2,1)S(1)} %get-tuple-element.49), channel_id=1, source_target_pairs={{0,12},{4,0},{8,4},{12,8},{1,13},{5,1},{9,5},{13,9},{2,14},{6,2},{... | collective-permute-start | bytes 294920 | tf_op jit(solution)/shard_map/ppermute | solution.py:370
  18.7 1.0 %copy-start.2 = (bf16[4,16,3072]{2,1,0:T(8,128)(2,1)S(1)}, bf16[4,16,3072]{2,1,0:T(8,128)(2,1)}, u32[]{:S(2)}) copy-start(bf16[4,16,3072]{2,1,0:T(8,128)(2,1)} %refs_0_.4) | copy-start | bytes 1179652
  19.3 11.2 %collective-permute-start.3 = (bf16[2,4,16,768]{3,2,1,0:T(8,128)(2,1)S(1)}, bf16[2,4,16,768]{3,2,1,0:T(8,128)(2,1)S(1)}, u32[]{:S(2)}, u32[]{:S(2)}) collective-permute-start(bf16[2,4,16,768]{3,2,1,0:T(8,128)(2,1)S(1)} %get-tuple-element.38.refs_1_.refs_4_), channel_id=1, source_target_pairs={{0,1},{1,2},{2,3},{3,0},{4,5},{5,6},{6,7},{7,4},{8,9},{9,10},{10,1... | collective-permute-start | bytes 589832 | tf_op jit(solution)/shard_map/ppermute | solution.py:370
  21.4 16.2 %all-to-all-start = ((bf16[4,4,16,768]{3,2,1,0:T(8,128)(2,1)}), bf16[4,4,16,768]{3,2,1,0:T(8,128)(2,1)S(1)}, u32[]{:S(2)}, u32[]{:S(2)}) async-start(bf16[4,4,16,768]{3,2,1,0:T(8,128)(2,1)} %get-tuple-element.39), calls=%async_computation | async-start | bytes 786432 | tf_op jit(solution)/shard_map/all_to_all | solution.py:408
  24.8 5.4 %collective-permute-start.4 = (bf16[1,4,16,768]{3,2,1,0:T(8,128)(2,1)S(1)}, bf16[1,4,16,768]{3,2,1,0:T(8,128)(2,1)S(1)}, u32[]{:S(2)}, u32[]{:S(2)}) collective-permute-start(bf16[1,4,16,768]{3,2,1,0:T(8,128)(2,1)S(1)} %get-tuple-element.40), channel_id=1, source_target_pairs={{0,2},{1,3},{2,0},{3,1},{4,6},{5,7},{6,4},{7,5},{8,10},{9,11},{10,... | collective-permute-start | bytes 294920 | tf_op jit(solution)/shard_map/ppermute | solution.py:370
  26.4 6.4 %collective-permute-start.5 = (bf16[2,4,16,768]{3,2,1,0:T(8,128)(2,1)S(1)}, bf16[2,4,16,768]{3,2,1,0:T(8,128)(2,1)S(1)}, u32[]{:S(2)}, u32[]{:S(2)}) collective-permute-start(bf16[2,4,16,768]{3,2,1,0:T(8,128)(2,1)S(1)} %get-tuple-element.41), channel_id=1, source_target_pairs={{0,3},{1,0},{2,1},{3,2},{4,7},{5,4},{6,5},{7,6},{8,11},{9,8},{10,9... | collective-permute-start | bytes 589832 | tf_op jit(solution)/shard_map/ppermute | solution.py:370
  27.5 10.1 %copy-start.4 = (f32[4,576]{1,0:T(4,128)S(1)}, f32[4,576]{1,0:T(4,128)}, u32[]{:S(2)}) copy-start(f32[4,576]{1,0:T(4,128)} %copy-done.3) | copy-start | bytes 27652
  28.1 14.1 %collective-permute-start.12 = (bf16[2,4,16,768]{3,2,1,0:T(8,128)(2,1)S(1)}, bf16[2,4,16,768]{3,2,1,0:T(8,128)(2,1)S(1)}, u32[]{:S(2)}, u32[]{:S(2)}) collective-permute-start(bf16[2,4,16,768]{3,2,1,0:T(8,128)(2,1)S(1)} %get-tuple-element.50), channel_id=1, source_target_pairs={{0,1},{1,2},{2,3},{3,0},{4,5},{5,6},{6,7},{7,4},{8,9},{9,10},{10,1... | collective-permute-start | bytes 589832 | tf_op jit(solution)/shard_map/ppermute | solution.py:370
  28.2 9.4 %copy-start.8 = (s32[16]{0:T(128)S(1)}, s32[16]{0:T(128)}, u32[]{:S(2)}) copy-start(s32[16]{0:T(128)} %tokens_ref.5) | copy-start | bytes 196
  28.2 13.3 %collective-permute-start.13 = (bf16[1,4,16,768]{3,2,1,0:T(8,128)(2,1)S(1)}, bf16[1,4,16,768]{3,2,1,0:T(8,128)(2,1)S(1)}, u32[]{:S(2)}, u32[]{:S(2)}) collective-permute-start(bf16[1,4,16,768]{3,2,1,0:T(8,128)(2,1)S(1)} %get-tuple-element.51), channel_id=1, source_target_pairs={{0,2},{1,3},{2,0},{3,1},{4,6},{5,7},{6,4},{7,5},{8,10},{9,11},{10,... | collective-permute-start | bytes 294920 | tf_op jit(solution)/shard_map/ppermute | solution.py:370
  30.3 11.9 %collective-permute-start.14 = (bf16[2,4,16,768]{3,2,1,0:T(8,128)(2,1)S(1)}, bf16[2,4,16,768]{3,2,1,0:T(8,128)(2,1)S(1)}, u32[]{:S(2)}, u32[]{:S(2)}) collective-permute-start(bf16[2,4,16,768]{3,2,1,0:T(8,128)(2,1)S(1)} %get-tuple-element.52), channel_id=1, source_target_pairs={{0,3},{1,0},{2,1},{3,2},{4,7},{5,4},{6,5},{7,6},{8,11},{9,8},{10,9... | collective-permute-start | bytes 589832 | tf_op jit(solution)/shard_map/ppermute | solution.py:370
  40.0 9.0 %collective-permute-start.6 = (bf16[4,16,384]{2,1,0:T(8,128)(2,1)S(1)}, bf16[4,16,384]{2,1,0:T(8,128)(2,1)S(1)}, u32[]{:S(2)}, u32[]{:S(2)}) collective-permute-start(bf16[4,16,384]{2,1,0:T(8,128)(2,1)S(1)} %get-tuple-element.43), channel_id=1, source_target_pairs={{0,12},{4,0},{8,4},{12,8},{1,13},{5,1},{9,5},{13,9},{2,14},{6,2},{... | collective-permute-start | bytes 147464 | tf_op jit(solution)/shard_map/ppermute | solution.py:370
  41.6 8.0 %collective-permute-start.7 = (bf16[4,16,384]{2,1,0:T(8,128)(2,1)S(1)}, bf16[4,16,384]{2,1,0:T(8,128)(2,1)S(1)}, u32[]{:S(2)}, u32[]{:S(2)}) collective-permute-start(bf16[4,16,384]{2,1,0:T(8,128)(2,1)S(1)} %get-tuple-element.44), channel_id=1, source_target_pairs={{0,8},{4,12},{8,0},{12,4},{1,9},{5,13},{9,1},{13,5},{2,10},{6,14},... | collective-permute-start | bytes 147464 | tf_op jit(solution)/shard_map/ppermute | solution.py:370
  41.6 8.0 %collective-permute-start.8 = (bf16[4,16,384]{2,1,0:T(8,128)(2,1)S(1)}, bf16[4,16,384]{2,1,0:T(8,128)(2,1)S(1)}, u32[]{:S(2)}, u32[]{:S(2)}) collective-permute-start(bf16[4,16,384]{2,1,0:T(8,128)(2,1)S(1)} %get-tuple-element.45), channel_id=1, source_target_pairs={{0,4},{4,8},{8,12},{12,0},{1,5},{5,9},{9,13},{13,1},{2,6},{6,10},{... | collective-permute-start | bytes 147464 | tf_op jit(solution)/shard_map/ppermute | solution.py:370
  44.6 5.1 %collective-permute-start.15 = (bf16[4,16,384]{2,1,0:T(8,128)(2,1)S(1)}, bf16[4,16,384]{2,1,0:T(8,128)(2,1)S(1)}, u32[]{:S(2)}, u32[]{:S(2)}) collective-permute-start(bf16[4,16,384]{2,1,0:T(8,128)(2,1)S(1)} %get-tuple-element.54), channel_id=1, source_target_pairs={{0,12},{4,0},{8,4},{12,8},{1,13},{5,1},{9,5},{13,9},{2,14},{6,2},{... | collective-permute-start | bytes 147464 | tf_op jit(solution)/shard_map/ppermute | solution.py:370
  47.9 5.3 %collective-permute-start.16 = (bf16[4,16,384]{2,1,0:T(8,128)(2,1)S(1)}, bf16[4,16,384]{2,1,0:T(8,128)(2,1)S(1)}, u32[]{:S(2)}, u32[]{:S(2)}) collective-permute-start(bf16[4,16,384]{2,1,0:T(8,128)(2,1)S(1)} %get-tuple-element.55), channel_id=1, source_target_pairs={{0,8},{4,12},{8,0},{12,4},{1,9},{5,13},{9,1},{13,5},{2,10},{6,14},... | collective-permute-start | bytes 147464 | tf_op jit(solution)/shard_map/ppermute | solution.py:370
  49.0 5.9 %collective-permute-start.17 = (bf16[4,16,384]{2,1,0:T(8,128)(2,1)S(1)}, bf16[4,16,384]{2,1,0:T(8,128)(2,1)S(1)}, u32[]{:S(2)}, u32[]{:S(2)}) collective-permute-start(bf16[4,16,384]{2,1,0:T(8,128)(2,1)S(1)} %get-tuple-element.56), channel_id=1, source_target_pairs={{0,4},{4,8},{8,12},{12,0},{1,5},{5,9},{9,13},{13,1},{2,6},{6,10},{... | collective-permute-start | bytes 147464 | tf_op jit(solution)/shard_map/ppermute | solution.py:370

commit v2 on v1

--- a/solution.py
+++ b/solution.py
@@ -389,7 +389,11 @@
     cut = (heads + 1) // 2 * HD
     parts = [(0, cut), (cut, width_here - cut)] if heads > 1 else [(0, width_here)]
     arrays = [query_rows, key_rows, value_rows]
-    messages = [[(1,) + part, (2,) + part] for part in parts]
+    messages = []
+    for at, part in enumerate(parts):
+        message = [(1,) + part, (2,) + part]
+        messages.append(message + ([(0,) + parts[at - 1]] if at else []))
+    query_at = [2 * size for _, size in parts[1:]] + [0]
     pieces, token = rotate_pieces(arrays, messages[0], count_head, limit=WIDE_VMEM)
     packed = [pieces]
     picks, bias = plan(pair_list, block_tokens, token, blocks, count_head, count_tm)
@@ -403,14 +407,15 @@
     for owns, (_, size) in zip(received, parts):
         sent.append(pick_blocks(picks, owns, (0, 2 * size), count_tm, after))
         after = (sent[-1][0],)
-    message = [(0, 0, width_here)]
+    message = [(0,) + parts[-1]]
     (query,), _ = rotate_pieces(arrays, message, count_head, (sent[0][0],), stacked=True)
     query = lax.all_to_all(query, "head", split_axis=0, concat_axis=0, tiled=True)
+    queries = received[1:] + [[query]]
     returned, after = [], ()
-    for at, (start, size) in enumerate(parts):
-        cost = NO_COST if at == len(parts) - 1 else HIGH_COST
+    for at, (_, size) in enumerate(parts):
         attended = attend(
-            block_tokens, bias, [query], start, received[at], 0, forward(sent[at]), size, after, cost
+            block_tokens, bias, queries[at], query_at[at], received[at], 0,
+            forward(sent[at]), size, after, NO_COST,
         )
         after = (attended[0],)
         returned.append(exchange(attended, -1))

time: 56 us -> 55.5 us (level)
  waiting for transfers between devices: 13.9 us -> 5.9 us
  starting transfers between devices: 25.1 us -> 31 us
  local copies, waits for them, and re-layouts: 1.06 us -> 2.05 us
    ppermute x18, starting transfers between devices: 21.6 us -> 27.6 us  [shifted(): lax.ppermute(array, axis, [(i, (i + distance) % count) for i in range(cou...]
    all_to_all x1, waiting for transfers between devices: 4.83 us -> 0.01 us  [shards(): lax.all_to_all(query, 'head', split_axis=0, concat_axis=0, tiled=True)]
    ppermute x18, waiting for transfers between devices: 9.04 us -> 5.9 us  [shifted(): lax.ppermute(array, axis, [(i, (i + distance) % count) for i in range(cou...]
    unnamed x20 -> x22, local copies, waits for them, and re-layouts: 1.06 us -> 2.05 us
  transfers between devices with their start and end apart: 19 -> 19, of which waited for: 6 -> 4; matrix products, arithmetic and copies ran while one was open for 0% -> 0% of each run, Pallas kernels for 21% -> 22%
where the time goes in v2:
time: 55.5 us; the launch traced here: 55.2 us
  starting transfers between devices  31 us (56%)
  Pallas kernels  16 us (29%)
  waiting for transfers between devices  5.9 us (11%)
  local copies, waits for them, and re-layouts  2.05 us (4%)
    ppermute x18, starting transfers between devices, shifted(): lax.ppermute(array, axis, [(i, (i + distance) % count) for i in range(cou...  27.6 us
    pallas_call x3, Pallas kernels, rotate_pieces(): pl.pallas_call(functools.partial(rotate_kernel, message, sources, count_h...  6.88 us
    ppermute x18, waiting for transfers between devices, shifted(): lax.ppermute(array, axis, [(i, (i + distance) % count) for i in range(cou...  5.9 us
    pallas_call x2, Pallas kernels, attend(): pl.pallas_call(functools.partial(attend_kernel, (count_head, count_tm, le...  4.89 us
    all_to_all x1, starting transfers between devices, shards(): lax.all_to_all(query, 'head', split_axis=0, concat_axis=0, tiled=True)  3.37 us
    pallas_call x1, Pallas kernels, plan(): pl.pallas_call(functools.partial(plan_kernel, count_head, count_tm, block...  2.25 us
    unnamed x22, local copies, waits for them, and re-layouts  2.05 us
    pallas_call x2, Pallas kernels, pick_blocks(): pl.pallas_call(functools.partial(pick_kernel, count_head, count_tm, lanes...  1.18 us
  transfers between devices with their start and end apart: 19, of which 4 were waited for; matrix products, arithmetic and copies ran while one was open for 0% of the time, Pallas kernels for 22%

profile of v2, /device:TPU:0, one launch (start us, length us, event | category | flops | bytes accessed | tf_op | source)
XLA Modules:
  0.0 55.2 jit_solution(10684689067440330389)
XLA Ops:
  0.0 0.0 copy-start
  0.0 2.9 %shard_map.55 = (bf16[4,16,768]{2,1,0:T(8,128)(2,1)}, bf16[4,16,768]{2,1,0:T(8,128)(2,1)}, bf16[4,16,768]{2,1,0:T(8,128)(2,1)}, bf16[4,16,768]{2,1,0:T(8,128)(2,1)}, f32[8,128]{1,0:T(8,128)}) custom-call(bf16[4,16,3072]{2,1,0:T(8,128)(2,1)} %refs_1_.3, bf16[4,16,3072]{2,1,0:T(8,128)(2,1)} %refs_2_.1), custom_call_target="tpu_custom_call" | custom-call | tf_op jit(solution)/shard_map/pallas_call | solution.py:101
  2.9 0.0 copy-start.10
  2.9 3.1 %collective-permute-start.3 = (bf16[4,16,768]{2,1,0:T(8,128)(2,1)}, bf16[4,16,768]{2,1,0:T(8,128)(2,1)S(1)}, u32[]{:S(2)}, u32[]{:S(2)}) collective-permute-start(bf16[4,16,768]{2,1,0:T(8,128)(2,1)} %get-tuple-element.38), channel_id=1, source_target_pairs={{0,4},{4,8},{8,12},{12,0},{1,5},{5,9},{9,13},{13,1},{2,6},{6,10},{... | collective-permute-start | bytes 294920 | tf_op jit(solution)/shard_map/ppermute | solution.py:370
  6.0 2.6 %collective-permute-start.4 = (bf16[4,16,768]{2,1,0:T(8,128)(2,1)}, bf16[4,16,768]{2,1,0:T(8,128)(2,1)S(1)}, u32[]{:S(2)}, u32[]{:S(2)}) collective-permute-start(bf16[4,16,768]{2,1,0:T(8,128)(2,1)} %get-tuple-element.39), channel_id=1, source_target_pairs={{0,8},{4,12},{8,0},{12,4},{1,9},{5,13},{9,1},{13,5},{2,10},{6,14},... | collective-permute-start | bytes 294920 | tf_op jit(solution)/shard_map/ppermute | solution.py:370
  8.6 1.3 %collective-permute-start.5 = (bf16[4,16,768]{2,1,0:T(8,128)(2,1)}, bf16[4,16,768]{2,1,0:T(8,128)(2,1)S(1)}, u32[]{:S(2)}, u32[]{:S(2)}) collective-permute-start(bf16[4,16,768]{2,1,0:T(8,128)(2,1)} %get-tuple-element.40), channel_id=1, source_target_pairs={{0,12},{4,0},{8,4},{12,8},{1,13},{5,1},{9,5},{13,9},{2,14},{6,2},{... | collective-permute-start | bytes 294920 | tf_op jit(solution)/shard_map/ppermute | solution.py:370
  9.9 0.0 copy-done.10
  9.9 0.0 copy-done.8
  9.9 0.7 %copy-done.7 = s32[16,32]{1,0:T(8,128)S(1)} copy-done((s32[16,32]{1,0:T(8,128)S(1)}, s32[16,32]{1,0:T(8,128)}, u32[]{:S(2)}) %copy-start.7) | copy-done | bytes 2072
  10.6 2.3 %shard_map.56 = (s32[8]{0:T(128)S(1)}, f32[4,576]{1,0:T(4,128)S(1)}) custom-call(s32[16,32]{1,0:T(8,128)S(1)} %copy-done.7, s32[16]{0:T(128)S(1)} %copy-done.8, f32[8,128]{1,0:T(8,128)S(1)} %copy-done.10), custom_call_target="tpu_custom_call" | custom-call | tf_op jit(solution)/shard_map/pallas_call | solution.py:237
  12.9 0.0 copy-start.5
  12.9 0.0 copy-done
  12.9 0.0 copy-done.1
  12.9 0.0 copy-start.2
  12.9 1.0 %copy-done.2 = bf16[4,16,3072]{2,1,0:T(8,128)(2,1)S(1)} copy-done((bf16[4,16,3072]{2,1,0:T(8,128)(2,1)S(1)}, bf16[4,16,3072]{2,1,0:T(8,128)(2,1)}, u32[]{:S(2)}) %copy-start.2) | copy-done | bytes 393240
  13.9 2.6 %shard_map.57 = (bf16[4,16,1152]{2,1,0:T(8,128)(2,1)S(1)}, bf16[4,16,1152]{2,1,0:T(8,128)(2,1)S(1)}, bf16[4,16,1152]{2,1,0:T(8,128)(2,1)S(1)}, bf16[4,16,1152]{2,1,0:T(8,128)(2,1)S(1)}, f32[8,128]{1,0:T(8,128)}) custom-call(bf16[4,16,3072]{2,1,0:T(8,128)(2,1)S(1)} %copy-done.2, bf16[4,16,3072]{2,1,0:T(8,128)(2,1)S(1)} %copy-done, ...), custom_call_target="tpu_custom_call" | custom-call | tf_op jit(solution)/shard_map/pallas_call | solution.py:101
  16.5 0.0 copy-done.5
  16.5 0.7 %collective-permute-start = (bf16[4,16,1152]{2,1,0:T(8,128)(2,1)S(1)}, bf16[4,16,1152]{2,1,0:T(8,128)(2,1)S(1)}, u32[]{:S(2)}, u32[]{:S(2)}) collective-permute-start(bf16[4,16,1152]{2,1,0:T(8,128)(2,1)S(1)} %get-tuple-element.34), channel_id=1, source_target_pairs={{0,4},{4,8},{8,12},{12,0},{1,5},{5,9},{9,13},{13,1},{2,6},{6,10},{... | collective-permute-start | bytes 442376 | tf_op jit(solution)/shard_map/ppermute | solution.py:370
  17.2 0.5 collective-permute-start.1
  17.8 0.0 collective-permute-done.3.refs_1_.refs_5_
  17.8 2.6 %collective-permute-start.2 = (bf16[4,16,1152]{2,1,0:T(8,128)(2,1)S(1)}, bf16[4,16,1152]{2,1,0:T(8,128)(2,1)S(1)}, u32[]{:S(2)}, u32[]{:S(2)}) collective-permute-start(bf16[4,16,1152]{2,1,0:T(8,128)(2,1)S(1)} %get-tuple-element.36), channel_id=1, source_target_pairs={{0,12},{4,0},{8,4},{12,8},{1,13},{5,1},{9,5},{13,9},{2,14},{6,2},{... | collective-permute-start | bytes 442376 | tf_op jit(solution)/shard_map/ppermute | solution.py:370
  20.4 0.0 collective-permute-done.4.refs_2_.refs_6_
  20.4 0.0 collective-permute-done.5.refs_3_.refs_7_
  20.4 0.0 copy-done.4
  20.4 0.0 copy-start.3
  20.4 0.6 %shard_map.58 = (bf16[2,4,16,768]{3,2,1,0:T(8,128)(2,1)S(1)}, bf16[1,4,16,768]{3,2,1,0:T(8,128)(2,1)S(1)}, bf16[2,4,16,768]{3,2,1,0:T(8,128)(2,1)S(1)}) custom-call(s32[8]{0:T(128)S(1)} %get-tuple-element.41.picks_ref, bf16[4,16,768]{2,1,0:T(8,128)(2,1)S(1)} %copy-done.4, bf16[4,16,768]{2,1,0:T(8,128)(2,1)S(1)} %collective-permute-done.3.refs_1_.refs_5_, ...), custom_call_target="tpu_custom_call" | custom-call | flops 99999997952 | tf_op jit(solution)/shard_map/pallas_call | solution.py:136
  21.0 0.1 collective-permute-start.6
  21.1 0.3 copy-done.3
  21.4 1.4 %shard_map.60 = (bf16[4,4,16,384]{3,2,1,0:T(8,128)(2,1)}, f32[8,128]{1,0:T(8,128)}) custom-call(bf16[4,16,3072]{2,1,0:T(8,128)(2,1)S(1)} %copy-done.3, bf16[2,4,16,768]{3,2,1,0:T(8,128)(2,1)S(1)} %get-tuple-element.42.refs_1_.refs_4_), custom_call_target="tpu_custom_call" | custom-call | tf_op jit(solution)/shard_map/pallas_call | solution.py:101
  22.8 1.6 %collective-permute-start.7 = (bf16[1,4,16,768]{3,2,1,0:T(8,128)(2,1)S(1)}, bf16[1,4,16,768]{3,2,1,0:T(8,128)(2,1)S(1)}, u32[]{:S(2)}, u32[]{:S(2)}) collective-permute-start(bf16[1,4,16,768]{3,2,1,0:T(8,128)(2,1)S(1)} %get-tuple-element.43), channel_id=1, source_target_pairs={{0,2},{1,3},{2,0},{3,1},{4,6},{5,7},{6,4},{7,5},{8,10},{9,11},{10,... | collective-permute-start | bytes 294920 | tf_op jit(solution)/shard_map/ppermute | solution.py:370
  24.4 3.4 %all-to-all-start = ((bf16[4,4,16,384]{3,2,1,0:T(8,128)(2,1)}), bf16[4,4,16,384]{3,2,1,0:T(8,128)(2,1)S(1)}, u32[]{:S(2)}, u32[]{:S(2)}) async-start(bf16[4,4,16,384]{3,2,1,0:T(8,128)(2,1)} %get-tuple-element.49), calls=%async_computation | async-start | bytes 393216 | tf_op jit(solution)/shard_map/all_to_all | solution.py:412
  27.8 0.0 collective-permute-done.refs_1_.refs_2_
  27.8 1.2 %collective-permute-start.8 = (bf16[2,4,16,768]{3,2,1,0:T(8,128)(2,1)S(1)}, bf16[2,4,16,768]{3,2,1,0:T(8,128)(2,1)S(1)}, u32[]{:S(2)}, u32[]{:S(2)}) collective-permute-start(bf16[2,4,16,768]{3,2,1,0:T(8,128)(2,1)S(1)} %get-tuple-element.44), channel_id=1, source_target_pairs={{0,3},{1,0},{2,1},{3,2},{4,7},{5,4},{6,5},{7,6},{8,11},{9,8},{10,9... | collective-permute-start | bytes 589832 | tf_op jit(solution)/shard_map/ppermute | solution.py:370
  29.0 0.6 %collective-permute-done.1.refs_2_.refs_3_ = bf16[4,16,1152]{2,1,0:T(8,128)(2,1)S(1)} collective-permute-done((bf16[4,16,1152]{2,1,0:T(8,128)(2,1)S(1)}, bf16[4,16,1152]{2,1,0:T(8,128)(2,1)S(1)}, u32[]{:S(2)}, u32[]{:S(2)}) %collective-permute-start.1) | collective-permute-done | bytes 147488 | tf_op jit(solution)/shard_map/ppermute | solution.py:370
  29.6 0.0 collective-permute-done.2.refs_3_.refs_4_
  29.6 0.6 %shard_map.61 = (bf16[2,4,16,768]{3,2,1,0:T(8,128)(2,1)S(1)}, bf16[1,4,16,768]{3,2,1,0:T(8,128)(2,1)S(1)}, bf16[2,4,16,768]{3,2,1,0:T(8,128)(2,1)S(1)}) custom-call(s32[8]{0:T(128)S(1)} %get-tuple-element.41.picks_ref, bf16[4,16,1152]{2,1,0:T(8,128)(2,1)S(1)} %get-tuple-element.33.refs_0_.refs_1_, ...), custom_call_target="tpu_custom_call" | custom-call | flops 99999997952 | tf_op jit(solution)/shard_map/pallas_call | solution.py:136
  30.2 0.1 collective-permute-start.12
  30.3 0.0 copy-start.9
  30.3 1.7 %collective-permute-start.14 = (bf16[2,4,16,768]{3,2,1,0:T(8,128)(2,1)S(1)}, bf16[2,4,16,768]{3,2,1,0:T(8,128)(2,1)S(1)}, u32[]{:S(2)}, u32[]{:S(2)}) collective-permute-start(bf16[2,4,16,768]{3,2,1,0:T(8,128)(2,1)S(1)} %get-tuple-element.52), channel_id=1, source_target_pairs={{0,3},{1,0},{2,1},{3,2},{4,7},{5,4},{6,5},{7,6},{8,11},{9,8},{10,9... | collective-permute-start | bytes 589832 | tf_op jit(solution)/shard_map/ppermute | solution.py:370
  32.0 0.0 collective-permute-done.7.refs_9_
  32.0 1.5 %collective-permute-start.13 = (bf16[1,4,16,768]{3,2,1,0:T(8,128)(2,1)S(1)}, bf16[1,4,16,768]{3,2,1,0:T(8,128)(2,1)S(1)}, u32[]{:S(2)}, u32[]{:S(2)}) collective-permute-start(bf16[1,4,16,768]{3,2,1,0:T(8,128)(2,1)S(1)} %get-tuple-element.51), channel_id=1, source_target_pairs={{0,2},{1,3},{2,0},{3,1},{4,6},{5,7},{6,4},{7,5},{8,10},{9,11},{10,... | collective-permute-start | bytes 294920 | tf_op jit(solution)/shard_map/ppermute | solution.py:370
  33.5 0.0 collective-permute-done.6.refs_8_
  33.5 0.0 collective-permute-done.8.refs_10_
  33.5 0.0 copy-done.6
  33.5 0.0 copy-done.9
  33.5 2.5 %shard_map.59 = (bf16[4,16,384]{2,1,0:T(8,128)(2,1)S(1)}, bf16[4,16,384]{2,1,0:T(8,128)(2,1)S(1)}, bf16[4,16,384]{2,1,0:T(8,128)(2,1)S(1)}, bf16[4,16,384]{2,1,0:T(8,128)(2,1)S(1)}) custom-call(s32[16]{0:T(128)S(1)} %copy-done.9, f32[4,576]{1,0:T(4,128)S(1)} %copy-done.6, bf16[4,16,1152]{2,1,0:T(8,128)(2,1)S(1)} %get-tuple-element.33.refs_0_.refs_1_, ...), custom_call_target="tpu_custom_call" | custom-call | tf_op jit(solution)/shard_map/pallas_call | solution.py:318
  36.0 2.9 %collective-permute-start.9 = (bf16[4,16,384]{2,1,0:T(8,128)(2,1)S(1)}, bf16[4,16,384]{2,1,0:T(8,128)(2,1)S(1)}, u32[]{:S(2)}, u32[]{:S(2)}) collective-permute-start(bf16[4,16,384]{2,1,0:T(8,128)(2,1)S(1)} %get-tuple-element.46), channel_id=1, source_target_pairs={{0,12},{4,0},{8,4},{12,8},{1,13},{5,1},{9,5},{13,9},{2,14},{6,2},{... | collective-permute-start | bytes 147464 | tf_op jit(solution)/shard_map/ppermute | solution.py:370
  38.8 3.3 %collective-permute-start.10 = (bf16[4,16,384]{2,1,0:T(8,128)(2,1)S(1)}, bf16[4,16,384]{2,1,0:T(8,128)(2,1)S(1)}, u32[]{:S(2)}, u32[]{:S(2)}) collective-permute-start(bf16[4,16,384]{2,1,0:T(8,128)(2,1)S(1)} %get-tuple-element.47), channel_id=1, source_target_pairs={{0,8},{4,12},{8,0},{12,4},{1,9},{5,13},{9,1},{13,5},{2,10},{6,14},... | collective-permute-start | bytes 147464 | tf_op jit(solution)/shard_map/ppermute | solution.py:370
  42.1 0.0 collective-permute-done.13.refs_6_
  42.1 1.5 %collective-permute-start.11 = (bf16[4,16,384]{2,1,0:T(8,128)(2,1)S(1)}, bf16[4,16,384]{2,1,0:T(8,128)(2,1)S(1)}, u32[]{:S(2)}, u32[]{:S(2)}) collective-permute-start(bf16[4,16,384]{2,1,0:T(8,128)(2,1)S(1)} %get-tuple-element.48), channel_id=1, source_target_pairs={{0,4},{4,8},{8,12},{12,0},{1,5},{5,9},{9,13},{13,1},{2,6},{6,10},{... | collective-permute-start | bytes 147464 | tf_op jit(solution)/shard_map/ppermute | solution.py:370
  43.7 0.0 collective-permute-done.12.refs_5_
  43.7 0.0 collective-permute-done.14.refs_7_
  43.7 0.0 all-to-all-done.refs_0_
  43.7 2.4 %shard_map.62 = (bf16[4,16,384]{2,1,0:T(8,128)(2,1)S(1)}, bf16[4,16,384]{2,1,0:T(8,128)(2,1)S(1)}, bf16[4,16,384]{2,1,0:T(8,128)(2,1)S(1)}, bf16[4,16,384]{2,1,0:T(8,128)(2,1)S(1)}) custom-call(s32[16]{0:T(128)S(1)} %copy-done.9, f32[4,576]{1,0:T(4,128)S(1)} %copy-done.6, bf16[4,4,16,384]{3,2,1,0:T(8,128)(2,1)S(1)} %all-to-all-done.refs_0_, ...), custom_call_target="tpu_custom_call" | custom-call | tf_op jit(solution)/shard_map/pallas_call | solution.py:318
  46.1 2.3 %collective-permute-start.15 = (bf16[4,16,384]{2,1,0:T(8,128)(2,1)S(1)}, bf16[4,16,384]{2,1,0:T(8,128)(2,1)S(1)}, u32[]{:S(2)}, u32[]{:S(2)}) collective-permute-start(bf16[4,16,384]{2,1,0:T(8,128)(2,1)S(1)} %get-tuple-element.54), channel_id=1, source_target_pairs={{0,12},{4,0},{8,4},{12,8},{1,13},{5,1},{9,5},{13,9},{2,14},{6,2},{... | collective-permute-start | bytes 147464 | tf_op jit(solution)/shard_map/ppermute | solution.py:370
  48.5 0.0 collective-permute-start.16
  48.5 0.0 collective-permute-done.9.refs_1_
  48.5 0.6 %collective-permute-start.17 = (bf16[4,16,384]{2,1,0:T(8,128)(2,1)S(1)}, bf16[4,16,384]{2,1,0:T(8,128)(2,1)S(1)}, u32[]{:S(2)}, u32[]{:S(2)}) collective-permute-start(bf16[4,16,384]{2,1,0:T(8,128)(2,1)S(1)} %get-tuple-element.56), channel_id=1, source_target_pairs={{0,4},{4,8},{8,12},{12,0},{1,5},{5,9},{9,13},{13,1},{2,6},{6,10},{... | collective-permute-start | bytes 147464 | tf_op jit(solution)/shard_map/ppermute | solution.py:370
  49.1 0.0 collective-permute-done.10.refs_2_
  49.1 0.0 collective-permute-done.11.refs_3_
  49.1 1.6 %collective-permute-done.15.refs_5_ = bf16[4,16,384]{2,1,0:T(8,128)(2,1)S(1)} collective-permute-done((bf16[4,16,384]{2,1,0:T(8,128)(2,1)S(1)}, bf16[4,16,384]{2,1,0:T(8,128)(2,1)S(1)}, u32[]{:S(2)}, u32[]{:S(2)}) %collective-permute-start.15) | collective-permute-done | bytes 49184 | tf_op jit(solution)/shard_map/ppermute | solution.py:370
  50.7 2.7 %collective-permute-done.16.refs_6_ = bf16[4,16,384]{2,1,0:T(8,128)(2,1)S(1)} collective-permute-done((bf16[4,16,384]{2,1,0:T(8,128)(2,1)S(1)}, bf16[4,16,384]{2,1,0:T(8,128)(2,1)S(1)}, u32[]{:S(2)}, u32[]{:S(2)}) %collective-permute-start.16) | collective-permute-done | bytes 49184 | tf_op jit(solution)/shard_map/ppermute | solution.py:370
  53.5 0.9 %collective-permute-done.17.refs_7_ = bf16[4,16,384]{2,1,0:T(8,128)(2,1)S(1)} collective-permute-done((bf16[4,16,384]{2,1,0:T(8,128)(2,1)S(1)}, bf16[4,16,384]{2,1,0:T(8,128)(2,1)S(1)}, u32[]{:S(2)}, u32[]{:S(2)}) %collective-permute-start.17) | collective-permute-done | bytes 49184 | tf_op jit(solution)/shard_map/ppermute | solution.py:370
  54.4 0.8 %shard_map.63 = bf16[4,16,3072]{2,1,0:T(8,128)(2,1)} custom-call(bf16[4,16,384]{2,1,0:T(8,128)(2,1)S(1)} %get-tuple-element.45.refs_8_.refs_0_, bf16[4,16,384]{2,1,0:T(8,128)(2,1)S(1)} %collective-permute-done.9.refs_1_, bf16[4,16,384]{2,1,0:T(8,128)(2,1)S(1)} %collective-permute-done.10.refs_2_, bf16[4,16,384]{2,1,0:T(8,128)(2,1)S(1)} %collective-permute-done.11.refs_3_, ...), custom_call_target="tpu_custom_call" | custom-call | tf_op jit(solution)/shard_map/pallas_call | solution.py:358
  (5 shorter events, 0.0 us)
Async XLA Ops:
  0.0 12.9 %copy-start = (bf16[4,16,3072]{2,1,0:T(8,128)(2,1)S(1)}, bf16[4,16,3072]{2,1,0:T(8,128)(2,1)}, u32[]{:S(2)}) copy-start(bf16[4,16,3072]{2,1,0:T(8,128)(2,1)} %refs_1_.3) | copy-start | bytes 1179652
  0.0 12.9 %copy-start.1 = (bf16[4,16,3072]{2,1,0:T(8,128)(2,1)S(1)}, bf16[4,16,3072]{2,1,0:T(8,128)(2,1)}, u32[]{:S(2)}) copy-start(bf16[4,16,3072]{2,1,0:T(8,128)(2,1)} %refs_2_.1) | copy-start | bytes 1179652
  2.9 7.0 %copy-start.10 = (f32[8,128]{1,0:T(8,128)S(1)}, f32[8,128]{1,0:T(8,128)}, u32[]{:S(2)}) copy-start(f32[8,128]{1,0:T(8,128)} %get-tuple-element.31._) | copy-start | bytes 12292
  2.9 14.9 %collective-permute-start.3 = (bf16[4,16,768]{2,1,0:T(8,128)(2,1)}, bf16[4,16,768]{2,1,0:T(8,128)(2,1)S(1)}, u32[]{:S(2)}, u32[]{:S(2)}) collective-permute-start(bf16[4,16,768]{2,1,0:T(8,128)(2,1)} %get-tuple-element.38), channel_id=1, source_target_pairs={{0,4},{4,8},{8,12},{12,0},{1,5},{5,9},{9,13},{13,1},{2,6},{6,10},{... | collective-permute-start | bytes 294920 | tf_op jit(solution)/shard_map/ppermute | solution.py:370
  6.0 14.4 %collective-permute-start.4 = (bf16[4,16,768]{2,1,0:T(8,128)(2,1)}, bf16[4,16,768]{2,1,0:T(8,128)(2,1)S(1)}, u32[]{:S(2)}, u32[]{:S(2)}) collective-permute-start(bf16[4,16,768]{2,1,0:T(8,128)(2,1)} %get-tuple-element.39), channel_id=1, source_target_pairs={{0,8},{4,12},{8,0},{12,4},{1,9},{5,13},{9,1},{13,5},{2,10},{6,14},... | collective-permute-start | bytes 294920 | tf_op jit(solution)/shard_map/ppermute | solution.py:370
  8.5 1.4 %copy-start.8 = (s32[16]{0:T(128)S(1)}, s32[16]{0:T(128)}, u32[]{:S(2)}) copy-start(s32[16]{0:T(128)} %tokens_ref.5) | copy-start | bytes 196
  8.6 11.8 %collective-permute-start.5 = (bf16[4,16,768]{2,1,0:T(8,128)(2,1)}, bf16[4,16,768]{2,1,0:T(8,128)(2,1)S(1)}, u32[]{:S(2)}, u32[]{:S(2)}) collective-permute-start(bf16[4,16,768]{2,1,0:T(8,128)(2,1)} %get-tuple-element.40), channel_id=1, source_target_pairs={{0,12},{4,0},{8,4},{12,8},{1,13},{5,1},{9,5},{13,9},{2,14},{6,2},{... | collective-permute-start | bytes 294920 | tf_op jit(solution)/shard_map/ppermute | solution.py:370
  9.9 0.7 %copy-start.7 = (s32[16,32]{1,0:T(8,128)S(1)}, s32[16,32]{1,0:T(8,128)}, u32[]{:S(2)}) copy-start(s32[16,32]{1,0:T(8,128)} %pair_ref.1) | copy-start | bytes 6148
  12.9 3.6 %copy-start.5 = (f32[4,576]{1,0:T(4,128)}, f32[4,576]{1,0:T(4,128)S(1)}, u32[]{:S(2)}) copy-start(f32[4,576]{1,0:T(4,128)S(1)} %get-tuple-element.32.refs_3_.bias_ref) | copy-start | bytes 27652
  12.9 1.0 %copy-start.2 = (bf16[4,16,3072]{2,1,0:T(8,128)(2,1)S(1)}, bf16[4,16,3072]{2,1,0:T(8,128)(2,1)}, u32[]{:S(2)}) copy-start(bf16[4,16,3072]{2,1,0:T(8,128)(2,1)} %refs_0_.5) | copy-start | bytes 1179652
  13.9 6.5 %copy-start.4 = (bf16[4,16,768]{2,1,0:T(8,128)(2,1)S(1)}, bf16[4,16,768]{2,1,0:T(8,128)(2,1)}, u32[]{:S(2)}) copy-start(bf16[4,16,768]{2,1,0:T(8,128)(2,1)} %get-tuple-element.37.refs_0_.refs_4_) | copy-start | bytes 294916
  16.5 11.3 %collective-permute-start = (bf16[4,16,1152]{2,1,0:T(8,128)(2,1)S(1)}, bf16[4,16,1152]{2,1,0:T(8,128)(2,1)S(1)}, u32[]{:S(2)}, u32[]{:S(2)}) collective-permute-start(bf16[4,16,1152]{2,1,0:T(8,128)(2,1)S(1)} %get-tuple-element.34), channel_id=1, source_target_pairs={{0,4},{4,8},{8,12},{12,0},{1,5},{5,9},{9,13},{13,1},{2,6},{6,10},{... | collective-permute-start | bytes 442376 | tf_op jit(solution)/shard_map/ppermute | solution.py:370
  17.2 12.3 %collective-permute-start.1 = (bf16[4,16,1152]{2,1,0:T(8,128)(2,1)S(1)}, bf16[4,16,1152]{2,1,0:T(8,128)(2,1)S(1)}, u32[]{:S(2)}, u32[]{:S(2)}) collective-permute-start(bf16[4,16,1152]{2,1,0:T(8,128)(2,1)S(1)} %get-tuple-element.35), channel_id=1, source_target_pairs={{0,8},{4,12},{8,0},{12,4},{1,9},{5,13},{9,1},{13,5},{2,10},{6,14},... | collective-permute-start | bytes 442376 | tf_op jit(solution)/shard_map/ppermute | solution.py:370
  17.8 11.8 %collective-permute-start.2 = (bf16[4,16,1152]{2,1,0:T(8,128)(2,1)S(1)}, bf16[4,16,1152]{2,1,0:T(8,128)(2,1)S(1)}, u32[]{:S(2)}, u32[]{:S(2)}) collective-permute-start(bf16[4,16,1152]{2,1,0:T(8,128)(2,1)S(1)} %get-tuple-element.36), channel_id=1, source_target_pairs={{0,12},{4,0},{8,4},{12,8},{1,13},{5,1},{9,5},{13,9},{2,14},{6,2},{... | collective-permute-start | bytes 442376 | tf_op jit(solution)/shard_map/ppermute | solution.py:370
  20.4 1.0 %copy-start.3 = (bf16[4,16,3072]{2,1,0:T(8,128)(2,1)S(1)}, bf16[4,16,3072]{2,1,0:T(8,128)(2,1)}, u32[]{:S(2)}) copy-start(bf16[4,16,3072]{2,1,0:T(8,128)(2,1)} %refs_0_.5) | copy-start | bytes 1179652
  21.0 12.5 %collective-permute-start.6 = (bf16[2,4,16,768]{3,2,1,0:T(8,128)(2,1)S(1)}, bf16[2,4,16,768]{3,2,1,0:T(8,128)(2,1)S(1)}, u32[]{:S(2)}, u32[]{:S(2)}) collective-permute-start(bf16[2,4,16,768]{3,2,1,0:T(8,128)(2,1)S(1)} %get-tuple-element.42.refs_1_.refs_4_), channel_id=1, source_target_pairs={{0,1},{1,2},{2,3},{3,0},{4,5},{5,6},{6,7},{7,4},{8,9},{9,10},{10,1... | collective-permute-start | bytes 589832 | tf_op jit(solution)/shard_map/ppermute | solution.py:370
  22.8 9.2 %collective-permute-start.7 = (bf16[1,4,16,768]{3,2,1,0:T(8,128)(2,1)S(1)}, bf16[1,4,16,768]{3,2,1,0:T(8,128)(2,1)S(1)}, u32[]{:S(2)}, u32[]{:S(2)}) collective-permute-start(bf16[1,4,16,768]{3,2,1,0:T(8,128)(2,1)S(1)} %get-tuple-element.43), channel_id=1, source_target_pairs={{0,2},{1,3},{2,0},{3,1},{4,6},{5,7},{6,4},{7,5},{8,10},{9,11},{10,... | collective-permute-start | bytes 294920 | tf_op jit(solution)/shard_map/ppermute | solution.py:370
  24.4 19.3 %all-to-all-start = ((bf16[4,4,16,384]{3,2,1,0:T(8,128)(2,1)}), bf16[4,4,16,384]{3,2,1,0:T(8,128)(2,1)S(1)}, u32[]{:S(2)}, u32[]{:S(2)}) async-start(bf16[4,4,16,384]{3,2,1,0:T(8,128)(2,1)} %get-tuple-element.49), calls=%async_computation | async-start | bytes 393216 | tf_op jit(solution)/shard_map/all_to_all | solution.py:412
  27.8 5.7 %collective-permute-start.8 = (bf16[2,4,16,768]{3,2,1,0:T(8,128)(2,1)S(1)}, bf16[2,4,16,768]{3,2,1,0:T(8,128)(2,1)S(1)}, u32[]{:S(2)}, u32[]{:S(2)}) collective-permute-start(bf16[2,4,16,768]{3,2,1,0:T(8,128)(2,1)S(1)} %get-tuple-element.44), channel_id=1, source_target_pairs={{0,3},{1,0},{2,1},{3,2},{4,7},{5,4},{6,5},{7,6},{8,11},{9,8},{10,9... | collective-permute-start | bytes 589832 | tf_op jit(solution)/shard_map/ppermute | solution.py:370
  29.6 3.9 %copy-start.6 = (f32[4,576]{1,0:T(4,128)S(1)}, f32[4,576]{1,0:T(4,128)}, u32[]{:S(2)}) copy-start(f32[4,576]{1,0:T(4,128)} %copy-done.5) | copy-start | bytes 27652
  30.2 13.5 %collective-permute-start.12 = (bf16[2,4,16,768]{3,2,1,0:T(8,128)(2,1)S(1)}, bf16[2,4,16,768]{3,2,1,0:T(8,128)(2,1)S(1)}, u32[]{:S(2)}, u32[]{:S(2)}) collective-permute-start(bf16[2,4,16,768]{3,2,1,0:T(8,128)(2,1)S(1)} %get-tuple-element.50), channel_id=1, source_target_pairs={{0,1},{1,2},{2,3},{3,0},{4,5},{5,6},{6,7},{7,4},{8,9},{9,10},{10,1... | collective-permute-start | bytes 589832 | tf_op jit(solution)/shard_map/ppermute | solution.py:370
  30.3 3.2 %copy-start.9 = (s32[16]{0:T(128)S(1)}, s32[16]{0:T(128)}, u32[]{:S(2)}) copy-start(s32[16]{0:T(128)} %tokens_ref.5) | copy-start | bytes 196
  30.3 13.4 %collective-permute-start.14 = (bf16[2,4,16,768]{3,2,1,0:T(8,128)(2,1)S(1)}, bf16[2,4,16,768]{3,2,1,0:T(8,128)(2,1)S(1)}, u32[]{:S(2)}, u32[]{:S(2)}) collective-permute-start(bf16[2,4,16,768]{3,2,1,0:T(8,128)(2,1)S(1)} %get-tuple-element.52), channel_id=1, source_target_pairs={{0,3},{1,0},{2,1},{3,2},{4,7},{5,4},{6,5},{7,6},{8,11},{9,8},{10,9... | collective-permute-start | bytes 589832 | tf_op jit(solution)/shard_map/ppermute | solution.py:370
  32.0 10.1 %collective-permute-start.13 = (bf16[1,4,16,768]{3,2,1,0:T(8,128)(2,1)S(1)}, bf16[1,4,16,768]{3,2,1,0:T(8,128)(2,1)S(1)}, u32[]{:S(2)}, u32[]{:S(2)}) collective-permute-start(bf16[1,4,16,768]{3,2,1,0:T(8,128)(2,1)S(1)} %get-tuple-element.51), channel_id=1, source_target_pairs={{0,2},{1,3},{2,0},{3,1},{4,6},{5,7},{6,4},{7,5},{8,10},{9,11},{10,... | collective-permute-start | bytes 294920 | tf_op jit(solution)/shard_map/ppermute | solution.py:370
  36.0 12.5 %collective-permute-start.9 = (bf16[4,16,384]{2,1,0:T(8,128)(2,1)S(1)}, bf16[4,16,384]{2,1,0:T(8,128)(2,1)S(1)}, u32[]{:S(2)}, u32[]{:S(2)}) collective-permute-start(bf16[4,16,384]{2,1,0:T(8,128)(2,1)S(1)} %get-tuple-element.46), channel_id=1, source_target_pairs={{0,12},{4,0},{8,4},{12,8},{1,13},{5,1},{9,5},{13,9},{2,14},{6,2},{... | collective-permute-start | bytes 147464 | tf_op jit(solution)/shard_map/ppermute | solution.py:370
  38.8 10.3 %collective-permute-start.10 = (bf16[4,16,384]{2,1,0:T(8,128)(2,1)S(1)}, bf16[4,16,384]{2,1,0:T(8,128)(2,1)S(1)}, u32[]{:S(2)}, u32[]{:S(2)}) collective-permute-start(bf16[4,16,384]{2,1,0:T(8,128)(2,1)S(1)} %get-tuple-element.47), channel_id=1, source_target_pairs={{0,8},{4,12},{8,0},{12,4},{1,9},{5,13},{9,1},{13,5},{2,10},{6,14},... | collective-permute-start | bytes 147464 | tf_op jit(solution)/shard_map/ppermute | solution.py:370
  42.1 7.0 %collective-permute-start.11 = (bf16[4,16,384]{2,1,0:T(8,128)(2,1)S(1)}, bf16[4,16,384]{2,1,0:T(8,128)(2,1)S(1)}, u32[]{:S(2)}, u32[]{:S(2)}) collective-permute-start(bf16[4,16,384]{2,1,0:T(8,128)(2,1)S(1)} %get-tuple-element.48), channel_id=1, source_target_pairs={{0,4},{4,8},{8,12},{12,0},{1,5},{5,9},{9,13},{13,1},{2,6},{6,10},{... | collective-permute-start | bytes 147464 | tf_op jit(solution)/shard_map/ppermute | solution.py:370
  46.1 4.6 %collective-permute-start.15 = (bf16[4,16,384]{2,1,0:T(8,128)(2,1)S(1)}, bf16[4,16,384]{2,1,0:T(8,128)(2,1)S(1)}, u32[]{:S(2)}, u32[]{:S(2)}) collective-permute-start(bf16[4,16,384]{2,1,0:T(8,128)(2,1)S(1)} %get-tuple-element.54), channel_id=1, source_target_pairs={{0,12},{4,0},{8,4},{12,8},{1,13},{5,1},{9,5},{13,9},{2,14},{6,2},{... | collective-permute-start | bytes 147464 | tf_op jit(solution)/shard_map/ppermute | solution.py:370
  48.5 5.0 %collective-permute-start.16 = (bf16[4,16,384]{2,1,0:T(8,128)(2,1)S(1)}, bf16[4,16,384]{2,1,0:T(8,128)(2,1)S(1)}, u32[]{:S(2)}, u32[]{:S(2)}) collective-permute-start(bf16[4,16,384]{2,1,0:T(8,128)(2,1)S(1)} %get-tuple-element.55), channel_id=1, source_target_pairs={{0,8},{4,12},{8,0},{12,4},{1,9},{5,13},{9,1},{13,5},{2,10},{6,14},... | collective-permute-start | bytes 147464 | tf_op jit(solution)/shard_map/ppermute | solution.py:370
  48.5 5.9 %collective-permute-start.17 = (bf16[4,16,384]{2,1,0:T(8,128)(2,1)S(1)}, bf16[4,16,384]{2,1,0:T(8,128)(2,1)S(1)}, u32[]{:S(2)}, u32[]{:S(2)}) collective-permute-start(bf16[4,16,384]{2,1,0:T(8,128)(2,1)S(1)} %get-tuple-element.56), channel_id=1, source_target_pairs={{0,4},{4,8},{8,12},{12,0},{1,5},{5,9},{9,13},{13,1},{2,6},{6,10},{... | collective-permute-start | bytes 147464 | tf_op jit(solution)/shard_map/ppermute | solution.py:370

commit v3 on v2

--- a/solution.py
+++ b/solution.py
@@ -261,7 +261,7 @@
     query_at, key_at = at
     queries, refs = by_distance(refs[:query_count], count_head, -1), refs[query_count:]
     owns, slots = refs[:count_head], refs[count_head : count_head + count_tm - 1]
-    outs = refs[count_head + count_tm - 1 + skipped :]
+    outs = by_distance(refs[count_head + count_tm - 1 + skipped :], count_head, -1)
     blocks, tokens, _ = owns[0].shape
     shard = lax.axis_index("tm")
     me = lax.axis_index("head")
@@ -311,9 +311,11 @@
                 ).astype(jnp.bfloat16)
 
 
-def attend(block_tokens, bias, queries, query_at, owns, key_at, slots, size, after, cost):
+def attend(block_tokens, bias, queries, query_at, owns, key_at, slots, size, after, cost, stacked):
     count_head, count_tm = len(owns), len(slots) + 1
     blocks, tokens, _ = owns[0].shape
+    one = (blocks, tokens, size)
+    shapes = [(count_head,) + one] if stacked else [one] * count_head
     vmem = pl.BlockSpec(memory_space=pltpu.VMEM)
     return pl.pallas_call(
         functools.partial(
@@ -325,42 +327,44 @@
         in_specs=[pl.BlockSpec(memory_space=pltpu.SMEM)]
         + [vmem] * (len(queries) + count_head + count_tm)
         + [pl.BlockSpec(memory_space=pl.ANY)] * len(after),
-        out_specs=[vmem] * count_head,
-        out_shape=[jax.ShapeDtypeStruct((blocks, tokens, size), jnp.bfloat16)] * count_head,
+        out_specs=[vmem] * len(shapes),
+        out_shape=[jax.ShapeDtypeStruct(shape, jnp.bfloat16) for shape in shapes],
         cost_estimate=cost,
         compiler_params=pltpu.CompilerParams(vmem_limit_bytes=VMEM),
     )(block_tokens, bias, *queries, *owns, *slots, *after)
 
 
-def place_kernel(count_head, starts, width_here, *refs):
-    pieces, out_ref, sems = refs[:-2], refs[-2], refs[-1]
+def place_kernel(count_head, counts, starts, width_here, *refs):
+    out_ref, sems = refs[-2:]
     me = lax.axis_index("head")
-    copies = []
-    for at, piece in enumerate(pieces):
-        part, s = at // count_head, at % count_head
-        column = lax.rem(me + s, count_head) * width_here + starts[part]
-        copies.append(
-            pltpu.make_async_copy(
-                piece,
-                out_ref.at[:, :, pl.ds(pl.multiple_of(column, HD), piece.shape[-1])],
-                sems.at[at],
+    copies, at = [], 0
+    for count, start in zip(counts, starts):
+        pieces = by_distance(refs[at : at + count], count_head, 1)
+        at += count
+        for s, piece in enumerate(pieces):
+            column = lax.rem(me + s, count_head) * width_here + start
+            copies.append(
+                pltpu.make_async_copy(
+                    piece,
+                    out_ref.at[:, :, pl.ds(pl.multiple_of(column, HD), piece.shape[-1])],
+                    sems.at[len(copies)],
+                )
             )
-        )
-        copies[-1].start()
+            copies[-1].start()
     for copy in copies:
         copy.wait()
 
 
-def place_pieces(parts, starts, width_here):
-    count_head = len(parts[0])
+def place_pieces(parts, starts, count_head, width_here):
     pieces = [piece for part in parts for piece in part]
-    blocks, tokens, _ = pieces[0].shape
+    blocks, tokens, _ = pieces[0].shape[-3:]
+    counts = [len(part) for part in parts]
     return pl.pallas_call(
-        functools.partial(place_kernel, count_head, starts, width_here),
+        functools.partial(place_kernel, count_head, counts, starts, width_here),
         in_specs=[pl.BlockSpec(memory_space=pl.ANY)] * len(pieces),
         out_specs=pl.BlockSpec(memory_space=pltpu.HBM),
         out_shape=jax.ShapeDtypeStruct((blocks, tokens, count_head * width_here), jnp.bfloat16),
-        scratch_shapes=[pltpu.SemaphoreType.DMA((len(pieces),))],
+        scratch_shapes=[pltpu.SemaphoreType.DMA((len(parts) * count_head,))],
         compiler_params=pltpu.CompilerParams(vmem_limit_bytes=VMEM),
     )(*pieces)
 
@@ -371,6 +375,8 @@
 
 
 def exchange(pieces, direction):
+    if len(pieces) == 1:
+        return [lax.all_to_all(pieces[0], "head", split_axis=0, concat_axis=0, tiled=True)]
     return [pieces[0]] + [
         shifted(piece, "head", direction * s) for s, piece in enumerate(pieces[1:], 1)
     ]
@@ -408,18 +414,18 @@
         sent.append(pick_blocks(picks, owns, (0, 2 * size), count_tm, after))
         after = (sent[-1][0],)
     message = [(0,) + parts[-1]]
-    (query,), _ = rotate_pieces(arrays, message, count_head, (sent[0][0],), stacked=True)
-    query = lax.all_to_all(query, "head", split_axis=0, concat_axis=0, tiled=True)
-    queries = received[1:] + [[query]]
+    query, _ = rotate_pieces(arrays, message, count_head, (sent[0][0],), stacked=True)
+    queries = received[1:] + [exchange(query, 1)]
     returned, after = [], ()
     for at, (_, size) in enumerate(parts):
+        last = at == len(parts) - 1
         attended = attend(
             block_tokens, bias, queries[at], query_at[at], received[at], 0,
-            forward(sent[at]), size, after, NO_COST,
+            forward(sent[at]), size, after, HIGH_COST if last else NO_COST, not last,
         )
         after = (attended[0],)
         returned.append(exchange(attended, -1))
-    return place_pieces(returned, [start for start, _ in parts], width_here)
+    return place_pieces(returned, [start for start, _ in parts], count_head, width_here)
 
 
 def solution(mesh):

time: 55.5 us -> 56 us (level)
  Pallas kernels: 16 us -> 16.7 us
    all_to_all x1 -> x2, starting transfers between devices: 3.37 us -> 9.29 us  [exchange(): lax.all_to_all(pieces[0], 'head', split_axis=0, concat_axis=0, tiled=True)]
    ppermute x18 -> x15, starting transfers between devices: 27.6 us -> 21.9 us  [shifted(): lax.ppermute(array, axis, [(i, (i + distance) % count) for i in range(cou...]
    pallas_call x2, Pallas kernels: 4.89 us -> 5.57 us  [attend(): pl.pallas_call(functools.partial(attend_kernel, (count_head, count_tm, le...]
    ppermute x18 -> x15, waiting for transfers between devices: 5.9 us -> 5.42 us  [shifted(): lax.ppermute(array, axis, [(i, (i + distance) % count) for i in range(cou...]
  transfers between devices with their start and end apart: 19 -> 17, of which waited for: 4 -> 4; matrix products, arithmetic and copies ran while one was open for 0% -> 0% of each run, Pallas kernels for 22% -> 23%
where the time goes in v3:
time: 56 us; the launch traced here: 55.6 us
  starting transfers between devices  31.2 us (56%)
  Pallas kernels  16.7 us (30%)
  waiting for transfers between devices  5.43 us (10%)
  local copies, waits for them, and re-layouts  2.05 us (4%)
    ppermute x15, starting transfers between devices, shifted(): lax.ppermute(array, axis, [(i, (i + distance) % count) for i in range(cou...  21.9 us
    all_to_all x2, starting transfers between devices, exchange(): lax.all_to_all(pieces[0], 'head', split_axis=0, concat_axis=0, tiled=True)  9.29 us
    pallas_call x3, Pallas kernels, rotate_pieces(): pl.pallas_call(functools.partial(rotate_kernel, message, sources, count_h...  6.87 us
    pallas_call x2, Pallas kernels, attend(): pl.pallas_call(functools.partial(attend_kernel, (count_head, count_tm, le...  5.57 us
    ppermute x15, waiting for transfers between devices, shifted(): lax.ppermute(array, axis, [(i, (i + distance) % count) for i in range(cou...  5.42 us
    pallas_call x1, Pallas kernels, plan(): pl.pallas_call(functools.partial(plan_kernel, count_head, count_tm, block...  2.25 us
    unnamed x22, local copies, waits for them, and re-layouts  2.05 us
    pallas_call x2, Pallas kernels, pick_blocks(): pl.pallas_call(functools.partial(pick_kernel, count_head, count_tm, lanes...  1.18 us
  transfers between devices with their start and end apart: 17, of which 4 were waited for; matrix products, arithmetic and copies ran while one was open for 0% of the time, Pallas kernels for 23%

profile of v3, /device:TPU:0, one launch (start us, length us, event | category | flops | bytes accessed | tf_op | source)
XLA Modules:
  0.0 55.6 jit_solution(14321844843701643295)
XLA Ops:
  0.0 0.0 copy-start
  0.0 0.0 copy-start.1
  0.0 2.9 %shard_map.55 = (bf16[4,16,768]{2,1,0:T(8,128)(2,1)}, bf16[4,16,768]{2,1,0:T(8,128)(2,1)}, bf16[4,16,768]{2,1,0:T(8,128)(2,1)}, bf16[4,16,768]{2,1,0:T(8,128)(2,1)}, f32[8,128]{1,0:T(8,128)}) custom-call(bf16[4,16,3072]{2,1,0:T(8,128)(2,1)} %refs_1_.3, bf16[4,16,3072]{2,1,0:T(8,128)(2,1)} %refs_2_.1), custom_call_target="tpu_custom_call" | custom-call | tf_op jit(solution)/shard_map/pallas_call | solution.py:101
  2.9 0.0 copy-start.8
  2.9 3.1 %collective-permute-start.3 = (bf16[4,16,768]{2,1,0:T(8,128)(2,1)}, bf16[4,16,768]{2,1,0:T(8,128)(2,1)S(1)}, u32[]{:S(2)}, u32[]{:S(2)}) collective-permute-start(bf16[4,16,768]{2,1,0:T(8,128)(2,1)} %get-tuple-element.34), channel_id=1, source_target_pairs={{0,4},{4,8},{8,12},{12,0},{1,5},{5,9},{9,13},{13,1},{2,6},{6,10},{... | collective-permute-start | bytes 294920 | tf_op jit(solution)/shard_map/ppermute | solution.py:374
  6.0 2.6 %collective-permute-start.4 = (bf16[4,16,768]{2,1,0:T(8,128)(2,1)}, bf16[4,16,768]{2,1,0:T(8,128)(2,1)S(1)}, u32[]{:S(2)}, u32[]{:S(2)}) collective-permute-start(bf16[4,16,768]{2,1,0:T(8,128)(2,1)} %get-tuple-element.35), channel_id=1, source_target_pairs={{0,8},{4,12},{8,0},{12,4},{1,9},{5,13},{9,1},{13,5},{2,10},{6,14},... | collective-permute-start | bytes 294920 | tf_op jit(solution)/shard_map/ppermute | solution.py:374
  8.5 0.0 copy-start.9
  8.6 1.3 %collective-permute-start.5 = (bf16[4,16,768]{2,1,0:T(8,128)(2,1)}, bf16[4,16,768]{2,1,0:T(8,128)(2,1)S(1)}, u32[]{:S(2)}, u32[]{:S(2)}) collective-permute-start(bf16[4,16,768]{2,1,0:T(8,128)(2,1)} %get-tuple-element.36), channel_id=1, source_target_pairs={{0,12},{4,0},{8,4},{12,8},{1,13},{5,1},{9,5},{13,9},{2,14},{6,2},{... | collective-permute-start | bytes 294920 | tf_op jit(solution)/shard_map/ppermute | solution.py:374
  9.9 0.0 copy-done.8
  9.9 0.0 copy-done.9
  9.9 0.0 copy-start.7
  9.9 0.7 %copy-done.7 = s32[16,32]{1,0:T(8,128)S(1)} copy-done((s32[16,32]{1,0:T(8,128)S(1)}, s32[16,32]{1,0:T(8,128)}, u32[]{:S(2)}) %copy-start.7) | copy-done | bytes 2072
  10.6 2.3 %shard_map.56 = (s32[8]{0:T(128)S(1)}, f32[4,576]{1,0:T(4,128)S(1)}) custom-call(s32[16,32]{1,0:T(8,128)S(1)} %copy-done.7, s32[16]{0:T(128)S(1)} %copy-done.9, f32[8,128]{1,0:T(8,128)S(1)} %copy-done.8), custom_call_target="tpu_custom_call" | custom-call | tf_op jit(solution)/shard_map/pallas_call | solution.py:237
  12.9 0.0 copy-start.5
  12.9 0.0 copy-done
  12.9 0.0 copy-done.1
  12.9 0.0 copy-start.2
  12.9 1.0 %copy-done.2 = bf16[4,16,3072]{2,1,0:T(8,128)(2,1)S(1)} copy-done((bf16[4,16,3072]{2,1,0:T(8,128)(2,1)S(1)}, bf16[4,16,3072]{2,1,0:T(8,128)(2,1)}, u32[]{:S(2)}) %copy-start.2) | copy-done | bytes 393240
  13.9 0.0 copy-start.4
  13.9 2.6 %shard_map.57 = (bf16[4,16,1152]{2,1,0:T(8,128)(2,1)S(1)}, bf16[4,16,1152]{2,1,0:T(8,128)(2,1)S(1)}, bf16[4,16,1152]{2,1,0:T(8,128)(2,1)S(1)}, bf16[4,16,1152]{2,1,0:T(8,128)(2,1)S(1)}, f32[8,128]{1,0:T(8,128)}) custom-call(bf16[4,16,3072]{2,1,0:T(8,128)(2,1)S(1)} %copy-done.2, bf16[4,16,3072]{2,1,0:T(8,128)(2,1)S(1)} %copy-done, ...), custom_call_target="tpu_custom_call" | custom-call | tf_op jit(solution)/shard_map/pallas_call | solution.py:101
  16.5 0.0 copy-done.5
  16.5 0.7 %collective-permute-start = (bf16[4,16,1152]{2,1,0:T(8,128)(2,1)S(1)}, bf16[4,16,1152]{2,1,0:T(8,128)(2,1)S(1)}, u32[]{:S(2)}, u32[]{:S(2)}) collective-permute-start(bf16[4,16,1152]{2,1,0:T(8,128)(2,1)S(1)} %get-tuple-element.30), channel_id=1, source_target_pairs={{0,4},{4,8},{8,12},{12,0},{1,5},{5,9},{9,13},{13,1},{2,6},{6,10},{... | collective-permute-start | bytes 442376 | tf_op jit(solution)/shard_map/ppermute | solution.py:374
  17.2 0.5 collective-permute-start.1
  17.8 0.0 collective-permute-done.3.refs_1_.refs_5_
  17.8 2.6 %collective-permute-start.2 = (bf16[4,16,1152]{2,1,0:T(8,128)(2,1)S(1)}, bf16[4,16,1152]{2,1,0:T(8,128)(2,1)S(1)}, u32[]{:S(2)}, u32[]{:S(2)}) collective-permute-start(bf16[4,16,1152]{2,1,0:T(8,128)(2,1)S(1)} %get-tuple-element.32), channel_id=1, source_target_pairs={{0,12},{4,0},{8,4},{12,8},{1,13},{5,1},{9,5},{13,9},{2,14},{6,2},{... | collective-permute-start | bytes 442376 | tf_op jit(solution)/shard_map/ppermute | solution.py:374
  20.4 0.0 collective-permute-done.4.refs_2_.refs_6_
  20.4 0.0 collective-permute-done.5.refs_3_.refs_7_
  20.4 0.0 copy-done.4
  20.4 0.0 copy-start.3
  20.4 0.6 %shard_map.58 = (bf16[2,4,16,768]{3,2,1,0:T(8,128)(2,1)S(1)}, bf16[1,4,16,768]{3,2,1,0:T(8,128)(2,1)S(1)}, bf16[2,4,16,768]{3,2,1,0:T(8,128)(2,1)S(1)}) custom-call(s32[8]{0:T(128)S(1)} %get-tuple-element.37.picks_ref, bf16[4,16,768]{2,1,0:T(8,128)(2,1)S(1)} %copy-done.4, bf16[4,16,768]{2,1,0:T(8,128)(2,1)S(1)} %collective-permute-done.3.refs_1_.refs_5_, ...), custom_call_target="tpu_custom_call" | custom-call | flops 99999997952 | tf_op jit(solution)/shard_map/pallas_call | solution.py:136
  21.0 0.1 collective-permute-start.6
  21.1 0.3 copy-done.3
  21.4 1.4 %shard_map.60 = (bf16[4,4,16,384]{3,2,1,0:T(8,128)(2,1)}, f32[8,128]{1,0:T(8,128)}) custom-call(bf16[4,16,3072]{2,1,0:T(8,128)(2,1)S(1)} %copy-done.3, bf16[2,4,16,768]{3,2,1,0:T(8,128)(2,1)S(1)} %get-tuple-element.38.refs_1_.refs_4_), custom_call_target="tpu_custom_call" | custom-call | tf_op jit(solution)/shard_map/pallas_call | solution.py:101
  22.8 1.6 %collective-permute-start.7 = (bf16[1,4,16,768]{3,2,1,0:T(8,128)(2,1)S(1)}, bf16[1,4,16,768]{3,2,1,0:T(8,128)(2,1)S(1)}, u32[]{:S(2)}, u32[]{:S(2)}) collective-permute-start(bf16[1,4,16,768]{3,2,1,0:T(8,128)(2,1)S(1)} %get-tuple-element.39), channel_id=1, source_target_pairs={{0,2},{1,3},{2,0},{3,1},{4,6},{5,7},{6,4},{7,5},{8,10},{9,11},{10,... | collective-permute-start | bytes 294920 | tf_op jit(solution)/shard_map/ppermute | solution.py:374
  24.4 3.4 %all-to-all-start.1 = ((bf16[4,4,16,384]{3,2,1,0:T(8,128)(2,1)}), bf16[4,4,16,384]{3,2,1,0:T(8,128)(2,1)S(1)}, u32[]{:S(2)}, u32[]{:S(2)}) async-start(bf16[4,4,16,384]{3,2,1,0:T(8,128)(2,1)} %get-tuple-element.41), calls=%async_computation.1 | async-start | bytes 393216 | tf_op jit(solution)/shard_map/all_to_all | solution.py:379
  27.8 0.0 collective-permute-done.refs_1_.refs_2_
  27.8 1.2 %collective-permute-start.8 = (bf16[2,4,16,768]{3,2,1,0:T(8,128)(2,1)S(1)}, bf16[2,4,16,768]{3,2,1,0:T(8,128)(2,1)S(1)}, u32[]{:S(2)}, u32[]{:S(2)}) collective-permute-start(bf16[2,4,16,768]{3,2,1,0:T(8,128)(2,1)S(1)} %get-tuple-element.40), channel_id=1, source_target_pairs={{0,3},{1,0},{2,1},{3,2},{4,7},{5,4},{6,5},{7,6},{8,11},{9,8},{10,9... | collective-permute-start | bytes 589832 | tf_op jit(solution)/shard_map/ppermute | solution.py:374
  28.9 0.6 %collective-permute-done.1.refs_2_.refs_3_ = bf16[4,16,1152]{2,1,0:T(8,128)(2,1)S(1)} collective-permute-done((bf16[4,16,1152]{2,1,0:T(8,128)(2,1)S(1)}, bf16[4,16,1152]{2,1,0:T(8,128)(2,1)S(1)}, u32[]{:S(2)}, u32[]{:S(2)}) %collective-permute-start.1) | collective-permute-done | bytes 147488 | tf_op jit(solution)/shard_map/ppermute | solution.py:374
  29.6 0.0 collective-permute-done.2.refs_3_.refs_4_
  29.6 0.6 %shard_map.61 = (bf16[2,4,16,768]{3,2,1,0:T(8,128)(2,1)S(1)}, bf16[1,4,16,768]{3,2,1,0:T(8,128)(2,1)S(1)}, bf16[2,4,16,768]{3,2,1,0:T(8,128)(2,1)S(1)}) custom-call(s32[8]{0:T(128)S(1)} %get-tuple-element.37.picks_ref, bf16[4,16,1152]{2,1,0:T(8,128)(2,1)S(1)} %get-tuple-element.29.refs_0_.refs_1_, ...), custom_call_target="tpu_custom_call" | custom-call | flops 99999997952 | tf_op jit(solution)/shard_map/pallas_call | solution.py:136
  30.2 0.1 collective-permute-start.9
  30.2 0.0 copy-start.10
  30.3 1.7 %collective-permute-start.11 = (bf16[2,4,16,768]{3,2,1,0:T(8,128)(2,1)S(1)}, bf16[2,4,16,768]{3,2,1,0:T(8,128)(2,1)S(1)}, u32[]{:S(2)}, u32[]{:S(2)}) collective-permute-start(bf16[2,4,16,768]{3,2,1,0:T(8,128)(2,1)S(1)} %get-tuple-element.44), channel_id=1, source_target_pairs={{0,3},{1,0},{2,1},{3,2},{4,7},{5,4},{6,5},{7,6},{8,11},{9,8},{10,9... | collective-permute-start | bytes 589832 | tf_op jit(solution)/shard_map/ppermute | solution.py:374
  32.0 0.0 collective-permute-done.7.refs_9_
  32.0 1.5 %collective-permute-start.10 = (bf16[1,4,16,768]{3,2,1,0:T(8,128)(2,1)S(1)}, bf16[1,4,16,768]{3,2,1,0:T(8,128)(2,1)S(1)}, u32[]{:S(2)}, u32[]{:S(2)}) collective-permute-start(bf16[1,4,16,768]{3,2,1,0:T(8,128)(2,1)S(1)} %get-tuple-element.43), channel_id=1, source_target_pairs={{0,2},{1,3},{2,0},{3,1},{4,6},{5,7},{6,4},{7,5},{8,10},{9,11},{10,... | collective-permute-start | bytes 294920 | tf_op jit(solution)/shard_map/ppermute | solution.py:374
  33.5 0.0 collective-permute-done.6.refs_8_
  33.5 0.0 collective-permute-done.8.refs_10_
  33.5 0.0 copy-done.6
  33.5 0.0 copy-done.10
  33.5 3.1 %shard_map.59.refs_8_ = bf16[4,4,16,384]{3,2,1,0:T(8,128)(2,1)} custom-call(s32[16]{0:T(128)S(1)} %copy-done.10, f32[4,576]{1,0:T(4,128)S(1)} %copy-done.6, bf16[4,16,1152]{2,1,0:T(8,128)(2,1)S(1)} %get-tuple-element.29.refs_0_.refs_1_, bf16[4,16,1152]{2,1,0:T(8,128)(2,1)S(1)} %collective-permute-done.refs_1_.refs_2_, ...), custom_call_target="tpu_custom_call" | custom-call | tf_op jit(solution)/shard_map/pallas_call | solution.py:320
  36.6 0.0 all-to-all-done.1.refs_0_
  36.6 5.9 %all-to-all-start = ((bf16[4,4,16,384]{3,2,1,0:T(8,128)(2,1)}), bf16[4,4,16,384]{3,2,1,0:T(8,128)(2,1)S(1)}, u32[]{:S(2)}, u32[]{:S(2)}) async-start(bf16[4,4,16,384]{3,2,1,0:T(8,128)(2,1)} %shard_map.59.refs_8_), calls=%async_computation | async-start | bytes 393216 | tf_op jit(solution)/shard_map/all_to_all | solution.py:379
  42.6 0.0 collective-permute-done.10.refs_6_
  42.6 0.0 collective-permute-done.9.refs_5_
  42.6 0.0 collective-permute-done.11.refs_7_
  42.6 2.4 %shard_map.62 = (bf16[4,16,384]{2,1,0:T(8,128)(2,1)S(1)}, bf16[4,16,384]{2,1,0:T(8,128)(2,1)S(1)}, bf16[4,16,384]{2,1,0:T(8,128)(2,1)S(1)}, bf16[4,16,384]{2,1,0:T(8,128)(2,1)S(1)}) custom-call(s32[16]{0:T(128)S(1)} %copy-done.10, f32[4,576]{1,0:T(4,128)S(1)} %copy-done.6, bf16[4,4,16,384]{3,2,1,0:T(8,128)(2,1)S(1)} %all-to-all-done.1.refs_0_, ...), custom_call_target="tpu_custom_call" | custom-call | flops 99999997952 | tf_op jit(solution)/shard_map/pallas_call | solution.py:320
  45.0 3.9 %collective-permute-start.12 = (bf16[4,16,384]{2,1,0:T(8,128)(2,1)S(1)}, bf16[4,16,384]{2,1,0:T(8,128)(2,1)S(1)}, u32[]{:S(2)}, u32[]{:S(2)}) collective-permute-start(bf16[4,16,384]{2,1,0:T(8,128)(2,1)S(1)} %get-tuple-element.46), channel_id=1, source_target_pairs={{0,12},{4,0},{8,4},{12,8},{1,13},{5,1},{9,5},{13,9},{2,14},{6,2},{... | collective-permute-start | bytes 147464 | tf_op jit(solution)/shard_map/ppermute | solution.py:374
  48.9 0.0 collective-permute-start.13
  48.9 1.1 %collective-permute-start.14 = (bf16[4,16,384]{2,1,0:T(8,128)(2,1)S(1)}, bf16[4,16,384]{2,1,0:T(8,128)(2,1)S(1)}, u32[]{:S(2)}, u32[]{:S(2)}) collective-permute-start(bf16[4,16,384]{2,1,0:T(8,128)(2,1)S(1)} %get-tuple-element.48), channel_id=1, source_target_pairs={{0,4},{4,8},{8,12},{12,0},{1,5},{5,9},{9,13},{13,1},{2,6},{6,10},{... | collective-permute-start | bytes 147464 | tf_op jit(solution)/shard_map/ppermute | solution.py:374
  50.0 0.6 %collective-permute-done.12.refs_2_ = bf16[4,16,384]{2,1,0:T(8,128)(2,1)S(1)} collective-permute-done((bf16[4,16,384]{2,1,0:T(8,128)(2,1)S(1)}, bf16[4,16,384]{2,1,0:T(8,128)(2,1)S(1)}, u32[]{:S(2)}, u32[]{:S(2)}) %collective-permute-start.12) | collective-permute-done | bytes 49184 | tf_op jit(solution)/shard_map/ppermute | solution.py:374
  50.6 3.2 %collective-permute-done.13.refs_3_ = bf16[4,16,384]{2,1,0:T(8,128)(2,1)S(1)} collective-permute-done((bf16[4,16,384]{2,1,0:T(8,128)(2,1)S(1)}, bf16[4,16,384]{2,1,0:T(8,128)(2,1)S(1)}, u32[]{:S(2)}, u32[]{:S(2)}) %collective-permute-start.13) | collective-permute-done | bytes 49184 | tf_op jit(solution)/shard_map/ppermute | solution.py:374
  53.9 0.9 %collective-permute-done.14.refs_4_ = bf16[4,16,384]{2,1,0:T(8,128)(2,1)S(1)} collective-permute-done((bf16[4,16,384]{2,1,0:T(8,128)(2,1)S(1)}, bf16[4,16,384]{2,1,0:T(8,128)(2,1)S(1)}, u32[]{:S(2)}, u32[]{:S(2)}) %collective-permute-start.14) | collective-permute-done | bytes 49184 | tf_op jit(solution)/shard_map/ppermute | solution.py:374
  54.8 0.0 all-to-all-done.refs_0_
  54.8 0.8 %shard_map.63 = bf16[4,16,3072]{2,1,0:T(8,128)(2,1)} custom-call(bf16[4,4,16,384]{3,2,1,0:T(8,128)(2,1)S(1)} %all-to-all-done.refs_0_, bf16[4,16,384]{2,1,0:T(8,128)(2,1)S(1)} %get-tuple-element.45.refs_1_, bf16[4,16,384]{2,1,0:T(8,128)(2,1)S(1)} %collective-permute-done.12.refs_2_, bf16[4,16,384]{2,1,0:T(8,128)(2,1)S(1)} %collective-permute-done.13.refs_3_, ...), custom_call_target="tpu_custom_call" | custom-call | tf_op jit(solution)/shard_map/pallas_call | solution.py:362
  (1 shorter events, 0.0 us)
Async XLA Ops:
  0.0 12.9 %copy-start = (bf16[4,16,3072]{2,1,0:T(8,128)(2,1)S(1)}, bf16[4,16,3072]{2,1,0:T(8,128)(2,1)}, u32[]{:S(2)}) copy-start(bf16[4,16,3072]{2,1,0:T(8,128)(2,1)} %refs_1_.3) | copy-start | bytes 1179652
  0.0 12.9 %copy-start.1 = (bf16[4,16,3072]{2,1,0:T(8,128)(2,1)S(1)}, bf16[4,16,3072]{2,1,0:T(8,128)(2,1)}, u32[]{:S(2)}) copy-start(bf16[4,16,3072]{2,1,0:T(8,128)(2,1)} %refs_2_.1) | copy-start | bytes 1179652
  2.9 7.0 %copy-start.8 = (f32[8,128]{1,0:T(8,128)S(1)}, f32[8,128]{1,0:T(8,128)}, u32[]{:S(2)}) copy-start(f32[8,128]{1,0:T(8,128)} %get-tuple-element.27._) | copy-start | bytes 12292
  2.9 14.9 %collective-permute-start.3 = (bf16[4,16,768]{2,1,0:T(8,128)(2,1)}, bf16[4,16,768]{2,1,0:T(8,128)(2,1)S(1)}, u32[]{:S(2)}, u32[]{:S(2)}) collective-permute-start(bf16[4,16,768]{2,1,0:T(8,128)(2,1)} %get-tuple-element.34), channel_id=1, source_target_pairs={{0,4},{4,8},{8,12},{12,0},{1,5},{5,9},{9,13},{13,1},{2,6},{6,10},{... | collective-permute-start | bytes 294920 | tf_op jit(solution)/shard_map/ppermute | solution.py:374
  6.0 14.4 %collective-permute-start.4 = (bf16[4,16,768]{2,1,0:T(8,128)(2,1)}, bf16[4,16,768]{2,1,0:T(8,128)(2,1)S(1)}, u32[]{:S(2)}, u32[]{:S(2)}) collective-permute-start(bf16[4,16,768]{2,1,0:T(8,128)(2,1)} %get-tuple-element.35), channel_id=1, source_target_pairs={{0,8},{4,12},{8,0},{12,4},{1,9},{5,13},{9,1},{13,5},{2,10},{6,14},... | collective-permute-start | bytes 294920 | tf_op jit(solution)/shard_map/ppermute | solution.py:374
  8.5 1.4 %copy-start.9 = (s32[16]{0:T(128)S(1)}, s32[16]{0:T(128)}, u32[]{:S(2)}) copy-start(s32[16]{0:T(128)} %tokens_ref.5) | copy-start | bytes 196
  8.6 11.8 %collective-permute-start.5 = (bf16[4,16,768]{2,1,0:T(8,128)(2,1)}, bf16[4,16,768]{2,1,0:T(8,128)(2,1)S(1)}, u32[]{:S(2)}, u32[]{:S(2)}) collective-permute-start(bf16[4,16,768]{2,1,0:T(8,128)(2,1)} %get-tuple-element.36), channel_id=1, source_target_pairs={{0,12},{4,0},{8,4},{12,8},{1,13},{5,1},{9,5},{13,9},{2,14},{6,2},{... | collective-permute-start | bytes 294920 | tf_op jit(solution)/shard_map/ppermute | solution.py:374
  9.9 0.7 %copy-start.7 = (s32[16,32]{1,0:T(8,128)S(1)}, s32[16,32]{1,0:T(8,128)}, u32[]{:S(2)}) copy-start(s32[16,32]{1,0:T(8,128)} %pair_ref.1) | copy-start | bytes 6148
  12.9 3.6 %copy-start.5 = (f32[4,576]{1,0:T(4,128)}, f32[4,576]{1,0:T(4,128)S(1)}, u32[]{:S(2)}) copy-start(f32[4,576]{1,0:T(4,128)S(1)} %get-tuple-element.28.refs_3_.bias_ref) | copy-start | bytes 27652
  12.9 1.0 %copy-start.2 = (bf16[4,16,3072]{2,1,0:T(8,128)(2,1)S(1)}, bf16[4,16,3072]{2,1,0:T(8,128)(2,1)}, u32[]{:S(2)}) copy-start(bf16[4,16,3072]{2,1,0:T(8,128)(2,1)} %refs_0_.5) | copy-start | bytes 1179652
  13.9 6.5 %copy-start.4 = (bf16[4,16,768]{2,1,0:T(8,128)(2,1)S(1)}, bf16[4,16,768]{2,1,0:T(8,128)(2,1)}, u32[]{:S(2)}) copy-start(bf16[4,16,768]{2,1,0:T(8,128)(2,1)} %get-tuple-element.33.refs_0_.refs_4_) | copy-start | bytes 294916
  16.5 11.3 %collective-permute-start = (bf16[4,16,1152]{2,1,0:T(8,128)(2,1)S(1)}, bf16[4,16,1152]{2,1,0:T(8,128)(2,1)S(1)}, u32[]{:S(2)}, u32[]{:S(2)}) collective-permute-start(bf16[4,16,1152]{2,1,0:T(8,128)(2,1)S(1)} %get-tuple-element.30), channel_id=1, source_target_pairs={{0,4},{4,8},{8,12},{12,0},{1,5},{5,9},{9,13},{13,1},{2,6},{6,10},{... | collective-permute-start | bytes 442376 | tf_op jit(solution)/shard_map/ppermute | solution.py:374
  17.2 12.3 %collective-permute-start.1 = (bf16[4,16,1152]{2,1,0:T(8,128)(2,1)S(1)}, bf16[4,16,1152]{2,1,0:T(8,128)(2,1)S(1)}, u32[]{:S(2)}, u32[]{:S(2)}) collective-permute-start(bf16[4,16,1152]{2,1,0:T(8,128)(2,1)S(1)} %get-tuple-element.31), channel_id=1, source_target_pairs={{0,8},{4,12},{8,0},{12,4},{1,9},{5,13},{9,1},{13,5},{2,10},{6,14},... | collective-permute-start | bytes 442376 | tf_op jit(solution)/shard_map/ppermute | solution.py:374
  17.8 11.8 %collective-permute-start.2 = (bf16[4,16,1152]{2,1,0:T(8,128)(2,1)S(1)}, bf16[4,16,1152]{2,1,0:T(8,128)(2,1)S(1)}, u32[]{:S(2)}, u32[]{:S(2)}) collective-permute-start(bf16[4,16,1152]{2,1,0:T(8,128)(2,1)S(1)} %get-tuple-element.32), channel_id=1, source_target_pairs={{0,12},{4,0},{8,4},{12,8},{1,13},{5,1},{9,5},{13,9},{2,14},{6,2},{... | collective-permute-start | bytes 442376 | tf_op jit(solution)/shard_map/ppermute | solution.py:374
  20.4 1.0 %copy-start.3 = (bf16[4,16,3072]{2,1,0:T(8,128)(2,1)S(1)}, bf16[4,16,3072]{2,1,0:T(8,128)(2,1)}, u32[]{:S(2)}) copy-start(bf16[4,16,3072]{2,1,0:T(8,128)(2,1)} %refs_0_.5) | copy-start | bytes 1179652
  21.0 12.5 %collective-permute-start.6 = (bf16[2,4,16,768]{3,2,1,0:T(8,128)(2,1)S(1)}, bf16[2,4,16,768]{3,2,1,0:T(8,128)(2,1)S(1)}, u32[]{:S(2)}, u32[]{:S(2)}) collective-permute-start(bf16[2,4,16,768]{3,2,1,0:T(8,128)(2,1)S(1)} %get-tuple-element.38.refs_1_.refs_4_), channel_id=1, source_target_pairs={{0,1},{1,2},{2,3},{3,0},{4,5},{5,6},{6,7},{7,4},{8,9},{9,10},{10,1... | collective-permute-start | bytes 589832 | tf_op jit(solution)/shard_map/ppermute | solution.py:374
  22.8 9.2 %collective-permute-start.7 = (bf16[1,4,16,768]{3,2,1,0:T(8,128)(2,1)S(1)}, bf16[1,4,16,768]{3,2,1,0:T(8,128)(2,1)S(1)}, u32[]{:S(2)}, u32[]{:S(2)}) collective-permute-start(bf16[1,4,16,768]{3,2,1,0:T(8,128)(2,1)S(1)} %get-tuple-element.39), channel_id=1, source_target_pairs={{0,2},{1,3},{2,0},{3,1},{4,6},{5,7},{6,4},{7,5},{8,10},{9,11},{10,... | collective-permute-start | bytes 294920 | tf_op jit(solution)/shard_map/ppermute | solution.py:374
  24.4 12.2 %all-to-all-start.1 = ((bf16[4,4,16,384]{3,2,1,0:T(8,128)(2,1)}), bf16[4,4,16,384]{3,2,1,0:T(8,128)(2,1)S(1)}, u32[]{:S(2)}, u32[]{:S(2)}) async-start(bf16[4,4,16,384]{3,2,1,0:T(8,128)(2,1)} %get-tuple-element.41), calls=%async_computation.1 | async-start | bytes 393216 | tf_op jit(solution)/shard_map/all_to_all | solution.py:379
  27.8 5.7 %collective-permute-start.8 = (bf16[2,4,16,768]{3,2,1,0:T(8,128)(2,1)S(1)}, bf16[2,4,16,768]{3,2,1,0:T(8,128)(2,1)S(1)}, u32[]{:S(2)}, u32[]{:S(2)}) collective-permute-start(bf16[2,4,16,768]{3,2,1,0:T(8,128)(2,1)S(1)} %get-tuple-element.40), channel_id=1, source_target_pairs={{0,3},{1,0},{2,1},{3,2},{4,7},{5,4},{6,5},{7,6},{8,11},{9,8},{10,9... | collective-permute-start | bytes 589832 | tf_op jit(solution)/shard_map/ppermute | solution.py:374
  29.6 3.9 %copy-start.6 = (f32[4,576]{1,0:T(4,128)S(1)}, f32[4,576]{1,0:T(4,128)}, u32[]{:S(2)}) copy-start(f32[4,576]{1,0:T(4,128)} %copy-done.5) | copy-start | bytes 27652
  30.2 12.4 %collective-permute-start.9 = (bf16[2,4,16,768]{3,2,1,0:T(8,128)(2,1)S(1)}, bf16[2,4,16,768]{3,2,1,0:T(8,128)(2,1)S(1)}, u32[]{:S(2)}, u32[]{:S(2)}) collective-permute-start(bf16[2,4,16,768]{3,2,1,0:T(8,128)(2,1)S(1)} %get-tuple-element.42), channel_id=1, source_target_pairs={{0,1},{1,2},{2,3},{3,0},{4,5},{5,6},{6,7},{7,4},{8,9},{9,10},{10,1... | collective-permute-start | bytes 589832 | tf_op jit(solution)/shard_map/ppermute | solution.py:374
  30.2 3.2 %copy-start.10 = (s32[16]{0:T(128)S(1)}, s32[16]{0:T(128)}, u32[]{:S(2)}) copy-start(s32[16]{0:T(128)} %tokens_ref.5) | copy-start | bytes 196
  30.3 12.3 %collective-permute-start.11 = (bf16[2,4,16,768]{3,2,1,0:T(8,128)(2,1)S(1)}, bf16[2,4,16,768]{3,2,1,0:T(8,128)(2,1)S(1)}, u32[]{:S(2)}, u32[]{:S(2)}) collective-permute-start(bf16[2,4,16,768]{3,2,1,0:T(8,128)(2,1)S(1)} %get-tuple-element.44), channel_id=1, source_target_pairs={{0,3},{1,0},{2,1},{3,2},{4,7},{5,4},{6,5},{7,6},{8,11},{9,8},{10,9... | collective-permute-start | bytes 589832 | tf_op jit(solution)/shard_map/ppermute | solution.py:374
  32.0 10.6 %collective-permute-start.10 = (bf16[1,4,16,768]{3,2,1,0:T(8,128)(2,1)S(1)}, bf16[1,4,16,768]{3,2,1,0:T(8,128)(2,1)S(1)}, u32[]{:S(2)}, u32[]{:S(2)}) collective-permute-start(bf16[1,4,16,768]{3,2,1,0:T(8,128)(2,1)S(1)} %get-tuple-element.43), channel_id=1, source_target_pairs={{0,2},{1,3},{2,0},{3,1},{4,6},{5,7},{6,4},{7,5},{8,10},{9,11},{10,... | collective-permute-start | bytes 294920 | tf_op jit(solution)/shard_map/ppermute | solution.py:374
  36.6 18.2 %all-to-all-start = ((bf16[4,4,16,384]{3,2,1,0:T(8,128)(2,1)}), bf16[4,4,16,384]{3,2,1,0:T(8,128)(2,1)S(1)}, u32[]{:S(2)}, u32[]{:S(2)}) async-start(bf16[4,4,16,384]{3,2,1,0:T(8,128)(2,1)} %shard_map.59.refs_8_), calls=%async_computation | async-start | bytes 393216 | tf_op jit(solution)/shard_map/all_to_all | solution.py:379
  45.0 5.6 %collective-permute-start.12 = (bf16[4,16,384]{2,1,0:T(8,128)(2,1)S(1)}, bf16[4,16,384]{2,1,0:T(8,128)(2,1)S(1)}, u32[]{:S(2)}, u32[]{:S(2)}) collective-permute-start(bf16[4,16,384]{2,1,0:T(8,128)(2,1)S(1)} %get-tuple-element.46), channel_id=1, source_target_pairs={{0,12},{4,0},{8,4},{12,8},{1,13},{5,1},{9,5},{13,9},{2,14},{6,2},{... | collective-permute-start | bytes 147464 | tf_op jit(solution)/shard_map/ppermute | solution.py:374
  48.9 5.0 %collective-permute-start.13 = (bf16[4,16,384]{2,1,0:T(8,128)(2,1)S(1)}, bf16[4,16,384]{2,1,0:T(8,128)(2,1)S(1)}, u32[]{:S(2)}, u32[]{:S(2)}) collective-permute-start(bf16[4,16,384]{2,1,0:T(8,128)(2,1)S(1)} %get-tuple-element.47), channel_id=1, source_target_pairs={{0,8},{4,12},{8,0},{12,4},{1,9},{5,13},{9,1},{13,5},{2,10},{6,14},... | collective-permute-start | bytes 147464 | tf_op jit(solution)/shard_map/ppermute | solution.py:374
  48.9 5.9 %collective-permute-start.14 = (bf16[4,16,384]{2,1,0:T(8,128)(2,1)S(1)}, bf16[4,16,384]{2,1,0:T(8,128)(2,1)S(1)}, u32[]{:S(2)}, u32[]{:S(2)}) collective-permute-start(bf16[4,16,384]{2,1,0:T(8,128)(2,1)S(1)} %get-tuple-element.48), channel_id=1, source_target_pairs={{0,4},{4,8},{8,12},{12,0},{1,5},{5,9},{9,13},{13,1},{2,6},{6,10},{... | collective-permute-start | bytes 147464 | tf_op jit(solution)/shard_map/ppermute | solution.py:374

commit v4 on v2

--- a/solution.py
+++ b/solution.py
@@ -59,9 +59,10 @@
 def rotate_kernel(message, sources, count_head, skipped, *refs):
     fields, total = fields_of(message)
     ins = dict(zip(sources, refs))
-    outs = by_distance(refs[len(sources) + skipped : -3], count_head, 1)
-    token, buffer, sems = refs[-3:]
+    outs = by_distance(refs[len(sources) + skipped : -5], count_head, 1)
+    token, buffer, sems, turned_ref, out_sems = refs[-5:]
     token[...] = jnp.zeros_like(token)
+    leaving = []
     blocks, tokens, width = refs[0].shape
     width_here = width // count_head
     me = lax.axis_index("head")
@@ -89,7 +90,11 @@
             turned = (turned * ROTATE_SCALE).reshape(size // HD, blocks, tokens, HD)
             for h in range(size // HD):
                 at = start + h * HD
-                outs[s][:, :, at : at + HD] = turned[h].astype(jnp.bfloat16)
+                turned_ref[s, :, :, at : at + HD] = turned[h].astype(jnp.bfloat16)
+        leaving.append(pltpu.make_async_copy(turned_ref.at[s], outs[s], out_sems.at[s]))
+        leaving[-1].start()
+    for copy in leaving:
+        copy.wait()
 
 
 def rotate_pieces(arrays, message, count_head, after=(), limit=VMEM, stacked=False):
@@ -102,11 +107,14 @@
         functools.partial(rotate_kernel, message, sources, count_head, len(after)),
         in_specs=[pl.BlockSpec(memory_space=pltpu.HBM)] * len(sources)
         + [pl.BlockSpec(memory_space=pl.ANY)] * len(after),
-        out_specs=[pl.BlockSpec(memory_space=pltpu.VMEM)] * (len(shapes) + 1),
+        out_specs=[pl.BlockSpec(memory_space=pl.ANY)] * len(shapes)
+        + [pl.BlockSpec(memory_space=pltpu.VMEM)],
         out_shape=[jax.ShapeDtypeStruct(shape, jnp.bfloat16) for shape in shapes] + [TOKEN],
         scratch_shapes=[
             pltpu.VMEM((count_head,) + one, jnp.bfloat16),
             pltpu.SemaphoreType.DMA((count_head, len(fields))),
+            pltpu.VMEM((count_head,) + one, jnp.bfloat16),
+            pltpu.SemaphoreType.DMA((count_head,)),
         ],
         cost_estimate=NO_COST,
         compiler_params=pltpu.CompilerParams(vmem_limit_bytes=limit),
@@ -265,49 +273,55 @@
     blocks, tokens, _ = owns[0].shape
     shard = lax.axis_index("tm")
     me = lax.axis_index("head")
-    sign = sign_matrix()
-    for h in range(size // HD):
-        lanes = slice(h * HD, (h + 1) * HD)
-        query_lanes = slice(query_at + h * HD, query_at + (h + 1) * HD)
+    heads = size // HD
+    bias = bias_ref[...][:, None, :]
+
+    def gathered(kind, h):
+        first = kind * size + h * HD
+        own_lanes = slice(key_at + first, key_at + first + HD)
+        pieces = [rows_of(own[:, :, own_lanes]) for own in owns]
+        pieces += [
+            rows_of(slots[distance - 1][k, :, :, first : first + HD])
+            for distance, k in remote_rows(count_tm)
+        ]
+        return jnp.concatenate(pieces, axis=0)
+
+    def products(h):
+        lanes = slice(query_at + h * HD, query_at + (h + 1) * HD)
         query = jnp.concatenate(
-            [rows_of(queries[s][i, :, query_lanes]) for i in range(blocks) for s in range(count_head)],
+            [rows_of(queries[s][i, :, lanes]) for i in range(blocks) for s in range(count_head)],
             axis=0,
         )
-
-        def gathered(kind):
-            first = kind * size + h * HD
-            own_lanes = slice(key_at + first, key_at + first + HD)
-            pieces = [rows_of(own[:, :, own_lanes]) for own in owns]
-            pieces += [
-                rows_of(slots[distance - 1][k, :, :, first : first + HD])
-                for distance, k in remote_rows(count_tm)
-            ]
-            return jnp.concatenate(pieces, axis=0)
-
-        keys, values = gathered(0), gathered(1)
-        total = keys.shape[0]
-        dots = lax.dot_general(
-            query, keys, (((1,), (1,)), ((), ())), preferred_element_type=jnp.float32
+        return lax.dot_general(
+            query, gathered(0, h), (((1,), (1,)), ((), ())), preferred_element_type=jnp.float32
         )
-        dots = dots.reshape(blocks, BLK, total) + bias_ref[...][:, None, :]
+
+    dots, mixed = products(0), []
+    for h in range(heads):
+        ahead = products(h + 1) if h + 1 < heads else None
+        dots = dots.reshape(blocks, BLK, -1) + bias
         peak = jnp.max(dots, axis=-1, keepdims=True)
         weights = jnp.exp2((dots - peak) * (SCORE_SCALE * LOG2E))
-        denominator = jnp.sum(weights, axis=-1, keepdims=True).reshape(blocks * BLK, 1)
-        weights_half = weights.astype(jnp.bfloat16).reshape(blocks * BLK, total)
-        mixed = jnp.dot(weights_half, values, preferred_element_type=jnp.float32) / denominator
-        turned = jnp.zeros_like(mixed)
-        rest = mixed
-        for _ in range(3):
-            piece = rest.astype(jnp.bfloat16)
-            turned = turned + jnp.dot(piece, sign, preferred_element_type=jnp.float32)
-            rest = rest - piece.astype(jnp.float32)
-        turned = (turned * ROTATE_SCALE).reshape(blocks, count_head, tokens, HD)
-        token = lax.broadcasted_iota(jnp.int32, (tokens, HD), 0)
-        for s in range(count_head):
-            position = lax.rem(me - s + count_head, count_head) * tokens + token
-            for i in range(blocks):
-                outs[s][i, :, lanes] = jnp.where(
-                    position < tokens_ref[shard * blocks + i], turned[i, s], 0.0
+        inverse = 1.0 / jnp.sum(weights, axis=-1, keepdims=True)
+        weights_half = weights.astype(jnp.bfloat16).reshape(blocks * BLK, -1)
+        rows = jnp.dot(weights_half, gathered(1, h), preferred_element_type=jnp.float32)
+        mixed.append(rows * inverse.reshape(blocks * BLK, 1))
+        dots = ahead
+    mixed = jnp.concatenate(mixed, axis=0)
+    sign = sign_matrix()
+    high = mixed.astype(jnp.bfloat16)
+    low = (mixed - high.astype(jnp.float32)).astype(jnp.bfloat16)
+    turned = jnp.dot(high, sign, preferred_element_type=jnp.float32)
+    turned = turned + jnp.dot(low, sign, preferred_element_type=jnp.float32)
+    turned = (turned * ROTATE_SCALE).reshape(heads, blocks, count_head, tokens, HD)
+    token = lax.broadcasted_iota(jnp.int32, (tokens, HD), 0)
+    for s in range(count_head):
+        position = lax.rem(me - s + count_head, count_head) * tokens + token
+        for i in range(blocks):
+            live = position < tokens_ref[shard * blocks + i]
+            for h in range(heads):
+                outs[s][i, :, h * HD : (h + 1) * HD] = jnp.where(
+                    live, turned[h, i, s], 0.0
                 ).astype(jnp.bfloat16)
 
 

time: 55.5 us -> 55 us (level)
  waiting for transfers between devices: 5.9 us -> 4.72 us
  Pallas kernels: 16 us -> 16.7 us
    pallas_call x3, Pallas kernels: 6.88 us -> 8.99 us  [rotate_pieces(): pl.pallas_call(functools.partial(rotate_kernel, message, sources, count_h...]
    pallas_call x2, Pallas kernels: 4.89 us -> 3.47 us  [attend(): pl.pallas_call(functools.partial(attend_kernel, (count_head, count_tm, le...]
    ppermute x18, waiting for transfers between devices: 5.9 us -> 4.72 us  [shifted(): lax.ppermute(array, axis, [(i, (i + distance) % count) for i in range(cou...]
  transfers between devices with their start and end apart: 19 -> 19, of which waited for: 4 -> 5; matrix products, arithmetic and copies ran while one was open for 0% -> 0% of each run, Pallas kernels for 22% -> 23%
where the time goes in v4:
time: 55 us; the launch traced here: 54.6 us
  starting transfers between devices  31 us (56%)
  Pallas kernels  16.7 us (30%)
  waiting for transfers between devices  4.72 us (9%)
  local copies, waits for them, and re-layouts  2.05 us (4%)
    ppermute x18, starting transfers between devices, shifted(): lax.ppermute(array, axis, [(i, (i + distance) % count) for i in range(cou...  27.6 us
    pallas_call x3, Pallas kernels, rotate_pieces(): pl.pallas_call(functools.partial(rotate_kernel, message, sources, count_h...  8.99 us
    ppermute x18, waiting for transfers between devices, shifted(): lax.ppermute(array, axis, [(i, (i + distance) % count) for i in range(cou...  4.72 us
    pallas_call x2, Pallas kernels, attend(): pl.pallas_call(functools.partial(attend_kernel, (count_head, count_tm, le...  3.47 us
    all_to_all x1, starting transfers between devices, shards(): lax.all_to_all(query, 'head', split_axis=0, concat_axis=0, tiled=True)  3.37 us
    pallas_call x1, Pallas kernels, plan(): pl.pallas_call(functools.partial(plan_kernel, count_head, count_tm, block...  2.25 us
    unnamed x22, local copies, waits for them, and re-layouts  2.05 us
    pallas_call x2, Pallas kernels, pick_blocks(): pl.pallas_call(functools.partial(pick_kernel, count_head, count_tm, lanes...  1.18 us
  transfers between devices with their start and end apart: 19, of which 5 were waited for; matrix products, arithmetic and copies ran while one was open for 0% of the time, Pallas kernels for 23%

profile of v4, /device:TPU:0, one launch (start us, length us, event | category | flops | bytes accessed | tf_op | source)
XLA Modules:
  0.0 54.6 jit_solution(8217559888235363660)
XLA Ops:
  0.0 0.0 copy-start
  0.0 3.5 %shard_map.55 = (bf16[4,16,768]{2,1,0:T(8,128)(2,1)}, bf16[4,16,768]{2,1,0:T(8,128)(2,1)}, bf16[4,16,768]{2,1,0:T(8,128)(2,1)}, bf16[4,16,768]{2,1,0:T(8,128)(2,1)}, f32[8,128]{1,0:T(8,128)}) custom-call(bf16[4,16,3072]{2,1,0:T(8,128)(2,1)} %refs_1_.3, bf16[4,16,3072]{2,1,0:T(8,128)(2,1)} %refs_2_.1), custom_call_target="tpu_custom_call" | custom-call | tf_op jit(solution)/shard_map/pallas_call | solution.py:106
  3.5 0.0 copy-start.10
  3.5 3.1 %collective-permute-start.3 = (bf16[4,16,768]{2,1,0:T(8,128)(2,1)}, bf16[4,16,768]{2,1,0:T(8,128)(2,1)S(1)}, u32[]{:S(2)}, u32[]{:S(2)}) collective-permute-start(bf16[4,16,768]{2,1,0:T(8,128)(2,1)} %get-tuple-element.38), channel_id=1, source_target_pairs={{0,4},{4,8},{8,12},{12,0},{1,5},{5,9},{9,13},{13,1},{2,6},{6,10},{... | collective-permute-start | bytes 294920 | tf_op jit(solution)/shard_map/ppermute | solution.py:384
  6.6 2.6 %collective-permute-start.4 = (bf16[4,16,768]{2,1,0:T(8,128)(2,1)}, bf16[4,16,768]{2,1,0:T(8,128)(2,1)S(1)}, u32[]{:S(2)}, u32[]{:S(2)}) collective-permute-start(bf16[4,16,768]{2,1,0:T(8,128)(2,1)} %get-tuple-element.39), channel_id=1, source_target_pairs={{0,8},{4,12},{8,0},{12,4},{1,9},{5,13},{9,1},{13,5},{2,10},{6,14},... | collective-permute-start | bytes 294920 | tf_op jit(solution)/shard_map/ppermute | solution.py:384
  9.2 1.3 %collective-permute-start.5 = (bf16[4,16,768]{2,1,0:T(8,128)(2,1)}, bf16[4,16,768]{2,1,0:T(8,128)(2,1)S(1)}, u32[]{:S(2)}, u32[]{:S(2)}) collective-permute-start(bf16[4,16,768]{2,1,0:T(8,128)(2,1)} %get-tuple-element.40), channel_id=1, source_target_pairs={{0,12},{4,0},{8,4},{12,8},{1,13},{5,1},{9,5},{13,9},{2,14},{6,2},{... | collective-permute-start | bytes 294920 | tf_op jit(solution)/shard_map/ppermute | solution.py:384
  10.5 0.0 copy-done.10
  10.5 0.0 copy-done.8
  10.5 0.7 %copy-done.7 = s32[16,32]{1,0:T(8,128)S(1)} copy-done((s32[16,32]{1,0:T(8,128)S(1)}, s32[16,32]{1,0:T(8,128)}, u32[]{:S(2)}) %copy-start.7) | copy-done | bytes 2072
  11.2 2.3 %shard_map.56 = (s32[8]{0:T(128)S(1)}, f32[4,576]{1,0:T(4,128)S(1)}) custom-call(s32[16,32]{1,0:T(8,128)S(1)} %copy-done.7, s32[16]{0:T(128)S(1)} %copy-done.8, f32[8,128]{1,0:T(8,128)S(1)} %copy-done.10), custom_call_target="tpu_custom_call" | custom-call | tf_op jit(solution)/shard_map/pallas_call | solution.py:245
  13.5 0.0 copy-start.5
  13.5 0.0 copy-done
  13.5 0.0 copy-done.1
  13.5 0.0 copy-start.2
  13.5 1.0 %copy-done.2 = bf16[4,16,3072]{2,1,0:T(8,128)(2,1)S(1)} copy-done((bf16[4,16,3072]{2,1,0:T(8,128)(2,1)S(1)}, bf16[4,16,3072]{2,1,0:T(8,128)(2,1)}, u32[]{:S(2)}) %copy-start.2) | copy-done | bytes 393240
  14.5 3.5 %shard_map.57 = (bf16[4,16,1152]{2,1,0:T(8,128)(2,1)S(1)}, bf16[4,16,1152]{2,1,0:T(8,128)(2,1)S(1)}, bf16[4,16,1152]{2,1,0:T(8,128)(2,1)S(1)}, bf16[4,16,1152]{2,1,0:T(8,128)(2,1)S(1)}, f32[8,128]{1,0:T(8,128)}) custom-call(bf16[4,16,3072]{2,1,0:T(8,128)(2,1)S(1)} %copy-done.2, bf16[4,16,3072]{2,1,0:T(8,128)(2,1)S(1)} %copy-done, ...), custom_call_target="tpu_custom_call" | custom-call | tf_op jit(solution)/shard_map/pallas_call | solution.py:106
  18.0 0.0 copy-done.5
  18.0 0.7 %collective-permute-start = (bf16[4,16,1152]{2,1,0:T(8,128)(2,1)S(1)}, bf16[4,16,1152]{2,1,0:T(8,128)(2,1)S(1)}, u32[]{:S(2)}, u32[]{:S(2)}) collective-permute-start(bf16[4,16,1152]{2,1,0:T(8,128)(2,1)S(1)} %get-tuple-element.34), channel_id=1, source_target_pairs={{0,4},{4,8},{8,12},{12,0},{1,5},{5,9},{9,13},{13,1},{2,6},{6,10},{... | collective-permute-start | bytes 442376 | tf_op jit(solution)/shard_map/ppermute | solution.py:384
  18.8 0.5 collective-permute-start.1
  19.3 0.0 collective-permute-done.3.refs_1_.refs_5_
  19.3 2.6 %collective-permute-start.2 = (bf16[4,16,1152]{2,1,0:T(8,128)(2,1)S(1)}, bf16[4,16,1152]{2,1,0:T(8,128)(2,1)S(1)}, u32[]{:S(2)}, u32[]{:S(2)}) collective-permute-start(bf16[4,16,1152]{2,1,0:T(8,128)(2,1)S(1)} %get-tuple-element.36), channel_id=1, source_target_pairs={{0,12},{4,0},{8,4},{12,8},{1,13},{5,1},{9,5},{13,9},{2,14},{6,2},{... | collective-permute-start | bytes 442376 | tf_op jit(solution)/shard_map/ppermute | solution.py:384
  21.9 0.0 collective-permute-done.4.refs_2_.refs_6_
  21.9 0.0 collective-permute-done.5.refs_3_.refs_7_
  21.9 0.0 copy-done.4
  21.9 0.0 copy-start.3
  22.0 0.6 %shard_map.58 = (bf16[2,4,16,768]{3,2,1,0:T(8,128)(2,1)S(1)}, bf16[1,4,16,768]{3,2,1,0:T(8,128)(2,1)S(1)}, bf16[2,4,16,768]{3,2,1,0:T(8,128)(2,1)S(1)}) custom-call(s32[8]{0:T(128)S(1)} %get-tuple-element.41.picks_ref, bf16[4,16,768]{2,1,0:T(8,128)(2,1)S(1)} %copy-done.4, bf16[4,16,768]{2,1,0:T(8,128)(2,1)S(1)} %collective-permute-done.3.refs_1_.refs_5_, ...), custom_call_target="tpu_custom_call" | custom-call | flops 99999997952 | tf_op jit(solution)/shard_map/pallas_call | solution.py:144
  22.6 0.1 collective-permute-start.6
  22.6 0.3 copy-done.3
  22.9 2.0 %shard_map.60 = (bf16[4,4,16,384]{3,2,1,0:T(8,128)(2,1)}, f32[8,128]{1,0:T(8,128)}) custom-call(bf16[4,16,3072]{2,1,0:T(8,128)(2,1)S(1)} %copy-done.3, bf16[2,4,16,768]{3,2,1,0:T(8,128)(2,1)S(1)} %get-tuple-element.42.refs_1_.refs_4_), custom_call_target="tpu_custom_call" | custom-call | tf_op jit(solution)/shard_map/pallas_call | solution.py:106
  24.9 1.6 %collective-permute-start.7 = (bf16[1,4,16,768]{3,2,1,0:T(8,128)(2,1)S(1)}, bf16[1,4,16,768]{3,2,1,0:T(8,128)(2,1)S(1)}, u32[]{:S(2)}, u32[]{:S(2)}) collective-permute-start(bf16[1,4,16,768]{3,2,1,0:T(8,128)(2,1)S(1)} %get-tuple-element.43), channel_id=1, source_target_pairs={{0,2},{1,3},{2,0},{3,1},{4,6},{5,7},{6,4},{7,5},{8,10},{9,11},{10,... | collective-permute-start | bytes 294920 | tf_op jit(solution)/shard_map/ppermute | solution.py:384
  26.5 3.4 %all-to-all-start = ((bf16[4,4,16,384]{3,2,1,0:T(8,128)(2,1)}), bf16[4,4,16,384]{3,2,1,0:T(8,128)(2,1)S(1)}, u32[]{:S(2)}, u32[]{:S(2)}) async-start(bf16[4,4,16,384]{3,2,1,0:T(8,128)(2,1)} %get-tuple-element.49), calls=%async_computation | async-start | bytes 393216 | tf_op jit(solution)/shard_map/all_to_all | solution.py:426
  29.9 0.0 collective-permute-done.refs_1_.refs_2_
  29.9 1.2 %collective-permute-start.8 = (bf16[2,4,16,768]{3,2,1,0:T(8,128)(2,1)S(1)}, bf16[2,4,16,768]{3,2,1,0:T(8,128)(2,1)S(1)}, u32[]{:S(2)}, u32[]{:S(2)}) collective-permute-start(bf16[2,4,16,768]{3,2,1,0:T(8,128)(2,1)S(1)} %get-tuple-element.44), channel_id=1, source_target_pairs={{0,3},{1,0},{2,1},{3,2},{4,7},{5,4},{6,5},{7,6},{8,11},{9,8},{10,9... | collective-permute-start | bytes 589832 | tf_op jit(solution)/shard_map/ppermute | solution.py:384
  31.1 0.1 collective-permute-done.1.refs_2_.refs_3_
  31.1 0.0 collective-permute-done.2.refs_3_.refs_4_
  31.1 0.6 %shard_map.61 = (bf16[2,4,16,768]{3,2,1,0:T(8,128)(2,1)S(1)}, bf16[1,4,16,768]{3,2,1,0:T(8,128)(2,1)S(1)}, bf16[2,4,16,768]{3,2,1,0:T(8,128)(2,1)S(1)}) custom-call(s32[8]{0:T(128)S(1)} %get-tuple-element.41.picks_ref, bf16[4,16,1152]{2,1,0:T(8,128)(2,1)S(1)} %get-tuple-element.33.refs_0_.refs_1_, ...), custom_call_target="tpu_custom_call" | custom-call | flops 99999997952 | tf_op jit(solution)/shard_map/pallas_call | solution.py:144
  31.7 0.1 collective-permute-start.12
  31.8 0.0 copy-start.9
  31.8 1.7 %collective-permute-start.14 = (bf16[2,4,16,768]{3,2,1,0:T(8,128)(2,1)S(1)}, bf16[2,4,16,768]{3,2,1,0:T(8,128)(2,1)S(1)}, u32[]{:S(2)}, u32[]{:S(2)}) collective-permute-start(bf16[2,4,16,768]{3,2,1,0:T(8,128)(2,1)S(1)} %get-tuple-element.52), channel_id=1, source_target_pairs={{0,3},{1,0},{2,1},{3,2},{4,7},{5,4},{6,5},{7,6},{8,11},{9,8},{10,9... | collective-permute-start | bytes 589832 | tf_op jit(solution)/shard_map/ppermute | solution.py:384
  33.5 0.0 collective-permute-done.7.refs_9_
  33.5 1.5 %collective-permute-start.13 = (bf16[1,4,16,768]{3,2,1,0:T(8,128)(2,1)S(1)}, bf16[1,4,16,768]{3,2,1,0:T(8,128)(2,1)S(1)}, u32[]{:S(2)}, u32[]{:S(2)}) collective-permute-start(bf16[1,4,16,768]{3,2,1,0:T(8,128)(2,1)S(1)} %get-tuple-element.51), channel_id=1, source_target_pairs={{0,2},{1,3},{2,0},{3,1},{4,6},{5,7},{6,4},{7,5},{8,10},{9,11},{10,... | collective-permute-start | bytes 294920 | tf_op jit(solution)/shard_map/ppermute | solution.py:384
  35.0 0.0 collective-permute-done.6.refs_8_
  35.0 0.0 collective-permute-done.8.refs_10_
  35.0 0.0 copy-done.6
  35.0 0.0 copy-done.9
  35.0 1.7 %shard_map.59 = (bf16[4,16,384]{2,1,0:T(8,128)(2,1)S(1)}, bf16[4,16,384]{2,1,0:T(8,128)(2,1)S(1)}, bf16[4,16,384]{2,1,0:T(8,128)(2,1)S(1)}, bf16[4,16,384]{2,1,0:T(8,128)(2,1)S(1)}) custom-call(s32[16]{0:T(128)S(1)} %copy-done.9, f32[4,576]{1,0:T(4,128)S(1)} %copy-done.6, bf16[4,16,1152]{2,1,0:T(8,128)(2,1)S(1)} %get-tuple-element.33.refs_0_.refs_1_, ...), custom_call_target="tpu_custom_call" | custom-call | tf_op jit(solution)/shard_map/pallas_call | solution.py:332
  36.8 3.8 %collective-permute-start.9 = (bf16[4,16,384]{2,1,0:T(8,128)(2,1)S(1)}, bf16[4,16,384]{2,1,0:T(8,128)(2,1)S(1)}, u32[]{:S(2)}, u32[]{:S(2)}) collective-permute-start(bf16[4,16,384]{2,1,0:T(8,128)(2,1)S(1)} %get-tuple-element.46), channel_id=1, source_target_pairs={{0,12},{4,0},{8,4},{12,8},{1,13},{5,1},{9,5},{13,9},{2,14},{6,2},{... | collective-permute-start | bytes 147464 | tf_op jit(solution)/shard_map/ppermute | solution.py:384
  40.6 0.8 %collective-permute-start.10 = (bf16[4,16,384]{2,1,0:T(8,128)(2,1)S(1)}, bf16[4,16,384]{2,1,0:T(8,128)(2,1)S(1)}, u32[]{:S(2)}, u32[]{:S(2)}) collective-permute-start(bf16[4,16,384]{2,1,0:T(8,128)(2,1)S(1)} %get-tuple-element.47), channel_id=1, source_target_pairs={{0,8},{4,12},{8,0},{12,4},{1,9},{5,13},{9,1},{13,5},{2,10},{6,14},... | collective-permute-start | bytes 147464 | tf_op jit(solution)/shard_map/ppermute | solution.py:384
  41.4 0.2 collective-permute-done.13.refs_6_
  41.6 2.6 %collective-permute-start.11 = (bf16[4,16,384]{2,1,0:T(8,128)(2,1)S(1)}, bf16[4,16,384]{2,1,0:T(8,128)(2,1)S(1)}, u32[]{:S(2)}, u32[]{:S(2)}) collective-permute-start(bf16[4,16,384]{2,1,0:T(8,128)(2,1)S(1)} %get-tuple-element.48), channel_id=1, source_target_pairs={{0,4},{4,8},{8,12},{12,0},{1,5},{5,9},{9,13},{13,1},{2,6},{6,10},{... | collective-permute-start | bytes 147464 | tf_op jit(solution)/shard_map/ppermute | solution.py:384
  44.1 0.0 collective-permute-done.12.refs_5_
  44.1 0.0 collective-permute-done.14.refs_7_
  44.2 0.0 all-to-all-done.refs_0_
  44.2 1.7 %shard_map.62 = (bf16[4,16,384]{2,1,0:T(8,128)(2,1)S(1)}, bf16[4,16,384]{2,1,0:T(8,128)(2,1)S(1)}, bf16[4,16,384]{2,1,0:T(8,128)(2,1)S(1)}, bf16[4,16,384]{2,1,0:T(8,128)(2,1)S(1)}) custom-call(s32[16]{0:T(128)S(1)} %copy-done.9, f32[4,576]{1,0:T(4,128)S(1)} %copy-done.6, bf16[4,4,16,384]{3,2,1,0:T(8,128)(2,1)S(1)} %all-to-all-done.refs_0_, ...), custom_call_target="tpu_custom_call" | custom-call | tf_op jit(solution)/shard_map/pallas_call | solution.py:332
  45.9 1.3 %collective-permute-start.15 = (bf16[4,16,384]{2,1,0:T(8,128)(2,1)S(1)}, bf16[4,16,384]{2,1,0:T(8,128)(2,1)S(1)}, u32[]{:S(2)}, u32[]{:S(2)}) collective-permute-start(bf16[4,16,384]{2,1,0:T(8,128)(2,1)S(1)} %get-tuple-element.54), channel_id=1, source_target_pairs={{0,12},{4,0},{8,4},{12,8},{1,13},{5,1},{9,5},{13,9},{2,14},{6,2},{... | collective-permute-start | bytes 147464 | tf_op jit(solution)/shard_map/ppermute | solution.py:384
  47.2 0.8 %collective-permute-start.16 = (bf16[4,16,384]{2,1,0:T(8,128)(2,1)S(1)}, bf16[4,16,384]{2,1,0:T(8,128)(2,1)S(1)}, u32[]{:S(2)}, u32[]{:S(2)}) collective-permute-start(bf16[4,16,384]{2,1,0:T(8,128)(2,1)S(1)} %get-tuple-element.55), channel_id=1, source_target_pairs={{0,8},{4,12},{8,0},{12,4},{1,9},{5,13},{9,1},{13,5},{2,10},{6,14},... | collective-permute-start | bytes 147464 | tf_op jit(solution)/shard_map/ppermute | solution.py:384
  47.9 0.0 collective-permute-done.9.refs_1_
  47.9 1.5 %collective-permute-start.17 = (bf16[4,16,384]{2,1,0:T(8,128)(2,1)S(1)}, bf16[4,16,384]{2,1,0:T(8,128)(2,1)S(1)}, u32[]{:S(2)}, u32[]{:S(2)}) collective-permute-start(bf16[4,16,384]{2,1,0:T(8,128)(2,1)S(1)} %get-tuple-element.56), channel_id=1, source_target_pairs={{0,4},{4,8},{8,12},{12,0},{1,5},{5,9},{9,13},{13,1},{2,6},{6,10},{... | collective-permute-start | bytes 147464 | tf_op jit(solution)/shard_map/ppermute | solution.py:384
  49.4 0.0 collective-permute-done.10.refs_2_
  49.4 0.0 collective-permute-done.11.refs_3_
  49.4 1.1 %collective-permute-done.15.refs_5_ = bf16[4,16,384]{2,1,0:T(8,128)(2,1)S(1)} collective-permute-done((bf16[4,16,384]{2,1,0:T(8,128)(2,1)S(1)}, bf16[4,16,384]{2,1,0:T(8,128)(2,1)S(1)}, u32[]{:S(2)}, u32[]{:S(2)}) %collective-permute-start.15) | collective-permute-done | bytes 49184 | tf_op jit(solution)/shard_map/ppermute | solution.py:384
  50.5 2.2 %collective-permute-done.16.refs_6_ = bf16[4,16,384]{2,1,0:T(8,128)(2,1)S(1)} collective-permute-done((bf16[4,16,384]{2,1,0:T(8,128)(2,1)S(1)}, bf16[4,16,384]{2,1,0:T(8,128)(2,1)S(1)}, u32[]{:S(2)}, u32[]{:S(2)}) %collective-permute-start.16) | collective-permute-done | bytes 49184 | tf_op jit(solution)/shard_map/ppermute | solution.py:384
  52.7 1.1 %collective-permute-done.17.refs_7_ = bf16[4,16,384]{2,1,0:T(8,128)(2,1)S(1)} collective-permute-done((bf16[4,16,384]{2,1,0:T(8,128)(2,1)S(1)}, bf16[4,16,384]{2,1,0:T(8,128)(2,1)S(1)}, u32[]{:S(2)}, u32[]{:S(2)}) %collective-permute-start.17) | collective-permute-done | bytes 49184 | tf_op jit(solution)/shard_map/ppermute | solution.py:384
  53.8 0.8 %shard_map.63 = bf16[4,16,3072]{2,1,0:T(8,128)(2,1)} custom-call(bf16[4,16,384]{2,1,0:T(8,128)(2,1)S(1)} %get-tuple-element.45.refs_8_.refs_0_, bf16[4,16,384]{2,1,0:T(8,128)(2,1)S(1)} %collective-permute-done.9.refs_1_, bf16[4,16,384]{2,1,0:T(8,128)(2,1)S(1)} %collective-permute-done.10.refs_2_, bf16[4,16,384]{2,1,0:T(8,128)(2,1)S(1)} %collective-permute-done.11.refs_3_, ...), custom_call_target="tpu_custom_call" | custom-call | tf_op jit(solution)/shard_map/pallas_call | solution.py:372
  (5 shorter events, 0.0 us)
Async XLA Ops:
  0.0 13.5 %copy-start = (bf16[4,16,3072]{2,1,0:T(8,128)(2,1)S(1)}, bf16[4,16,3072]{2,1,0:T(8,128)(2,1)}, u32[]{:S(2)}) copy-start(bf16[4,16,3072]{2,1,0:T(8,128)(2,1)} %refs_1_.3) | copy-start | bytes 1179652
  0.0 13.5 %copy-start.1 = (bf16[4,16,3072]{2,1,0:T(8,128)(2,1)S(1)}, bf16[4,16,3072]{2,1,0:T(8,128)(2,1)}, u32[]{:S(2)}) copy-start(bf16[4,16,3072]{2,1,0:T(8,128)(2,1)} %refs_2_.1) | copy-start | bytes 1179652
  3.5 7.0 %copy-start.10 = (f32[8,128]{1,0:T(8,128)S(1)}, f32[8,128]{1,0:T(8,128)}, u32[]{:S(2)}) copy-start(f32[8,128]{1,0:T(8,128)} %get-tuple-element.31._) | copy-start | bytes 12292
  3.5 15.8 %collective-permute-start.3 = (bf16[4,16,768]{2,1,0:T(8,128)(2,1)}, bf16[4,16,768]{2,1,0:T(8,128)(2,1)S(1)}, u32[]{:S(2)}, u32[]{:S(2)}) collective-permute-start(bf16[4,16,768]{2,1,0:T(8,128)(2,1)} %get-tuple-element.38), channel_id=1, source_target_pairs={{0,4},{4,8},{8,12},{12,0},{1,5},{5,9},{9,13},{13,1},{2,6},{6,10},{... | collective-permute-start | bytes 294920 | tf_op jit(solution)/shard_map/ppermute | solution.py:384
  6.6 15.4 %collective-permute-start.4 = (bf16[4,16,768]{2,1,0:T(8,128)(2,1)}, bf16[4,16,768]{2,1,0:T(8,128)(2,1)S(1)}, u32[]{:S(2)}, u32[]{:S(2)}) collective-permute-start(bf16[4,16,768]{2,1,0:T(8,128)(2,1)} %get-tuple-element.39), channel_id=1, source_target_pairs={{0,8},{4,12},{8,0},{12,4},{1,9},{5,13},{9,1},{13,5},{2,10},{6,14},... | collective-permute-start | bytes 294920 | tf_op jit(solution)/shard_map/ppermute | solution.py:384
  9.2 1.4 %copy-start.8 = (s32[16]{0:T(128)S(1)}, s32[16]{0:T(128)}, u32[]{:S(2)}) copy-start(s32[16]{0:T(128)} %tokens_ref.5) | copy-start | bytes 196
  9.2 12.8 %collective-permute-start.5 = (bf16[4,16,768]{2,1,0:T(8,128)(2,1)}, bf16[4,16,768]{2,1,0:T(8,128)(2,1)S(1)}, u32[]{:S(2)}, u32[]{:S(2)}) collective-permute-start(bf16[4,16,768]{2,1,0:T(8,128)(2,1)} %get-tuple-element.40), channel_id=1, source_target_pairs={{0,12},{4,0},{8,4},{12,8},{1,13},{5,1},{9,5},{13,9},{2,14},{6,2},{... | collective-permute-start | bytes 294920 | tf_op jit(solution)/shard_map/ppermute | solution.py:384
  10.5 0.7 %copy-start.7 = (s32[16,32]{1,0:T(8,128)S(1)}, s32[16,32]{1,0:T(8,128)}, u32[]{:S(2)}) copy-start(s32[16,32]{1,0:T(8,128)} %pair_ref.1) | copy-start | bytes 6148
  13.5 4.6 %copy-start.5 = (f32[4,576]{1,0:T(4,128)}, f32[4,576]{1,0:T(4,128)S(1)}, u32[]{:S(2)}) copy-start(f32[4,576]{1,0:T(4,128)S(1)} %get-tuple-element.32.refs_3_.bias_ref) | copy-start | bytes 27652
  13.5 1.0 %copy-start.2 = (bf16[4,16,3072]{2,1,0:T(8,128)(2,1)S(1)}, bf16[4,16,3072]{2,1,0:T(8,128)(2,1)}, u32[]{:S(2)}) copy-start(bf16[4,16,3072]{2,1,0:T(8,128)(2,1)} %refs_0_.5) | copy-start | bytes 1179652
  14.5 7.4 %copy-start.4 = (bf16[4,16,768]{2,1,0:T(8,128)(2,1)S(1)}, bf16[4,16,768]{2,1,0:T(8,128)(2,1)}, u32[]{:S(2)}) copy-start(bf16[4,16,768]{2,1,0:T(8,128)(2,1)} %get-tuple-element.37.refs_0_.refs_4_) | copy-start | bytes 294916
  18.0 11.8 %collective-permute-start = (bf16[4,16,1152]{2,1,0:T(8,128)(2,1)S(1)}, bf16[4,16,1152]{2,1,0:T(8,128)(2,1)S(1)}, u32[]{:S(2)}, u32[]{:S(2)}) collective-permute-start(bf16[4,16,1152]{2,1,0:T(8,128)(2,1)S(1)} %get-tuple-element.34), channel_id=1, source_target_pairs={{0,4},{4,8},{8,12},{12,0},{1,5},{5,9},{9,13},{13,1},{2,6},{6,10},{... | collective-permute-start | bytes 442376 | tf_op jit(solution)/shard_map/ppermute | solution.py:384
  18.8 12.3 %collective-permute-start.1 = (bf16[4,16,1152]{2,1,0:T(8,128)(2,1)S(1)}, bf16[4,16,1152]{2,1,0:T(8,128)(2,1)S(1)}, u32[]{:S(2)}, u32[]{:S(2)}) collective-permute-start(bf16[4,16,1152]{2,1,0:T(8,128)(2,1)S(1)} %get-tuple-element.35), channel_id=1, source_target_pairs={{0,8},{4,12},{8,0},{12,4},{1,9},{5,13},{9,1},{13,5},{2,10},{6,14},... | collective-permute-start | bytes 442376 | tf_op jit(solution)/shard_map/ppermute | solution.py:384
  19.3 11.8 %collective-permute-start.2 = (bf16[4,16,1152]{2,1,0:T(8,128)(2,1)S(1)}, bf16[4,16,1152]{2,1,0:T(8,128)(2,1)S(1)}, u32[]{:S(2)}, u32[]{:S(2)}) collective-permute-start(bf16[4,16,1152]{2,1,0:T(8,128)(2,1)S(1)} %get-tuple-element.36), channel_id=1, source_target_pairs={{0,12},{4,0},{8,4},{12,8},{1,13},{5,1},{9,5},{13,9},{2,14},{6,2},{... | collective-permute-start | bytes 442376 | tf_op jit(solution)/shard_map/ppermute | solution.py:384
  21.9 1.0 %copy-start.3 = (bf16[4,16,3072]{2,1,0:T(8,128)(2,1)S(1)}, bf16[4,16,3072]{2,1,0:T(8,128)(2,1)}, u32[]{:S(2)}) copy-start(bf16[4,16,3072]{2,1,0:T(8,128)(2,1)} %refs_0_.5) | copy-start | bytes 1179652
  22.6 12.5 %collective-permute-start.6 = (bf16[2,4,16,768]{3,2,1,0:T(8,128)(2,1)S(1)}, bf16[2,4,16,768]{3,2,1,0:T(8,128)(2,1)S(1)}, u32[]{:S(2)}, u32[]{:S(2)}) collective-permute-start(bf16[2,4,16,768]{3,2,1,0:T(8,128)(2,1)S(1)} %get-tuple-element.42.refs_1_.refs_4_), channel_id=1, source_target_pairs={{0,1},{1,2},{2,3},{3,0},{4,5},{5,6},{6,7},{7,4},{8,9},{9,10},{10,1... | collective-permute-start | bytes 589832 | tf_op jit(solution)/shard_map/ppermute | solution.py:384
  24.9 8.6 %collective-permute-start.7 = (bf16[1,4,16,768]{3,2,1,0:T(8,128)(2,1)S(1)}, bf16[1,4,16,768]{3,2,1,0:T(8,128)(2,1)S(1)}, u32[]{:S(2)}, u32[]{:S(2)}) collective-permute-start(bf16[1,4,16,768]{3,2,1,0:T(8,128)(2,1)S(1)} %get-tuple-element.43), channel_id=1, source_target_pairs={{0,2},{1,3},{2,0},{3,1},{4,6},{5,7},{6,4},{7,5},{8,10},{9,11},{10,... | collective-permute-start | bytes 294920 | tf_op jit(solution)/shard_map/ppermute | solution.py:384
  26.5 17.7 %all-to-all-start = ((bf16[4,4,16,384]{3,2,1,0:T(8,128)(2,1)}), bf16[4,4,16,384]{3,2,1,0:T(8,128)(2,1)S(1)}, u32[]{:S(2)}, u32[]{:S(2)}) async-start(bf16[4,4,16,384]{3,2,1,0:T(8,128)(2,1)} %get-tuple-element.49), calls=%async_computation | async-start | bytes 393216 | tf_op jit(solution)/shard_map/all_to_all | solution.py:426
  29.9 5.1 %collective-permute-start.8 = (bf16[2,4,16,768]{3,2,1,0:T(8,128)(2,1)S(1)}, bf16[2,4,16,768]{3,2,1,0:T(8,128)(2,1)S(1)}, u32[]{:S(2)}, u32[]{:S(2)}) collective-permute-start(bf16[2,4,16,768]{3,2,1,0:T(8,128)(2,1)S(1)} %get-tuple-element.44), channel_id=1, source_target_pairs={{0,3},{1,0},{2,1},{3,2},{4,7},{5,4},{6,5},{7,6},{8,11},{9,8},{10,9... | collective-permute-start | bytes 589832 | tf_op jit(solution)/shard_map/ppermute | solution.py:384
  31.1 3.9 %copy-start.6 = (f32[4,576]{1,0:T(4,128)S(1)}, f32[4,576]{1,0:T(4,128)}, u32[]{:S(2)}) copy-start(f32[4,576]{1,0:T(4,128)} %copy-done.5) | copy-start | bytes 27652
  31.7 12.4 %collective-permute-start.12 = (bf16[2,4,16,768]{3,2,1,0:T(8,128)(2,1)S(1)}, bf16[2,4,16,768]{3,2,1,0:T(8,128)(2,1)S(1)}, u32[]{:S(2)}, u32[]{:S(2)}) collective-permute-start(bf16[2,4,16,768]{3,2,1,0:T(8,128)(2,1)S(1)} %get-tuple-element.50), channel_id=1, source_target_pairs={{0,1},{1,2},{2,3},{3,0},{4,5},{5,6},{6,7},{7,4},{8,9},{9,10},{10,1... | collective-permute-start | bytes 589832 | tf_op jit(solution)/shard_map/ppermute | solution.py:384
  31.8 3.2 %copy-start.9 = (s32[16]{0:T(128)S(1)}, s32[16]{0:T(128)}, u32[]{:S(2)}) copy-start(s32[16]{0:T(128)} %tokens_ref.5) | copy-start | bytes 196
  31.8 12.3 %collective-permute-start.14 = (bf16[2,4,16,768]{3,2,1,0:T(8,128)(2,1)S(1)}, bf16[2,4,16,768]{3,2,1,0:T(8,128)(2,1)S(1)}, u32[]{:S(2)}, u32[]{:S(2)}) collective-permute-start(bf16[2,4,16,768]{3,2,1,0:T(8,128)(2,1)S(1)} %get-tuple-element.52), channel_id=1, source_target_pairs={{0,3},{1,0},{2,1},{3,2},{4,7},{5,4},{6,5},{7,6},{8,11},{9,8},{10,9... | collective-permute-start | bytes 589832 | tf_op jit(solution)/shard_map/ppermute | solution.py:384
  33.5 8.0 %collective-permute-start.13 = (bf16[1,4,16,768]{3,2,1,0:T(8,128)(2,1)S(1)}, bf16[1,4,16,768]{3,2,1,0:T(8,128)(2,1)S(1)}, u32[]{:S(2)}, u32[]{:S(2)}) collective-permute-start(bf16[1,4,16,768]{3,2,1,0:T(8,128)(2,1)S(1)} %get-tuple-element.51), channel_id=1, source_target_pairs={{0,2},{1,3},{2,0},{3,1},{4,6},{5,7},{6,4},{7,5},{8,10},{9,11},{10,... | collective-permute-start | bytes 294920 | tf_op jit(solution)/shard_map/ppermute | solution.py:384
  36.8 11.2 %collective-permute-start.9 = (bf16[4,16,384]{2,1,0:T(8,128)(2,1)S(1)}, bf16[4,16,384]{2,1,0:T(8,128)(2,1)S(1)}, u32[]{:S(2)}, u32[]{:S(2)}) collective-permute-start(bf16[4,16,384]{2,1,0:T(8,128)(2,1)S(1)} %get-tuple-element.46), channel_id=1, source_target_pairs={{0,12},{4,0},{8,4},{12,8},{1,13},{5,1},{9,5},{13,9},{2,14},{6,2},{... | collective-permute-start | bytes 147464 | tf_op jit(solution)/shard_map/ppermute | solution.py:384
  40.6 8.8 %collective-permute-start.10 = (bf16[4,16,384]{2,1,0:T(8,128)(2,1)S(1)}, bf16[4,16,384]{2,1,0:T(8,128)(2,1)S(1)}, u32[]{:S(2)}, u32[]{:S(2)}) collective-permute-start(bf16[4,16,384]{2,1,0:T(8,128)(2,1)S(1)} %get-tuple-element.47), channel_id=1, source_target_pairs={{0,8},{4,12},{8,0},{12,4},{1,9},{5,13},{9,1},{13,5},{2,10},{6,14},... | collective-permute-start | bytes 147464 | tf_op jit(solution)/shard_map/ppermute | solution.py:384
  41.6 7.9 %collective-permute-start.11 = (bf16[4,16,384]{2,1,0:T(8,128)(2,1)S(1)}, bf16[4,16,384]{2,1,0:T(8,128)(2,1)S(1)}, u32[]{:S(2)}, u32[]{:S(2)}) collective-permute-start(bf16[4,16,384]{2,1,0:T(8,128)(2,1)S(1)} %get-tuple-element.48), channel_id=1, source_target_pairs={{0,4},{4,8},{8,12},{12,0},{1,5},{5,9},{9,13},{13,1},{2,6},{6,10},{... | collective-permute-start | bytes 147464 | tf_op jit(solution)/shard_map/ppermute | solution.py:384
  45.9 4.6 %collective-permute-start.15 = (bf16[4,16,384]{2,1,0:T(8,128)(2,1)S(1)}, bf16[4,16,384]{2,1,0:T(8,128)(2,1)S(1)}, u32[]{:S(2)}, u32[]{:S(2)}) collective-permute-start(bf16[4,16,384]{2,1,0:T(8,128)(2,1)S(1)} %get-tuple-element.54), channel_id=1, source_target_pairs={{0,12},{4,0},{8,4},{12,8},{1,13},{5,1},{9,5},{13,9},{2,14},{6,2},{... | collective-permute-start | bytes 147464 | tf_op jit(solution)/shard_map/ppermute | solution.py:384
  47.2 5.5 %collective-permute-start.16 = (bf16[4,16,384]{2,1,0:T(8,128)(2,1)S(1)}, bf16[4,16,384]{2,1,0:T(8,128)(2,1)S(1)}, u32[]{:S(2)}, u32[]{:S(2)}) collective-permute-start(bf16[4,16,384]{2,1,0:T(8,128)(2,1)S(1)} %get-tuple-element.55), channel_id=1, source_target_pairs={{0,8},{4,12},{8,0},{12,4},{1,9},{5,13},{9,1},{13,5},{2,10},{6,14},... | collective-permute-start | bytes 147464 | tf_op jit(solution)/shard_map/ppermute | solution.py:384
  47.9 5.9 %collective-permute-start.17 = (bf16[4,16,384]{2,1,0:T(8,128)(2,1)S(1)}, bf16[4,16,384]{2,1,0:T(8,128)(2,1)S(1)}, u32[]{:S(2)}, u32[]{:S(2)}) collective-permute-start(bf16[4,16,384]{2,1,0:T(8,128)(2,1)S(1)} %get-tuple-element.56), channel_id=1, source_target_pairs={{0,4},{4,8},{8,12},{12,0},{1,5},{5,9},{9,13},{13,1},{2,6},{6,10},{... | collective-permute-start | bytes 147464 | tf_op jit(solution)/shard_map/ppermute | solution.py:384

commit v5 on v4

--- a/solution.py
+++ b/solution.py
@@ -59,10 +59,9 @@
 def rotate_kernel(message, sources, count_head, skipped, *refs):
     fields, total = fields_of(message)
     ins = dict(zip(sources, refs))
-    outs = by_distance(refs[len(sources) + skipped : -5], count_head, 1)
-    token, buffer, sems, turned_ref, out_sems = refs[-5:]
+    outs = by_distance(refs[len(sources) + skipped : -3], count_head, 1)
+    token, buffer, sems = refs[-3:]
     token[...] = jnp.zeros_like(token)
-    leaving = []
     blocks, tokens, width = refs[0].shape
     width_here = width // count_head
     me = lax.axis_index("head")
@@ -90,11 +89,7 @@
             turned = (turned * ROTATE_SCALE).reshape(size // HD, blocks, tokens, HD)
             for h in range(size // HD):
                 at = start + h * HD
-                turned_ref[s, :, :, at : at + HD] = turned[h].astype(jnp.bfloat16)
-        leaving.append(pltpu.make_async_copy(turned_ref.at[s], outs[s], out_sems.at[s]))
-        leaving[-1].start()
-    for copy in leaving:
-        copy.wait()
+                outs[s][:, :, at : at + HD] = turned[h].astype(jnp.bfloat16)
 
 
 def rotate_pieces(arrays, message, count_head, after=(), limit=VMEM, stacked=False):
@@ -107,14 +102,11 @@
         functools.partial(rotate_kernel, message, sources, count_head, len(after)),
         in_specs=[pl.BlockSpec(memory_space=pltpu.HBM)] * len(sources)
         + [pl.BlockSpec(memory_space=pl.ANY)] * len(after),
-        out_specs=[pl.BlockSpec(memory_space=pl.ANY)] * len(shapes)
-        + [pl.BlockSpec(memory_space=pltpu.VMEM)],
+        out_specs=[pl.BlockSpec(memory_space=pltpu.VMEM)] * (len(shapes) + 1),
         out_shape=[jax.ShapeDtypeStruct(shape, jnp.bfloat16) for shape in shapes] + [TOKEN],
         scratch_shapes=[
             pltpu.VMEM((count_head,) + one, jnp.bfloat16),
             pltpu.SemaphoreType.DMA((count_head, len(fields))),
-            pltpu.VMEM((count_head,) + one, jnp.bfloat16),
-            pltpu.SemaphoreType.DMA((count_head,)),
         ],
         cost_estimate=NO_COST,
         compiler_params=pltpu.CompilerParams(vmem_limit_bytes=limit),
@@ -264,48 +256,50 @@
     )(pair_list, block_tokens, after)
 
 
-def attend_kernel(counts, at, size, tokens_ref, bias_ref, *refs):
-    count_head, count_tm, query_count, skipped = counts
-    query_at, key_at = at
-    queries, refs = by_distance(refs[:query_count], count_head, -1), refs[query_count:]
-    owns, slots = refs[:count_head], refs[count_head : count_head + count_tm - 1]
-    outs = refs[count_head + count_tm - 1 + skipped :]
-    blocks, tokens, _ = owns[0].shape
+def attend_kernel(counts, sizes, distances, tokens_ref, bias_ref, query_ref, *refs):
+    count_head, count_tm = counts
+    queries = by_distance([query_ref], count_head, -1)
+    per_part = count_head + count_tm - 1
+    parts = [refs[p * per_part : (p + 1) * per_part] for p in range(len(sizes))]
+    outs = refs[len(sizes) * per_part :][-len(distances) :]
+    blocks, tokens, _ = outs[0].shape
+    rows = len(distances) * tokens
     shard = lax.axis_index("tm")
     me = lax.axis_index("head")
-    heads = size // HD
     bias = bias_ref[...][:, None, :]
-
-    def gathered(kind, h):
-        first = kind * size + h * HD
-        own_lanes = slice(key_at + first, key_at + first + HD)
-        pieces = [rows_of(own[:, :, own_lanes]) for own in owns]
+    place_of = [(p, h) for p, size in enumerate(sizes) for h in range(size // HD)]
+
+    def gathered(kind, head):
+        p, h = place_of[head]
+        first = kind * sizes[p] + h * HD
+        lanes = slice(first, first + HD)
+        pieces = [rows_of(own[:, :, lanes]) for own in parts[p][:count_head]]
         pieces += [
-            rows_of(slots[distance - 1][k, :, :, first : first + HD])
+            rows_of(parts[p][count_head + distance - 1][k, :, :, lanes])
             for distance, k in remote_rows(count_tm)
         ]
         return jnp.concatenate(pieces, axis=0)
 
-    def products(h):
-        lanes = slice(query_at + h * HD, query_at + (h + 1) * HD)
+    def products(head):
+        lanes = slice(head * HD, (head + 1) * HD)
         query = jnp.concatenate(
-            [rows_of(queries[s][i, :, lanes]) for i in range(blocks) for s in range(count_head)],
-            axis=0,
+            [rows_of(queries[s][i, :, lanes]) for i in range(blocks) for s in distances], axis=0
         )
         return lax.dot_general(
-            query, gathered(0, h), (((1,), (1,)), ((), ())), preferred_element_type=jnp.float32
+            query, gathered(0, head), (((1,), (1,)), ((), ())), preferred_element_type=jnp.float32
         )
 
+    heads = len(place_of)
     dots, mixed = products(0), []
     for h in range(heads):
         ahead = products(h + 1) if h + 1 < heads else None
-        dots = dots.reshape(blocks, BLK, -1) + bias
+        dots = dots.reshape(blocks, rows, -1) + bias
         peak = jnp.max(dots, axis=-1, keepdims=True)
         weights = jnp.exp2((dots - peak) * (SCORE_SCALE * LOG2E))
         inverse = 1.0 / jnp.sum(weights, axis=-1, keepdims=True)
-        weights_half = weights.astype(jnp.bfloat16).reshape(blocks * BLK, -1)
-        rows = jnp.dot(weights_half, gathered(1, h), preferred_element_type=jnp.float32)
-        mixed.append(rows * inverse.reshape(blocks * BLK, 1))
+        weights_half = weights.astype(jnp.bfloat16).reshape(blocks * rows, -1)
+        part = jnp.dot(weights_half, gathered(1, h), preferred_element_type=jnp.float32)
+        mixed.append(part * inverse.reshape(blocks * rows, 1))
         dots = ahead
     mixed = jnp.concatenate(mixed, axis=0)
     sign = sign_matrix()
@@ -313,51 +307,43 @@
     low = (mixed - high.astype(jnp.float32)).astype(jnp.bfloat16)
     turned = jnp.dot(high, sign, preferred_element_type=jnp.float32)
     turned = turned + jnp.dot(low, sign, preferred_element_type=jnp.float32)
-    turned = (turned * ROTATE_SCALE).reshape(heads, blocks, count_head, tokens, HD)
+    turned = (turned * ROTATE_SCALE).reshape(heads, blocks, len(distances), tokens, HD)
     token = lax.broadcasted_iota(jnp.int32, (tokens, HD), 0)
-    for s in range(count_head):
+    for at, s in enumerate(distances):
         position = lax.rem(me - s + count_head, count_head) * tokens + token
         for i in range(blocks):
             live = position < tokens_ref[shard * blocks + i]
             for h in range(heads):
-                outs[s][i, :, h * HD : (h + 1) * HD] = jnp.where(
-                    live, turned[h, i, s], 0.0
+                outs[at][i, :, h * HD : (h + 1) * HD] = jnp.where(
+                    live, turned[h, i, at], 0.0
                 ).astype(jnp.bfloat16)
 
 
-def attend(block_tokens, bias, queries, query_at, owns, key_at, slots, size, after, cost):
-    count_head, count_tm = len(owns), len(slots) + 1
-    blocks, tokens, _ = owns[0].shape
+def attend(block_tokens, bias, query, parts, sizes, distances, after, cost):
+    count_head, count_tm = query.shape[0], len(parts[0][1]) + 1
+    operands = [ref for owns, slots in parts for ref in owns + slots]
     vmem = pl.BlockSpec(memory_space=pltpu.VMEM)
     return pl.pallas_call(
-        functools.partial(
-            attend_kernel,
-            (count_head, count_tm, len(queries), len(after)),
-            (query_at, key_at),
-            size,
-        ),
+        functools.partial(attend_kernel, (count_head, count_tm), sizes, distances),
         in_specs=[pl.BlockSpec(memory_space=pltpu.SMEM)]
-        + [vmem] * (len(queries) + count_head + count_tm)
+        + [vmem] * (2 + len(operands))
         + [pl.BlockSpec(memory_space=pl.ANY)] * len(after),
-        out_specs=[vmem] * count_head,
-        out_shape=[jax.ShapeDtypeStruct((blocks, tokens, size), jnp.bfloat16)] * count_head,
+        out_specs=[vmem] * len(distances),
+        out_shape=[jax.ShapeDtypeStruct(query.shape[1:], jnp.bfloat16)] * len(distances),
         cost_estimate=cost,
         compiler_params=pltpu.CompilerParams(vmem_limit_bytes=VMEM),
-    )(block_tokens, bias, *queries, *owns, *slots, *after)
-
-
-def place_kernel(count_head, starts, width_here, *refs):
+    )(block_tokens, bias, query, *operands, *after)
+
+
+def place_kernel(width_here, *refs):
     pieces, out_ref, sems = refs[:-2], refs[-2], refs[-1]
     me = lax.axis_index("head")
     copies = []
-    for at, piece in enumerate(pieces):
-        part, s = at // count_head, at % count_head
-        column = lax.rem(me + s, count_head) * width_here + starts[part]
+    for s, piece in enumerate(pieces):
+        column = pl.multiple_of(lax.rem(me + s, len(pieces)) * width_here, HD)
         copies.append(
             pltpu.make_async_copy(
-                piece,
-                out_ref.at[:, :, pl.ds(pl.multiple_of(column, HD), piece.shape[-1])],
-                sems.at[at],
+                piece, out_ref.at[:, :, pl.ds(column, width_here)], sems.at[s]
             )
         )
         copies[-1].start()
@@ -365,15 +351,13 @@
         copy.wait()
 
 
-def place_pieces(parts, starts, width_here):
-    count_head = len(parts[0])
-    pieces = [piece for part in parts for piece in part]
-    blocks, tokens, _ = pieces[0].shape
+def place_pieces(pieces):
+    blocks, tokens, width_here = pieces[0].shape
     return pl.pallas_call(
-        functools.partial(place_kernel, count_head, starts, width_here),
+        functools.partial(place_kernel, width_here),
         in_specs=[pl.BlockSpec(memory_space=pl.ANY)] * len(pieces),
         out_specs=pl.BlockSpec(memory_space=pltpu.HBM),
-        out_shape=jax.ShapeDtypeStruct((blocks, tokens, count_head * width_here), jnp.bfloat16),
+        out_shape=jax.ShapeDtypeStruct((blocks, tokens, len(pieces) * width_here), jnp.bfloat16),
         scratch_shapes=[pltpu.SemaphoreType.DMA((len(pieces),))],
         compiler_params=pltpu.CompilerParams(vmem_limit_bytes=VMEM),
     )(*pieces)
@@ -403,37 +387,28 @@
     cut = (heads + 1) // 2 * HD
     parts = [(0, cut), (cut, width_here - cut)] if heads > 1 else [(0, width_here)]
     arrays = [query_rows, key_rows, value_rows]
-    messages = []
-    for at, part in enumerate(parts):
+    packed, after, limit = [], (), WIDE_VMEM
+    for part in parts:
         message = [(1,) + part, (2,) + part]
-        messages.append(message + ([(0,) + parts[at - 1]] if at else []))
-    query_at = [2 * size for _, size in parts[1:]] + [0]
-    pieces, token = rotate_pieces(arrays, messages[0], count_head, limit=WIDE_VMEM)
-    packed = [pieces]
+        pieces, token = rotate_pieces(arrays, message, count_head, after, limit)
+        packed.append(pieces)
+        after, limit = (token,), VMEM
+    received = [exchange(pieces, 1) for pieces in packed]
     picks, bias = plan(pair_list, block_tokens, token, blocks, count_head, count_tm)
-    after = (bias,)
-    for message in messages[1:]:
-        pieces, token = rotate_pieces(arrays, message, count_head, after)
-        packed.append(pieces)
-        after = (token,)
-    received = [exchange(pieces, 1) for pieces in packed]
     sent, after = [], ()
     for owns, (_, size) in zip(received, parts):
         sent.append(pick_blocks(picks, owns, (0, 2 * size), count_tm, after))
         after = (sent[-1][0],)
-    message = [(0,) + parts[-1]]
+    message = [(0, 0, width_here)]
     (query,), _ = rotate_pieces(arrays, message, count_head, (sent[0][0],), stacked=True)
     query = lax.all_to_all(query, "head", split_axis=0, concat_axis=0, tiled=True)
-    queries = received[1:] + [[query]]
-    returned, after = [], ()
-    for at, (_, size) in enumerate(parts):
-        attended = attend(
-            block_tokens, bias, queries[at], query_at[at], received[at], 0,
-            forward(sent[at]), size, after, NO_COST,
-        )
-        after = (attended[0],)
-        returned.append(exchange(attended, -1))
-    return place_pieces(returned, [start for start, _ in parts], width_here)
+    inputs = [(owns, forward(picked)) for owns, picked in zip(received, sent)]
+    sizes = [size for _, size in parts]
+    leaving = attend(
+        block_tokens, bias, query, inputs, sizes, list(range(1, count_head)), (), NO_COST
+    )
+    staying = attend(block_tokens, bias, query, inputs, sizes, [0], (leaving[0],), NO_COST)
+    return place_pieces(exchange(staying + leaving, -1))
 
 
 def solution(mesh):

time: 55 us -> 54.7 us (level)
  waiting for transfers between devices: 4.72 us -> 10.9 us
  Pallas kernels: 16.7 us -> 14.1 us
  starting transfers between devices: 31 us -> 28.9 us
  local copies, waits for them, and re-layouts: 2.05 us -> 0.35 us
    ppermute x18 -> x15, waiting for transfers between devices: 4.72 us -> 10.4 us  [shifted(): lax.ppermute(array, axis, [(i, (i + distance) % count) for i in range(cou...]
    ppermute x18 -> x15, starting transfers between devices: 27.6 us -> 22.7 us  [shifted(): lax.ppermute(array, axis, [(i, (i + distance) % count) for i in range(cou...]
    pallas_call x3, Pallas kernels: 8.99 us -> 5.97 us  [rotate_pieces(): pl.pallas_call(functools.partial(rotate_kernel, message, sources, count_h...]
    all_to_all x1, starting transfers between devices: 3.37 us -> 6.23 us  [shards(): lax.all_to_all(query, 'head', split_axis=0, concat_axis=0, tiled=True)]
    unnamed x22 -> x16, local copies, waits for them, and re-layouts: 2.05 us -> 0.35 us
  transfers between devices with their start and end apart: 19 -> 16, of which waited for: 5 -> 4; matrix products, arithmetic and copies ran while one was open for 0% -> 0% of each run, Pallas kernels for 23% -> 15%
where the time goes in v5:
time: 54.7 us; the launch traced here: 54.5 us
  starting transfers between devices  28.9 us (53%)
  Pallas kernels  14.1 us (26%)
  waiting for transfers between devices  10.9 us (20%)
    ppermute x15, starting transfers between devices, shifted(): lax.ppermute(array, axis, [(i, (i + distance) % count) for i in range(cou...  22.7 us
    ppermute x15, waiting for transfers between devices, shifted(): lax.ppermute(array, axis, [(i, (i + distance) % count) for i in range(cou...  10.4 us
    all_to_all x1, starting transfers between devices, shards(): lax.all_to_all(query, 'head', split_axis=0, concat_axis=0, tiled=True)  6.23 us
    pallas_call x3, Pallas kernels, rotate_pieces(): pl.pallas_call(functools.partial(rotate_kernel, message, sources, count_h...  5.97 us
    pallas_call x2, Pallas kernels, attend(): pl.pallas_call(functools.partial(attend_kernel, (count_head, count_tm), s...  3.96 us
    pallas_call x1, Pallas kernels, plan(): pl.pallas_call(functools.partial(plan_kernel, count_head, count_tm, block...  2.25 us
    pallas_call x2, Pallas kernels, pick_blocks(): pl.pallas_call(functools.partial(pick_kernel, count_head, count_tm, lanes...  1.18 us
  transfers between devices with their start and end apart: 16, of which 4 were waited for; matrix products, arithmetic and copies ran while one was open for 0% of the time, Pallas kernels for 15%

profile of v5, /device:TPU:0, one launch (start us, length us, event | category | flops | bytes accessed | tf_op | source)
XLA Modules:
  0.0 54.5 jit_solution(1112021508756584221)
XLA Ops:
  0.0 0.0 copy-start.1
  0.0 0.0 copy-start
  0.0 2.9 %shard_map.55 = (bf16[4,16,768]{2,1,0:T(8,128)(2,1)}, bf16[4,16,768]{2,1,0:T(8,128)(2,1)}, bf16[4,16,768]{2,1,0:T(8,128)(2,1)}, bf16[4,16,768]{2,1,0:T(8,128)(2,1)}, f32[8,128]{1,0:T(8,128)}) custom-call(bf16[4,16,3072]{2,1,0:T(8,128)(2,1)} %refs_0_.4, bf16[4,16,3072]{2,1,0:T(8,128)(2,1)} %refs_1_.3), custom_call_target="tpu_custom_call" | custom-call | tf_op jit(solution)/shard_map/pallas_call | solution.py:101
  2.9 0.0 copy-start.7
  2.9 3.1 %collective-permute-start = (bf16[4,16,768]{2,1,0:T(8,128)(2,1)}, bf16[4,16,768]{2,1,0:T(8,128)(2,1)S(1)}, u32[]{:S(2)}, u32[]{:S(2)}) collective-permute-start(bf16[4,16,768]{2,1,0:T(8,128)(2,1)} %get-tuple-element.32), channel_id=1, source_target_pairs={{0,4},{4,8},{8,12},{12,0},{1,5},{5,9},{9,13},{13,1},{2,6},{6,10},{... | collective-permute-start | bytes 294920 | tf_op jit(solution)/shard_map/ppermute | solution.py:368
  6.0 2.6 %collective-permute-start.1 = (bf16[4,16,768]{2,1,0:T(8,128)(2,1)}, bf16[4,16,768]{2,1,0:T(8,128)(2,1)S(1)}, u32[]{:S(2)}, u32[]{:S(2)}) collective-permute-start(bf16[4,16,768]{2,1,0:T(8,128)(2,1)} %get-tuple-element.33), channel_id=1, source_target_pairs={{0,8},{4,12},{8,0},{12,4},{1,9},{5,13},{9,1},{13,5},{2,10},{6,14},... | collective-permute-start | bytes 294920 | tf_op jit(solution)/shard_map/ppermute | solution.py:368
  8.5 1.3 %collective-permute-start.2 = (bf16[4,16,768]{2,1,0:T(8,128)(2,1)}, bf16[4,16,768]{2,1,0:T(8,128)(2,1)S(1)}, u32[]{:S(2)}, u32[]{:S(2)}) collective-permute-start(bf16[4,16,768]{2,1,0:T(8,128)(2,1)} %get-tuple-element.34), channel_id=1, source_target_pairs={{0,12},{4,0},{8,4},{12,8},{1,13},{5,1},{9,5},{13,9},{2,14},{6,2},{... | collective-permute-start | bytes 294920 | tf_op jit(solution)/shard_map/ppermute | solution.py:368
  9.9 0.0 copy-done.1
  9.9 0.0 copy-done
  9.9 0.0 copy-done.7
  9.9 0.0 copy-start.4
  9.9 0.0 copy-start.2
  9.9 1.5 %shard_map.56 = (bf16[4,16,768]{2,1,0:T(8,128)(2,1)S(1)}, bf16[4,16,768]{2,1,0:T(8,128)(2,1)S(1)}, bf16[4,16,768]{2,1,0:T(8,128)(2,1)S(1)}, bf16[4,16,768]{2,1,0:T(8,128)(2,1)S(1)}, f32[8,128]{1,0:T(8,128)S(1)}) custom-call(bf16[4,16,3072]{2,1,0:T(8,128)(2,1)S(1)} %copy-done, bf16[4,16,3072]{2,1,0:T(8,128)(2,1)S(1)} %copy-done.1, f32[8,128]{1,0:T(8,128)S(1)} %copy-done.7), custom_call_target="tpu_custom_call" | custom-call | tf_op jit(solution)/shard_map/pallas_call | solution.py:101
  11.4 0.7 %collective-permute-start.6 = (bf16[4,16,768]{2,1,0:T(8,128)(2,1)S(1)}, bf16[4,16,768]{2,1,0:T(8,128)(2,1)S(1)}, u32[]{:S(2)}, u32[]{:S(2)}) collective-permute-start(bf16[4,16,768]{2,1,0:T(8,128)(2,1)S(1)} %get-tuple-element.40), channel_id=1, source_target_pairs={{0,4},{4,8},{8,12},{12,0},{1,5},{5,9},{9,13},{13,1},{2,6},{6,10},{... | collective-permute-start | bytes 294920 | tf_op jit(solution)/shard_map/ppermute | solution.py:368
  12.1 0.0 copy-start.5
  12.1 0.3 collective-permute-start.7
  12.5 0.0 copy-done.4
  12.5 0.3 copy-done.5
  12.8 2.3 %shard_map.57 = (s32[8]{0:T(128)S(1)}, f32[4,576]{1,0:T(4,128)S(1)}) custom-call(s32[16,32]{1,0:T(8,128)S(1)} %copy-done.4, s32[16]{0:T(128)S(1)} %copy-done.5, f32[8,128]{1,0:T(8,128)S(1)} %get-tuple-element.28._), custom_call_target="tpu_custom_call" | custom-call | tf_op jit(solution)/shard_map/pallas_call | solution.py:237
  15.1 0.0 collective-permute-done.refs_1_
  15.1 3.2 %collective-permute-start.8 = (bf16[4,16,768]{2,1,0:T(8,128)(2,1)S(1)}, bf16[4,16,768]{2,1,0:T(8,128)(2,1)S(1)}, u32[]{:S(2)}, u32[]{:S(2)}) collective-permute-start(bf16[4,16,768]{2,1,0:T(8,128)(2,1)S(1)} %get-tuple-element.42), channel_id=1, source_target_pairs={{0,12},{4,0},{8,4},{12,8},{1,13},{5,1},{9,5},{13,9},{2,14},{6,2},{... | collective-permute-start | bytes 294920 | tf_op jit(solution)/shard_map/ppermute | solution.py:368
  18.3 0.0 collective-permute-done.1.refs_2_
  18.3 0.0 collective-permute-done.2.refs_3_
  18.3 0.0 copy-done.2
  18.3 0.0 copy-start.3
  18.3 0.6 %shard_map.58 = (bf16[2,4,16,768]{3,2,1,0:T(8,128)(2,1)S(1)}, bf16[1,4,16,768]{3,2,1,0:T(8,128)(2,1)S(1)}, bf16[2,4,16,768]{3,2,1,0:T(8,128)(2,1)S(1)}) custom-call(s32[8]{0:T(128)S(1)} %get-tuple-element.30.picks_ref, bf16[4,16,768]{2,1,0:T(8,128)(2,1)S(1)} %copy-done.2, bf16[4,16,768]{2,1,0:T(8,128)(2,1)S(1)} %collective-permute-done.refs_1_, ...), custom_call_target="tpu_custom_call" | custom-call | flops 99999997952 | tf_op jit(solution)/shard_map/pallas_call | solution.py:136
  18.9 1.6 %collective-permute-start.4 = (bf16[1,4,16,768]{3,2,1,0:T(8,128)(2,1)S(1)}, bf16[1,4,16,768]{3,2,1,0:T(8,128)(2,1)S(1)}, u32[]{:S(2)}, u32[]{:S(2)}) collective-permute-start(bf16[1,4,16,768]{3,2,1,0:T(8,128)(2,1)S(1)} %get-tuple-element.37), channel_id=1, source_target_pairs={{0,2},{1,3},{2,0},{3,1},{4,6},{5,7},{6,4},{7,5},{8,10},{9,11},{10,... | collective-permute-start | bytes 294920 | tf_op jit(solution)/shard_map/ppermute | solution.py:368
  20.4 0.0 collective-permute-start.3
  20.4 0.0 copy-done.3
  20.5 1.6 %shard_map.59 = (bf16[4,4,16,768]{3,2,1,0:T(8,128)(2,1)}, f32[8,128]{1,0:T(8,128)}) custom-call(bf16[4,16,3072]{2,1,0:T(8,128)(2,1)S(1)} %copy-done.3, bf16[2,4,16,768]{3,2,1,0:T(8,128)(2,1)S(1)} %get-tuple-element.35.refs_1_.refs_4_), custom_call_target="tpu_custom_call" | custom-call | tf_op jit(solution)/shard_map/pallas_call | solution.py:101
  22.1 6.2 %all-to-all-start = ((bf16[4,4,16,768]{3,2,1,0:T(8,128)(2,1)}), bf16[4,4,16,768]{3,2,1,0:T(8,128)(2,1)S(1)}, u32[]{:S(2)}, u32[]{:S(2)}) async-start(bf16[4,4,16,768]{3,2,1,0:T(8,128)(2,1)} %get-tuple-element.36), calls=%async_computation | async-start | bytes 786432 | tf_op jit(solution)/shard_map/all_to_all | solution.py:404
  28.3 0.0 collective-permute-done.6.refs_1_.refs_8_
  28.3 1.5 %collective-permute-start.5 = (bf16[2,4,16,768]{3,2,1,0:T(8,128)(2,1)S(1)}, bf16[2,4,16,768]{3,2,1,0:T(8,128)(2,1)S(1)}, u32[]{:S(2)}, u32[]{:S(2)}) collective-permute-start(bf16[2,4,16,768]{3,2,1,0:T(8,128)(2,1)S(1)} %get-tuple-element.38), channel_id=1, source_target_pairs={{0,3},{1,0},{2,1},{3,2},{4,7},{5,4},{6,5},{7,6},{8,11},{9,8},{10,9... | collective-permute-start | bytes 589832 | tf_op jit(solution)/shard_map/ppermute | solution.py:368
  29.8 0.0 collective-permute-done.7.refs_2_.refs_9_
  29.8 0.0 collective-permute-done.8.refs_3_.refs_10_
  29.8 0.6 %shard_map.60 = (bf16[2,4,16,768]{3,2,1,0:T(8,128)(2,1)S(1)}, bf16[1,4,16,768]{3,2,1,0:T(8,128)(2,1)S(1)}, bf16[2,4,16,768]{3,2,1,0:T(8,128)(2,1)S(1)}) custom-call(s32[8]{0:T(128)S(1)} %get-tuple-element.30.picks_ref, bf16[4,16,768]{2,1,0:T(8,128)(2,1)S(1)} %get-tuple-element.39.refs_0_.refs_7_, ...), custom_call_target="tpu_custom_call" | custom-call | flops 99999997952 | tf_op jit(solution)/shard_map/pallas_call | solution.py:136
  30.4 0.1 collective-permute-start.9
  30.5 1.7 %collective-permute-start.11 = (bf16[2,4,16,768]{3,2,1,0:T(8,128)(2,1)S(1)}, bf16[2,4,16,768]{3,2,1,0:T(8,128)(2,1)S(1)}, u32[]{:S(2)}, u32[]{:S(2)}) collective-permute-start(bf16[2,4,16,768]{3,2,1,0:T(8,128)(2,1)S(1)} %get-tuple-element.45), channel_id=1, source_target_pairs={{0,3},{1,0},{2,1},{3,2},{4,7},{5,4},{6,5},{7,6},{8,11},{9,8},{10,9... | collective-permute-start | bytes 589832 | tf_op jit(solution)/shard_map/ppermute | solution.py:368
  32.2 0.0 collective-permute-done.4.refs_5_
  32.2 0.0 copy-start.6
  32.2 0.5 collective-permute-start.10
  32.7 7.6 %collective-permute-done.10.refs_12_ = bf16[1,4,16,768]{3,2,1,0:T(8,128)(2,1)S(1)} collective-permute-done((bf16[1,4,16,768]{3,2,1,0:T(8,128)(2,1)S(1)}, bf16[1,4,16,768]{3,2,1,0:T(8,128)(2,1)S(1)}, u32[]{:S(2)}, u32[]{:S(2)}) %collective-permute-start.10) | collective-permute-done | bytes 98336 | tf_op jit(solution)/shard_map/ppermute | solution.py:368
  40.3 0.0 collective-permute-done.5.refs_6_
  40.3 0.0 collective-permute-done.3.refs_4_
  40.3 0.0 collective-permute-done.9.refs_11_
  40.3 0.0 collective-permute-done.11.refs_13_
  40.3 0.5 all-to-all-done.query_ref
  40.8 0.0 copy-done.6
  40.8 2.2 %shard_map.61 = (bf16[4,16,768]{2,1,0:T(8,128)(2,1)S(1)}, bf16[4,16,768]{2,1,0:T(8,128)(2,1)S(1)}, bf16[4,16,768]{2,1,0:T(8,128)(2,1)S(1)}) custom-call(s32[16]{0:T(128)S(1)} %copy-done.6, f32[4,576]{1,0:T(4,128)S(1)} %get-tuple-element.29.bias_ref, bf16[4,4,16,768]{3,2,1,0:T(8,128)(2,1)S(1)} %all-to-all-done.query_ref, bf16[4,16,768]{2,1,0:T(8,128)(2,1)S(1)} %copy-done.2, ...), custom_call_target="tpu_custom_call" | custom-call | tf_op jit(solution)/shard_map/pallas_call | solution.py:326
  43.1 2.2 %collective-permute-start.13 = (bf16[4,16,768]{2,1,0:T(8,128)(2,1)S(1)}, bf16[4,16,768]{2,1,0:T(8,128)(2,1)S(1)}, u32[]{:S(2)}, u32[]{:S(2)}) collective-permute-start(bf16[4,16,768]{2,1,0:T(8,128)(2,1)S(1)} %get-tuple-element.47), channel_id=1, source_target_pairs={{0,8},{4,12},{8,0},{12,4},{1,9},{5,13},{9,1},{13,5},{2,10},{6,14},... | collective-permute-start | bytes 294920 | tf_op jit(solution)/shard_map/ppermute | solution.py:368
  45.3 1.5 %collective-permute-start.14 = (bf16[4,16,768]{2,1,0:T(8,128)(2,1)S(1)}, bf16[4,16,768]{2,1,0:T(8,128)(2,1)S(1)}, u32[]{:S(2)}, u32[]{:S(2)}) collective-permute-start(bf16[4,16,768]{2,1,0:T(8,128)(2,1)S(1)} %get-tuple-element.48), channel_id=1, source_target_pairs={{0,4},{4,8},{8,12},{12,0},{1,5},{5,9},{9,13},{13,1},{2,6},{6,10},{... | collective-permute-start | bytes 294920 | tf_op jit(solution)/shard_map/ppermute | solution.py:368
  46.8 2.4 %collective-permute-start.12 = (bf16[4,16,768]{2,1,0:T(8,128)(2,1)S(1)}, bf16[4,16,768]{2,1,0:T(8,128)(2,1)S(1)}, u32[]{:S(2)}, u32[]{:S(2)}) collective-permute-start(bf16[4,16,768]{2,1,0:T(8,128)(2,1)S(1)} %get-tuple-element.46.refs_14_), channel_id=1, source_target_pairs={{0,12},{4,0},{8,4},{12,8},{1,13},{5,1},{9,5},{13,9},{2,14},{6,2},{... | collective-permute-start | bytes 294920 | tf_op jit(solution)/shard_map/ppermute | solution.py:368
  49.1 1.7 %shard_map.62.refs_0_ = bf16[4,16,768]{2,1,0:T(8,128)(2,1)S(1)} custom-call(s32[16]{0:T(128)S(1)} %copy-done.6, f32[4,576]{1,0:T(4,128)S(1)} %get-tuple-element.29.bias_ref, bf16[4,4,16,768]{3,2,1,0:T(8,128)(2,1)S(1)} %all-to-all-done.query_ref, bf16[4,16,768]{2,1,0:T(8,128)(2,1)S(1)} %copy-done.2, bf16[4,16,768]{2,1,0:T(8,128)(2,1)S(1)} %collective-permute-done.refs_1_, ...), custom_call_target="tpu_custom_call" | custom-call | tf_op jit(solution)/shard_map/pallas_call | solution.py:326
  50.9 2.6 %collective-permute-done.13.refs_2_ = bf16[4,16,768]{2,1,0:T(8,128)(2,1)S(1)} collective-permute-done((bf16[4,16,768]{2,1,0:T(8,128)(2,1)S(1)}, bf16[4,16,768]{2,1,0:T(8,128)(2,1)S(1)}, u32[]{:S(2)}, u32[]{:S(2)}) %collective-permute-start.13) | collective-permute-done | bytes 98336 | tf_op jit(solution)/shard_map/ppermute | solution.py:368
  53.4 0.0 collective-permute-done.14.refs_3_
  53.4 0.2 collective-permute-done.12.refs_1_
  53.7 0.8 %shard_map.63 = bf16[4,16,3072]{2,1,0:T(8,128)(2,1)} custom-call(bf16[4,16,768]{2,1,0:T(8,128)(2,1)S(1)} %shard_map.62.refs_0_, bf16[4,16,768]{2,1,0:T(8,128)(2,1)S(1)} %collective-permute-done.12.refs_1_, bf16[4,16,768]{2,1,0:T(8,128)(2,1)S(1)} %collective-permute-done.13.refs_2_, bf16[4,16,768]{2,1,0:T(8,128)(2,1)S(1)} %collective-permute-done.14.refs_3_), custom_call_target="tpu_custom_call" | custom-call | tf_op jit(solution)/shard_map/pallas_call | solution.py:356
Async XLA Ops:
  0.0 9.9 %copy-start.1 = (bf16[4,16,3072]{2,1,0:T(8,128)(2,1)S(1)}, bf16[4,16,3072]{2,1,0:T(8,128)(2,1)}, u32[]{:S(2)}) copy-start(bf16[4,16,3072]{2,1,0:T(8,128)(2,1)} %refs_1_.3) | copy-start | bytes 1179652
  0.0 9.9 %copy-start = (bf16[4,16,3072]{2,1,0:T(8,128)(2,1)S(1)}, bf16[4,16,3072]{2,1,0:T(8,128)(2,1)}, u32[]{:S(2)}) copy-start(bf16[4,16,3072]{2,1,0:T(8,128)(2,1)} %refs_0_.4) | copy-start | bytes 1179652
  2.9 7.0 %copy-start.7 = (f32[8,128]{1,0:T(8,128)S(1)}, f32[8,128]{1,0:T(8,128)}, u32[]{:S(2)}) copy-start(f32[8,128]{1,0:T(8,128)} %get-tuple-element.27.refs_2_) | copy-start | bytes 12292
  2.9 12.2 %collective-permute-start = (bf16[4,16,768]{2,1,0:T(8,128)(2,1)}, bf16[4,16,768]{2,1,0:T(8,128)(2,1)S(1)}, u32[]{:S(2)}, u32[]{:S(2)}) collective-permute-start(bf16[4,16,768]{2,1,0:T(8,128)(2,1)} %get-tuple-element.32), channel_id=1, source_target_pairs={{0,4},{4,8},{8,12},{12,0},{1,5},{5,9},{9,13},{13,1},{2,6},{6,10},{... | collective-permute-start | bytes 294920 | tf_op jit(solution)/shard_map/ppermute | solution.py:368
  6.0 12.3 %collective-permute-start.1 = (bf16[4,16,768]{2,1,0:T(8,128)(2,1)}, bf16[4,16,768]{2,1,0:T(8,128)(2,1)S(1)}, u32[]{:S(2)}, u32[]{:S(2)}) collective-permute-start(bf16[4,16,768]{2,1,0:T(8,128)(2,1)} %get-tuple-element.33), channel_id=1, source_target_pairs={{0,8},{4,12},{8,0},{12,4},{1,9},{5,13},{9,1},{13,5},{2,10},{6,14},... | collective-permute-start | bytes 294920 | tf_op jit(solution)/shard_map/ppermute | solution.py:368
  8.5 9.7 %collective-permute-start.2 = (bf16[4,16,768]{2,1,0:T(8,128)(2,1)}, bf16[4,16,768]{2,1,0:T(8,128)(2,1)S(1)}, u32[]{:S(2)}, u32[]{:S(2)}) collective-permute-start(bf16[4,16,768]{2,1,0:T(8,128)(2,1)} %get-tuple-element.34), channel_id=1, source_target_pairs={{0,12},{4,0},{8,4},{12,8},{1,13},{5,1},{9,5},{13,9},{2,14},{6,2},{... | collective-permute-start | bytes 294920 | tf_op jit(solution)/shard_map/ppermute | solution.py:368
  9.9 2.6 %copy-start.4 = (s32[16,32]{1,0:T(8,128)S(1)}, s32[16,32]{1,0:T(8,128)}, u32[]{:S(2)}) copy-start(s32[16,32]{1,0:T(8,128)} %pair_ref.1) | copy-start | bytes 6148
  9.9 8.4 %copy-start.2 = (bf16[4,16,768]{2,1,0:T(8,128)(2,1)S(1)}, bf16[4,16,768]{2,1,0:T(8,128)(2,1)}, u32[]{:S(2)}) copy-start(bf16[4,16,768]{2,1,0:T(8,128)(2,1)} %get-tuple-element.31.refs_0_) | copy-start | bytes 294916
  11.4 16.9 %collective-permute-start.6 = (bf16[4,16,768]{2,1,0:T(8,128)(2,1)S(1)}, bf16[4,16,768]{2,1,0:T(8,128)(2,1)S(1)}, u32[]{:S(2)}, u32[]{:S(2)}) collective-permute-start(bf16[4,16,768]{2,1,0:T(8,128)(2,1)S(1)} %get-tuple-element.40), channel_id=1, source_target_pairs={{0,4},{4,8},{8,12},{12,0},{1,5},{5,9},{9,13},{13,1},{2,6},{6,10},{... | collective-permute-start | bytes 294920 | tf_op jit(solution)/shard_map/ppermute | solution.py:368
  12.1 0.7 %copy-start.5 = (s32[16]{0:T(128)S(1)}, s32[16]{0:T(128)}, u32[]{:S(2)}) copy-start(s32[16]{0:T(128)} %tokens_ref.5) | copy-start | bytes 196
  12.1 17.7 %collective-permute-start.7 = (bf16[4,16,768]{2,1,0:T(8,128)(2,1)S(1)}, bf16[4,16,768]{2,1,0:T(8,128)(2,1)S(1)}, u32[]{:S(2)}, u32[]{:S(2)}) collective-permute-start(bf16[4,16,768]{2,1,0:T(8,128)(2,1)S(1)} %get-tuple-element.41), channel_id=1, source_target_pairs={{0,8},{4,12},{8,0},{12,4},{1,9},{5,13},{9,1},{13,5},{2,10},{6,14},... | collective-permute-start | bytes 294920 | tf_op jit(solution)/shard_map/ppermute | solution.py:368
  15.1 14.7 %collective-permute-start.8 = (bf16[4,16,768]{2,1,0:T(8,128)(2,1)S(1)}, bf16[4,16,768]{2,1,0:T(8,128)(2,1)S(1)}, u32[]{:S(2)}, u32[]{:S(2)}) collective-permute-start(bf16[4,16,768]{2,1,0:T(8,128)(2,1)S(1)} %get-tuple-element.42), channel_id=1, source_target_pairs={{0,12},{4,0},{8,4},{12,8},{1,13},{5,1},{9,5},{13,9},{2,14},{6,2},{... | collective-permute-start | bytes 294920 | tf_op jit(solution)/shard_map/ppermute | solution.py:368
  18.3 2.2 %copy-start.3 = (bf16[4,16,3072]{2,1,0:T(8,128)(2,1)S(1)}, bf16[4,16,3072]{2,1,0:T(8,128)(2,1)}, u32[]{:S(2)}) copy-start(bf16[4,16,3072]{2,1,0:T(8,128)(2,1)} %refs_0_.5) | copy-start | bytes 1179652
  18.9 13.3 %collective-permute-start.4 = (bf16[1,4,16,768]{3,2,1,0:T(8,128)(2,1)S(1)}, bf16[1,4,16,768]{3,2,1,0:T(8,128)(2,1)S(1)}, u32[]{:S(2)}, u32[]{:S(2)}) collective-permute-start(bf16[1,4,16,768]{3,2,1,0:T(8,128)(2,1)S(1)} %get-tuple-element.37), channel_id=1, source_target_pairs={{0,2},{1,3},{2,0},{3,1},{4,6},{5,7},{6,4},{7,5},{8,10},{9,11},{10,... | collective-permute-start | bytes 294920 | tf_op jit(solution)/shard_map/ppermute | solution.py:368
  20.4 19.9 %collective-permute-start.3 = (bf16[2,4,16,768]{3,2,1,0:T(8,128)(2,1)S(1)}, bf16[2,4,16,768]{3,2,1,0:T(8,128)(2,1)S(1)}, u32[]{:S(2)}, u32[]{:S(2)}) collective-permute-start(bf16[2,4,16,768]{3,2,1,0:T(8,128)(2,1)S(1)} %get-tuple-element.35.refs_1_.refs_4_), channel_id=1, source_target_pairs={{0,1},{1,2},{2,3},{3,0},{4,5},{5,6},{6,7},{7,4},{8,9},{9,10},{10,1... | collective-permute-start | bytes 589832 | tf_op jit(solution)/shard_map/ppermute | solution.py:368
  22.1 18.7 %all-to-all-start = ((bf16[4,4,16,768]{3,2,1,0:T(8,128)(2,1)}), bf16[4,4,16,768]{3,2,1,0:T(8,128)(2,1)S(1)}, u32[]{:S(2)}, u32[]{:S(2)}) async-start(bf16[4,4,16,768]{3,2,1,0:T(8,128)(2,1)} %get-tuple-element.36), calls=%async_computation | async-start | bytes 786432 | tf_op jit(solution)/shard_map/all_to_all | solution.py:404
  28.3 12.0 %collective-permute-start.5 = (bf16[2,4,16,768]{3,2,1,0:T(8,128)(2,1)S(1)}, bf16[2,4,16,768]{3,2,1,0:T(8,128)(2,1)S(1)}, u32[]{:S(2)}, u32[]{:S(2)}) collective-permute-start(bf16[2,4,16,768]{3,2,1,0:T(8,128)(2,1)S(1)} %get-tuple-element.38), channel_id=1, source_target_pairs={{0,3},{1,0},{2,1},{3,2},{4,7},{5,4},{6,5},{7,6},{8,11},{9,8},{10,9... | collective-permute-start | bytes 589832 | tf_op jit(solution)/shard_map/ppermute | solution.py:368
  30.4 9.9 %collective-permute-start.9 = (bf16[2,4,16,768]{3,2,1,0:T(8,128)(2,1)S(1)}, bf16[2,4,16,768]{3,2,1,0:T(8,128)(2,1)S(1)}, u32[]{:S(2)}, u32[]{:S(2)}) collective-permute-start(bf16[2,4,16,768]{3,2,1,0:T(8,128)(2,1)S(1)} %get-tuple-element.43), channel_id=1, source_target_pairs={{0,1},{1,2},{2,3},{3,0},{4,5},{5,6},{6,7},{7,4},{8,9},{9,10},{10,1... | collective-permute-start | bytes 589832 | tf_op jit(solution)/shard_map/ppermute | solution.py:368
  30.5 9.8 %collective-permute-start.11 = (bf16[2,4,16,768]{3,2,1,0:T(8,128)(2,1)S(1)}, bf16[2,4,16,768]{3,2,1,0:T(8,128)(2,1)S(1)}, u32[]{:S(2)}, u32[]{:S(2)}) collective-permute-start(bf16[2,4,16,768]{3,2,1,0:T(8,128)(2,1)S(1)} %get-tuple-element.45), channel_id=1, source_target_pairs={{0,3},{1,0},{2,1},{3,2},{4,7},{5,4},{6,5},{7,6},{8,11},{9,8},{10,9... | collective-permute-start | bytes 589832 | tf_op jit(solution)/shard_map/ppermute | solution.py:368
  32.2 8.6 %copy-start.6 = (s32[16]{0:T(128)S(1)}, s32[16]{0:T(128)}, u32[]{:S(2)}) copy-start(s32[16]{0:T(128)} %tokens_ref.5) | copy-start | bytes 196
  32.2 8.1 %collective-permute-start.10 = (bf16[1,4,16,768]{3,2,1,0:T(8,128)(2,1)S(1)}, bf16[1,4,16,768]{3,2,1,0:T(8,128)(2,1)S(1)}, u32[]{:S(2)}, u32[]{:S(2)}) collective-permute-start(bf16[1,4,16,768]{3,2,1,0:T(8,128)(2,1)S(1)} %get-tuple-element.44), channel_id=1, source_target_pairs={{0,2},{1,3},{2,0},{3,1},{4,6},{5,7},{6,4},{7,5},{8,10},{9,11},{10,... | collective-permute-start | bytes 294920 | tf_op jit(solution)/shard_map/ppermute | solution.py:368
  43.1 10.4 %collective-permute-start.13 = (bf16[4,16,768]{2,1,0:T(8,128)(2,1)S(1)}, bf16[4,16,768]{2,1,0:T(8,128)(2,1)S(1)}, u32[]{:S(2)}, u32[]{:S(2)}) collective-permute-start(bf16[4,16,768]{2,1,0:T(8,128)(2,1)S(1)} %get-tuple-element.47), channel_id=1, source_target_pairs={{0,8},{4,12},{8,0},{12,4},{1,9},{5,13},{9,1},{13,5},{2,10},{6,14},... | collective-permute-start | bytes 294920 | tf_op jit(solution)/shard_map/ppermute | solution.py:368
  45.3 8.1 %collective-permute-start.14 = (bf16[4,16,768]{2,1,0:T(8,128)(2,1)S(1)}, bf16[4,16,768]{2,1,0:T(8,128)(2,1)S(1)}, u32[]{:S(2)}, u32[]{:S(2)}) collective-permute-start(bf16[4,16,768]{2,1,0:T(8,128)(2,1)S(1)} %get-tuple-element.48), channel_id=1, source_target_pairs={{0,4},{4,8},{8,12},{12,0},{1,5},{5,9},{9,13},{13,1},{2,6},{6,10},{... | collective-permute-start | bytes 294920 | tf_op jit(solution)/shard_map/ppermute | solution.py:368
  46.8 6.9 %collective-permute-start.12 = (bf16[4,16,768]{2,1,0:T(8,128)(2,1)S(1)}, bf16[4,16,768]{2,1,0:T(8,128)(2,1)S(1)}, u32[]{:S(2)}, u32[]{:S(2)}) collective-permute-start(bf16[4,16,768]{2,1,0:T(8,128)(2,1)S(1)} %get-tuple-element.46.refs_14_), channel_id=1, source_target_pairs={{0,12},{4,0},{8,4},{12,8},{1,13},{5,1},{9,5},{13,9},{2,14},{6,2},{... | collective-permute-start | bytes 294920 | tf_op jit(solution)/shard_map/ppermute | solution.py:368

commit v6 on v5

--- a/solution.py
+++ b/solution.py
@@ -395,14 +395,16 @@
         after, limit = (token,), VMEM
     received = [exchange(pieces, 1) for pieces in packed]
     picks, bias = plan(pair_list, block_tokens, token, blocks, count_head, count_tm)
-    sent, after = [], ()
+    inputs, after = [], ()
     for owns, (_, size) in zip(received, parts):
-        sent.append(pick_blocks(picks, owns, (0, 2 * size), count_tm, after))
-        after = (sent[-1][0],)
-    message = [(0, 0, width_here)]
-    (query,), _ = rotate_pieces(arrays, message, count_head, (sent[0][0],), stacked=True)
+        sent = pick_blocks(picks, owns, (0, 2 * size), count_tm, after)
+        if not inputs:
+            (query,), _ = rotate_pieces(
+                arrays, [(0, 0, width_here)], count_head, (sent[0],), stacked=True
+            )
+        inputs.append((owns, forward(sent)))
+        after = inputs[-1][1]
     query = lax.all_to_all(query, "head", split_axis=0, concat_axis=0, tiled=True)
-    inputs = [(owns, forward(picked)) for owns, picked in zip(received, sent)]
     sizes = [size for _, size in parts]
     leaving = attend(
         block_tokens, bias, query, inputs, sizes, list(range(1, count_head)), (), NO_COST

time: 54.7 us -> 55.6 us (1.016)
  waiting for transfers between devices: 10.9 us -> 14.3 us
  starting transfers between devices: 28.9 us -> 26.8 us
    all_to_all x1, starting transfers between devices: 6.23 us -> 3.47 us  [shards(): lax.all_to_all(query, 'head', split_axis=0, concat_axis=0, tiled=True)]
    all_to_all x1, waiting for transfers between devices: 0.5 us -> 2.5 us  [shards(): lax.all_to_all(query, 'head', split_axis=0, concat_axis=0, tiled=True)]
    ppermute x15, waiting for transfers between devices: 10.4 us -> 11.8 us  [shifted(): lax.ppermute(array, axis, [(i, (i + distance) % count) for i in range(cou...]
    ppermute x15, starting transfers between devices: 22.7 us -> 23.3 us  [shifted(): lax.ppermute(array, axis, [(i, (i + distance) % count) for i in range(cou...]
  transfers between devices with their start and end apart: 16 -> 16, of which waited for: 4 -> 6; matrix products, arithmetic and copies ran while one was open for 0% -> 0% of each run, Pallas kernels for 15% -> 15%
where the time goes in v6:
time: 55.6 us; the launch traced here: 55.4 us
  starting transfers between devices  26.8 us (48%)
  waiting for transfers between devices  14.3 us (26%)
  Pallas kernels  14.1 us (25%)
    ppermute x15, starting transfers between devices, shifted(): lax.ppermute(array, axis, [(i, (i + distance) % count) for i in range(cou...  23.3 us
    ppermute x15, waiting for transfers between devices, shifted(): lax.ppermute(array, axis, [(i, (i + distance) % count) for i in range(cou...  11.8 us
    pallas_call x3, Pallas kernels, rotate_pieces(): pl.pallas_call(functools.partial(rotate_kernel, message, sources, count_h...  5.97 us
    pallas_call x2, Pallas kernels, attend(): pl.pallas_call(functools.partial(attend_kernel, (count_head, count_tm), s...  3.96 us
    all_to_all x1, starting transfers between devices, shards(): lax.all_to_all(query, 'head', split_axis=0, concat_axis=0, tiled=True)  3.47 us
    all_to_all x1, waiting for transfers between devices, shards(): lax.all_to_all(query, 'head', split_axis=0, concat_axis=0, tiled=True)  2.5 us
    pallas_call x1, Pallas kernels, plan(): pl.pallas_call(functools.partial(plan_kernel, count_head, count_tm, block...  2.25 us
    pallas_call x2, Pallas kernels, pick_blocks(): pl.pallas_call(functools.partial(pick_kernel, count_head, count_tm, lanes...  1.18 us
  transfers between devices with their start and end apart: 16, of which 6 were waited for; matrix products, arithmetic and copies ran while one was open for 0% of the time, Pallas kernels for 15%

profile of v6, /device:TPU:0, one launch (start us, length us, event | category | flops | bytes accessed | tf_op | source)
XLA Modules:
  0.0 55.4 jit_solution(12918681218716429734)
XLA Ops:
  0.0 0.0 copy-start.1
  0.0 0.0 copy-start
  0.0 2.9 %shard_map.55 = (bf16[4,16,768]{2,1,0:T(8,128)(2,1)}, bf16[4,16,768]{2,1,0:T(8,128)(2,1)}, bf16[4,16,768]{2,1,0:T(8,128)(2,1)}, bf16[4,16,768]{2,1,0:T(8,128)(2,1)}, f32[8,128]{1,0:T(8,128)}) custom-call(bf16[4,16,3072]{2,1,0:T(8,128)(2,1)} %refs_0_.4, bf16[4,16,3072]{2,1,0:T(8,128)(2,1)} %refs_1_.3), custom_call_target="tpu_custom_call" | custom-call | tf_op jit(solution)/shard_map/pallas_call | solution.py:101
  2.9 0.0 copy-start.7
  2.9 3.1 %collective-permute-start = (bf16[4,16,768]{2,1,0:T(8,128)(2,1)}, bf16[4,16,768]{2,1,0:T(8,128)(2,1)S(1)}, u32[]{:S(2)}, u32[]{:S(2)}) collective-permute-start(bf16[4,16,768]{2,1,0:T(8,128)(2,1)} %get-tuple-element.32), channel_id=1, source_target_pairs={{0,4},{4,8},{8,12},{12,0},{1,5},{5,9},{9,13},{13,1},{2,6},{6,10},{... | collective-permute-start | bytes 294920 | tf_op jit(solution)/shard_map/ppermute | solution.py:368
  6.0 2.6 %collective-permute-start.1 = (bf16[4,16,768]{2,1,0:T(8,128)(2,1)}, bf16[4,16,768]{2,1,0:T(8,128)(2,1)S(1)}, u32[]{:S(2)}, u32[]{:S(2)}) collective-permute-start(bf16[4,16,768]{2,1,0:T(8,128)(2,1)} %get-tuple-element.33), channel_id=1, source_target_pairs={{0,8},{4,12},{8,0},{12,4},{1,9},{5,13},{9,1},{13,5},{2,10},{6,14},... | collective-permute-start | bytes 294920 | tf_op jit(solution)/shard_map/ppermute | solution.py:368
  8.5 1.3 %collective-permute-start.2 = (bf16[4,16,768]{2,1,0:T(8,128)(2,1)}, bf16[4,16,768]{2,1,0:T(8,128)(2,1)S(1)}, u32[]{:S(2)}, u32[]{:S(2)}) collective-permute-start(bf16[4,16,768]{2,1,0:T(8,128)(2,1)} %get-tuple-element.34), channel_id=1, source_target_pairs={{0,12},{4,0},{8,4},{12,8},{1,13},{5,1},{9,5},{13,9},{2,14},{6,2},{... | collective-permute-start | bytes 294920 | tf_op jit(solution)/shard_map/ppermute | solution.py:368
  9.9 0.0 copy-done.1
  9.9 0.0 copy-done
  9.9 0.0 copy-done.7
  9.9 0.0 copy-start.4
  9.9 0.0 copy-start.2
  9.9 1.5 %shard_map.56 = (bf16[4,16,768]{2,1,0:T(8,128)(2,1)S(1)}, bf16[4,16,768]{2,1,0:T(8,128)(2,1)S(1)}, bf16[4,16,768]{2,1,0:T(8,128)(2,1)S(1)}, bf16[4,16,768]{2,1,0:T(8,128)(2,1)S(1)}, f32[8,128]{1,0:T(8,128)S(1)}) custom-call(bf16[4,16,3072]{2,1,0:T(8,128)(2,1)S(1)} %copy-done, bf16[4,16,3072]{2,1,0:T(8,128)(2,1)S(1)} %copy-done.1, f32[8,128]{1,0:T(8,128)S(1)} %copy-done.7), custom_call_target="tpu_custom_call" | custom-call | tf_op jit(solution)/shard_map/pallas_call | solution.py:101
  11.4 0.0 copy-start.5
  11.4 0.7 %collective-permute-start.6 = (bf16[4,16,768]{2,1,0:T(8,128)(2,1)S(1)}, bf16[4,16,768]{2,1,0:T(8,128)(2,1)S(1)}, u32[]{:S(2)}, u32[]{:S(2)}) collective-permute-start(bf16[4,16,768]{2,1,0:T(8,128)(2,1)S(1)} %get-tuple-element.40), channel_id=1, source_target_pairs={{0,4},{4,8},{8,12},{12,0},{1,5},{5,9},{9,13},{13,1},{2,6},{6,10},{... | collective-permute-start | bytes 294920 | tf_op jit(solution)/shard_map/ppermute | solution.py:368
  12.1 0.0 copy-done.4
  12.2 0.0 copy-done.5
  12.2 2.3 %shard_map.57 = (s32[8]{0:T(128)S(1)}, f32[4,576]{1,0:T(4,128)S(1)}) custom-call(s32[16,32]{1,0:T(8,128)S(1)} %copy-done.4, s32[16]{0:T(128)S(1)} %copy-done.5, f32[8,128]{1,0:T(8,128)S(1)} %get-tuple-element.28._), custom_call_target="tpu_custom_call" | custom-call | tf_op jit(solution)/shard_map/pallas_call | solution.py:237
  14.4 0.0 collective-permute-done.refs_1_
  14.4 1.2 %collective-permute-done.1.refs_2_ = bf16[4,16,768]{2,1,0:T(8,128)(2,1)S(1)} collective-permute-done((bf16[4,16,768]{2,1,0:T(8,128)(2,1)}, bf16[4,16,768]{2,1,0:T(8,128)(2,1)S(1)}, u32[]{:S(2)}, u32[]{:S(2)}) %collective-permute-start.1) | collective-permute-done | bytes 98336 | tf_op jit(solution)/shard_map/ppermute | solution.py:368
  15.7 0.4 collective-permute-done.2.refs_3_
  16.1 0.0 copy-done.2
  16.1 0.0 copy-start.3
  16.1 0.6 %shard_map.58 = (bf16[2,4,16,768]{3,2,1,0:T(8,128)(2,1)S(1)}, bf16[1,4,16,768]{3,2,1,0:T(8,128)(2,1)S(1)}, bf16[2,4,16,768]{3,2,1,0:T(8,128)(2,1)S(1)}) custom-call(s32[8]{0:T(128)S(1)} %get-tuple-element.30.picks_ref, bf16[4,16,768]{2,1,0:T(8,128)(2,1)S(1)} %copy-done.2, bf16[4,16,768]{2,1,0:T(8,128)(2,1)S(1)} %collective-permute-done.refs_1_, ...), custom_call_target="tpu_custom_call" | custom-call | flops 99999997952 | tf_op jit(solution)/shard_map/pallas_call | solution.py:136
  16.7 0.6 %collective-permute-start.5 = (bf16[2,4,16,768]{3,2,1,0:T(8,128)(2,1)S(1)}, bf16[2,4,16,768]{3,2,1,0:T(8,128)(2,1)S(1)}, u32[]{:S(2)}, u32[]{:S(2)}) collective-permute-start(bf16[2,4,16,768]{3,2,1,0:T(8,128)(2,1)S(1)} %get-tuple-element.38), channel_id=1, source_target_pairs={{0,3},{1,0},{2,1},{3,2},{4,7},{5,4},{6,5},{7,6},{8,11},{9,8},{10,9... | collective-permute-start | bytes 589832 | tf_op jit(solution)/shard_map/ppermute | solution.py:368
  17.2 0.0 collective-permute-start.3
  17.2 3.6 %collective-permute-start.7 = (bf16[4,16,768]{2,1,0:T(8,128)(2,1)S(1)}, bf16[4,16,768]{2,1,0:T(8,128)(2,1)S(1)}, u32[]{:S(2)}, u32[]{:S(2)}) collective-permute-start(bf16[4,16,768]{2,1,0:T(8,128)(2,1)S(1)} %get-tuple-element.41), channel_id=1, source_target_pairs={{0,8},{4,12},{8,0},{12,4},{1,9},{5,13},{9,1},{13,5},{2,10},{6,14},... | collective-permute-start | bytes 294920 | tf_op jit(solution)/shard_map/ppermute | solution.py:368
  20.9 3.3 %collective-permute-start.8 = (bf16[4,16,768]{2,1,0:T(8,128)(2,1)S(1)}, bf16[4,16,768]{2,1,0:T(8,128)(2,1)S(1)}, u32[]{:S(2)}, u32[]{:S(2)}) collective-permute-start(bf16[4,16,768]{2,1,0:T(8,128)(2,1)S(1)} %get-tuple-element.42), channel_id=1, source_target_pairs={{0,12},{4,0},{8,4},{12,8},{1,13},{5,1},{9,5},{13,9},{2,14},{6,2},{... | collective-permute-start | bytes 294920 | tf_op jit(solution)/shard_map/ppermute | solution.py:368
  24.2 0.0 collective-permute-done.6.refs_1_.refs_8_
  24.2 0.9 %collective-permute-start.4 = (bf16[1,4,16,768]{3,2,1,0:T(8,128)(2,1)S(1)}, bf16[1,4,16,768]{3,2,1,0:T(8,128)(2,1)S(1)}, u32[]{:S(2)}, u32[]{:S(2)}) collective-permute-start(bf16[1,4,16,768]{3,2,1,0:T(8,128)(2,1)S(1)} %get-tuple-element.37), channel_id=1, source_target_pairs={{0,2},{1,3},{2,0},{3,1},{4,6},{5,7},{6,4},{7,5},{8,10},{9,11},{10,... | collective-permute-start | bytes 294920 | tf_op jit(solution)/shard_map/ppermute | solution.py:368
  25.0 0.0 copy-done.3
  25.0 1.6 %shard_map.59 = (bf16[4,4,16,768]{3,2,1,0:T(8,128)(2,1)}, f32[8,128]{1,0:T(8,128)}) custom-call(bf16[4,16,3072]{2,1,0:T(8,128)(2,1)S(1)} %copy-done.3, bf16[2,4,16,768]{3,2,1,0:T(8,128)(2,1)S(1)} %get-tuple-element.35.refs_1_), custom_call_target="tpu_custom_call" | custom-call | tf_op jit(solution)/shard_map/pallas_call | solution.py:101
  26.7 3.5 %all-to-all-start = ((bf16[4,4,16,768]{3,2,1,0:T(8,128)(2,1)}), bf16[4,4,16,768]{3,2,1,0:T(8,128)(2,1)S(1)}, u32[]{:S(2)}, u32[]{:S(2)}) async-start(bf16[4,4,16,768]{3,2,1,0:T(8,128)(2,1)} %get-tuple-element.36), calls=%async_computation | async-start | bytes 786432 | tf_op jit(solution)/shard_map/all_to_all | solution.py:407
  30.2 0.0 collective-permute-done.7.refs_2_.refs_9_
  30.2 0.0 collective-permute-done.8.refs_3_.refs_10_
  30.2 0.0 collective-permute-done.4.refs_5_
  30.2 0.0 collective-permute-done.5.refs_6_
  30.2 0.0 collective-permute-done.3.refs_4_
  30.2 0.6 %shard_map.60 = (bf16[2,4,16,768]{3,2,1,0:T(8,128)(2,1)S(1)}, bf16[1,4,16,768]{3,2,1,0:T(8,128)(2,1)S(1)}, bf16[2,4,16,768]{3,2,1,0:T(8,128)(2,1)S(1)}) custom-call(s32[8]{0:T(128)S(1)} %get-tuple-element.30.picks_ref, bf16[4,16,768]{2,1,0:T(8,128)(2,1)S(1)} %get-tuple-element.39.refs_0_.refs_7_, ...), custom_call_target="tpu_custom_call" | custom-call | flops 99999997952 | tf_op jit(solution)/shard_map/pallas_call | solution.py:136
  30.8 0.5 collective-permute-start.9
  31.3 1.3 %collective-permute-start.11 = (bf16[2,4,16,768]{3,2,1,0:T(8,128)(2,1)S(1)}, bf16[2,4,16,768]{3,2,1,0:T(8,128)(2,1)S(1)}, u32[]{:S(2)}, u32[]{:S(2)}) collective-permute-start(bf16[2,4,16,768]{3,2,1,0:T(8,128)(2,1)S(1)} %get-tuple-element.45), channel_id=1, source_target_pairs={{0,3},{1,0},{2,1},{3,2},{4,7},{5,4},{6,5},{7,6},{8,11},{9,8},{10,9... | collective-permute-start | bytes 589832 | tf_op jit(solution)/shard_map/ppermute | solution.py:368
  32.6 0.0 copy-start.6
  32.6 1.2 %collective-permute-start.10 = (bf16[1,4,16,768]{3,2,1,0:T(8,128)(2,1)S(1)}, bf16[1,4,16,768]{3,2,1,0:T(8,128)(2,1)S(1)}, u32[]{:S(2)}, u32[]{:S(2)}) collective-permute-start(bf16[1,4,16,768]{3,2,1,0:T(8,128)(2,1)S(1)} %get-tuple-element.44), channel_id=1, source_target_pairs={{0,2},{1,3},{2,0},{3,1},{4,6},{5,7},{6,4},{7,5},{8,10},{9,11},{10,... | collective-permute-start | bytes 294920 | tf_op jit(solution)/shard_map/ppermute | solution.py:368
  33.8 6.4 %collective-permute-done.10.refs_12_ = bf16[1,4,16,768]{3,2,1,0:T(8,128)(2,1)S(1)} collective-permute-done((bf16[1,4,16,768]{3,2,1,0:T(8,128)(2,1)S(1)}, bf16[1,4,16,768]{3,2,1,0:T(8,128)(2,1)S(1)}, u32[]{:S(2)}, u32[]{:S(2)}) %collective-permute-start.10) | collective-permute-done | bytes 98336 | tf_op jit(solution)/shard_map/ppermute | solution.py:368
  40.2 0.0 collective-permute-done.9.refs_11_
  40.2 0.0 collective-permute-done.11.refs_13_
  40.2 2.5 %all-to-all-done.query_ref = bf16[4,4,16,768]{3,2,1,0:T(8,128)(2,1)S(1)} async-done(((bf16[4,4,16,768]{3,2,1,0:T(8,128)(2,1)}), bf16[4,4,16,768]{3,2,1,0:T(8,128)(2,1)S(1)}, u32[]{:S(2)}, u32[]{:S(2)}) %all-to-all-start) | async-done | bytes 393248 | tf_op jit(solution)/shard_map/all_to_all | solution.py:407
  42.7 0.0 copy-done.6
  42.7 2.2 %shard_map.61 = (bf16[4,16,768]{2,1,0:T(8,128)(2,1)S(1)}, bf16[4,16,768]{2,1,0:T(8,128)(2,1)S(1)}, bf16[4,16,768]{2,1,0:T(8,128)(2,1)S(1)}) custom-call(s32[16]{0:T(128)S(1)} %copy-done.6, f32[4,576]{1,0:T(4,128)S(1)} %get-tuple-element.29.bias_ref, bf16[4,4,16,768]{3,2,1,0:T(8,128)(2,1)S(1)} %all-to-all-done.query_ref, bf16[4,16,768]{2,1,0:T(8,128)(2,1)S(1)} %copy-done.2, ...), custom_call_target="tpu_custom_call" | custom-call | tf_op jit(solution)/shard_map/pallas_call | solution.py:326
  44.9 0.5 collective-permute-start.13
  45.4 1.6 %collective-permute-start.14 = (bf16[4,16,768]{2,1,0:T(8,128)(2,1)S(1)}, bf16[4,16,768]{2,1,0:T(8,128)(2,1)S(1)}, u32[]{:S(2)}, u32[]{:S(2)}) collective-permute-start(bf16[4,16,768]{2,1,0:T(8,128)(2,1)S(1)} %get-tuple-element.48), channel_id=1, source_target_pairs={{0,4},{4,8},{8,12},{12,0},{1,5},{5,9},{9,13},{13,1},{2,6},{6,10},{... | collective-permute-start | bytes 294920 | tf_op jit(solution)/shard_map/ppermute | solution.py:368
  47.0 2.2 %collective-permute-start.12 = (bf16[4,16,768]{2,1,0:T(8,128)(2,1)S(1)}, bf16[4,16,768]{2,1,0:T(8,128)(2,1)S(1)}, u32[]{:S(2)}, u32[]{:S(2)}) collective-permute-start(bf16[4,16,768]{2,1,0:T(8,128)(2,1)S(1)} %get-tuple-element.46.refs_14_), channel_id=1, source_target_pairs={{0,12},{4,0},{8,4},{12,8},{1,13},{5,1},{9,5},{13,9},{2,14},{6,2},{... | collective-permute-start | bytes 294920 | tf_op jit(solution)/shard_map/ppermute | solution.py:368
  49.2 1.7 %shard_map.62.refs_0_ = bf16[4,16,768]{2,1,0:T(8,128)(2,1)S(1)} custom-call(s32[16]{0:T(128)S(1)} %copy-done.6, f32[4,576]{1,0:T(4,128)S(1)} %get-tuple-element.29.bias_ref, bf16[4,4,16,768]{3,2,1,0:T(8,128)(2,1)S(1)} %all-to-all-done.query_ref, bf16[4,16,768]{2,1,0:T(8,128)(2,1)S(1)} %copy-done.2, bf16[4,16,768]{2,1,0:T(8,128)(2,1)S(1)} %collective-permute-done.refs_1_, ...), custom_call_target="tpu_custom_call" | custom-call | tf_op jit(solution)/shard_map/pallas_call | solution.py:326
  50.9 2.9 %collective-permute-done.13.refs_2_ = bf16[4,16,768]{2,1,0:T(8,128)(2,1)S(1)} collective-permute-done((bf16[4,16,768]{2,1,0:T(8,128)(2,1)S(1)}, bf16[4,16,768]{2,1,0:T(8,128)(2,1)S(1)}, u32[]{:S(2)}, u32[]{:S(2)}) %collective-permute-start.13) | collective-permute-done | bytes 98336 | tf_op jit(solution)/shard_map/ppermute | solution.py:368
  53.8 0.0 collective-permute-done.14.refs_3_
  53.8 0.8 %collective-permute-done.12.refs_1_ = bf16[4,16,768]{2,1,0:T(8,128)(2,1)S(1)} collective-permute-done((bf16[4,16,768]{2,1,0:T(8,128)(2,1)S(1)}, bf16[4,16,768]{2,1,0:T(8,128)(2,1)S(1)}, u32[]{:S(2)}, u32[]{:S(2)}) %collective-permute-start.12) | collective-permute-done | bytes 98336 | tf_op jit(solution)/shard_map/ppermute | solution.py:368
  54.6 0.8 %shard_map.63 = bf16[4,16,3072]{2,1,0:T(8,128)(2,1)} custom-call(bf16[4,16,768]{2,1,0:T(8,128)(2,1)S(1)} %shard_map.62.refs_0_, bf16[4,16,768]{2,1,0:T(8,128)(2,1)S(1)} %collective-permute-done.12.refs_1_, bf16[4,16,768]{2,1,0:T(8,128)(2,1)S(1)} %collective-permute-done.13.refs_2_, bf16[4,16,768]{2,1,0:T(8,128)(2,1)S(1)} %collective-permute-done.14.refs_3_), custom_call_target="tpu_custom_call" | custom-call | tf_op jit(solution)/shard_map/pallas_call | solution.py:356
Async XLA Ops:
  0.0 9.9 %copy-start.1 = (bf16[4,16,3072]{2,1,0:T(8,128)(2,1)S(1)}, bf16[4,16,3072]{2,1,0:T(8,128)(2,1)}, u32[]{:S(2)}) copy-start(bf16[4,16,3072]{2,1,0:T(8,128)(2,1)} %refs_1_.3) | copy-start | bytes 1179652
  0.0 9.9 %copy-start = (bf16[4,16,3072]{2,1,0:T(8,128)(2,1)S(1)}, bf16[4,16,3072]{2,1,0:T(8,128)(2,1)}, u32[]{:S(2)}) copy-start(bf16[4,16,3072]{2,1,0:T(8,128)(2,1)} %refs_0_.4) | copy-start | bytes 1179652
  2.9 7.0 %copy-start.7 = (f32[8,128]{1,0:T(8,128)S(1)}, f32[8,128]{1,0:T(8,128)}, u32[]{:S(2)}) copy-start(f32[8,128]{1,0:T(8,128)} %get-tuple-element.27.refs_2_) | copy-start | bytes 12292
  2.9 11.5 %collective-permute-start = (bf16[4,16,768]{2,1,0:T(8,128)(2,1)}, bf16[4,16,768]{2,1,0:T(8,128)(2,1)S(1)}, u32[]{:S(2)}, u32[]{:S(2)}) collective-permute-start(bf16[4,16,768]{2,1,0:T(8,128)(2,1)} %get-tuple-element.32), channel_id=1, source_target_pairs={{0,4},{4,8},{8,12},{12,0},{1,5},{5,9},{9,13},{13,1},{2,6},{6,10},{... | collective-permute-start | bytes 294920 | tf_op jit(solution)/shard_map/ppermute | solution.py:368
  6.0 9.7 %collective-permute-start.1 = (bf16[4,16,768]{2,1,0:T(8,128)(2,1)}, bf16[4,16,768]{2,1,0:T(8,128)(2,1)S(1)}, u32[]{:S(2)}, u32[]{:S(2)}) collective-permute-start(bf16[4,16,768]{2,1,0:T(8,128)(2,1)} %get-tuple-element.33), channel_id=1, source_target_pairs={{0,8},{4,12},{8,0},{12,4},{1,9},{5,13},{9,1},{13,5},{2,10},{6,14},... | collective-permute-start | bytes 294920 | tf_op jit(solution)/shard_map/ppermute | solution.py:368
  8.5 7.5 %collective-permute-start.2 = (bf16[4,16,768]{2,1,0:T(8,128)(2,1)}, bf16[4,16,768]{2,1,0:T(8,128)(2,1)S(1)}, u32[]{:S(2)}, u32[]{:S(2)}) collective-permute-start(bf16[4,16,768]{2,1,0:T(8,128)(2,1)} %get-tuple-element.34), channel_id=1, source_target_pairs={{0,12},{4,0},{8,4},{12,8},{1,13},{5,1},{9,5},{13,9},{2,14},{6,2},{... | collective-permute-start | bytes 294920 | tf_op jit(solution)/shard_map/ppermute | solution.py:368
  9.9 2.2 %copy-start.4 = (s32[16,32]{1,0:T(8,128)S(1)}, s32[16,32]{1,0:T(8,128)}, u32[]{:S(2)}) copy-start(s32[16,32]{1,0:T(8,128)} %pair_ref.1) | copy-start | bytes 6148
  9.9 6.1 %copy-start.2 = (bf16[4,16,768]{2,1,0:T(8,128)(2,1)S(1)}, bf16[4,16,768]{2,1,0:T(8,128)(2,1)}, u32[]{:S(2)}) copy-start(bf16[4,16,768]{2,1,0:T(8,128)(2,1)} %get-tuple-element.31.refs_0_) | copy-start | bytes 294916
  11.4 0.7 %copy-start.5 = (s32[16]{0:T(128)S(1)}, s32[16]{0:T(128)}, u32[]{:S(2)}) copy-start(s32[16]{0:T(128)} %tokens_ref.5) | copy-start | bytes 196
  11.4 12.8 %collective-permute-start.6 = (bf16[4,16,768]{2,1,0:T(8,128)(2,1)S(1)}, bf16[4,16,768]{2,1,0:T(8,128)(2,1)S(1)}, u32[]{:S(2)}, u32[]{:S(2)}) collective-permute-start(bf16[4,16,768]{2,1,0:T(8,128)(2,1)S(1)} %get-tuple-element.40), channel_id=1, source_target_pairs={{0,4},{4,8},{8,12},{12,0},{1,5},{5,9},{9,13},{13,1},{2,6},{6,10},{... | collective-permute-start | bytes 294920 | tf_op jit(solution)/shard_map/ppermute | solution.py:368
  16.1 9.0 %copy-start.3 = (bf16[4,16,3072]{2,1,0:T(8,128)(2,1)S(1)}, bf16[4,16,3072]{2,1,0:T(8,128)(2,1)}, u32[]{:S(2)}) copy-start(bf16[4,16,3072]{2,1,0:T(8,128)(2,1)} %refs_0_.5) | copy-start | bytes 1179652
  16.7 13.5 %collective-permute-start.5 = (bf16[2,4,16,768]{3,2,1,0:T(8,128)(2,1)S(1)}, bf16[2,4,16,768]{3,2,1,0:T(8,128)(2,1)S(1)}, u32[]{:S(2)}, u32[]{:S(2)}) collective-permute-start(bf16[2,4,16,768]{3,2,1,0:T(8,128)(2,1)S(1)} %get-tuple-element.38), channel_id=1, source_target_pairs={{0,3},{1,0},{2,1},{3,2},{4,7},{5,4},{6,5},{7,6},{8,11},{9,8},{10,9... | collective-permute-start | bytes 589832 | tf_op jit(solution)/shard_map/ppermute | solution.py:368
  17.2 13.0 %collective-permute-start.3 = (bf16[2,4,16,768]{3,2,1,0:T(8,128)(2,1)S(1)}, bf16[2,4,16,768]{3,2,1,0:T(8,128)(2,1)S(1)}, u32[]{:S(2)}, u32[]{:S(2)}) collective-permute-start(bf16[2,4,16,768]{3,2,1,0:T(8,128)(2,1)S(1)} %get-tuple-element.35.refs_1_), channel_id=1, source_target_pairs={{0,1},{1,2},{2,3},{3,0},{4,5},{5,6},{6,7},{7,4},{8,9},{9,10},{10,1... | collective-permute-start | bytes 589832 | tf_op jit(solution)/shard_map/ppermute | solution.py:368
  17.2 12.9 %collective-permute-start.7 = (bf16[4,16,768]{2,1,0:T(8,128)(2,1)S(1)}, bf16[4,16,768]{2,1,0:T(8,128)(2,1)S(1)}, u32[]{:S(2)}, u32[]{:S(2)}) collective-permute-start(bf16[4,16,768]{2,1,0:T(8,128)(2,1)S(1)} %get-tuple-element.41), channel_id=1, source_target_pairs={{0,8},{4,12},{8,0},{12,4},{1,9},{5,13},{9,1},{13,5},{2,10},{6,14},... | collective-permute-start | bytes 294920 | tf_op jit(solution)/shard_map/ppermute | solution.py:368
  20.9 9.3 %collective-permute-start.8 = (bf16[4,16,768]{2,1,0:T(8,128)(2,1)S(1)}, bf16[4,16,768]{2,1,0:T(8,128)(2,1)S(1)}, u32[]{:S(2)}, u32[]{:S(2)}) collective-permute-start(bf16[4,16,768]{2,1,0:T(8,128)(2,1)S(1)} %get-tuple-element.42), channel_id=1, source_target_pairs={{0,12},{4,0},{8,4},{12,8},{1,13},{5,1},{9,5},{13,9},{2,14},{6,2},{... | collective-permute-start | bytes 294920 | tf_op jit(solution)/shard_map/ppermute | solution.py:368
  24.2 6.0 %collective-permute-start.4 = (bf16[1,4,16,768]{3,2,1,0:T(8,128)(2,1)S(1)}, bf16[1,4,16,768]{3,2,1,0:T(8,128)(2,1)S(1)}, u32[]{:S(2)}, u32[]{:S(2)}) collective-permute-start(bf16[1,4,16,768]{3,2,1,0:T(8,128)(2,1)S(1)} %get-tuple-element.37), channel_id=1, source_target_pairs={{0,2},{1,3},{2,0},{3,1},{4,6},{5,7},{6,4},{7,5},{8,10},{9,11},{10,... | collective-permute-start | bytes 294920 | tf_op jit(solution)/shard_map/ppermute | solution.py:368
  26.7 16.0 %all-to-all-start = ((bf16[4,4,16,768]{3,2,1,0:T(8,128)(2,1)}), bf16[4,4,16,768]{3,2,1,0:T(8,128)(2,1)S(1)}, u32[]{:S(2)}, u32[]{:S(2)}) async-start(bf16[4,4,16,768]{3,2,1,0:T(8,128)(2,1)} %get-tuple-element.36), calls=%async_computation | async-start | bytes 786432 | tf_op jit(solution)/shard_map/all_to_all | solution.py:407
  30.8 9.4 %collective-permute-start.9 = (bf16[2,4,16,768]{3,2,1,0:T(8,128)(2,1)S(1)}, bf16[2,4,16,768]{3,2,1,0:T(8,128)(2,1)S(1)}, u32[]{:S(2)}, u32[]{:S(2)}) collective-permute-start(bf16[2,4,16,768]{3,2,1,0:T(8,128)(2,1)S(1)} %get-tuple-element.43), channel_id=1, source_target_pairs={{0,1},{1,2},{2,3},{3,0},{4,5},{5,6},{6,7},{7,4},{8,9},{9,10},{10,1... | collective-permute-start | bytes 589832 | tf_op jit(solution)/shard_map/ppermute | solution.py:368
  31.3 8.9 %collective-permute-start.11 = (bf16[2,4,16,768]{3,2,1,0:T(8,128)(2,1)S(1)}, bf16[2,4,16,768]{3,2,1,0:T(8,128)(2,1)S(1)}, u32[]{:S(2)}, u32[]{:S(2)}) collective-permute-start(bf16[2,4,16,768]{3,2,1,0:T(8,128)(2,1)S(1)} %get-tuple-element.45), channel_id=1, source_target_pairs={{0,3},{1,0},{2,1},{3,2},{4,7},{5,4},{6,5},{7,6},{8,11},{9,8},{10,9... | collective-permute-start | bytes 589832 | tf_op jit(solution)/shard_map/ppermute | solution.py:368
  32.6 10.1 %copy-start.6 = (s32[16]{0:T(128)S(1)}, s32[16]{0:T(128)}, u32[]{:S(2)}) copy-start(s32[16]{0:T(128)} %tokens_ref.5) | copy-start | bytes 196
  32.6 7.6 %collective-permute-start.10 = (bf16[1,4,16,768]{3,2,1,0:T(8,128)(2,1)S(1)}, bf16[1,4,16,768]{3,2,1,0:T(8,128)(2,1)S(1)}, u32[]{:S(2)}, u32[]{:S(2)}) collective-permute-start(bf16[1,4,16,768]{3,2,1,0:T(8,128)(2,1)S(1)} %get-tuple-element.44), channel_id=1, source_target_pairs={{0,2},{1,3},{2,0},{3,1},{4,6},{5,7},{6,4},{7,5},{8,10},{9,11},{10,... | collective-permute-start | bytes 294920 | tf_op jit(solution)/shard_map/ppermute | solution.py:368
  44.9 8.9 %collective-permute-start.13 = (bf16[4,16,768]{2,1,0:T(8,128)(2,1)S(1)}, bf16[4,16,768]{2,1,0:T(8,128)(2,1)S(1)}, u32[]{:S(2)}, u32[]{:S(2)}) collective-permute-start(bf16[4,16,768]{2,1,0:T(8,128)(2,1)S(1)} %get-tuple-element.47), channel_id=1, source_target_pairs={{0,8},{4,12},{8,0},{12,4},{1,9},{5,13},{9,1},{13,5},{2,10},{6,14},... | collective-permute-start | bytes 294920 | tf_op jit(solution)/shard_map/ppermute | solution.py:368
  45.4 8.4 %collective-permute-start.14 = (bf16[4,16,768]{2,1,0:T(8,128)(2,1)S(1)}, bf16[4,16,768]{2,1,0:T(8,128)(2,1)S(1)}, u32[]{:S(2)}, u32[]{:S(2)}) collective-permute-start(bf16[4,16,768]{2,1,0:T(8,128)(2,1)S(1)} %get-tuple-element.48), channel_id=1, source_target_pairs={{0,4},{4,8},{8,12},{12,0},{1,5},{5,9},{9,13},{13,1},{2,6},{6,10},{... | collective-permute-start | bytes 294920 | tf_op jit(solution)/shard_map/ppermute | solution.py:368
  47.0 7.6 %collective-permute-start.12 = (bf16[4,16,768]{2,1,0:T(8,128)(2,1)S(1)}, bf16[4,16,768]{2,1,0:T(8,128)(2,1)S(1)}, u32[]{:S(2)}, u32[]{:S(2)}) collective-permute-start(bf16[4,16,768]{2,1,0:T(8,128)(2,1)S(1)} %get-tuple-element.46.refs_14_), channel_id=1, source_target_pairs={{0,12},{4,0},{8,4},{12,8},{1,13},{5,1},{9,5},{13,9},{2,14},{6,2},{... | collective-permute-start | bytes 294920 | tf_op jit(solution)/shard_map/ppermute | solution.py:368

commit v7 on v5

--- a/solution.py
+++ b/solution.py
@@ -384,7 +384,7 @@
     blocks, tokens, width = query_rows.shape
     width_here = width // count_head
     heads = width_here // HD
-    cut = (heads + 1) // 2 * HD
+    cut = (2 * heads + 2) // 3 * HD
     parts = [(0, cut), (cut, width_here - cut)] if heads > 1 else [(0, width_here)]
     arrays = [query_rows, key_rows, value_rows]
     packed, after, limit = [], (), WIDE_VMEM

time: 54.7 us -> 59.6 us (1.090)
  waiting for transfers between devices: 10.9 us -> 16.4 us
  starting transfers between devices: 28.9 us -> 28 us
    ppermute x15, waiting for transfers between devices: 10.4 us -> 16.4 us  [shifted(): lax.ppermute(array, axis, [(i, (i + distance) % count) for i in range(cou...]
    ppermute x15, starting transfers between devices: 22.7 us -> 19.3 us  [shifted(): lax.ppermute(array, axis, [(i, (i + distance) % count) for i in range(cou...]
    all_to_all x1, starting transfers between devices: 6.23 us -> 8.74 us  [shards(): lax.all_to_all(query, 'head', split_axis=0, concat_axis=0, tiled=True)]
  transfers between devices with their start and end apart: 16 -> 16, of which waited for: 4 -> 6; matrix products, arithmetic and copies ran while one was open for 0% -> 0% of each run, Pallas kernels for 15% -> 14%
where the time goes in v7:
time: 59.6 us; the launch traced here: 59.4 us
  starting transfers between devices  28 us (47%)
  waiting for transfers between devices  16.4 us (28%)
  Pallas kernels  14.2 us (24%)
  local copies, waits for them, and re-layouts  0.66 us (1%)
    ppermute x15, starting transfers between devices, shifted(): lax.ppermute(array, axis, [(i, (i + distance) % count) for i in range(cou...  19.3 us
    ppermute x15, waiting for transfers between devices, shifted(): lax.ppermute(array, axis, [(i, (i + distance) % count) for i in range(cou...  16.4 us
    all_to_all x1, starting transfers between devices, shards(): lax.all_to_all(query, 'head', split_axis=0, concat_axis=0, tiled=True)  8.74 us
    pallas_call x3, Pallas kernels, rotate_pieces(): pl.pallas_call(functools.partial(rotate_kernel, message, sources, count_h...  5.99 us
    pallas_call x2, Pallas kernels, attend(): pl.pallas_call(functools.partial(attend_kernel, (count_head, count_tm), s...  3.98 us
    pallas_call x1, Pallas kernels, plan(): pl.pallas_call(functools.partial(plan_kernel, count_head, count_tm, block...  2.25 us
  transfers between devices with their start and end apart: 16, of which 6 were waited for; matrix products, arithmetic and copies ran while one was open for 0% of the time, Pallas kernels for 14%

profile of v7, /device:TPU:0, one launch (start us, length us, event | category | flops | bytes accessed | tf_op | source)
XLA Modules:
  0.0 59.4 jit_solution(6919841366834835134)
XLA Ops:
  0.0 0.0 copy-start
  0.0 0.0 copy-start.1
  0.0 3.0 %shard_map.55 = (bf16[4,16,1024]{2,1,0:T(8,128)(2,1)}, bf16[4,16,1024]{2,1,0:T(8,128)(2,1)}, bf16[4,16,1024]{2,1,0:T(8,128)(2,1)}, bf16[4,16,1024]{2,1,0:T(8,128)(2,1)}, f32[8,128]{1,0:T(8,128)}) custom-call(bf16[4,16,3072]{2,1,0:T(8,128)(2,1)} %refs_0_.4, bf16[4,16,3072]{2,1,0:T(8,128)(2,1)} %refs_1_.3), custom_call_target="tpu_custom_call" | custom-call | tf_op jit(solution)/shard_map/pallas_call | solution.py:101
  3.0 0.0 copy-start.7
  3.0 3.1 %collective-permute-start = (bf16[4,16,1024]{2,1,0:T(8,128)(2,1)}, bf16[4,16,1024]{2,1,0:T(8,128)(2,1)S(1)}, u32[]{:S(2)}, u32[]{:S(2)}) collective-permute-start(bf16[4,16,1024]{2,1,0:T(8,128)(2,1)} %get-tuple-element.32), channel_id=1, source_target_pairs={{0,4},{4,8},{8,12},{12,0},{1,5},{5,9},{9,13},{13,1},{2,6},{6,10},{... | collective-permute-start | bytes 393224 | tf_op jit(solution)/shard_map/ppermute | solution.py:368
  6.1 2.6 %collective-permute-start.1 = (bf16[4,16,1024]{2,1,0:T(8,128)(2,1)}, bf16[4,16,1024]{2,1,0:T(8,128)(2,1)S(1)}, u32[]{:S(2)}, u32[]{:S(2)}) collective-permute-start(bf16[4,16,1024]{2,1,0:T(8,128)(2,1)} %get-tuple-element.33), channel_id=1, source_target_pairs={{0,8},{4,12},{8,0},{12,4},{1,9},{5,13},{9,1},{13,5},{2,10},{6,14},... | collective-permute-start | bytes 393224 | tf_op jit(solution)/shard_map/ppermute | solution.py:368
  8.7 1.3 %collective-permute-start.2 = (bf16[4,16,1024]{2,1,0:T(8,128)(2,1)}, bf16[4,16,1024]{2,1,0:T(8,128)(2,1)S(1)}, u32[]{:S(2)}, u32[]{:S(2)}) collective-permute-start(bf16[4,16,1024]{2,1,0:T(8,128)(2,1)} %get-tuple-element.34), channel_id=1, source_target_pairs={{0,12},{4,0},{8,4},{12,8},{1,13},{5,1},{9,5},{13,9},{2,14},{6,2},{... | collective-permute-start | bytes 393224 | tf_op jit(solution)/shard_map/ppermute | solution.py:368
  10.0 0.0 copy-done
  10.0 0.0 copy-done.1
  10.0 0.0 copy-done.7
  10.0 0.0 copy-start.4
  10.0 0.0 copy-start.2
  10.0 1.4 %shard_map.56 = (bf16[4,16,512]{2,1,0:T(8,128)(2,1)S(1)}, bf16[4,16,512]{2,1,0:T(8,128)(2,1)S(1)}, bf16[4,16,512]{2,1,0:T(8,128)(2,1)S(1)}, bf16[4,16,512]{2,1,0:T(8,128)(2,1)S(1)}, f32[8,128]{1,0:T(8,128)S(1)}) custom-call(bf16[4,16,3072]{2,1,0:T(8,128)(2,1)S(1)} %copy-done, bf16[4,16,3072]{2,1,0:T(8,128)(2,1)S(1)} %copy-done.1, f32[8,128]{1,0:T(8,128)S(1)} %copy-done.7), custom_call_target="tpu_custom_call" | custom-call | tf_op jit(solution)/shard_map/pallas_call | solution.py:101
  11.4 0.7 %collective-permute-start.6 = (bf16[4,16,512]{2,1,0:T(8,128)(2,1)S(1)}, bf16[4,16,512]{2,1,0:T(8,128)(2,1)S(1)}, u32[]{:S(2)}, u32[]{:S(2)}) collective-permute-start(bf16[4,16,512]{2,1,0:T(8,128)(2,1)S(1)} %get-tuple-element.40), channel_id=1, source_target_pairs={{0,4},{4,8},{8,12},{12,0},{1,5},{5,9},{9,13},{13,1},{2,6},{6,10},{... | collective-permute-start | bytes 196616 | tf_op jit(solution)/shard_map/ppermute | solution.py:368
  12.2 0.0 copy-start.5
  12.2 0.3 collective-permute-start.7
  12.5 0.0 copy-done.4
  12.5 0.3 copy-done.5
  12.8 2.3 %shard_map.57 = (s32[8]{0:T(128)S(1)}, f32[4,576]{1,0:T(4,128)S(1)}) custom-call(s32[16,32]{1,0:T(8,128)S(1)} %copy-done.4, s32[16]{0:T(128)S(1)} %copy-done.5, f32[8,128]{1,0:T(8,128)S(1)} %get-tuple-element.28._), custom_call_target="tpu_custom_call" | custom-call | tf_op jit(solution)/shard_map/pallas_call | solution.py:237
  15.1 0.0 collective-permute-done.refs_1_
  15.1 3.2 %collective-permute-start.8 = (bf16[4,16,512]{2,1,0:T(8,128)(2,1)S(1)}, bf16[4,16,512]{2,1,0:T(8,128)(2,1)S(1)}, u32[]{:S(2)}, u32[]{:S(2)}) collective-permute-start(bf16[4,16,512]{2,1,0:T(8,128)(2,1)S(1)} %get-tuple-element.42), channel_id=1, source_target_pairs={{0,12},{4,0},{8,4},{12,8},{1,13},{5,1},{9,5},{13,9},{2,14},{6,2},{... | collective-permute-start | bytes 196616 | tf_op jit(solution)/shard_map/ppermute | solution.py:368
  18.3 0.1 collective-permute-done.1.refs_2_
  18.4 0.0 collective-permute-done.2.refs_3_
  18.4 0.0 copy-done.2
  18.4 0.0 copy-start.3
  18.4 0.6 %shard_map.58 = (bf16[2,4,16,1024]{3,2,1,0:T(8,128)(2,1)S(1)}, bf16[1,4,16,1024]{3,2,1,0:T(8,128)(2,1)S(1)}, bf16[2,4,16,1024]{3,2,1,0:T(8,128)(2,1)S(1)}) custom-call(s32[8]{0:T(128)S(1)} %get-tuple-element.30.picks_ref, bf16[4,16,1024]{2,1,0:T(8,128)(2,1)S(1)} %copy-done.2, bf16[4,16,1024]{2,1,0:T(8,128)(2,1)S(1)} %collective-permute-done.refs_1_, ...), custom_call_target="tpu_custom_call" | custom-call | flops 99999997952 | tf_op jit(solution)/shard_map/pallas_call | solution.py:136
  19.0 0.1 collective-permute-start.3
  19.0 0.3 copy-done.3
  19.4 1.6 %shard_map.59 = (bf16[4,4,16,768]{3,2,1,0:T(8,128)(2,1)}, f32[8,128]{1,0:T(8,128)}) custom-call(bf16[4,16,3072]{2,1,0:T(8,128)(2,1)S(1)} %copy-done.3, bf16[2,4,16,1024]{3,2,1,0:T(8,128)(2,1)S(1)} %get-tuple-element.35.refs_1_.refs_4_), custom_call_target="tpu_custom_call" | custom-call | tf_op jit(solution)/shard_map/pallas_call | solution.py:101
  21.0 8.7 %all-to-all-start = ((bf16[4,4,16,768]{3,2,1,0:T(8,128)(2,1)}), bf16[4,4,16,768]{3,2,1,0:T(8,128)(2,1)S(1)}, u32[]{:S(2)}, u32[]{:S(2)}) async-start(bf16[4,4,16,768]{3,2,1,0:T(8,128)(2,1)} %get-tuple-element.36), calls=%async_computation | async-start | bytes 786432 | tf_op jit(solution)/shard_map/all_to_all | solution.py:404
  29.7 1.1 %collective-permute-start.5 = (bf16[2,4,16,1024]{3,2,1,0:T(8,128)(2,1)S(1)}, bf16[2,4,16,1024]{3,2,1,0:T(8,128)(2,1)S(1)}, u32[]{:S(2)}, u32[]{:S(2)}) collective-permute-start(bf16[2,4,16,1024]{3,2,1,0:T(8,128)(2,1)S(1)} %get-tuple-element.38), channel_id=1, source_target_pairs={{0,3},{1,0},{2,1},{3,2},{4,7},{5,4},{6,5},{7,6},{8,11},{9,8},{10,9... | collective-permute-start | bytes 786440 | tf_op jit(solution)/shard_map/ppermute | solution.py:368
  30.9 0.0 collective-permute-done.6.refs_1_.refs_8_
  30.9 0.0 collective-permute-done.7.refs_2_.refs_9_
  30.9 0.0 collective-permute-done.8.refs_3_.refs_10_
  30.9 0.6 shard_map.60
  31.5 1.6 %collective-permute-start.10 = (bf16[1,4,16,512]{3,2,1,0:T(8,128)(2,1)S(1)}, bf16[1,4,16,512]{3,2,1,0:T(8,128)(2,1)S(1)}, u32[]{:S(2)}, u32[]{:S(2)}) collective-permute-start(bf16[1,4,16,512]{3,2,1,0:T(8,128)(2,1)S(1)} %get-tuple-element.44), channel_id=1, source_target_pairs={{0,2},{1,3},{2,0},{3,1},{4,6},{5,7},{6,4},{7,5},{8,10},{9,11},{10,... | collective-permute-start | bytes 196616 | tf_op jit(solution)/shard_map/ppermute | solution.py:368
  33.0 0.5 collective-permute-start.4
  33.6 0.0 collective-permute-start.9
  33.6 7.2 %collective-permute-done.10.refs_12_ = bf16[1,4,16,512]{3,2,1,0:T(8,128)(2,1)S(1)} collective-permute-done((bf16[1,4,16,512]{3,2,1,0:T(8,128)(2,1)S(1)}, bf16[1,4,16,512]{3,2,1,0:T(8,128)(2,1)S(1)}, u32[]{:S(2)}, u32[]{:S(2)}) %collective-permute-start.10) | collective-permute-done | bytes 65568 | tf_op jit(solution)/shard_map/ppermute | solution.py:368
  40.8 0.0 copy-start.6
  40.8 0.0 collective-permute-start.11
  40.8 1.5 %collective-permute-done.4.refs_5_ = bf16[1,4,16,1024]{3,2,1,0:T(8,128)(2,1)S(1)} collective-permute-done((bf16[1,4,16,1024]{3,2,1,0:T(8,128)(2,1)S(1)}, bf16[1,4,16,1024]{3,2,1,0:T(8,128)(2,1)S(1)}, u32[]{:S(2)}, u32[]{:S(2)}) %collective-permute-start.4) | collective-permute-done | bytes 131104 | tf_op jit(solution)/shard_map/ppermute | solution.py:368
  42.3 0.0 collective-permute-done.9.refs_11_
  42.3 1.0 %collective-permute-done.11.refs_13_ = bf16[2,4,16,512]{3,2,1,0:T(8,128)(2,1)S(1)} collective-permute-done((bf16[2,4,16,512]{3,2,1,0:T(8,128)(2,1)S(1)}, bf16[2,4,16,512]{3,2,1,0:T(8,128)(2,1)S(1)}, u32[]{:S(2)}, u32[]{:S(2)}) %collective-permute-start.11) | collective-permute-done | bytes 131104 | tf_op jit(solution)/shard_map/ppermute | solution.py:368
  43.4 0.0 collective-permute-done.3.refs_4_
  43.4 0.0 collective-permute-done.5.refs_6_
  43.4 0.0 all-to-all-done.query_ref
  43.4 0.0 copy-done.6
  43.4 2.2 %shard_map.61 = (bf16[4,16,768]{2,1,0:T(8,128)(2,1)S(1)}, bf16[4,16,768]{2,1,0:T(8,128)(2,1)S(1)}, bf16[4,16,768]{2,1,0:T(8,128)(2,1)S(1)}) custom-call(s32[16]{0:T(128)S(1)} %copy-done.6, f32[4,576]{1,0:T(4,128)S(1)} %get-tuple-element.29.bias_ref, bf16[4,4,16,768]{3,2,1,0:T(8,128)(2,1)S(1)} %all-to-all-done.query_ref, bf16[4,16,1024]{2,1,0:T(8,128)(2,1)S(1)} %copy-done.2, ...), custom_call_target="tpu_custom_call" | custom-call | tf_op jit(solution)/shard_map/pallas_call | solution.py:326
  45.6 3.6 %collective-permute-start.12 = (bf16[4,16,768]{2,1,0:T(8,128)(2,1)S(1)}, bf16[4,16,768]{2,1,0:T(8,128)(2,1)S(1)}, u32[]{:S(2)}, u32[]{:S(2)}) collective-permute-start(bf16[4,16,768]{2,1,0:T(8,128)(2,1)S(1)} %get-tuple-element.46.refs_14_), channel_id=1, source_target_pairs={{0,12},{4,0},{8,4},{12,8},{1,13},{5,1},{9,5},{13,9},{2,14},{6,2},{... | collective-permute-start | bytes 294920 | tf_op jit(solution)/shard_map/ppermute | solution.py:368
  49.2 0.0 collective-permute-start.13
  49.2 1.1 %collective-permute-start.14 = (bf16[4,16,768]{2,1,0:T(8,128)(2,1)S(1)}, bf16[4,16,768]{2,1,0:T(8,128)(2,1)S(1)}, u32[]{:S(2)}, u32[]{:S(2)}) collective-permute-start(bf16[4,16,768]{2,1,0:T(8,128)(2,1)S(1)} %get-tuple-element.48), channel_id=1, source_target_pairs={{0,4},{4,8},{8,12},{12,0},{1,5},{5,9},{9,13},{13,1},{2,6},{6,10},{... | collective-permute-start | bytes 294920 | tf_op jit(solution)/shard_map/ppermute | solution.py:368
  50.3 1.8 %shard_map.62.refs_0_ = bf16[4,16,768]{2,1,0:T(8,128)(2,1)S(1)} custom-call(s32[16]{0:T(128)S(1)} %copy-done.6, f32[4,576]{1,0:T(4,128)S(1)} %get-tuple-element.29.bias_ref, bf16[4,4,16,768]{3,2,1,0:T(8,128)(2,1)S(1)} %all-to-all-done.query_ref, bf16[4,16,1024]{2,1,0:T(8,128)(2,1)S(1)} %copy-done.2, bf16[4,16,1024]{2,1,0:T(8,128)(2,1)S(1)} %collective-permute-done.refs_1_, ...), custom_call_target="tpu_custom_call" | custom-call | tf_op jit(solution)/shard_map/pallas_call | solution.py:326
  52.1 0.3 collective-permute-done.12.refs_1_
  52.4 6.2 %collective-permute-done.13.refs_2_ = bf16[4,16,768]{2,1,0:T(8,128)(2,1)S(1)} collective-permute-done((bf16[4,16,768]{2,1,0:T(8,128)(2,1)S(1)}, bf16[4,16,768]{2,1,0:T(8,128)(2,1)S(1)}, u32[]{:S(2)}, u32[]{:S(2)}) %collective-permute-start.13) | collective-permute-done | bytes 98336 | tf_op jit(solution)/shard_map/ppermute | solution.py:368
  58.6 0.0 collective-permute-done.14.refs_3_
  58.6 0.8 %shard_map.63 = bf16[4,16,3072]{2,1,0:T(8,128)(2,1)} custom-call(bf16[4,16,768]{2,1,0:T(8,128)(2,1)S(1)} %shard_map.62.refs_0_, bf16[4,16,768]{2,1,0:T(8,128)(2,1)S(1)} %collective-permute-done.12.refs_1_, bf16[4,16,768]{2,1,0:T(8,128)(2,1)S(1)} %collective-permute-done.13.refs_2_, bf16[4,16,768]{2,1,0:T(8,128)(2,1)S(1)} %collective-permute-done.14.refs_3_), custom_call_target="tpu_custom_call" | custom-call | tf_op jit(solution)/shard_map/pallas_call | solution.py:356
Async XLA Ops:
  0.0 10.0 %copy-start = (bf16[4,16,3072]{2,1,0:T(8,128)(2,1)S(1)}, bf16[4,16,3072]{2,1,0:T(8,128)(2,1)}, u32[]{:S(2)}) copy-start(bf16[4,16,3072]{2,1,0:T(8,128)(2,1)} %refs_0_.4) | copy-start | bytes 1179652
  0.0 10.0 %copy-start.1 = (bf16[4,16,3072]{2,1,0:T(8,128)(2,1)S(1)}, bf16[4,16,3072]{2,1,0:T(8,128)(2,1)}, u32[]{:S(2)}) copy-start(bf16[4,16,3072]{2,1,0:T(8,128)(2,1)} %refs_1_.3) | copy-start | bytes 1179652
  3.0 7.0 %copy-start.7 = (f32[8,128]{1,0:T(8,128)S(1)}, f32[8,128]{1,0:T(8,128)}, u32[]{:S(2)}) copy-start(f32[8,128]{1,0:T(8,128)} %get-tuple-element.27.refs_2_) | copy-start | bytes 12292
  3.0 12.1 %collective-permute-start = (bf16[4,16,1024]{2,1,0:T(8,128)(2,1)}, bf16[4,16,1024]{2,1,0:T(8,128)(2,1)S(1)}, u32[]{:S(2)}, u32[]{:S(2)}) collective-permute-start(bf16[4,16,1024]{2,1,0:T(8,128)(2,1)} %get-tuple-element.32), channel_id=1, source_target_pairs={{0,4},{4,8},{8,12},{12,0},{1,5},{5,9},{9,13},{13,1},{2,6},{6,10},{... | collective-permute-start | bytes 393224 | tf_op jit(solution)/shard_map/ppermute | solution.py:368
  6.1 12.3 %collective-permute-start.1 = (bf16[4,16,1024]{2,1,0:T(8,128)(2,1)}, bf16[4,16,1024]{2,1,0:T(8,128)(2,1)S(1)}, u32[]{:S(2)}, u32[]{:S(2)}) collective-permute-start(bf16[4,16,1024]{2,1,0:T(8,128)(2,1)} %get-tuple-element.33), channel_id=1, source_target_pairs={{0,8},{4,12},{8,0},{12,4},{1,9},{5,13},{9,1},{13,5},{2,10},{6,14},... | collective-permute-start | bytes 393224 | tf_op jit(solution)/shard_map/ppermute | solution.py:368
  8.7 9.7 %collective-permute-start.2 = (bf16[4,16,1024]{2,1,0:T(8,128)(2,1)}, bf16[4,16,1024]{2,1,0:T(8,128)(2,1)S(1)}, u32[]{:S(2)}, u32[]{:S(2)}) collective-permute-start(bf16[4,16,1024]{2,1,0:T(8,128)(2,1)} %get-tuple-element.34), channel_id=1, source_target_pairs={{0,12},{4,0},{8,4},{12,8},{1,13},{5,1},{9,5},{13,9},{2,14},{6,2},{... | collective-permute-start | bytes 393224 | tf_op jit(solution)/shard_map/ppermute | solution.py:368
  10.0 2.5 %copy-start.4 = (s32[16,32]{1,0:T(8,128)S(1)}, s32[16,32]{1,0:T(8,128)}, u32[]{:S(2)}) copy-start(s32[16,32]{1,0:T(8,128)} %pair_ref.1) | copy-start | bytes 6148
  10.0 8.3 %copy-start.2 = (bf16[4,16,1024]{2,1,0:T(8,128)(2,1)S(1)}, bf16[4,16,1024]{2,1,0:T(8,128)(2,1)}, u32[]{:S(2)}) copy-start(bf16[4,16,1024]{2,1,0:T(8,128)(2,1)} %get-tuple-element.31.refs_0_) | copy-start | bytes 393220
  11.4 19.5 %collective-permute-start.6 = (bf16[4,16,512]{2,1,0:T(8,128)(2,1)S(1)}, bf16[4,16,512]{2,1,0:T(8,128)(2,1)S(1)}, u32[]{:S(2)}, u32[]{:S(2)}) collective-permute-start(bf16[4,16,512]{2,1,0:T(8,128)(2,1)S(1)} %get-tuple-element.40), channel_id=1, source_target_pairs={{0,4},{4,8},{8,12},{12,0},{1,5},{5,9},{9,13},{13,1},{2,6},{6,10},{... | collective-permute-start | bytes 196616 | tf_op jit(solution)/shard_map/ppermute | solution.py:368
  12.2 0.7 %copy-start.5 = (s32[16]{0:T(128)S(1)}, s32[16]{0:T(128)}, u32[]{:S(2)}) copy-start(s32[16]{0:T(128)} %tokens_ref.5) | copy-start | bytes 196
  12.2 18.7 %collective-permute-start.7 = (bf16[4,16,512]{2,1,0:T(8,128)(2,1)S(1)}, bf16[4,16,512]{2,1,0:T(8,128)(2,1)S(1)}, u32[]{:S(2)}, u32[]{:S(2)}) collective-permute-start(bf16[4,16,512]{2,1,0:T(8,128)(2,1)S(1)} %get-tuple-element.41), channel_id=1, source_target_pairs={{0,8},{4,12},{8,0},{12,4},{1,9},{5,13},{9,1},{13,5},{2,10},{6,14},... | collective-permute-start | bytes 196616 | tf_op jit(solution)/shard_map/ppermute | solution.py:368
  15.1 15.8 %collective-permute-start.8 = (bf16[4,16,512]{2,1,0:T(8,128)(2,1)S(1)}, bf16[4,16,512]{2,1,0:T(8,128)(2,1)S(1)}, u32[]{:S(2)}, u32[]{:S(2)}) collective-permute-start(bf16[4,16,512]{2,1,0:T(8,128)(2,1)S(1)} %get-tuple-element.42), channel_id=1, source_target_pairs={{0,12},{4,0},{8,4},{12,8},{1,13},{5,1},{9,5},{13,9},{2,14},{6,2},{... | collective-permute-start | bytes 196616 | tf_op jit(solution)/shard_map/ppermute | solution.py:368
  18.4 1.0 %copy-start.3 = (bf16[4,16,3072]{2,1,0:T(8,128)(2,1)S(1)}, bf16[4,16,3072]{2,1,0:T(8,128)(2,1)}, u32[]{:S(2)}) copy-start(bf16[4,16,3072]{2,1,0:T(8,128)(2,1)} %refs_0_.5) | copy-start | bytes 1179652
  19.0 24.4 %collective-permute-start.3 = (bf16[2,4,16,1024]{3,2,1,0:T(8,128)(2,1)S(1)}, bf16[2,4,16,1024]{3,2,1,0:T(8,128)(2,1)S(1)}, u32[]{:S(2)}, u32[]{:S(2)}) collective-permute-start(bf16[2,4,16,1024]{3,2,1,0:T(8,128)(2,1)S(1)} %get-tuple-element.35.refs_1_.refs_4_), channel_id=1, source_target_pairs={{0,1},{1,2},{2,3},{3,0},{4,5},{5,6},{6,7},{7,4},{8,9},{9,10},{10,1... | collective-permute-start | bytes 786440 | tf_op jit(solution)/shard_map/ppermute | solution.py:368
  21.0 22.4 %all-to-all-start = ((bf16[4,4,16,768]{3,2,1,0:T(8,128)(2,1)}), bf16[4,4,16,768]{3,2,1,0:T(8,128)(2,1)S(1)}, u32[]{:S(2)}, u32[]{:S(2)}) async-start(bf16[4,4,16,768]{3,2,1,0:T(8,128)(2,1)} %get-tuple-element.36), calls=%async_computation | async-start | bytes 786432 | tf_op jit(solution)/shard_map/all_to_all | solution.py:404
  29.7 13.6 %collective-permute-start.5 = (bf16[2,4,16,1024]{3,2,1,0:T(8,128)(2,1)S(1)}, bf16[2,4,16,1024]{3,2,1,0:T(8,128)(2,1)S(1)}, u32[]{:S(2)}, u32[]{:S(2)}) collective-permute-start(bf16[2,4,16,1024]{3,2,1,0:T(8,128)(2,1)S(1)} %get-tuple-element.38), channel_id=1, source_target_pairs={{0,3},{1,0},{2,1},{3,2},{4,7},{5,4},{6,5},{7,6},{8,11},{9,8},{10,9... | collective-permute-start | bytes 786440 | tf_op jit(solution)/shard_map/ppermute | solution.py:368
  31.5 9.3 %collective-permute-start.10 = (bf16[1,4,16,512]{3,2,1,0:T(8,128)(2,1)S(1)}, bf16[1,4,16,512]{3,2,1,0:T(8,128)(2,1)S(1)}, u32[]{:S(2)}, u32[]{:S(2)}) collective-permute-start(bf16[1,4,16,512]{3,2,1,0:T(8,128)(2,1)S(1)} %get-tuple-element.44), channel_id=1, source_target_pairs={{0,2},{1,3},{2,0},{3,1},{4,6},{5,7},{6,4},{7,5},{8,10},{9,11},{10,... | collective-permute-start | bytes 196616 | tf_op jit(solution)/shard_map/ppermute | solution.py:368
  33.0 9.3 %collective-permute-start.4 = (bf16[1,4,16,1024]{3,2,1,0:T(8,128)(2,1)S(1)}, bf16[1,4,16,1024]{3,2,1,0:T(8,128)(2,1)S(1)}, u32[]{:S(2)}, u32[]{:S(2)}) collective-permute-start(bf16[1,4,16,1024]{3,2,1,0:T(8,128)(2,1)S(1)} %get-tuple-element.37), channel_id=1, source_target_pairs={{0,2},{1,3},{2,0},{3,1},{4,6},{5,7},{6,4},{7,5},{8,10},{9,11},{10,... | collective-permute-start | bytes 393224 | tf_op jit(solution)/shard_map/ppermute | solution.py:368
  33.6 8.8 %collective-permute-start.9 = (bf16[2,4,16,512]{3,2,1,0:T(8,128)(2,1)S(1)}, bf16[2,4,16,512]{3,2,1,0:T(8,128)(2,1)S(1)}, u32[]{:S(2)}, u32[]{:S(2)}) collective-permute-start(bf16[2,4,16,512]{3,2,1,0:T(8,128)(2,1)S(1)} %get-tuple-element.43), channel_id=1, source_target_pairs={{0,1},{1,2},{2,3},{3,0},{4,5},{5,6},{6,7},{7,4},{8,9},{9,10},{10,1... | collective-permute-start | bytes 393224 | tf_op jit(solution)/shard_map/ppermute | solution.py:368
  40.8 2.5 %copy-start.6 = (s32[16]{0:T(128)S(1)}, s32[16]{0:T(128)}, u32[]{:S(2)}) copy-start(s32[16]{0:T(128)} %tokens_ref.5) | copy-start | bytes 196
  40.8 2.5 %collective-permute-start.11 = (bf16[2,4,16,512]{3,2,1,0:T(8,128)(2,1)S(1)}, bf16[2,4,16,512]{3,2,1,0:T(8,128)(2,1)S(1)}, u32[]{:S(2)}, u32[]{:S(2)}) collective-permute-start(bf16[2,4,16,512]{3,2,1,0:T(8,128)(2,1)S(1)} %get-tuple-element.45), channel_id=1, source_target_pairs={{0,3},{1,0},{2,1},{3,2},{4,7},{5,4},{6,5},{7,6},{8,11},{9,8},{10,9... | collective-permute-start | bytes 393224 | tf_op jit(solution)/shard_map/ppermute | solution.py:368
  45.6 6.8 %collective-permute-start.12 = (bf16[4,16,768]{2,1,0:T(8,128)(2,1)S(1)}, bf16[4,16,768]{2,1,0:T(8,128)(2,1)S(1)}, u32[]{:S(2)}, u32[]{:S(2)}) collective-permute-start(bf16[4,16,768]{2,1,0:T(8,128)(2,1)S(1)} %get-tuple-element.46.refs_14_), channel_id=1, source_target_pairs={{0,12},{4,0},{8,4},{12,8},{1,13},{5,1},{9,5},{13,9},{2,14},{6,2},{... | collective-permute-start | bytes 294920 | tf_op jit(solution)/shard_map/ppermute | solution.py:368
  49.2 9.4 %collective-permute-start.13 = (bf16[4,16,768]{2,1,0:T(8,128)(2,1)S(1)}, bf16[4,16,768]{2,1,0:T(8,128)(2,1)S(1)}, u32[]{:S(2)}, u32[]{:S(2)}) collective-permute-start(bf16[4,16,768]{2,1,0:T(8,128)(2,1)S(1)} %get-tuple-element.47), channel_id=1, source_target_pairs={{0,8},{4,12},{8,0},{12,4},{1,9},{5,13},{9,1},{13,5},{2,10},{6,14},... | collective-permute-start | bytes 294920 | tf_op jit(solution)/shard_map/ppermute | solution.py:368
  49.2 9.4 %collective-permute-start.14 = (bf16[4,16,768]{2,1,0:T(8,128)(2,1)S(1)}, bf16[4,16,768]{2,1,0:T(8,128)(2,1)S(1)}, u32[]{:S(2)}, u32[]{:S(2)}) collective-permute-start(bf16[4,16,768]{2,1,0:T(8,128)(2,1)S(1)} %get-tuple-element.48), channel_id=1, source_target_pairs={{0,4},{4,8},{8,12},{12,0},{1,5},{5,9},{9,13},{13,1},{2,6},{6,10},{... | collective-permute-start | bytes 294920 | tf_op jit(solution)/shard_map/ppermute | solution.py:368

commit v8 on v5

--- a/solution.py
+++ b/solution.py
@@ -387,15 +387,17 @@
     cut = (heads + 1) // 2 * HD
     parts = [(0, cut), (cut, width_here - cut)] if heads > 1 else [(0, width_here)]
     arrays = [query_rows, key_rows, value_rows]
-    packed, after, limit = [], (), WIDE_VMEM
-    for part in parts:
-        message = [(1,) + part, (2,) + part]
-        pieces, token = rotate_pieces(arrays, message, count_head, after, limit)
+    messages = [[(1,) + part, (2,) + part] for part in parts]
+    pieces, token = rotate_pieces(arrays, messages[0], count_head, limit=WIDE_VMEM)
+    packed = [pieces]
+    picks, bias = plan(pair_list, block_tokens, token, blocks, count_head, count_tm)
+    after = (bias,)
+    for message in messages[1:]:
+        pieces, token = rotate_pieces(arrays, message, count_head, after)
         packed.append(pieces)
-        after, limit = (token,), VMEM
+        after = (token,)
     received = [exchange(pieces, 1) for pieces in packed]
-    picks, bias = plan(pair_list, block_tokens, token, blocks, count_head, count_tm)
-    sent, after = [], ()
+    sent, after = [], (received[-1][1],)
     for owns, (_, size) in zip(received, parts):
         sent.append(pick_blocks(picks, owns, (0, 2 * size), count_tm, after))
         after = (sent[-1][0],)

time: 54.7 us -> 55.9 us (1.022)
  waiting for transfers between devices: 10.9 us -> 16 us
  starting transfers between devices: 28.9 us -> 24.2 us
    ppermute x15, waiting for transfers between devices: 10.4 us -> 14 us  [shifted(): lax.ppermute(array, axis, [(i, (i + distance) % count) for i in range(cou...]
    ppermute x15, starting transfers between devices: 22.7 us -> 20.1 us  [shifted(): lax.ppermute(array, axis, [(i, (i + distance) % count) for i in range(cou...]
    all_to_all x1, starting transfers between devices: 6.23 us -> 4.08 us  [shards(): lax.all_to_all(query, 'head', split_axis=0, concat_axis=0, tiled=True)]
    all_to_all x1, waiting for transfers between devices: 0.5 us -> 1.99 us  [shards(): lax.all_to_all(query, 'head', split_axis=0, concat_axis=0, tiled=True)]
  transfers between devices with their start and end apart: 16 -> 16, of which waited for: 4 -> 5; matrix products, arithmetic and copies ran while one was open for 0% -> 0% of each run, Pallas kernels for 15% -> 16%
where the time goes in v8:
time: 55.9 us; the launch traced here: 55.6 us
  starting transfers between devices  24.2 us (43%)
  waiting for transfers between devices  16 us (29%)
  Pallas kernels  14.6 us (26%)
  local copies, waits for them, and re-layouts  0.74 us (1%)
    ppermute x15, starting transfers between devices, shifted(): lax.ppermute(array, axis, [(i, (i + distance) % count) for i in range(cou...  20.1 us
    ppermute x15, waiting for transfers between devices, shifted(): lax.ppermute(array, axis, [(i, (i + distance) % count) for i in range(cou...  14 us
    pallas_call x3, Pallas kernels, rotate_pieces(): pl.pallas_call(functools.partial(rotate_kernel, message, sources, count_h...  6.41 us
    all_to_all x1, starting transfers between devices, shards(): lax.all_to_all(query, 'head', split_axis=0, concat_axis=0, tiled=True)  4.08 us
    pallas_call x2, Pallas kernels, attend(): pl.pallas_call(functools.partial(attend_kernel, (count_head, count_tm), s...  3.96 us
    pallas_call x1, Pallas kernels, plan(): pl.pallas_call(functools.partial(plan_kernel, count_head, count_tm, block...  2.25 us
    all_to_all x1, waiting for transfers between devices, shards(): lax.all_to_all(query, 'head', split_axis=0, concat_axis=0, tiled=True)  1.99 us
    pallas_call x2, Pallas kernels, pick_blocks(): pl.pallas_call(functools.partial(pick_kernel, count_head, count_tm, lanes...  1.18 us
  transfers between devices with their start and end apart: 16, of which 5 were waited for; matrix products, arithmetic and copies ran while one was open for 0% of the time, Pallas kernels for 16%

profile of v8, /device:TPU:0, one launch (start us, length us, event | category | flops | bytes accessed | tf_op | source)
XLA Modules:
  0.0 55.6 jit_solution(12888588504892178912)
XLA Ops:
  0.0 0.0 copy-start.1
  0.0 0.0 copy-start
  0.0 2.9 %shard_map.55 = (bf16[4,16,768]{2,1,0:T(8,128)(2,1)}, bf16[4,16,768]{2,1,0:T(8,128)(2,1)}, bf16[4,16,768]{2,1,0:T(8,128)(2,1)}, bf16[4,16,768]{2,1,0:T(8,128)(2,1)}, f32[8,128]{1,0:T(8,128)}) custom-call(bf16[4,16,3072]{2,1,0:T(8,128)(2,1)} %refs_0_.4, bf16[4,16,3072]{2,1,0:T(8,128)(2,1)} %refs_1_.3), custom_call_target="tpu_custom_call" | custom-call | tf_op jit(solution)/shard_map/pallas_call | solution.py:101
  2.9 0.0 copy-start.9
  2.9 3.1 %collective-permute-start = (bf16[4,16,768]{2,1,0:T(8,128)(2,1)}, bf16[4,16,768]{2,1,0:T(8,128)(2,1)S(1)}, u32[]{:S(2)}, u32[]{:S(2)}) collective-permute-start(bf16[4,16,768]{2,1,0:T(8,128)(2,1)} %get-tuple-element.30), channel_id=1, source_target_pairs={{0,4},{4,8},{8,12},{12,0},{1,5},{5,9},{9,13},{13,1},{2,6},{6,10},{... | collective-permute-start | bytes 294920 | tf_op jit(solution)/shard_map/ppermute | solution.py:368
  6.0 2.6 %collective-permute-start.1 = (bf16[4,16,768]{2,1,0:T(8,128)(2,1)}, bf16[4,16,768]{2,1,0:T(8,128)(2,1)S(1)}, u32[]{:S(2)}, u32[]{:S(2)}) collective-permute-start(bf16[4,16,768]{2,1,0:T(8,128)(2,1)} %get-tuple-element.31), channel_id=1, source_target_pairs={{0,8},{4,12},{8,0},{12,4},{1,9},{5,13},{9,1},{13,5},{2,10},{6,14},... | collective-permute-start | bytes 294920 | tf_op jit(solution)/shard_map/ppermute | solution.py:368
  8.5 0.0 copy-start.7
  8.6 1.3 %collective-permute-start.2 = (bf16[4,16,768]{2,1,0:T(8,128)(2,1)}, bf16[4,16,768]{2,1,0:T(8,128)(2,1)S(1)}, u32[]{:S(2)}, u32[]{:S(2)}) collective-permute-start(bf16[4,16,768]{2,1,0:T(8,128)(2,1)} %get-tuple-element.32), channel_id=1, source_target_pairs={{0,12},{4,0},{8,4},{12,8},{1,13},{5,1},{9,5},{13,9},{2,14},{6,2},{... | collective-permute-start | bytes 294920 | tf_op jit(solution)/shard_map/ppermute | solution.py:368
  9.9 0.0 copy-done.9
  9.9 0.0 copy-done.7
  9.9 0.0 copy-start.6
  9.9 0.7 %copy-done.6 = s32[16,32]{1,0:T(8,128)S(1)} copy-done((s32[16,32]{1,0:T(8,128)S(1)}, s32[16,32]{1,0:T(8,128)}, u32[]{:S(2)}) %copy-start.6) | copy-done | bytes 2072
  10.6 2.3 %shard_map.56 = (s32[8]{0:T(128)S(1)}, f32[4,576]{1,0:T(4,128)S(1)}) custom-call(s32[16,32]{1,0:T(8,128)S(1)} %copy-done.6, s32[16]{0:T(128)S(1)} %copy-done.7, f32[8,128]{1,0:T(8,128)S(1)} %copy-done.9), custom_call_target="tpu_custom_call" | custom-call | tf_op jit(solution)/shard_map/pallas_call | solution.py:237
  12.9 0.0 copy-start.4
  12.9 0.0 copy-done.1
  12.9 0.0 copy-done
  12.9 0.0 copy-start.2
  12.9 1.9 %shard_map.57 = (bf16[4,16,768]{2,1,0:T(8,128)(2,1)S(1)}, bf16[4,16,768]{2,1,0:T(8,128)(2,1)S(1)}, bf16[4,16,768]{2,1,0:T(8,128)(2,1)S(1)}, bf16[4,16,768]{2,1,0:T(8,128)(2,1)S(1)}, f32[8,128]{1,0:T(8,128)}) custom-call(bf16[4,16,3072]{2,1,0:T(8,128)(2,1)S(1)} %copy-done, bf16[4,16,3072]{2,1,0:T(8,128)(2,1)S(1)} %copy-done.1, ...), custom_call_target="tpu_custom_call" | custom-call | tf_op jit(solution)/shard_map/pallas_call | solution.py:101
  14.8 0.0 copy-done.4
  14.8 0.7 %collective-permute-start.3 = (bf16[4,16,768]{2,1,0:T(8,128)(2,1)S(1)}, bf16[4,16,768]{2,1,0:T(8,128)(2,1)S(1)}, u32[]{:S(2)}, u32[]{:S(2)}) collective-permute-start(bf16[4,16,768]{2,1,0:T(8,128)(2,1)S(1)} %get-tuple-element.33), channel_id=1, source_target_pairs={{0,4},{4,8},{8,12},{12,0},{1,5},{5,9},{9,13},{13,1},{2,6},{6,10},{... | collective-permute-start | bytes 294920 | tf_op jit(solution)/shard_map/ppermute | solution.py:368
  15.6 0.5 collective-permute-start.7
  16.1 0.0 collective-permute-done.refs_1_
  16.1 2.6 %collective-permute-start.8 = (bf16[4,16,768]{2,1,0:T(8,128)(2,1)S(1)}, bf16[4,16,768]{2,1,0:T(8,128)(2,1)S(1)}, u32[]{:S(2)}, u32[]{:S(2)}) collective-permute-start(bf16[4,16,768]{2,1,0:T(8,128)(2,1)S(1)} %get-tuple-element.40), channel_id=1, source_target_pairs={{0,12},{4,0},{8,4},{12,8},{1,13},{5,1},{9,5},{13,9},{2,14},{6,2},{... | collective-permute-start | bytes 294920 | tf_op jit(solution)/shard_map/ppermute | solution.py:368
  18.7 0.0 collective-permute-done.1.refs_2_
  18.7 0.0 collective-permute-done.2.refs_3_
  18.7 3.8 %collective-permute-done.3.refs_4_.refs_1_.refs_8_ = bf16[4,16,768]{2,1,0:T(8,128)(2,1)S(1)} collective-permute-done((bf16[4,16,768]{2,1,0:T(8,128)(2,1)S(1)}, bf16[4,16,768]{2,1,0:T(8,128)(2,1)S(1)}, u32[]{:S(2)}, u32[]{:S(2)}) %collective-permute-start.3) | collective-permute-done | bytes 98336 | tf_op jit(solution)/shard_map/ppermute | solution.py:368
  22.5 0.0 copy-done.2
  22.5 0.0 copy-start.3
  22.5 0.6 %shard_map.58 = (bf16[2,4,16,768]{3,2,1,0:T(8,128)(2,1)S(1)}, bf16[1,4,16,768]{3,2,1,0:T(8,128)(2,1)S(1)}, bf16[2,4,16,768]{3,2,1,0:T(8,128)(2,1)S(1)}) custom-call(s32[8]{0:T(128)S(1)} %get-tuple-element.28.picks_ref, bf16[4,16,768]{2,1,0:T(8,128)(2,1)S(1)} %copy-done.2, bf16[4,16,768]{2,1,0:T(8,128)(2,1)S(1)} %collective-permute-done.refs_1_, ...), custom_call_target="tpu_custom_call" | custom-call | flops 99999997952 | tf_op jit(solution)/shard_map/pallas_call | solution.py:136
  23.1 1.6 %collective-permute-start.5 = (bf16[1,4,16,768]{3,2,1,0:T(8,128)(2,1)S(1)}, bf16[1,4,16,768]{3,2,1,0:T(8,128)(2,1)S(1)}, u32[]{:S(2)}, u32[]{:S(2)}) collective-permute-start(bf16[1,4,16,768]{3,2,1,0:T(8,128)(2,1)S(1)} %get-tuple-element.36), channel_id=1, source_target_pairs={{0,2},{1,3},{2,0},{3,1},{4,6},{5,7},{6,4},{7,5},{8,10},{9,11},{10,... | collective-permute-start | bytes 294920 | tf_op jit(solution)/shard_map/ppermute | solution.py:368
  24.7 0.0 collective-permute-start.6
  24.7 0.5 collective-permute-start.4
  25.2 0.0 copy-done.3
  25.2 1.6 %shard_map.59 = (bf16[4,4,16,768]{3,2,1,0:T(8,128)(2,1)}, f32[8,128]{1,0:T(8,128)}) custom-call(bf16[4,16,3072]{2,1,0:T(8,128)(2,1)S(1)} %copy-done.3, bf16[2,4,16,768]{3,2,1,0:T(8,128)(2,1)S(1)} %get-tuple-element.34.refs_1_.refs_4_), custom_call_target="tpu_custom_call" | custom-call | tf_op jit(solution)/shard_map/pallas_call | solution.py:101
  26.8 4.1 %all-to-all-start = ((bf16[4,4,16,768]{3,2,1,0:T(8,128)(2,1)}), bf16[4,4,16,768]{3,2,1,0:T(8,128)(2,1)S(1)}, u32[]{:S(2)}, u32[]{:S(2)}) async-start(bf16[4,4,16,768]{3,2,1,0:T(8,128)(2,1)} %get-tuple-element.35), calls=%async_computation | async-start | bytes 786432 | tf_op jit(solution)/shard_map/all_to_all | solution.py:406
  30.9 0.0 collective-permute-done.7.refs_2_.refs_9_
  30.9 0.0 collective-permute-done.8.refs_3_.refs_10_
  30.9 0.0 copy-start.5
  30.9 0.6 %shard_map.60 = (bf16[2,4,16,768]{3,2,1,0:T(8,128)(2,1)S(1)}, bf16[1,4,16,768]{3,2,1,0:T(8,128)(2,1)S(1)}, bf16[2,4,16,768]{3,2,1,0:T(8,128)(2,1)S(1)}) custom-call(s32[8]{0:T(128)S(1)} %get-tuple-element.28.picks_ref, bf16[4,16,768]{2,1,0:T(8,128)(2,1)S(1)} %get-tuple-element.38.refs_0_.refs_7_, ...), custom_call_target="tpu_custom_call" | custom-call | flops 99999997952 | tf_op jit(solution)/shard_map/pallas_call | solution.py:136
  31.5 0.1 collective-permute-start.9
  31.6 0.0 copy-start.8
  31.6 1.7 %collective-permute-start.11 = (bf16[2,4,16,768]{3,2,1,0:T(8,128)(2,1)S(1)}, bf16[2,4,16,768]{3,2,1,0:T(8,128)(2,1)S(1)}, u32[]{:S(2)}, u32[]{:S(2)}) collective-permute-start(bf16[2,4,16,768]{3,2,1,0:T(8,128)(2,1)S(1)} %get-tuple-element.43), channel_id=1, source_target_pairs={{0,3},{1,0},{2,1},{3,2},{4,7},{5,4},{6,5},{7,6},{8,11},{9,8},{10,9... | collective-permute-start | bytes 589832 | tf_op jit(solution)/shard_map/ppermute | solution.py:368
  33.3 0.0 collective-permute-done.5.refs_5_
  33.3 0.5 collective-permute-start.10
  33.9 7.0 %collective-permute-done.10.refs_12_ = bf16[1,4,16,768]{3,2,1,0:T(8,128)(2,1)S(1)} collective-permute-done((bf16[1,4,16,768]{3,2,1,0:T(8,128)(2,1)S(1)}, bf16[1,4,16,768]{3,2,1,0:T(8,128)(2,1)S(1)}, u32[]{:S(2)}, u32[]{:S(2)}) %collective-permute-start.10) | collective-permute-done | bytes 98336 | tf_op jit(solution)/shard_map/ppermute | solution.py:368
  40.9 0.0 collective-permute-done.6.refs_6_
  40.9 0.0 collective-permute-done.4.refs_4_
  40.9 0.0 collective-permute-done.9.refs_11_
  40.9 0.0 collective-permute-done.11.refs_13_
  40.9 2.0 %all-to-all-done.query_ref = bf16[4,4,16,768]{3,2,1,0:T(8,128)(2,1)S(1)} async-done(((bf16[4,4,16,768]{3,2,1,0:T(8,128)(2,1)}), bf16[4,4,16,768]{3,2,1,0:T(8,128)(2,1)S(1)}, u32[]{:S(2)}, u32[]{:S(2)}) %all-to-all-start) | async-done | bytes 393248 | tf_op jit(solution)/shard_map/all_to_all | solution.py:406
  42.9 0.0 copy-done.5
  42.9 0.0 copy-done.8
  42.9 2.2 %shard_map.61 = (bf16[4,16,768]{2,1,0:T(8,128)(2,1)S(1)}, bf16[4,16,768]{2,1,0:T(8,128)(2,1)S(1)}, bf16[4,16,768]{2,1,0:T(8,128)(2,1)S(1)}) custom-call(s32[16]{0:T(128)S(1)} %copy-done.8, f32[4,576]{1,0:T(4,128)S(1)} %copy-done.5, bf16[4,4,16,768]{3,2,1,0:T(8,128)(2,1)S(1)} %all-to-all-done.query_ref, bf16[4,16,768]{2,1,0:T(8,128)(2,1)S(1)} %copy-done.2, ...), custom_call_target="tpu_custom_call" | custom-call | tf_op jit(solution)/shard_map/pallas_call | solution.py:326
  45.1 1.0 %collective-permute-start.13 = (bf16[4,16,768]{2,1,0:T(8,128)(2,1)S(1)}, bf16[4,16,768]{2,1,0:T(8,128)(2,1)S(1)}, u32[]{:S(2)}, u32[]{:S(2)}) collective-permute-start(bf16[4,16,768]{2,1,0:T(8,128)(2,1)S(1)} %get-tuple-element.45), channel_id=1, source_target_pairs={{0,8},{4,12},{8,0},{12,4},{1,9},{5,13},{9,1},{13,5},{2,10},{6,14},... | collective-permute-start | bytes 294920 | tf_op jit(solution)/shard_map/ppermute | solution.py:368
  46.2 1.5 %collective-permute-start.14 = (bf16[4,16,768]{2,1,0:T(8,128)(2,1)S(1)}, bf16[4,16,768]{2,1,0:T(8,128)(2,1)S(1)}, u32[]{:S(2)}, u32[]{:S(2)}) collective-permute-start(bf16[4,16,768]{2,1,0:T(8,128)(2,1)S(1)} %get-tuple-element.46), channel_id=1, source_target_pairs={{0,4},{4,8},{8,12},{12,0},{1,5},{5,9},{9,13},{13,1},{2,6},{6,10},{... | collective-permute-start | bytes 294920 | tf_op jit(solution)/shard_map/ppermute | solution.py:368
  47.6 2.4 %collective-permute-start.12 = (bf16[4,16,768]{2,1,0:T(8,128)(2,1)S(1)}, bf16[4,16,768]{2,1,0:T(8,128)(2,1)S(1)}, u32[]{:S(2)}, u32[]{:S(2)}) collective-permute-start(bf16[4,16,768]{2,1,0:T(8,128)(2,1)S(1)} %get-tuple-element.44.refs_14_), channel_id=1, source_target_pairs={{0,12},{4,0},{8,4},{12,8},{1,13},{5,1},{9,5},{13,9},{2,14},{6,2},{... | collective-permute-start | bytes 294920 | tf_op jit(solution)/shard_map/ppermute | solution.py:368
  50.0 1.7 %shard_map.62.refs_0_ = bf16[4,16,768]{2,1,0:T(8,128)(2,1)S(1)} custom-call(s32[16]{0:T(128)S(1)} %copy-done.8, f32[4,576]{1,0:T(4,128)S(1)} %copy-done.5, bf16[4,4,16,768]{3,2,1,0:T(8,128)(2,1)S(1)} %all-to-all-done.query_ref, bf16[4,16,768]{2,1,0:T(8,128)(2,1)S(1)} %copy-done.2, bf16[4,16,768]{2,1,0:T(8,128)(2,1)S(1)} %collective-permute-done.refs_1_, ...), custom_call_target="tpu_custom_call" | custom-call | tf_op jit(solution)/shard_map/pallas_call | solution.py:326
  51.7 2.9 %collective-permute-done.13.refs_2_ = bf16[4,16,768]{2,1,0:T(8,128)(2,1)S(1)} collective-permute-done((bf16[4,16,768]{2,1,0:T(8,128)(2,1)S(1)}, bf16[4,16,768]{2,1,0:T(8,128)(2,1)S(1)}, u32[]{:S(2)}, u32[]{:S(2)}) %collective-permute-start.13) | collective-permute-done | bytes 98336 | tf_op jit(solution)/shard_map/ppermute | solution.py:368
  54.6 0.0 collective-permute-done.14.refs_3_
  54.6 0.3 collective-permute-done.12.refs_1_
  54.9 0.8 %shard_map.63 = bf16[4,16,3072]{2,1,0:T(8,128)(2,1)} custom-call(bf16[4,16,768]{2,1,0:T(8,128)(2,1)S(1)} %shard_map.62.refs_0_, bf16[4,16,768]{2,1,0:T(8,128)(2,1)S(1)} %collective-permute-done.12.refs_1_, bf16[4,16,768]{2,1,0:T(8,128)(2,1)S(1)} %collective-permute-done.13.refs_2_, bf16[4,16,768]{2,1,0:T(8,128)(2,1)S(1)} %collective-permute-done.14.refs_3_), custom_call_target="tpu_custom_call" | custom-call | tf_op jit(solution)/shard_map/pallas_call | solution.py:356
Async XLA Ops:
  0.0 12.9 %copy-start.1 = (bf16[4,16,3072]{2,1,0:T(8,128)(2,1)S(1)}, bf16[4,16,3072]{2,1,0:T(8,128)(2,1)}, u32[]{:S(2)}) copy-start(bf16[4,16,3072]{2,1,0:T(8,128)(2,1)} %refs_1_.3) | copy-start | bytes 1179652
  0.0 12.9 %copy-start = (bf16[4,16,3072]{2,1,0:T(8,128)(2,1)S(1)}, bf16[4,16,3072]{2,1,0:T(8,128)(2,1)}, u32[]{:S(2)}) copy-start(bf16[4,16,3072]{2,1,0:T(8,128)(2,1)} %refs_0_.4) | copy-start | bytes 1179652
  2.9 7.0 %copy-start.9 = (f32[8,128]{1,0:T(8,128)S(1)}, f32[8,128]{1,0:T(8,128)}, u32[]{:S(2)}) copy-start(f32[8,128]{1,0:T(8,128)} %get-tuple-element.26._) | copy-start | bytes 12292
  2.9 13.2 %collective-permute-start = (bf16[4,16,768]{2,1,0:T(8,128)(2,1)}, bf16[4,16,768]{2,1,0:T(8,128)(2,1)S(1)}, u32[]{:S(2)}, u32[]{:S(2)}) collective-permute-start(bf16[4,16,768]{2,1,0:T(8,128)(2,1)} %get-tuple-element.30), channel_id=1, source_target_pairs={{0,4},{4,8},{8,12},{12,0},{1,5},{5,9},{9,13},{13,1},{2,6},{6,10},{... | collective-permute-start | bytes 294920 | tf_op jit(solution)/shard_map/ppermute | solution.py:368
  6.0 12.8 %collective-permute-start.1 = (bf16[4,16,768]{2,1,0:T(8,128)(2,1)}, bf16[4,16,768]{2,1,0:T(8,128)(2,1)S(1)}, u32[]{:S(2)}, u32[]{:S(2)}) collective-permute-start(bf16[4,16,768]{2,1,0:T(8,128)(2,1)} %get-tuple-element.31), channel_id=1, source_target_pairs={{0,8},{4,12},{8,0},{12,4},{1,9},{5,13},{9,1},{13,5},{2,10},{6,14},... | collective-permute-start | bytes 294920 | tf_op jit(solution)/shard_map/ppermute | solution.py:368
  8.5 1.4 %copy-start.7 = (s32[16]{0:T(128)S(1)}, s32[16]{0:T(128)}, u32[]{:S(2)}) copy-start(s32[16]{0:T(128)} %tokens_ref.5) | copy-start | bytes 196
  8.6 10.2 %collective-permute-start.2 = (bf16[4,16,768]{2,1,0:T(8,128)(2,1)}, bf16[4,16,768]{2,1,0:T(8,128)(2,1)S(1)}, u32[]{:S(2)}, u32[]{:S(2)}) collective-permute-start(bf16[4,16,768]{2,1,0:T(8,128)(2,1)} %get-tuple-element.32), channel_id=1, source_target_pairs={{0,12},{4,0},{8,4},{12,8},{1,13},{5,1},{9,5},{13,9},{2,14},{6,2},{... | collective-permute-start | bytes 294920 | tf_op jit(solution)/shard_map/ppermute | solution.py:368
  9.9 0.7 %copy-start.6 = (s32[16,32]{1,0:T(8,128)S(1)}, s32[16,32]{1,0:T(8,128)}, u32[]{:S(2)}) copy-start(s32[16,32]{1,0:T(8,128)} %pair_ref.1) | copy-start | bytes 6148
  12.9 2.0 %copy-start.4 = (f32[4,576]{1,0:T(4,128)}, f32[4,576]{1,0:T(4,128)S(1)}, u32[]{:S(2)}) copy-start(f32[4,576]{1,0:T(4,128)S(1)} %get-tuple-element.27.refs_2_.bias_ref) | copy-start | bytes 27652
  12.9 9.6 %copy-start.2 = (bf16[4,16,768]{2,1,0:T(8,128)(2,1)S(1)}, bf16[4,16,768]{2,1,0:T(8,128)(2,1)}, u32[]{:S(2)}) copy-start(bf16[4,16,768]{2,1,0:T(8,128)(2,1)} %get-tuple-element.29.refs_0_) | copy-start | bytes 294916
  14.8 7.7 %collective-permute-start.3 = (bf16[4,16,768]{2,1,0:T(8,128)(2,1)S(1)}, bf16[4,16,768]{2,1,0:T(8,128)(2,1)S(1)}, u32[]{:S(2)}, u32[]{:S(2)}) collective-permute-start(bf16[4,16,768]{2,1,0:T(8,128)(2,1)S(1)} %get-tuple-element.33), channel_id=1, source_target_pairs={{0,4},{4,8},{8,12},{12,0},{1,5},{5,9},{9,13},{13,1},{2,6},{6,10},{... | collective-permute-start | bytes 294920 | tf_op jit(solution)/shard_map/ppermute | solution.py:368
  15.6 15.3 %collective-permute-start.7 = (bf16[4,16,768]{2,1,0:T(8,128)(2,1)S(1)}, bf16[4,16,768]{2,1,0:T(8,128)(2,1)S(1)}, u32[]{:S(2)}, u32[]{:S(2)}) collective-permute-start(bf16[4,16,768]{2,1,0:T(8,128)(2,1)S(1)} %get-tuple-element.39), channel_id=1, source_target_pairs={{0,8},{4,12},{8,0},{12,4},{1,9},{5,13},{9,1},{13,5},{2,10},{6,14},... | collective-permute-start | bytes 294920 | tf_op jit(solution)/shard_map/ppermute | solution.py:368
  16.1 14.8 %collective-permute-start.8 = (bf16[4,16,768]{2,1,0:T(8,128)(2,1)S(1)}, bf16[4,16,768]{2,1,0:T(8,128)(2,1)S(1)}, u32[]{:S(2)}, u32[]{:S(2)}) collective-permute-start(bf16[4,16,768]{2,1,0:T(8,128)(2,1)S(1)} %get-tuple-element.40), channel_id=1, source_target_pairs={{0,12},{4,0},{8,4},{12,8},{1,13},{5,1},{9,5},{13,9},{2,14},{6,2},{... | collective-permute-start | bytes 294920 | tf_op jit(solution)/shard_map/ppermute | solution.py:368
  22.5 2.7 %copy-start.3 = (bf16[4,16,3072]{2,1,0:T(8,128)(2,1)S(1)}, bf16[4,16,3072]{2,1,0:T(8,128)(2,1)}, u32[]{:S(2)}) copy-start(bf16[4,16,3072]{2,1,0:T(8,128)(2,1)} %refs_0_.5) | copy-start | bytes 1179652
  23.1 10.2 %collective-permute-start.5 = (bf16[1,4,16,768]{3,2,1,0:T(8,128)(2,1)S(1)}, bf16[1,4,16,768]{3,2,1,0:T(8,128)(2,1)S(1)}, u32[]{:S(2)}, u32[]{:S(2)}) collective-permute-start(bf16[1,4,16,768]{3,2,1,0:T(8,128)(2,1)S(1)} %get-tuple-element.36), channel_id=1, source_target_pairs={{0,2},{1,3},{2,0},{3,1},{4,6},{5,7},{6,4},{7,5},{8,10},{9,11},{10,... | collective-permute-start | bytes 294920 | tf_op jit(solution)/shard_map/ppermute | solution.py:368
  24.7 16.2 %collective-permute-start.6 = (bf16[2,4,16,768]{3,2,1,0:T(8,128)(2,1)S(1)}, bf16[2,4,16,768]{3,2,1,0:T(8,128)(2,1)S(1)}, u32[]{:S(2)}, u32[]{:S(2)}) collective-permute-start(bf16[2,4,16,768]{3,2,1,0:T(8,128)(2,1)S(1)} %get-tuple-element.37), channel_id=1, source_target_pairs={{0,3},{1,0},{2,1},{3,2},{4,7},{5,4},{6,5},{7,6},{8,11},{9,8},{10,9... | collective-permute-start | bytes 589832 | tf_op jit(solution)/shard_map/ppermute | solution.py:368
  24.7 16.2 %collective-permute-start.4 = (bf16[2,4,16,768]{3,2,1,0:T(8,128)(2,1)S(1)}, bf16[2,4,16,768]{3,2,1,0:T(8,128)(2,1)S(1)}, u32[]{:S(2)}, u32[]{:S(2)}) collective-permute-start(bf16[2,4,16,768]{3,2,1,0:T(8,128)(2,1)S(1)} %get-tuple-element.34.refs_1_.refs_4_), channel_id=1, source_target_pairs={{0,1},{1,2},{2,3},{3,0},{4,5},{5,6},{6,7},{7,4},{8,9},{9,10},{10,1... | collective-permute-start | bytes 589832 | tf_op jit(solution)/shard_map/ppermute | solution.py:368
  26.8 16.1 %all-to-all-start = ((bf16[4,4,16,768]{3,2,1,0:T(8,128)(2,1)}), bf16[4,4,16,768]{3,2,1,0:T(8,128)(2,1)S(1)}, u32[]{:S(2)}, u32[]{:S(2)}) async-start(bf16[4,4,16,768]{3,2,1,0:T(8,128)(2,1)} %get-tuple-element.35), calls=%async_computation | async-start | bytes 786432 | tf_op jit(solution)/shard_map/all_to_all | solution.py:406
  30.9 12.0 %copy-start.5 = (f32[4,576]{1,0:T(4,128)S(1)}, f32[4,576]{1,0:T(4,128)}, u32[]{:S(2)}) copy-start(f32[4,576]{1,0:T(4,128)} %copy-done.4) | copy-start | bytes 27652
  31.5 9.4 %collective-permute-start.9 = (bf16[2,4,16,768]{3,2,1,0:T(8,128)(2,1)S(1)}, bf16[2,4,16,768]{3,2,1,0:T(8,128)(2,1)S(1)}, u32[]{:S(2)}, u32[]{:S(2)}) collective-permute-start(bf16[2,4,16,768]{3,2,1,0:T(8,128)(2,1)S(1)} %get-tuple-element.41), channel_id=1, source_target_pairs={{0,1},{1,2},{2,3},{3,0},{4,5},{5,6},{6,7},{7,4},{8,9},{9,10},{10,1... | collective-permute-start | bytes 589832 | tf_op jit(solution)/shard_map/ppermute | solution.py:368
  31.6 11.3 %copy-start.8 = (s32[16]{0:T(128)S(1)}, s32[16]{0:T(128)}, u32[]{:S(2)}) copy-start(s32[16]{0:T(128)} %tokens_ref.5) | copy-start | bytes 196
  31.6 9.3 %collective-permute-start.11 = (bf16[2,4,16,768]{3,2,1,0:T(8,128)(2,1)S(1)}, bf16[2,4,16,768]{3,2,1,0:T(8,128)(2,1)S(1)}, u32[]{:S(2)}, u32[]{:S(2)}) collective-permute-start(bf16[2,4,16,768]{3,2,1,0:T(8,128)(2,1)S(1)} %get-tuple-element.43), channel_id=1, source_target_pairs={{0,3},{1,0},{2,1},{3,2},{4,7},{5,4},{6,5},{7,6},{8,11},{9,8},{10,9... | collective-permute-start | bytes 589832 | tf_op jit(solution)/shard_map/ppermute | solution.py:368
  33.3 7.6 %collective-permute-start.10 = (bf16[1,4,16,768]{3,2,1,0:T(8,128)(2,1)S(1)}, bf16[1,4,16,768]{3,2,1,0:T(8,128)(2,1)S(1)}, u32[]{:S(2)}, u32[]{:S(2)}) collective-permute-start(bf16[1,4,16,768]{3,2,1,0:T(8,128)(2,1)S(1)} %get-tuple-element.42), channel_id=1, source_target_pairs={{0,2},{1,3},{2,0},{3,1},{4,6},{5,7},{6,4},{7,5},{8,10},{9,11},{10,... | collective-permute-start | bytes 294920 | tf_op jit(solution)/shard_map/ppermute | solution.py:368
  45.1 9.5 %collective-permute-start.13 = (bf16[4,16,768]{2,1,0:T(8,128)(2,1)S(1)}, bf16[4,16,768]{2,1,0:T(8,128)(2,1)S(1)}, u32[]{:S(2)}, u32[]{:S(2)}) collective-permute-start(bf16[4,16,768]{2,1,0:T(8,128)(2,1)S(1)} %get-tuple-element.45), channel_id=1, source_target_pairs={{0,8},{4,12},{8,0},{12,4},{1,9},{5,13},{9,1},{13,5},{2,10},{6,14},... | collective-permute-start | bytes 294920 | tf_op jit(solution)/shard_map/ppermute | solution.py:368
  46.2 8.4 %collective-permute-start.14 = (bf16[4,16,768]{2,1,0:T(8,128)(2,1)S(1)}, bf16[4,16,768]{2,1,0:T(8,128)(2,1)S(1)}, u32[]{:S(2)}, u32[]{:S(2)}) collective-permute-start(bf16[4,16,768]{2,1,0:T(8,128)(2,1)S(1)} %get-tuple-element.46), channel_id=1, source_target_pairs={{0,4},{4,8},{8,12},{12,0},{1,5},{5,9},{9,13},{13,1},{2,6},{6,10},{... | collective-permute-start | bytes 294920 | tf_op jit(solution)/shard_map/ppermute | solution.py:368
  47.6 7.3 %collective-permute-start.12 = (bf16[4,16,768]{2,1,0:T(8,128)(2,1)S(1)}, bf16[4,16,768]{2,1,0:T(8,128)(2,1)S(1)}, u32[]{:S(2)}, u32[]{:S(2)}) collective-permute-start(bf16[4,16,768]{2,1,0:T(8,128)(2,1)S(1)} %get-tuple-element.44.refs_14_), channel_id=1, source_target_pairs={{0,12},{4,0},{8,4},{12,8},{1,13},{5,1},{9,5},{13,9},{2,14},{6,2},{... | collective-permute-start | bytes 294920 | tf_op jit(solution)/shard_map/ppermute | solution.py:368

commit v9 on v8

--- a/solution.py
+++ b/solution.py
@@ -256,22 +256,22 @@
     )(pair_list, block_tokens, after)
 
 
-def attend_kernel(counts, sizes, distances, tokens_ref, bias_ref, query_ref, *refs):
+def attend_kernel(counts, heads_of, distances, tokens_ref, bias_ref, query_ref, *refs):
     count_head, count_tm = counts
     queries = by_distance([query_ref], count_head, -1)
     per_part = count_head + count_tm - 1
-    parts = [refs[p * per_part : (p + 1) * per_part] for p in range(len(sizes))]
-    outs = refs[len(sizes) * per_part :][-len(distances) :]
+    parts = [refs[p * per_part : (p + 1) * per_part] for p in range(len(heads_of))]
+    outs = refs[len(heads_of) * per_part :][-len(distances) :]
     blocks, tokens, _ = outs[0].shape
     rows = len(distances) * tokens
     shard = lax.axis_index("tm")
     me = lax.axis_index("head")
     bias = bias_ref[...][:, None, :]
-    place_of = [(p, h) for p, size in enumerate(sizes) for h in range(size // HD)]
+    place_of = [(p, h) for p, (_, size) in enumerate(heads_of) for h in range(size // HD)]
 
     def gathered(kind, head):
         p, h = place_of[head]
-        first = kind * sizes[p] + h * HD
+        first = kind * heads_of[p][1] + h * HD
         lanes = slice(first, first + HD)
         pieces = [rows_of(own[:, :, lanes]) for own in parts[p][:count_head]]
         pieces += [
@@ -281,7 +281,8 @@
         return jnp.concatenate(pieces, axis=0)
 
     def products(head):
-        lanes = slice(head * HD, (head + 1) * HD)
+        first = heads_of[0][0] + head * HD
+        lanes = slice(first, first + HD)
         query = jnp.concatenate(
             [rows_of(queries[s][i, :, lanes]) for i in range(blocks) for s in distances], axis=0
         )
@@ -319,31 +320,32 @@
                 ).astype(jnp.bfloat16)
 
 
-def attend(block_tokens, bias, query, parts, sizes, distances, after, cost):
+def attend(block_tokens, bias, query, parts, heads_of, distances, after=(), cost=NO_COST):
     count_head, count_tm = query.shape[0], len(parts[0][1]) + 1
     operands = [ref for owns, slots in parts for ref in owns + slots]
+    shape = query.shape[1:3] + (sum(size for _, size in heads_of),)
     vmem = pl.BlockSpec(memory_space=pltpu.VMEM)
     return pl.pallas_call(
-        functools.partial(attend_kernel, (count_head, count_tm), sizes, distances),
+        functools.partial(attend_kernel, (count_head, count_tm), heads_of, distances),
         in_specs=[pl.BlockSpec(memory_space=pltpu.SMEM)]
         + [vmem] * (2 + len(operands))
         + [pl.BlockSpec(memory_space=pl.ANY)] * len(after),
         out_specs=[vmem] * len(distances),
-        out_shape=[jax.ShapeDtypeStruct(query.shape[1:], jnp.bfloat16)] * len(distances),
+        out_shape=[jax.ShapeDtypeStruct(shape, jnp.bfloat16)] * len(distances),
         cost_estimate=cost,
         compiler_params=pltpu.CompilerParams(vmem_limit_bytes=VMEM),
     )(block_tokens, bias, query, *operands, *after)
 
 
-def place_kernel(width_here, *refs):
+def place_kernel(places, width_here, *refs):
     pieces, out_ref, sems = refs[:-2], refs[-2], refs[-1]
-    me = lax.axis_index("head")
+    me, count = lax.axis_index("head"), lax.axis_size("head")
     copies = []
-    for s, piece in enumerate(pieces):
-        column = pl.multiple_of(lax.rem(me + s, len(pieces)) * width_here, HD)
+    for at, (piece, (s, start)) in enumerate(zip(pieces, places)):
+        column = pl.multiple_of(lax.rem(me + s, count) * width_here + start, HD)
         copies.append(
             pltpu.make_async_copy(
-                piece, out_ref.at[:, :, pl.ds(column, width_here)], sems.at[s]
+                piece, out_ref.at[:, :, pl.ds(column, piece.shape[-1])], sems.at[at]
             )
         )
         copies[-1].start()
@@ -351,13 +353,14 @@
         copy.wait()
 
 
-def place_pieces(pieces):
-    blocks, tokens, width_here = pieces[0].shape
+def place_pieces(pieces, places, width_here):
+    blocks, tokens, _ = pieces[0].shape
+    width = width_here * lax.axis_size("head")
     return pl.pallas_call(
-        functools.partial(place_kernel, width_here),
+        functools.partial(place_kernel, places, width_here),
         in_specs=[pl.BlockSpec(memory_space=pl.ANY)] * len(pieces),
         out_specs=pl.BlockSpec(memory_space=pltpu.HBM),
-        out_shape=jax.ShapeDtypeStruct((blocks, tokens, len(pieces) * width_here), jnp.bfloat16),
+        out_shape=jax.ShapeDtypeStruct((blocks, tokens, width), jnp.bfloat16),
         scratch_shapes=[pltpu.SemaphoreType.DMA((len(pieces),))],
         compiler_params=pltpu.CompilerParams(vmem_limit_bytes=VMEM),
     )(*pieces)
@@ -369,9 +372,7 @@
 
 
 def exchange(pieces, direction):
-    return [pieces[0]] + [
-        shifted(piece, "head", direction * s) for s, piece in enumerate(pieces[1:], 1)
-    ]
+    return [shifted(piece, "head", direction * s) for s, piece in enumerate(pieces, 1)]
 
 
 def forward(sent):
@@ -396,8 +397,8 @@
         pieces, token = rotate_pieces(arrays, message, count_head, after)
         packed.append(pieces)
         after = (token,)
-    received = [exchange(pieces, 1) for pieces in packed]
-    sent, after = [], (received[-1][1],)
+    received = [pieces[:1] + exchange(pieces[1:], 1) for pieces in packed]
+    sent, after = [], ()
     for owns, (_, size) in zip(received, parts):
         sent.append(pick_blocks(picks, owns, (0, 2 * size), count_tm, after))
         after = (sent[-1][0],)
@@ -405,12 +406,18 @@
     (query,), _ = rotate_pieces(arrays, message, count_head, (sent[0][0],), stacked=True)
     query = lax.all_to_all(query, "head", split_axis=0, concat_axis=0, tiled=True)
     inputs = [(owns, forward(picked)) for owns, picked in zip(received, sent)]
-    sizes = [size for _, size in parts]
-    leaving = attend(
-        block_tokens, bias, query, inputs, sizes, list(range(1, count_head)), (), NO_COST
-    )
-    staying = attend(block_tokens, bias, query, inputs, sizes, [0], (leaving[0],), NO_COST)
-    return place_pieces(exchange(staying + leaving, -1))
+    distances, after = list(range(1, count_head)), ()
+    pieces, places = [], []
+    for at, part in enumerate(parts):
+        cost = NO_COST if at == len(parts) - 1 else HIGH_COST
+        leaving = attend(
+            block_tokens, bias, query, [inputs[at]], [part], distances, after, cost
+        )
+        after = (leaving[0],)
+        pieces += exchange(leaving, -1)
+        places += [(s, part[0]) for s in distances]
+    pieces += attend(block_tokens, bias, query, inputs, parts, [0], after)
+    return place_pieces(pieces, places + [(0, 0)], width_here)
 
 
 def solution(mesh):

time: 55.9 us -> 54 us (0.966)
  waiting for transfers between devices: 16 us -> 8.35 us
  starting transfers between devices: 24.2 us -> 28.9 us
  Pallas kernels: 14.6 us -> 15.5 us
    ppermute x15 -> x18, waiting for transfers between devices: 14 us -> 2.58 us  [shifted(): lax.ppermute(array, axis, [(i, (i + distance) % count) for i in range(cou...]
    ppermute x15 -> x18, starting transfers between devices: 20.1 us -> 25.5 us  [shifted(): lax.ppermute(array, axis, [(i, (i + distance) % count) for i in range(cou...]
    all_to_all x1, waiting for transfers between devices: 1.99 us -> 5.77 us  [shards(): lax.all_to_all(query, 'head', split_axis=0, concat_axis=0, tiled=True)]
    pallas_call x3 -> x4, Pallas kernels: 4.73 us -> 5.71 us  [the longest x3 4.91 us: attend(): pl.pallas_call(functools.partial(attend_kernel, (count_head, count_tm), h...]
    all_to_all x1, starting transfers between devices: 4.08 us -> 3.47 us  [shards(): lax.all_to_all(query, 'head', split_axis=0, concat_axis=0, tiled=True)]
  transfers between devices with their start and end apart: 16 -> 19, of which waited for: 5 -> 3; matrix products, arithmetic and copies ran while one was open for 0% -> 0% of each run, Pallas kernels for 16% -> 22%
where the time goes in v9:
time: 54 us; the launch traced here: 53.8 us
  starting transfers between devices  28.9 us (54%)
  Pallas kernels  15.5 us (29%)
  waiting for transfers between devices  8.35 us (15%)
  local copies, waits for them, and re-layouts  0.74 us (1%)
    ppermute x18, starting transfers between devices, shifted(): lax.ppermute(array, axis, [(i, (i + distance) % count) for i in range(cou...  25.5 us
    pallas_call x3, Pallas kernels, rotate_pieces(): pl.pallas_call(functools.partial(rotate_kernel, message, sources, count_h...  6.4 us
    all_to_all x1, waiting for transfers between devices, shards(): lax.all_to_all(query, 'head', split_axis=0, concat_axis=0, tiled=True)  5.77 us
    pallas_call x3, Pallas kernels, attend(): pl.pallas_call(functools.partial(attend_kernel, (count_head, count_tm), h...  4.91 us
    all_to_all x1, starting transfers between devices, shards(): lax.all_to_all(query, 'head', split_axis=0, concat_axis=0, tiled=True)  3.47 us
    ppermute x18, waiting for transfers between devices, shifted(): lax.ppermute(array, axis, [(i, (i + distance) % count) for i in range(cou...  2.58 us
    pallas_call x1, Pallas kernels, plan(): pl.pallas_call(functools.partial(plan_kernel, count_head, count_tm, block...  2.25 us
    pallas_call x2, Pallas kernels, pick_blocks(): pl.pallas_call(functools.partial(pick_kernel, count_head, count_tm, lanes...  1.18 us
  transfers between devices with their start and end apart: 19, of which 3 were waited for; matrix products, arithmetic and copies ran while one was open for 0% of the time, Pallas kernels for 22%

profile of v9, /device:TPU:0, one launch (start us, length us, event | category | flops | bytes accessed | tf_op | source)
XLA Modules:
  0.0 53.8 jit_solution(7276711943172936782)
XLA Ops:
  0.0 0.0 copy-start.1
  0.0 0.0 copy-start
  0.0 2.9 %shard_map.55 = (bf16[4,16,768]{2,1,0:T(8,128)(2,1)}, bf16[4,16,768]{2,1,0:T(8,128)(2,1)}, bf16[4,16,768]{2,1,0:T(8,128)(2,1)}, bf16[4,16,768]{2,1,0:T(8,128)(2,1)}, f32[8,128]{1,0:T(8,128)}) custom-call(bf16[4,16,3072]{2,1,0:T(8,128)(2,1)} %refs_0_.5, bf16[4,16,3072]{2,1,0:T(8,128)(2,1)} %refs_1_.3), custom_call_target="tpu_custom_call" | custom-call | tf_op jit(solution)/shard_map/pallas_call | solution.py:101
  2.9 0.0 copy-start.9
  2.9 3.1 %collective-permute-start = (bf16[4,16,768]{2,1,0:T(8,128)(2,1)}, bf16[4,16,768]{2,1,0:T(8,128)(2,1)S(1)}, u32[]{:S(2)}, u32[]{:S(2)}) collective-permute-start(bf16[4,16,768]{2,1,0:T(8,128)(2,1)} %get-tuple-element.33), channel_id=1, source_target_pairs={{0,4},{4,8},{8,12},{12,0},{1,5},{5,9},{9,13},{13,1},{2,6},{6,10},{... | collective-permute-start | bytes 294920 | tf_op jit(solution)/shard_map/ppermute | solution.py:371
  6.0 2.6 %collective-permute-start.1 = (bf16[4,16,768]{2,1,0:T(8,128)(2,1)}, bf16[4,16,768]{2,1,0:T(8,128)(2,1)S(1)}, u32[]{:S(2)}, u32[]{:S(2)}) collective-permute-start(bf16[4,16,768]{2,1,0:T(8,128)(2,1)} %get-tuple-element.34), channel_id=1, source_target_pairs={{0,8},{4,12},{8,0},{12,4},{1,9},{5,13},{9,1},{13,5},{2,10},{6,14},... | collective-permute-start | bytes 294920 | tf_op jit(solution)/shard_map/ppermute | solution.py:371
  8.6 1.3 %collective-permute-start.2 = (bf16[4,16,768]{2,1,0:T(8,128)(2,1)}, bf16[4,16,768]{2,1,0:T(8,128)(2,1)S(1)}, u32[]{:S(2)}, u32[]{:S(2)}) collective-permute-start(bf16[4,16,768]{2,1,0:T(8,128)(2,1)} %get-tuple-element.35), channel_id=1, source_target_pairs={{0,12},{4,0},{8,4},{12,8},{1,13},{5,1},{9,5},{13,9},{2,14},{6,2},{... | collective-permute-start | bytes 294920 | tf_op jit(solution)/shard_map/ppermute | solution.py:371
  9.9 0.0 copy-done.9
  9.9 0.0 copy-done.7
  9.9 0.7 %copy-done.6 = s32[16,32]{1,0:T(8,128)S(1)} copy-done((s32[16,32]{1,0:T(8,128)S(1)}, s32[16,32]{1,0:T(8,128)}, u32[]{:S(2)}) %copy-start.6) | copy-done | bytes 2072
  10.6 2.3 %shard_map.56 = (s32[8]{0:T(128)S(1)}, f32[4,576]{1,0:T(4,128)S(1)}) custom-call(s32[16,32]{1,0:T(8,128)S(1)} %copy-done.6, s32[16]{0:T(128)S(1)} %copy-done.7, f32[8,128]{1,0:T(8,128)S(1)} %copy-done.9), custom_call_target="tpu_custom_call" | custom-call | tf_op jit(solution)/shard_map/pallas_call | solution.py:237
  12.9 0.0 copy-start.4
  12.9 0.0 copy-done.1
  12.9 0.0 copy-done
  12.9 0.0 copy-start.3
  12.9 1.9 %shard_map.60 = (bf16[4,16,768]{2,1,0:T(8,128)(2,1)S(1)}, bf16[4,16,768]{2,1,0:T(8,128)(2,1)S(1)}, bf16[4,16,768]{2,1,0:T(8,128)(2,1)S(1)}, bf16[4,16,768]{2,1,0:T(8,128)(2,1)S(1)}, f32[8,128]{1,0:T(8,128)}) custom-call(bf16[4,16,3072]{2,1,0:T(8,128)(2,1)S(1)} %copy-done, bf16[4,16,3072]{2,1,0:T(8,128)(2,1)S(1)} %copy-done.1, ...), custom_call_target="tpu_custom_call" | custom-call | tf_op jit(solution)/shard_map/pallas_call | solution.py:101
  14.8 0.0 copy-done.4
  14.8 0.7 %collective-permute-start.9 = (bf16[4,16,768]{2,1,0:T(8,128)(2,1)S(1)}, bf16[4,16,768]{2,1,0:T(8,128)(2,1)S(1)}, u32[]{:S(2)}, u32[]{:S(2)}) collective-permute-start(bf16[4,16,768]{2,1,0:T(8,128)(2,1)S(1)} %get-tuple-element.44), channel_id=1, source_target_pairs={{0,4},{4,8},{8,12},{12,0},{1,5},{5,9},{9,13},{13,1},{2,6},{6,10},{... | collective-permute-start | bytes 294920 | tf_op jit(solution)/shard_map/ppermute | solution.py:371
  15.6 0.5 collective-permute-start.10
  16.1 0.0 collective-permute-done.refs_1_
  16.1 2.6 %collective-permute-start.11 = (bf16[4,16,768]{2,1,0:T(8,128)(2,1)S(1)}, bf16[4,16,768]{2,1,0:T(8,128)(2,1)S(1)}, u32[]{:S(2)}, u32[]{:S(2)}) collective-permute-start(bf16[4,16,768]{2,1,0:T(8,128)(2,1)S(1)} %get-tuple-element.46), channel_id=1, source_target_pairs={{0,12},{4,0},{8,4},{12,8},{1,13},{5,1},{9,5},{13,9},{2,14},{6,2},{... | collective-permute-start | bytes 294920 | tf_op jit(solution)/shard_map/ppermute | solution.py:371
  18.7 0.0 collective-permute-done.1.refs_2_
  18.7 0.0 collective-permute-done.2.refs_3_
  18.7 0.0 copy-done.3
  18.7 0.0 copy-start.2
  18.7 0.6 %shard_map.57 = (bf16[2,4,16,768]{3,2,1,0:T(8,128)(2,1)S(1)}, bf16[1,4,16,768]{3,2,1,0:T(8,128)(2,1)S(1)}, bf16[2,4,16,768]{3,2,1,0:T(8,128)(2,1)S(1)}) custom-call(s32[8]{0:T(128)S(1)} %get-tuple-element.31.picks_ref, bf16[4,16,768]{2,1,0:T(8,128)(2,1)S(1)} %copy-done.3, bf16[4,16,768]{2,1,0:T(8,128)(2,1)S(1)} %collective-permute-done.refs_1_, ...), custom_call_target="tpu_custom_call" | custom-call | flops 99999997952 | tf_op jit(solution)/shard_map/pallas_call | solution.py:136
  19.3 1.6 %collective-permute-start.4 = (bf16[1,4,16,768]{3,2,1,0:T(8,128)(2,1)S(1)}, bf16[1,4,16,768]{3,2,1,0:T(8,128)(2,1)S(1)}, u32[]{:S(2)}, u32[]{:S(2)}) collective-permute-start(bf16[1,4,16,768]{3,2,1,0:T(8,128)(2,1)S(1)} %get-tuple-element.38), channel_id=1, source_target_pairs={{0,2},{1,3},{2,0},{3,1},{4,6},{5,7},{6,4},{7,5},{8,10},{9,11},{10,... | collective-permute-start | bytes 294920 | tf_op jit(solution)/shard_map/ppermute | solution.py:371
  20.9 0.0 collective-permute-start.3
  20.9 0.0 copy-done.2
  20.9 1.6 %shard_map.58 = (bf16[4,4,16,768]{3,2,1,0:T(8,128)(2,1)}, f32[8,128]{1,0:T(8,128)}) custom-call(bf16[4,16,3072]{2,1,0:T(8,128)(2,1)S(1)} %copy-done.2, bf16[2,4,16,768]{3,2,1,0:T(8,128)(2,1)S(1)} %get-tuple-element.36.refs_1_.refs_4_), custom_call_target="tpu_custom_call" | custom-call | tf_op jit(solution)/shard_map/pallas_call | solution.py:101
  22.5 3.5 %all-to-all-start = ((bf16[4,4,16,768]{3,2,1,0:T(8,128)(2,1)}), bf16[4,4,16,768]{3,2,1,0:T(8,128)(2,1)S(1)}, u32[]{:S(2)}, u32[]{:S(2)}) async-start(bf16[4,4,16,768]{3,2,1,0:T(8,128)(2,1)} %get-tuple-element.37), calls=%async_computation | async-start | bytes 786432 | tf_op jit(solution)/shard_map/all_to_all | solution.py:407
  26.0 0.0 collective-permute-done.9.refs_1_.refs_8_
  26.0 1.8 %collective-permute-start.5 = (bf16[2,4,16,768]{3,2,1,0:T(8,128)(2,1)S(1)}, bf16[2,4,16,768]{3,2,1,0:T(8,128)(2,1)S(1)}, u32[]{:S(2)}, u32[]{:S(2)}) collective-permute-start(bf16[2,4,16,768]{3,2,1,0:T(8,128)(2,1)S(1)} %get-tuple-element.39), channel_id=1, source_target_pairs={{0,3},{1,0},{2,1},{3,2},{4,7},{5,4},{6,5},{7,6},{8,11},{9,8},{10,9... | collective-permute-start | bytes 589832 | tf_op jit(solution)/shard_map/ppermute | solution.py:371
  27.8 0.0 collective-permute-done.10.refs_2_.refs_9_
  27.8 0.0 collective-permute-done.11.refs_3_.refs_10_
  27.8 0.6 %shard_map.61 = (bf16[2,4,16,768]{3,2,1,0:T(8,128)(2,1)S(1)}, bf16[1,4,16,768]{3,2,1,0:T(8,128)(2,1)S(1)}, bf16[2,4,16,768]{3,2,1,0:T(8,128)(2,1)S(1)}) custom-call(s32[8]{0:T(128)S(1)} %get-tuple-element.31.picks_ref, bf16[4,16,768]{2,1,0:T(8,128)(2,1)S(1)} %get-tuple-element.43.refs_0_.refs_7_, ...), custom_call_target="tpu_custom_call" | custom-call | flops 99999997952 | tf_op jit(solution)/shard_map/pallas_call | solution.py:136
  28.4 0.6 %collective-permute-start.13 = (bf16[1,4,16,768]{3,2,1,0:T(8,128)(2,1)S(1)}, bf16[1,4,16,768]{3,2,1,0:T(8,128)(2,1)S(1)}, u32[]{:S(2)}, u32[]{:S(2)}) collective-permute-start(bf16[1,4,16,768]{3,2,1,0:T(8,128)(2,1)S(1)} %get-tuple-element.48), channel_id=1, source_target_pairs={{0,2},{1,3},{2,0},{3,1},{4,6},{5,7},{6,4},{7,5},{8,10},{9,11},{10,... | collective-permute-start | bytes 294920 | tf_op jit(solution)/shard_map/ppermute | solution.py:371
  29.0 0.0 collective-permute-start.12
  29.0 0.0 collective-permute-done.4.refs_5_
  29.0 1.7 %collective-permute-start.14 = (bf16[2,4,16,768]{3,2,1,0:T(8,128)(2,1)S(1)}, bf16[2,4,16,768]{3,2,1,0:T(8,128)(2,1)S(1)}, u32[]{:S(2)}, u32[]{:S(2)}) collective-permute-start(bf16[2,4,16,768]{3,2,1,0:T(8,128)(2,1)S(1)} %get-tuple-element.49), channel_id=1, source_target_pairs={{0,3},{1,0},{2,1},{3,2},{4,7},{5,4},{6,5},{7,6},{8,11},{9,8},{10,9... | collective-permute-start | bytes 589832 | tf_op jit(solution)/shard_map/ppermute | solution.py:371
  30.8 2.2 %collective-permute-done.5.refs_6_ = bf16[2,4,16,768]{3,2,1,0:T(8,128)(2,1)S(1)} collective-permute-done((bf16[2,4,16,768]{3,2,1,0:T(8,128)(2,1)S(1)}, bf16[2,4,16,768]{3,2,1,0:T(8,128)(2,1)S(1)}, u32[]{:S(2)}, u32[]{:S(2)}) %collective-permute-start.5) | collective-permute-done | bytes 196640 | tf_op jit(solution)/shard_map/ppermute | solution.py:371
  33.0 0.0 collective-permute-done.3.refs_4_
  33.0 5.8 %all-to-all-done.query_ref = bf16[4,4,16,768]{3,2,1,0:T(8,128)(2,1)S(1)} async-done(((bf16[4,4,16,768]{3,2,1,0:T(8,128)(2,1)}), bf16[4,4,16,768]{3,2,1,0:T(8,128)(2,1)S(1)}, u32[]{:S(2)}, u32[]{:S(2)}) %all-to-all-start) | async-done | bytes 393248 | tf_op jit(solution)/shard_map/all_to_all | solution.py:407
  38.8 0.0 copy-done.5
  38.8 0.0 copy-done.8
  38.8 1.6 %shard_map.59 = (bf16[4,16,384]{2,1,0:T(8,128)(2,1)S(1)}, bf16[4,16,384]{2,1,0:T(8,128)(2,1)S(1)}, bf16[4,16,384]{2,1,0:T(8,128)(2,1)S(1)}) custom-call(s32[16]{0:T(128)S(1)} %copy-done.8, f32[4,576]{1,0:T(4,128)S(1)} %copy-done.5, bf16[4,4,16,768]{3,2,1,0:T(8,128)(2,1)S(1)} %all-to-all-done.query_ref, bf16[4,16,768]{2,1,0:T(8,128)(2,1)S(1)} %copy-done.3, ...), custom_call_target="tpu_custom_call" | custom-call | flops 99999997952 | tf_op jit(solution)/shard_map/pallas_call | solution.py:328
  40.4 0.1 collective-permute-start.7
  40.4 2.0 %collective-permute-start.8 = (bf16[4,16,384]{2,1,0:T(8,128)(2,1)S(1)}, bf16[4,16,384]{2,1,0:T(8,128)(2,1)S(1)}, u32[]{:S(2)}, u32[]{:S(2)}) collective-permute-start(bf16[4,16,384]{2,1,0:T(8,128)(2,1)S(1)} %get-tuple-element.42), channel_id=1, source_target_pairs={{0,4},{4,8},{8,12},{12,0},{1,5},{5,9},{9,13},{13,1},{2,6},{6,10},{... | collective-permute-start | bytes 147464 | tf_op jit(solution)/shard_map/ppermute | solution.py:371
  42.5 0.0 collective-permute-done.13.refs_5_.refs_12_
  42.5 1.9 %collective-permute-start.6 = (bf16[4,16,384]{2,1,0:T(8,128)(2,1)S(1)}, bf16[4,16,384]{2,1,0:T(8,128)(2,1)S(1)}, u32[]{:S(2)}, u32[]{:S(2)}) collective-permute-start(bf16[4,16,384]{2,1,0:T(8,128)(2,1)S(1)} %get-tuple-element.40.refs_7_), channel_id=1, source_target_pairs={{0,12},{4,0},{8,4},{12,8},{1,13},{5,1},{9,5},{13,9},{2,14},{6,2},{... | collective-permute-start | bytes 147464 | tf_op jit(solution)/shard_map/ppermute | solution.py:371
  44.3 0.0 collective-permute-done.12.refs_4_.refs_11_
  44.3 0.0 collective-permute-done.14.refs_6_.refs_13_
  44.3 1.6 %shard_map.62 = (bf16[4,16,384]{2,1,0:T(8,128)(2,1)S(1)}, bf16[4,16,384]{2,1,0:T(8,128)(2,1)S(1)}, bf16[4,16,384]{2,1,0:T(8,128)(2,1)S(1)}) custom-call(s32[16]{0:T(128)S(1)} %copy-done.8, f32[4,576]{1,0:T(4,128)S(1)} %copy-done.5, bf16[4,4,16,768]{3,2,1,0:T(8,128)(2,1)S(1)} %all-to-all-done.query_ref, ...), custom_call_target="tpu_custom_call" | custom-call | tf_op jit(solution)/shard_map/pallas_call | solution.py:328
  45.9 1.1 %collective-permute-start.16 = (bf16[4,16,384]{2,1,0:T(8,128)(2,1)S(1)}, bf16[4,16,384]{2,1,0:T(8,128)(2,1)S(1)}, u32[]{:S(2)}, u32[]{:S(2)}) collective-permute-start(bf16[4,16,384]{2,1,0:T(8,128)(2,1)S(1)} %get-tuple-element.51), channel_id=1, source_target_pairs={{0,8},{4,12},{8,0},{12,4},{1,9},{5,13},{9,1},{13,5},{2,10},{6,14},... | collective-permute-start | bytes 147464 | tf_op jit(solution)/shard_map/ppermute | solution.py:371
  47.0 0.0 collective-permute-start.17
  47.0 0.0 collective-permute-done.7.refs_1_
  47.1 3.8 %collective-permute-start.15 = (bf16[4,16,384]{2,1,0:T(8,128)(2,1)S(1)}, bf16[4,16,384]{2,1,0:T(8,128)(2,1)S(1)}, u32[]{:S(2)}, u32[]{:S(2)}) collective-permute-start(bf16[4,16,384]{2,1,0:T(8,128)(2,1)S(1)} %get-tuple-element.50.refs_14_), channel_id=1, source_target_pairs={{0,12},{4,0},{8,4},{12,8},{1,13},{5,1},{9,5},{13,9},{2,14},{6,2},{... | collective-permute-start | bytes 147464 | tf_op jit(solution)/shard_map/ppermute | solution.py:371
  50.9 1.7 %shard_map.63.refs_6_ = bf16[4,16,768]{2,1,0:T(8,128)(2,1)S(1)} custom-call(s32[16]{0:T(128)S(1)} %copy-done.8, f32[4,576]{1,0:T(4,128)S(1)} %copy-done.5, bf16[4,4,16,768]{3,2,1,0:T(8,128)(2,1)S(1)} %all-to-all-done.query_ref, bf16[4,16,768]{2,1,0:T(8,128)(2,1)S(1)} %copy-done.3, bf16[4,16,768]{2,1,0:T(8,128)(2,1)S(1)} %collective-permute-done.refs_1_, ...), custom_call_target="tpu_custom_call" | custom-call | tf_op jit(solution)/shard_map/pallas_call | solution.py:328
  52.6 0.0 collective-permute-done.8.refs_2_
  52.6 0.0 collective-permute-done.6.refs_0_
  52.6 0.0 collective-permute-done.16.refs_4_
  52.6 0.3 collective-permute-done.17.refs_5_
  53.0 0.0 collective-permute-done.15.refs_3_
  53.0 0.8 %shard_map.64 = bf16[4,16,3072]{2,1,0:T(8,128)(2,1)} custom-call(bf16[4,16,384]{2,1,0:T(8,128)(2,1)S(1)} %collective-permute-done.6.refs_0_, bf16[4,16,384]{2,1,0:T(8,128)(2,1)S(1)} %collective-permute-done.7.refs_1_, bf16[4,16,384]{2,1,0:T(8,128)(2,1)S(1)} %collective-permute-done.8.refs_2_, bf16[4,16,384]{2,1,0:T(8,128)(2,1)S(1)} %collective-permute-done.15.refs_3_, ...), custom_call_target="tpu_custom_call" | custom-call | tf_op jit(solution)/shard_map/pallas_call | solution.py:359
  (4 shorter events, 0.0 us)
Async XLA Ops:
  0.0 12.9 %copy-start.1 = (bf16[4,16,3072]{2,1,0:T(8,128)(2,1)S(1)}, bf16[4,16,3072]{2,1,0:T(8,128)(2,1)}, u32[]{:S(2)}) copy-start(bf16[4,16,3072]{2,1,0:T(8,128)(2,1)} %refs_1_.3) | copy-start | bytes 1179652
  0.0 12.9 %copy-start = (bf16[4,16,3072]{2,1,0:T(8,128)(2,1)S(1)}, bf16[4,16,3072]{2,1,0:T(8,128)(2,1)}, u32[]{:S(2)}) copy-start(bf16[4,16,3072]{2,1,0:T(8,128)(2,1)} %refs_0_.5) | copy-start | bytes 1179652
  2.9 7.0 %copy-start.9 = (f32[8,128]{1,0:T(8,128)S(1)}, f32[8,128]{1,0:T(8,128)}, u32[]{:S(2)}) copy-start(f32[8,128]{1,0:T(8,128)} %get-tuple-element.29._) | copy-start | bytes 12292
  2.9 13.2 %collective-permute-start = (bf16[4,16,768]{2,1,0:T(8,128)(2,1)}, bf16[4,16,768]{2,1,0:T(8,128)(2,1)S(1)}, u32[]{:S(2)}, u32[]{:S(2)}) collective-permute-start(bf16[4,16,768]{2,1,0:T(8,128)(2,1)} %get-tuple-element.33), channel_id=1, source_target_pairs={{0,4},{4,8},{8,12},{12,0},{1,5},{5,9},{9,13},{13,1},{2,6},{6,10},{... | collective-permute-start | bytes 294920 | tf_op jit(solution)/shard_map/ppermute | solution.py:371
  6.0 12.8 %collective-permute-start.1 = (bf16[4,16,768]{2,1,0:T(8,128)(2,1)}, bf16[4,16,768]{2,1,0:T(8,128)(2,1)S(1)}, u32[]{:S(2)}, u32[]{:S(2)}) collective-permute-start(bf16[4,16,768]{2,1,0:T(8,128)(2,1)} %get-tuple-element.34), channel_id=1, source_target_pairs={{0,8},{4,12},{8,0},{12,4},{1,9},{5,13},{9,1},{13,5},{2,10},{6,14},... | collective-permute-start | bytes 294920 | tf_op jit(solution)/shard_map/ppermute | solution.py:371
  8.5 1.4 %copy-start.7 = (s32[16]{0:T(128)S(1)}, s32[16]{0:T(128)}, u32[]{:S(2)}) copy-start(s32[16]{0:T(128)} %tokens_ref.7) | copy-start | bytes 196
  8.6 10.2 %collective-permute-start.2 = (bf16[4,16,768]{2,1,0:T(8,128)(2,1)}, bf16[4,16,768]{2,1,0:T(8,128)(2,1)S(1)}, u32[]{:S(2)}, u32[]{:S(2)}) collective-permute-start(bf16[4,16,768]{2,1,0:T(8,128)(2,1)} %get-tuple-element.35), channel_id=1, source_target_pairs={{0,12},{4,0},{8,4},{12,8},{1,13},{5,1},{9,5},{13,9},{2,14},{6,2},{... | collective-permute-start | bytes 294920 | tf_op jit(solution)/shard_map/ppermute | solution.py:371
  9.9 0.7 %copy-start.6 = (s32[16,32]{1,0:T(8,128)S(1)}, s32[16,32]{1,0:T(8,128)}, u32[]{:S(2)}) copy-start(s32[16,32]{1,0:T(8,128)} %pair_ref.1) | copy-start | bytes 6148
  12.9 2.0 %copy-start.4 = (f32[4,576]{1,0:T(4,128)}, f32[4,576]{1,0:T(4,128)S(1)}, u32[]{:S(2)}) copy-start(f32[4,576]{1,0:T(4,128)S(1)} %get-tuple-element.30.bias_ref.refs_2_) | copy-start | bytes 27652
  12.9 5.8 %copy-start.3 = (bf16[4,16,768]{2,1,0:T(8,128)(2,1)S(1)}, bf16[4,16,768]{2,1,0:T(8,128)(2,1)}, u32[]{:S(2)}) copy-start(bf16[4,16,768]{2,1,0:T(8,128)(2,1)} %get-tuple-element.32.refs_0_) | copy-start | bytes 294916
  14.8 11.2 %collective-permute-start.9 = (bf16[4,16,768]{2,1,0:T(8,128)(2,1)S(1)}, bf16[4,16,768]{2,1,0:T(8,128)(2,1)S(1)}, u32[]{:S(2)}, u32[]{:S(2)}) collective-permute-start(bf16[4,16,768]{2,1,0:T(8,128)(2,1)S(1)} %get-tuple-element.44), channel_id=1, source_target_pairs={{0,4},{4,8},{8,12},{12,0},{1,5},{5,9},{9,13},{13,1},{2,6},{6,10},{... | collective-permute-start | bytes 294920 | tf_op jit(solution)/shard_map/ppermute | solution.py:371
  15.6 12.3 %collective-permute-start.10 = (bf16[4,16,768]{2,1,0:T(8,128)(2,1)S(1)}, bf16[4,16,768]{2,1,0:T(8,128)(2,1)S(1)}, u32[]{:S(2)}, u32[]{:S(2)}) collective-permute-start(bf16[4,16,768]{2,1,0:T(8,128)(2,1)S(1)} %get-tuple-element.45), channel_id=1, source_target_pairs={{0,8},{4,12},{8,0},{12,4},{1,9},{5,13},{9,1},{13,5},{2,10},{6,14},... | collective-permute-start | bytes 294920 | tf_op jit(solution)/shard_map/ppermute | solution.py:371
  16.1 11.7 %collective-permute-start.11 = (bf16[4,16,768]{2,1,0:T(8,128)(2,1)S(1)}, bf16[4,16,768]{2,1,0:T(8,128)(2,1)S(1)}, u32[]{:S(2)}, u32[]{:S(2)}) collective-permute-start(bf16[4,16,768]{2,1,0:T(8,128)(2,1)S(1)} %get-tuple-element.46), channel_id=1, source_target_pairs={{0,12},{4,0},{8,4},{12,8},{1,13},{5,1},{9,5},{13,9},{2,14},{6,2},{... | collective-permute-start | bytes 294920 | tf_op jit(solution)/shard_map/ppermute | solution.py:371
  18.7 2.2 %copy-start.2 = (bf16[4,16,3072]{2,1,0:T(8,128)(2,1)S(1)}, bf16[4,16,3072]{2,1,0:T(8,128)(2,1)}, u32[]{:S(2)}) copy-start(bf16[4,16,3072]{2,1,0:T(8,128)(2,1)} %refs_0_.4) | copy-start | bytes 1179652
  19.3 9.7 %collective-permute-start.4 = (bf16[1,4,16,768]{3,2,1,0:T(8,128)(2,1)S(1)}, bf16[1,4,16,768]{3,2,1,0:T(8,128)(2,1)S(1)}, u32[]{:S(2)}, u32[]{:S(2)}) collective-permute-start(bf16[1,4,16,768]{3,2,1,0:T(8,128)(2,1)S(1)} %get-tuple-element.38), channel_id=1, source_target_pairs={{0,2},{1,3},{2,0},{3,1},{4,6},{5,7},{6,4},{7,5},{8,10},{9,11},{10,... | collective-permute-start | bytes 294920 | tf_op jit(solution)/shard_map/ppermute | solution.py:371
  20.9 12.1 %collective-permute-start.3 = (bf16[2,4,16,768]{3,2,1,0:T(8,128)(2,1)S(1)}, bf16[2,4,16,768]{3,2,1,0:T(8,128)(2,1)S(1)}, u32[]{:S(2)}, u32[]{:S(2)}) collective-permute-start(bf16[2,4,16,768]{3,2,1,0:T(8,128)(2,1)S(1)} %get-tuple-element.36.refs_1_.refs_4_), channel_id=1, source_target_pairs={{0,1},{1,2},{2,3},{3,0},{4,5},{5,6},{6,7},{7,4},{8,9},{9,10},{10,1... | collective-permute-start | bytes 589832 | tf_op jit(solution)/shard_map/ppermute | solution.py:371
  22.5 16.2 %all-to-all-start = ((bf16[4,4,16,768]{3,2,1,0:T(8,128)(2,1)}), bf16[4,4,16,768]{3,2,1,0:T(8,128)(2,1)S(1)}, u32[]{:S(2)}, u32[]{:S(2)}) async-start(bf16[4,4,16,768]{3,2,1,0:T(8,128)(2,1)} %get-tuple-element.37), calls=%async_computation | async-start | bytes 786432 | tf_op jit(solution)/shard_map/all_to_all | solution.py:407
  26.0 7.0 %collective-permute-start.5 = (bf16[2,4,16,768]{3,2,1,0:T(8,128)(2,1)S(1)}, bf16[2,4,16,768]{3,2,1,0:T(8,128)(2,1)S(1)}, u32[]{:S(2)}, u32[]{:S(2)}) collective-permute-start(bf16[2,4,16,768]{3,2,1,0:T(8,128)(2,1)S(1)} %get-tuple-element.39), channel_id=1, source_target_pairs={{0,3},{1,0},{2,1},{3,2},{4,7},{5,4},{6,5},{7,6},{8,11},{9,8},{10,9... | collective-permute-start | bytes 589832 | tf_op jit(solution)/shard_map/ppermute | solution.py:371
  27.8 10.9 %copy-start.5 = (f32[4,576]{1,0:T(4,128)S(1)}, f32[4,576]{1,0:T(4,128)}, u32[]{:S(2)}) copy-start(f32[4,576]{1,0:T(4,128)} %copy-done.4) | copy-start | bytes 27652
  28.4 14.0 %collective-permute-start.13 = (bf16[1,4,16,768]{3,2,1,0:T(8,128)(2,1)S(1)}, bf16[1,4,16,768]{3,2,1,0:T(8,128)(2,1)S(1)}, u32[]{:S(2)}, u32[]{:S(2)}) collective-permute-start(bf16[1,4,16,768]{3,2,1,0:T(8,128)(2,1)S(1)} %get-tuple-element.48), channel_id=1, source_target_pairs={{0,2},{1,3},{2,0},{3,1},{4,6},{5,7},{6,4},{7,5},{8,10},{9,11},{10,... | collective-permute-start | bytes 294920 | tf_op jit(solution)/shard_map/ppermute | solution.py:371
  29.0 9.7 %copy-start.8 = (s32[16]{0:T(128)S(1)}, s32[16]{0:T(128)}, u32[]{:S(2)}) copy-start(s32[16]{0:T(128)} %tokens_ref.7) | copy-start | bytes 196
  29.0 15.3 %collective-permute-start.12 = (bf16[2,4,16,768]{3,2,1,0:T(8,128)(2,1)S(1)}, bf16[2,4,16,768]{3,2,1,0:T(8,128)(2,1)S(1)}, u32[]{:S(2)}, u32[]{:S(2)}) collective-permute-start(bf16[2,4,16,768]{3,2,1,0:T(8,128)(2,1)S(1)} %get-tuple-element.47), channel_id=1, source_target_pairs={{0,1},{1,2},{2,3},{3,0},{4,5},{5,6},{6,7},{7,4},{8,9},{9,10},{10,1... | collective-permute-start | bytes 589832 | tf_op jit(solution)/shard_map/ppermute | solution.py:371
  29.0 15.3 %collective-permute-start.14 = (bf16[2,4,16,768]{3,2,1,0:T(8,128)(2,1)S(1)}, bf16[2,4,16,768]{3,2,1,0:T(8,128)(2,1)S(1)}, u32[]{:S(2)}, u32[]{:S(2)}) collective-permute-start(bf16[2,4,16,768]{3,2,1,0:T(8,128)(2,1)S(1)} %get-tuple-element.49), channel_id=1, source_target_pairs={{0,3},{1,0},{2,1},{3,2},{4,7},{5,4},{6,5},{7,6},{8,11},{9,8},{10,9... | collective-permute-start | bytes 589832 | tf_op jit(solution)/shard_map/ppermute | solution.py:371
  40.4 6.7 %collective-permute-start.7 = (bf16[4,16,384]{2,1,0:T(8,128)(2,1)S(1)}, bf16[4,16,384]{2,1,0:T(8,128)(2,1)S(1)}, u32[]{:S(2)}, u32[]{:S(2)}) collective-permute-start(bf16[4,16,384]{2,1,0:T(8,128)(2,1)S(1)} %get-tuple-element.41), channel_id=1, source_target_pairs={{0,8},{4,12},{8,0},{12,4},{1,9},{5,13},{9,1},{13,5},{2,10},{6,14},... | collective-permute-start | bytes 147464 | tf_op jit(solution)/shard_map/ppermute | solution.py:371
  40.4 12.2 %collective-permute-start.8 = (bf16[4,16,384]{2,1,0:T(8,128)(2,1)S(1)}, bf16[4,16,384]{2,1,0:T(8,128)(2,1)S(1)}, u32[]{:S(2)}, u32[]{:S(2)}) collective-permute-start(bf16[4,16,384]{2,1,0:T(8,128)(2,1)S(1)} %get-tuple-element.42), channel_id=1, source_target_pairs={{0,4},{4,8},{8,12},{12,0},{1,5},{5,9},{9,13},{13,1},{2,6},{6,10},{... | collective-permute-start | bytes 147464 | tf_op jit(solution)/shard_map/ppermute | solution.py:371
  42.5 10.2 %collective-permute-start.6 = (bf16[4,16,384]{2,1,0:T(8,128)(2,1)S(1)}, bf16[4,16,384]{2,1,0:T(8,128)(2,1)S(1)}, u32[]{:S(2)}, u32[]{:S(2)}) collective-permute-start(bf16[4,16,384]{2,1,0:T(8,128)(2,1)S(1)} %get-tuple-element.40.refs_7_), channel_id=1, source_target_pairs={{0,12},{4,0},{8,4},{12,8},{1,13},{5,1},{9,5},{13,9},{2,14},{6,2},{... | collective-permute-start | bytes 147464 | tf_op jit(solution)/shard_map/ppermute | solution.py:371
  45.9 6.7 %collective-permute-start.16 = (bf16[4,16,384]{2,1,0:T(8,128)(2,1)S(1)}, bf16[4,16,384]{2,1,0:T(8,128)(2,1)S(1)}, u32[]{:S(2)}, u32[]{:S(2)}) collective-permute-start(bf16[4,16,384]{2,1,0:T(8,128)(2,1)S(1)} %get-tuple-element.51), channel_id=1, source_target_pairs={{0,8},{4,12},{8,0},{12,4},{1,9},{5,13},{9,1},{13,5},{2,10},{6,14},... | collective-permute-start | bytes 147464 | tf_op jit(solution)/shard_map/ppermute | solution.py:371
  47.0 5.9 %collective-permute-start.17 = (bf16[4,16,384]{2,1,0:T(8,128)(2,1)S(1)}, bf16[4,16,384]{2,1,0:T(8,128)(2,1)S(1)}, u32[]{:S(2)}, u32[]{:S(2)}) collective-permute-start(bf16[4,16,384]{2,1,0:T(8,128)(2,1)S(1)} %get-tuple-element.52), channel_id=1, source_target_pairs={{0,4},{4,8},{8,12},{12,0},{1,5},{5,9},{9,13},{13,1},{2,6},{6,10},{... | collective-permute-start | bytes 147464 | tf_op jit(solution)/shard_map/ppermute | solution.py:371
  47.1 5.9 %collective-permute-start.15 = (bf16[4,16,384]{2,1,0:T(8,128)(2,1)S(1)}, bf16[4,16,384]{2,1,0:T(8,128)(2,1)S(1)}, u32[]{:S(2)}, u32[]{:S(2)}) collective-permute-start(bf16[4,16,384]{2,1,0:T(8,128)(2,1)S(1)} %get-tuple-element.50.refs_14_), channel_id=1, source_target_pairs={{0,12},{4,0},{8,4},{12,8},{1,13},{5,1},{9,5},{13,9},{2,14},{6,2},{... | collective-permute-start | bytes 147464 | tf_op jit(solution)/shard_map/ppermute | solution.py:371

commit v10 on v9

--- a/solution.py
+++ b/solution.py
@@ -50,38 +50,38 @@
 
 
 def by_distance(refs, count, direction):
-    if len(refs) > 1:
+    if len(refs[0].shape) == 3:
         return list(refs)
     me = lax.axis_index("head")
     return [refs[0].at[lax.rem(me + direction * s + count, count)] for s in range(count)]
 
 
-def rotate_kernel(message, sources, count_head, skipped, *refs):
+def rotate_kernel(message, sources, count_head, distances, skipped, *refs):
     fields, total = fields_of(message)
     ins = dict(zip(sources, refs))
     outs = by_distance(refs[len(sources) + skipped : -3], count_head, 1)
+    outs = dict(zip(distances, outs))
     token, buffer, sems = refs[-3:]
     token[...] = jnp.zeros_like(token)
     blocks, tokens, width = refs[0].shape
     width_here = width // count_head
     me = lax.axis_index("head")
-    order = list(range(1, count_head)) + [0]
     copies = {}
-    for s in order:
+    for at_piece, s in enumerate(distances):
         goal = lax.rem(me + s, count_head)
         for f, (source, start, size, at) in enumerate(fields):
             column = pl.multiple_of(goal * width_here + start, HD)
             copies[s, f] = pltpu.make_async_copy(
                 ins[source].at[:, :, pl.ds(column, size)],
-                buffer.at[s, :, :, pl.ds(at, size)],
-                sems.at[s, f],
+                buffer.at[at_piece, :, :, pl.ds(at, size)],
+                sems.at[at_piece, f],
             )
             copies[s, f].start()
     sign = sign_matrix()
-    for s in order:
+    for at_piece, s in enumerate(distances):
         for f, (_, _, size, start) in enumerate(fields):
             copies[s, f].wait()
-            flat = rows_of(buffer[s, :, :, start : start + size])
+            flat = rows_of(buffer[at_piece, :, :, start : start + size])
             heads = [flat[:, at : at + HD] for at in range(0, size, HD)]
             turned = jnp.dot(
                 jnp.concatenate(heads, axis=0), sign, preferred_element_type=jnp.float32
@@ -92,21 +92,22 @@
                 outs[s][:, :, at : at + HD] = turned[h].astype(jnp.bfloat16)
 
 
-def rotate_pieces(arrays, message, count_head, after=(), limit=VMEM, stacked=False):
+def rotate_pieces(arrays, message, count_head, distances, after=(), limit=VMEM, stacked=False):
     blocks, tokens, _ = arrays[0].shape
     fields, total = fields_of(message)
     sources = sorted({source for source, _, _ in message})
+    count = len(distances)
     one = (blocks, tokens, total)
-    shapes = [(count_head,) + one] if stacked else [one] * count_head
+    shapes = [(count,) + one] if stacked else [one] * count
     *pieces, token = pl.pallas_call(
-        functools.partial(rotate_kernel, message, sources, count_head, len(after)),
+        functools.partial(rotate_kernel, message, sources, count_head, distances, len(after)),
         in_specs=[pl.BlockSpec(memory_space=pltpu.HBM)] * len(sources)
         + [pl.BlockSpec(memory_space=pl.ANY)] * len(after),
         out_specs=[pl.BlockSpec(memory_space=pltpu.VMEM)] * (len(shapes) + 1),
         out_shape=[jax.ShapeDtypeStruct(shape, jnp.bfloat16) for shape in shapes] + [TOKEN],
         scratch_shapes=[
-            pltpu.VMEM((count_head,) + one, jnp.bfloat16),
-            pltpu.SemaphoreType.DMA((count_head, len(fields))),
+            pltpu.VMEM((count,) + one, jnp.bfloat16),
+            pltpu.SemaphoreType.DMA((count, len(fields))),
         ],
         cost_estimate=NO_COST,
         compiler_params=pltpu.CompilerParams(vmem_limit_bytes=limit),
@@ -389,25 +390,37 @@
     parts = [(0, cut), (cut, width_here - cut)] if heads > 1 else [(0, width_here)]
     arrays = [query_rows, key_rows, value_rows]
     messages = [[(1,) + part, (2,) + part] for part in parts]
-    pieces, token = rotate_pieces(arrays, messages[0], count_head, limit=WIDE_VMEM)
-    packed = [pieces]
+    half = count_head // 2
+    others = [s for s in range(1, count_head) if s != half]
+    (farthest,), token = rotate_pieces(
+        arrays, messages[0], count_head, [half], limit=WIDE_VMEM
+    )
+    (*near, own), token = rotate_pieces(
+        arrays, messages[0], count_head, others + [0], (token,), WIDE_VMEM
+    )
+    farthest = shifted(farthest, "head", half)
+    near = [shifted(piece, "head", s) for s, piece in zip(others, near)]
+    received = [[own] + near[: half - 1] + [farthest] + near[half - 1 :]]
     picks, bias = plan(pair_list, block_tokens, token, blocks, count_head, count_tm)
-    after = (bias,)
+    after = (bias, farthest)
+    distances = list(range(1, count_head))
     for message in messages[1:]:
-        pieces, token = rotate_pieces(arrays, message, count_head, after)
-        packed.append(pieces)
+        (*pieces, own), token = rotate_pieces(
+            arrays, message, count_head, distances + [0], after
+        )
+        received.append([own] + exchange(pieces, 1))
         after = (token,)
-    received = [pieces[:1] + exchange(pieces[1:], 1) for pieces in packed]
     sent, after = [], ()
     for owns, (_, size) in zip(received, parts):
         sent.append(pick_blocks(picks, owns, (0, 2 * size), count_tm, after))
         after = (sent[-1][0],)
     message = [(0, 0, width_here)]
-    (query,), _ = rotate_pieces(arrays, message, count_head, (sent[0][0],), stacked=True)
+    (query,), _ = rotate_pieces(
+        arrays, message, count_head, list(range(count_head)), (sent[0][0],), stacked=True
+    )
     query = lax.all_to_all(query, "head", split_axis=0, concat_axis=0, tiled=True)
     inputs = [(owns, forward(picked)) for owns, picked in zip(received, sent)]
-    distances, after = list(range(1, count_head)), ()
-    pieces, places = [], []
+    after, pieces, places = (), [], []
     for at, part in enumerate(parts):
         cost = NO_COST if at == len(parts) - 1 else HIGH_COST
         leaving = attend(

time: 54 us -> 56.5 us (1.046)
  Pallas kernels: 15.5 us -> 17 us
  starting transfers between devices: 28.9 us -> 29.9 us
    pallas_call x3 -> x4, Pallas kernels: 6.4 us -> 7.86 us  [rotate_pieces(): pl.pallas_call(functools.partial(rotate_kernel, message, sources, count_h...]
    ppermute x18, starting transfers between devices: 25.5 us -> 26.4 us  [shifted(): lax.ppermute(array, axis, [(i, (i + distance) % count) for i in range(cou...]
  transfers between devices with their start and end apart: 19 -> 19, of which waited for: 3 -> 3; matrix products, arithmetic and copies ran while one was open for 0% -> 0% of each run, Pallas kernels for 22% -> 26%
where the time goes in v10:
time: 56.5 us; the launch traced here: 56.2 us
  starting transfers between devices  29.9 us (53%)
  Pallas kernels  17 us (30%)
  waiting for transfers between devices  8.35 us (15%)
  local copies, waits for them, and re-layouts  0.71 us (1%)
    ppermute x18, starting transfers between devices, shifted(): lax.ppermute(array, axis, [(i, (i + distance) % count) for i in range(cou...  26.4 us
    pallas_call x4, Pallas kernels, rotate_pieces(): pl.pallas_call(functools.partial(rotate_kernel, message, sources, count_h...  7.86 us
    all_to_all x1, waiting for transfers between devices, shards(): lax.all_to_all(query, 'head', split_axis=0, concat_axis=0, tiled=True)  5.77 us
    pallas_call x3, Pallas kernels, attend(): pl.pallas_call(functools.partial(attend_kernel, (count_head, count_tm), h...  4.91 us
    all_to_all x1, starting transfers between devices, shards(): lax.all_to_all(query, 'head', split_axis=0, concat_axis=0, tiled=True)  3.47 us
    ppermute x18, waiting for transfers between devices, shifted(): lax.ppermute(array, axis, [(i, (i + distance) % count) for i in range(cou...  2.58 us
    pallas_call x1, Pallas kernels, plan(): pl.pallas_call(functools.partial(plan_kernel, count_head, count_tm, block...  2.25 us
    pallas_call x2, Pallas kernels, pick_blocks(): pl.pallas_call(functools.partial(pick_kernel, count_head, count_tm, lanes...  1.18 us
  transfers between devices with their start and end apart: 19, of which 3 were waited for; matrix products, arithmetic and copies ran while one was open for 0% of the time, Pallas kernels for 26%

profile of v10, /device:TPU:0, one launch (start us, length us, event | category | flops | bytes accessed | tf_op | source)
XLA Modules:
  0.0 56.2 jit_solution(17566894392182225561)
XLA Ops:
  0.0 1.8 %shard_map.55 = (bf16[4,16,768]{2,1,0:T(8,128)(2,1)}, f32[8,128]{1,0:T(8,128)}) custom-call(bf16[4,16,3072]{2,1,0:T(8,128)(2,1)} %refs_0_.7, bf16[4,16,3072]{2,1,0:T(8,128)(2,1)} %refs_1_.5), custom_call_target="tpu_custom_call" | custom-call | tf_op jit(solution)/shard_map/pallas_call | solution.py:102
  1.8 4.1 %collective-permute-start.1 = (bf16[4,16,768]{2,1,0:T(8,128)(2,1)}, bf16[4,16,768]{2,1,0:T(8,128)(2,1)S(1)}, u32[]{:S(2)}, u32[]{:S(2)}) collective-permute-start(bf16[4,16,768]{2,1,0:T(8,128)(2,1)} %get-tuple-element.36), channel_id=1, source_target_pairs={{0,8},{4,12},{8,0},{12,4},{1,9},{5,13},{9,1},{13,5},{2,10},{6,14},... | collective-permute-start | bytes 294920 | tf_op jit(solution)/shard_map/ppermute | solution.py:372
  5.9 0.0 copy-start
  5.9 0.0 copy-start.1
  5.9 2.5 %shard_map.56 = (bf16[4,16,768]{2,1,0:T(8,128)(2,1)}, bf16[4,16,768]{2,1,0:T(8,128)(2,1)}, bf16[4,16,768]{2,1,0:T(8,128)(2,1)}, f32[8,128]{1,0:T(8,128)}) custom-call(bf16[4,16,3072]{2,1,0:T(8,128)(2,1)} %refs_0_.7, bf16[4,16,3072]{2,1,0:T(8,128)(2,1)} %refs_1_.5, f32[8,128]{1,0:T(8,128)} %get-tuple-element.30.refs_2_), custom_call_target="tpu_custom_call" | custom-call | tf_op jit(solution)/shard_map/pallas_call | solution.py:102
  8.4 1.6 %collective-permute-start = (bf16[4,16,768]{2,1,0:T(8,128)(2,1)}, bf16[4,16,768]{2,1,0:T(8,128)(2,1)S(1)}, u32[]{:S(2)}, u32[]{:S(2)}) collective-permute-start(bf16[4,16,768]{2,1,0:T(8,128)(2,1)} %get-tuple-element.35), channel_id=1, source_target_pairs={{0,4},{4,8},{8,12},{12,0},{1,5},{5,9},{9,13},{13,1},{2,6},{6,10},{... | collective-permute-start | bytes 294920 | tf_op jit(solution)/shard_map/ppermute | solution.py:372
  10.1 2.3 %collective-permute-start.2 = (bf16[4,16,768]{2,1,0:T(8,128)(2,1)}, bf16[4,16,768]{2,1,0:T(8,128)(2,1)S(1)}, u32[]{:S(2)}, u32[]{:S(2)}) collective-permute-start(bf16[4,16,768]{2,1,0:T(8,128)(2,1)} %get-tuple-element.37), channel_id=1, source_target_pairs={{0,12},{4,0},{8,4},{12,8},{1,13},{5,1},{9,5},{13,9},{2,14},{6,2},{... | collective-permute-start | bytes 294920 | tf_op jit(solution)/shard_map/ppermute | solution.py:372
  12.3 0.0 copy-done.6
  12.3 0.0 copy-done.7
  12.3 0.7 %copy-done.9 = f32[8,128]{1,0:T(8,128)S(1)} copy-done((f32[8,128]{1,0:T(8,128)S(1)}, f32[8,128]{1,0:T(8,128)}, u32[]{:S(2)}) %copy-start.9) | copy-done | bytes 4120
  13.0 2.3 %shard_map.57 = (s32[8]{0:T(128)S(1)}, f32[4,576]{1,0:T(4,128)S(1)}) custom-call(s32[16,32]{1,0:T(8,128)S(1)} %copy-done.6, s32[16]{0:T(128)S(1)} %copy-done.7, f32[8,128]{1,0:T(8,128)S(1)} %copy-done.9), custom_call_target="tpu_custom_call" | custom-call | tf_op jit(solution)/shard_map/pallas_call | solution.py:238
  15.3 0.0 copy-start.4
  15.3 0.0 collective-permute-done.1.refs_2_.refs_3_
  15.3 0.0 copy-done
  15.3 0.0 copy-done.1
  15.3 0.0 copy-start.3
  15.3 1.9 %shard_map.61 = (bf16[4,16,768]{2,1,0:T(8,128)(2,1)S(1)}, bf16[4,16,768]{2,1,0:T(8,128)(2,1)S(1)}, bf16[4,16,768]{2,1,0:T(8,128)(2,1)S(1)}, bf16[4,16,768]{2,1,0:T(8,128)(2,1)S(1)}, f32[8,128]{1,0:T(8,128)}) custom-call(bf16[4,16,3072]{2,1,0:T(8,128)(2,1)S(1)} %copy-done, bf16[4,16,3072]{2,1,0:T(8,128)(2,1)S(1)} %copy-done.1, ...), custom_call_target="tpu_custom_call" | custom-call | tf_op jit(solution)/shard_map/pallas_call | solution.py:102
  17.2 0.0 copy-done.4
  17.2 0.1 collective-permute-start.9
  17.3 1.2 %collective-permute-start.10 = (bf16[4,16,768]{2,1,0:T(8,128)(2,1)S(1)}, bf16[4,16,768]{2,1,0:T(8,128)(2,1)S(1)}, u32[]{:S(2)}, u32[]{:S(2)}) collective-permute-start(bf16[4,16,768]{2,1,0:T(8,128)(2,1)S(1)} %get-tuple-element.47), channel_id=1, source_target_pairs={{0,8},{4,12},{8,0},{12,4},{1,9},{5,13},{9,1},{13,5},{2,10},{6,14},... | collective-permute-start | bytes 294920 | tf_op jit(solution)/shard_map/ppermute | solution.py:372
  18.5 2.6 %collective-permute-start.11 = (bf16[4,16,768]{2,1,0:T(8,128)(2,1)S(1)}, bf16[4,16,768]{2,1,0:T(8,128)(2,1)S(1)}, u32[]{:S(2)}, u32[]{:S(2)}) collective-permute-start(bf16[4,16,768]{2,1,0:T(8,128)(2,1)S(1)} %get-tuple-element.48), channel_id=1, source_target_pairs={{0,12},{4,0},{8,4},{12,8},{1,13},{5,1},{9,5},{13,9},{2,14},{6,2},{... | collective-permute-start | bytes 294920 | tf_op jit(solution)/shard_map/ppermute | solution.py:372
  21.1 0.0 collective-permute-done.refs_1_
  21.1 0.0 collective-permute-done.2.refs_3_
  21.1 0.0 copy-done.3
  21.1 0.0 copy-start.2
  21.1 0.6 %shard_map.58 = (bf16[2,4,16,768]{3,2,1,0:T(8,128)(2,1)S(1)}, bf16[1,4,16,768]{3,2,1,0:T(8,128)(2,1)S(1)}, bf16[2,4,16,768]{3,2,1,0:T(8,128)(2,1)S(1)}) custom-call(s32[8]{0:T(128)S(1)} %get-tuple-element.33.picks_ref, bf16[4,16,768]{2,1,0:T(8,128)(2,1)S(1)} %copy-done.3, bf16[4,16,768]{2,1,0:T(8,128)(2,1)S(1)} %collective-permute-done.refs_1_, ...), custom_call_target="tpu_custom_call" | custom-call | flops 99999997952 | tf_op jit(solution)/shard_map/pallas_call | solution.py:137
  21.7 1.6 %collective-permute-start.4 = (bf16[1,4,16,768]{3,2,1,0:T(8,128)(2,1)S(1)}, bf16[1,4,16,768]{3,2,1,0:T(8,128)(2,1)S(1)}, u32[]{:S(2)}, u32[]{:S(2)}) collective-permute-start(bf16[1,4,16,768]{3,2,1,0:T(8,128)(2,1)S(1)} %get-tuple-element.40), channel_id=1, source_target_pairs={{0,2},{1,3},{2,0},{3,1},{4,6},{5,7},{6,4},{7,5},{8,10},{9,11},{10,... | collective-permute-start | bytes 294920 | tf_op jit(solution)/shard_map/ppermute | solution.py:372
  23.3 0.0 collective-permute-start.3
  23.3 0.0 copy-done.2
  23.3 1.6 %shard_map.59 = (bf16[4,4,16,768]{3,2,1,0:T(8,128)(2,1)}, f32[8,128]{1,0:T(8,128)}) custom-call(bf16[4,16,3072]{2,1,0:T(8,128)(2,1)S(1)} %copy-done.2, bf16[2,4,16,768]{3,2,1,0:T(8,128)(2,1)S(1)} %get-tuple-element.38.refs_1_.refs_4_), custom_call_target="tpu_custom_call" | custom-call | tf_op jit(solution)/shard_map/pallas_call | solution.py:102
  25.0 3.5 %all-to-all-start = ((bf16[4,4,16,768]{3,2,1,0:T(8,128)(2,1)}), bf16[4,4,16,768]{3,2,1,0:T(8,128)(2,1)S(1)}, u32[]{:S(2)}, u32[]{:S(2)}) async-start(bf16[4,4,16,768]{3,2,1,0:T(8,128)(2,1)} %get-tuple-element.39), calls=%async_computation | async-start | bytes 786432 | tf_op jit(solution)/shard_map/all_to_all | solution.py:421
  28.4 0.0 collective-permute-done.9.refs_1_.refs_8_
  28.4 1.8 %collective-permute-start.5 = (bf16[2,4,16,768]{3,2,1,0:T(8,128)(2,1)S(1)}, bf16[2,4,16,768]{3,2,1,0:T(8,128)(2,1)S(1)}, u32[]{:S(2)}, u32[]{:S(2)}) collective-permute-start(bf16[2,4,16,768]{3,2,1,0:T(8,128)(2,1)S(1)} %get-tuple-element.41), channel_id=1, source_target_pairs={{0,3},{1,0},{2,1},{3,2},{4,7},{5,4},{6,5},{7,6},{8,11},{9,8},{10,9... | collective-permute-start | bytes 589832 | tf_op jit(solution)/shard_map/ppermute | solution.py:372
  30.2 0.0 collective-permute-done.10.refs_2_.refs_9_
  30.2 0.0 collective-permute-done.11.refs_3_.refs_10_
  30.2 0.6 %shard_map.62 = (bf16[2,4,16,768]{3,2,1,0:T(8,128)(2,1)S(1)}, bf16[1,4,16,768]{3,2,1,0:T(8,128)(2,1)S(1)}, bf16[2,4,16,768]{3,2,1,0:T(8,128)(2,1)S(1)}) custom-call(s32[8]{0:T(128)S(1)} %get-tuple-element.33.picks_ref, bf16[4,16,768]{2,1,0:T(8,128)(2,1)S(1)} %get-tuple-element.45.refs_0_.refs_7_, ...), custom_call_target="tpu_custom_call" | custom-call | flops 99999997952 | tf_op jit(solution)/shard_map/pallas_call | solution.py:137
  30.8 0.6 %collective-permute-start.13 = (bf16[1,4,16,768]{3,2,1,0:T(8,128)(2,1)S(1)}, bf16[1,4,16,768]{3,2,1,0:T(8,128)(2,1)S(1)}, u32[]{:S(2)}, u32[]{:S(2)}) collective-permute-start(bf16[1,4,16,768]{3,2,1,0:T(8,128)(2,1)S(1)} %get-tuple-element.50), channel_id=1, source_target_pairs={{0,2},{1,3},{2,0},{3,1},{4,6},{5,7},{6,4},{7,5},{8,10},{9,11},{10,... | collective-permute-start | bytes 294920 | tf_op jit(solution)/shard_map/ppermute | solution.py:372
  31.4 0.0 collective-permute-start.12
  31.5 0.0 collective-permute-done.4.refs_5_
  31.5 1.7 %collective-permute-start.14 = (bf16[2,4,16,768]{3,2,1,0:T(8,128)(2,1)S(1)}, bf16[2,4,16,768]{3,2,1,0:T(8,128)(2,1)S(1)}, u32[]{:S(2)}, u32[]{:S(2)}) collective-permute-start(bf16[2,4,16,768]{3,2,1,0:T(8,128)(2,1)S(1)} %get-tuple-element.51), channel_id=1, source_target_pairs={{0,3},{1,0},{2,1},{3,2},{4,7},{5,4},{6,5},{7,6},{8,11},{9,8},{10,9... | collective-permute-start | bytes 589832 | tf_op jit(solution)/shard_map/ppermute | solution.py:372
  33.2 2.2 %collective-permute-done.5.refs_6_ = bf16[2,4,16,768]{3,2,1,0:T(8,128)(2,1)S(1)} collective-permute-done((bf16[2,4,16,768]{3,2,1,0:T(8,128)(2,1)S(1)}, bf16[2,4,16,768]{3,2,1,0:T(8,128)(2,1)S(1)}, u32[]{:S(2)}, u32[]{:S(2)}) %collective-permute-start.5) | collective-permute-done | bytes 196640 | tf_op jit(solution)/shard_map/ppermute | solution.py:372
  35.4 0.0 collective-permute-done.3.refs_4_
  35.4 5.8 %all-to-all-done.query_ref = bf16[4,4,16,768]{3,2,1,0:T(8,128)(2,1)S(1)} async-done(((bf16[4,4,16,768]{3,2,1,0:T(8,128)(2,1)}), bf16[4,4,16,768]{3,2,1,0:T(8,128)(2,1)S(1)}, u32[]{:S(2)}, u32[]{:S(2)}) %all-to-all-start) | async-done | bytes 393248 | tf_op jit(solution)/shard_map/all_to_all | solution.py:421
  41.2 0.0 copy-done.5
  41.2 0.0 copy-done.8
  41.2 1.6 %shard_map.60 = (bf16[4,16,384]{2,1,0:T(8,128)(2,1)S(1)}, bf16[4,16,384]{2,1,0:T(8,128)(2,1)S(1)}, bf16[4,16,384]{2,1,0:T(8,128)(2,1)S(1)}) custom-call(s32[16]{0:T(128)S(1)} %copy-done.8, f32[4,576]{1,0:T(4,128)S(1)} %copy-done.5, bf16[4,4,16,768]{3,2,1,0:T(8,128)(2,1)S(1)} %all-to-all-done.query_ref, bf16[4,16,768]{2,1,0:T(8,128)(2,1)S(1)} %copy-done.3, ...), custom_call_target="tpu_custom_call" | custom-call | flops 99999997952 | tf_op jit(solution)/shard_map/pallas_call | solution.py:329
  42.8 0.1 collective-permute-start.7
  42.8 2.0 %collective-permute-start.8 = (bf16[4,16,384]{2,1,0:T(8,128)(2,1)S(1)}, bf16[4,16,384]{2,1,0:T(8,128)(2,1)S(1)}, u32[]{:S(2)}, u32[]{:S(2)}) collective-permute-start(bf16[4,16,384]{2,1,0:T(8,128)(2,1)S(1)} %get-tuple-element.44), channel_id=1, source_target_pairs={{0,4},{4,8},{8,12},{12,0},{1,5},{5,9},{9,13},{13,1},{2,6},{6,10},{... | collective-permute-start | bytes 147464 | tf_op jit(solution)/shard_map/ppermute | solution.py:372
  44.9 0.0 collective-permute-done.13.refs_5_.refs_12_
  44.9 1.9 %collective-permute-start.6 = (bf16[4,16,384]{2,1,0:T(8,128)(2,1)S(1)}, bf16[4,16,384]{2,1,0:T(8,128)(2,1)S(1)}, u32[]{:S(2)}, u32[]{:S(2)}) collective-permute-start(bf16[4,16,384]{2,1,0:T(8,128)(2,1)S(1)} %get-tuple-element.42.refs_7_), channel_id=1, source_target_pairs={{0,12},{4,0},{8,4},{12,8},{1,13},{5,1},{9,5},{13,9},{2,14},{6,2},{... | collective-permute-start | bytes 147464 | tf_op jit(solution)/shard_map/ppermute | solution.py:372
  46.7 0.0 collective-permute-done.12.refs_4_.refs_11_
  46.7 0.0 collective-permute-done.14.refs_6_.refs_13_
  46.7 1.6 %shard_map.63 = (bf16[4,16,384]{2,1,0:T(8,128)(2,1)S(1)}, bf16[4,16,384]{2,1,0:T(8,128)(2,1)S(1)}, bf16[4,16,384]{2,1,0:T(8,128)(2,1)S(1)}) custom-call(s32[16]{0:T(128)S(1)} %copy-done.8, f32[4,576]{1,0:T(4,128)S(1)} %copy-done.5, bf16[4,4,16,768]{3,2,1,0:T(8,128)(2,1)S(1)} %all-to-all-done.query_ref, ...), custom_call_target="tpu_custom_call" | custom-call | tf_op jit(solution)/shard_map/pallas_call | solution.py:329
  48.3 1.1 %collective-permute-start.16 = (bf16[4,16,384]{2,1,0:T(8,128)(2,1)S(1)}, bf16[4,16,384]{2,1,0:T(8,128)(2,1)S(1)}, u32[]{:S(2)}, u32[]{:S(2)}) collective-permute-start(bf16[4,16,384]{2,1,0:T(8,128)(2,1)S(1)} %get-tuple-element.53), channel_id=1, source_target_pairs={{0,8},{4,12},{8,0},{12,4},{1,9},{5,13},{9,1},{13,5},{2,10},{6,14},... | collective-permute-start | bytes 147464 | tf_op jit(solution)/shard_map/ppermute | solution.py:372
  49.5 0.0 collective-permute-start.17
  49.5 0.0 collective-permute-done.7.refs_1_
  49.5 3.8 %collective-permute-start.15 = (bf16[4,16,384]{2,1,0:T(8,128)(2,1)S(1)}, bf16[4,16,384]{2,1,0:T(8,128)(2,1)S(1)}, u32[]{:S(2)}, u32[]{:S(2)}) collective-permute-start(bf16[4,16,384]{2,1,0:T(8,128)(2,1)S(1)} %get-tuple-element.52.refs_14_), channel_id=1, source_target_pairs={{0,12},{4,0},{8,4},{12,8},{1,13},{5,1},{9,5},{13,9},{2,14},{6,2},{... | collective-permute-start | bytes 147464 | tf_op jit(solution)/shard_map/ppermute | solution.py:372
  53.3 1.7 %shard_map.64.refs_6_ = bf16[4,16,768]{2,1,0:T(8,128)(2,1)S(1)} custom-call(s32[16]{0:T(128)S(1)} %copy-done.8, f32[4,576]{1,0:T(4,128)S(1)} %copy-done.5, bf16[4,4,16,768]{3,2,1,0:T(8,128)(2,1)S(1)} %all-to-all-done.query_ref, bf16[4,16,768]{2,1,0:T(8,128)(2,1)S(1)} %copy-done.3, bf16[4,16,768]{2,1,0:T(8,128)(2,1)S(1)} %collective-permute-done.refs_1_, ...), custom_call_target="tpu_custom_call" | custom-call | tf_op jit(solution)/shard_map/pallas_call | solution.py:329
  55.0 0.0 collective-permute-done.8.refs_2_
  55.0 0.0 collective-permute-done.6.refs_0_
  55.0 0.0 collective-permute-done.16.refs_4_
  55.0 0.3 collective-permute-done.17.refs_5_
  55.4 0.0 collective-permute-done.15.refs_3_
  55.4 0.8 %shard_map.65 = bf16[4,16,3072]{2,1,0:T(8,128)(2,1)} custom-call(bf16[4,16,384]{2,1,0:T(8,128)(2,1)S(1)} %collective-permute-done.6.refs_0_, bf16[4,16,384]{2,1,0:T(8,128)(2,1)S(1)} %collective-permute-done.7.refs_1_, bf16[4,16,384]{2,1,0:T(8,128)(2,1)S(1)} %collective-permute-done.8.refs_2_, bf16[4,16,384]{2,1,0:T(8,128)(2,1)S(1)} %collective-permute-done.15.refs_3_, ...), custom_call_target="tpu_custom_call" | custom-call | tf_op jit(solution)/shard_map/pallas_call | solution.py:360
  (5 shorter events, 0.0 us)
Async XLA Ops:
  1.8 13.5 %collective-permute-start.1 = (bf16[4,16,768]{2,1,0:T(8,128)(2,1)}, bf16[4,16,768]{2,1,0:T(8,128)(2,1)S(1)}, u32[]{:S(2)}, u32[]{:S(2)}) collective-permute-start(bf16[4,16,768]{2,1,0:T(8,128)(2,1)} %get-tuple-element.36), channel_id=1, source_target_pairs={{0,8},{4,12},{8,0},{12,4},{1,9},{5,13},{9,1},{13,5},{2,10},{6,14},... | collective-permute-start | bytes 294920 | tf_op jit(solution)/shard_map/ppermute | solution.py:372
  5.9 6.4 %copy-start.6 = (s32[16,32]{1,0:T(8,128)S(1)}, s32[16,32]{1,0:T(8,128)}, u32[]{:S(2)}) copy-start(s32[16,32]{1,0:T(8,128)} %pair_ref.1) | copy-start | bytes 6148
  5.9 9.4 %copy-start = (bf16[4,16,3072]{2,1,0:T(8,128)(2,1)S(1)}, bf16[4,16,3072]{2,1,0:T(8,128)(2,1)}, u32[]{:S(2)}) copy-start(bf16[4,16,3072]{2,1,0:T(8,128)(2,1)} %refs_0_.7) | copy-start | bytes 1179652
  5.9 9.4 %copy-start.1 = (bf16[4,16,3072]{2,1,0:T(8,128)(2,1)S(1)}, bf16[4,16,3072]{2,1,0:T(8,128)(2,1)}, u32[]{:S(2)}) copy-start(bf16[4,16,3072]{2,1,0:T(8,128)(2,1)} %refs_1_.5) | copy-start | bytes 1179652
  8.4 12.7 %collective-permute-start = (bf16[4,16,768]{2,1,0:T(8,128)(2,1)}, bf16[4,16,768]{2,1,0:T(8,128)(2,1)S(1)}, u32[]{:S(2)}, u32[]{:S(2)}) collective-permute-start(bf16[4,16,768]{2,1,0:T(8,128)(2,1)} %get-tuple-element.35), channel_id=1, source_target_pairs={{0,4},{4,8},{8,12},{12,0},{1,5},{5,9},{9,13},{13,1},{2,6},{6,10},{... | collective-permute-start | bytes 294920 | tf_op jit(solution)/shard_map/ppermute | solution.py:372
  10.1 2.3 %copy-start.7 = (s32[16]{0:T(128)S(1)}, s32[16]{0:T(128)}, u32[]{:S(2)}) copy-start(s32[16]{0:T(128)} %tokens_ref.7) | copy-start | bytes 196
  10.1 11.1 %collective-permute-start.2 = (bf16[4,16,768]{2,1,0:T(8,128)(2,1)}, bf16[4,16,768]{2,1,0:T(8,128)(2,1)S(1)}, u32[]{:S(2)}, u32[]{:S(2)}) collective-permute-start(bf16[4,16,768]{2,1,0:T(8,128)(2,1)} %get-tuple-element.37), channel_id=1, source_target_pairs={{0,12},{4,0},{8,4},{12,8},{1,13},{5,1},{9,5},{13,9},{2,14},{6,2},{... | collective-permute-start | bytes 294920 | tf_op jit(solution)/shard_map/ppermute | solution.py:372
  12.3 0.7 %copy-start.9 = (f32[8,128]{1,0:T(8,128)S(1)}, f32[8,128]{1,0:T(8,128)}, u32[]{:S(2)}) copy-start(f32[8,128]{1,0:T(8,128)} %get-tuple-element.31._) | copy-start | bytes 12292
  15.3 2.0 %copy-start.4 = (f32[4,576]{1,0:T(4,128)}, f32[4,576]{1,0:T(4,128)S(1)}, u32[]{:S(2)}) copy-start(f32[4,576]{1,0:T(4,128)S(1)} %get-tuple-element.32.bias_ref.refs_2_) | copy-start | bytes 27652
  15.3 5.8 %copy-start.3 = (bf16[4,16,768]{2,1,0:T(8,128)(2,1)S(1)}, bf16[4,16,768]{2,1,0:T(8,128)(2,1)}, u32[]{:S(2)}) copy-start(bf16[4,16,768]{2,1,0:T(8,128)(2,1)} %get-tuple-element.34.refs_0_) | copy-start | bytes 294916
  17.2 11.2 %collective-permute-start.9 = (bf16[4,16,768]{2,1,0:T(8,128)(2,1)S(1)}, bf16[4,16,768]{2,1,0:T(8,128)(2,1)S(1)}, u32[]{:S(2)}, u32[]{:S(2)}) collective-permute-start(bf16[4,16,768]{2,1,0:T(8,128)(2,1)S(1)} %get-tuple-element.46), channel_id=1, source_target_pairs={{0,4},{4,8},{8,12},{12,0},{1,5},{5,9},{9,13},{13,1},{2,6},{6,10},{... | collective-permute-start | bytes 294920 | tf_op jit(solution)/shard_map/ppermute | solution.py:372
  17.3 12.9 %collective-permute-start.10 = (bf16[4,16,768]{2,1,0:T(8,128)(2,1)S(1)}, bf16[4,16,768]{2,1,0:T(8,128)(2,1)S(1)}, u32[]{:S(2)}, u32[]{:S(2)}) collective-permute-start(bf16[4,16,768]{2,1,0:T(8,128)(2,1)S(1)} %get-tuple-element.47), channel_id=1, source_target_pairs={{0,8},{4,12},{8,0},{12,4},{1,9},{5,13},{9,1},{13,5},{2,10},{6,14},... | collective-permute-start | bytes 294920 | tf_op jit(solution)/shard_map/ppermute | solution.py:372
  18.5 11.7 %collective-permute-start.11 = (bf16[4,16,768]{2,1,0:T(8,128)(2,1)S(1)}, bf16[4,16,768]{2,1,0:T(8,128)(2,1)S(1)}, u32[]{:S(2)}, u32[]{:S(2)}) collective-permute-start(bf16[4,16,768]{2,1,0:T(8,128)(2,1)S(1)} %get-tuple-element.48), channel_id=1, source_target_pairs={{0,12},{4,0},{8,4},{12,8},{1,13},{5,1},{9,5},{13,9},{2,14},{6,2},{... | collective-permute-start | bytes 294920 | tf_op jit(solution)/shard_map/ppermute | solution.py:372
  21.1 2.2 %copy-start.2 = (bf16[4,16,3072]{2,1,0:T(8,128)(2,1)S(1)}, bf16[4,16,3072]{2,1,0:T(8,128)(2,1)}, u32[]{:S(2)}) copy-start(bf16[4,16,3072]{2,1,0:T(8,128)(2,1)} %refs_0_.6) | copy-start | bytes 1179652
  21.7 9.7 %collective-permute-start.4 = (bf16[1,4,16,768]{3,2,1,0:T(8,128)(2,1)S(1)}, bf16[1,4,16,768]{3,2,1,0:T(8,128)(2,1)S(1)}, u32[]{:S(2)}, u32[]{:S(2)}) collective-permute-start(bf16[1,4,16,768]{3,2,1,0:T(8,128)(2,1)S(1)} %get-tuple-element.40), channel_id=1, source_target_pairs={{0,2},{1,3},{2,0},{3,1},{4,6},{5,7},{6,4},{7,5},{8,10},{9,11},{10,... | collective-permute-start | bytes 294920 | tf_op jit(solution)/shard_map/ppermute | solution.py:372
  23.3 12.1 %collective-permute-start.3 = (bf16[2,4,16,768]{3,2,1,0:T(8,128)(2,1)S(1)}, bf16[2,4,16,768]{3,2,1,0:T(8,128)(2,1)S(1)}, u32[]{:S(2)}, u32[]{:S(2)}) collective-permute-start(bf16[2,4,16,768]{3,2,1,0:T(8,128)(2,1)S(1)} %get-tuple-element.38.refs_1_.refs_4_), channel_id=1, source_target_pairs={{0,1},{1,2},{2,3},{3,0},{4,5},{5,6},{6,7},{7,4},{8,9},{9,10},{10,1... | collective-permute-start | bytes 589832 | tf_op jit(solution)/shard_map/ppermute | solution.py:372
  25.0 16.2 %all-to-all-start = ((bf16[4,4,16,768]{3,2,1,0:T(8,128)(2,1)}), bf16[4,4,16,768]{3,2,1,0:T(8,128)(2,1)S(1)}, u32[]{:S(2)}, u32[]{:S(2)}) async-start(bf16[4,4,16,768]{3,2,1,0:T(8,128)(2,1)} %get-tuple-element.39), calls=%async_computation | async-start | bytes 786432 | tf_op jit(solution)/shard_map/all_to_all | solution.py:421
  28.4 7.0 %collective-permute-start.5 = (bf16[2,4,16,768]{3,2,1,0:T(8,128)(2,1)S(1)}, bf16[2,4,16,768]{3,2,1,0:T(8,128)(2,1)S(1)}, u32[]{:S(2)}, u32[]{:S(2)}) collective-permute-start(bf16[2,4,16,768]{3,2,1,0:T(8,128)(2,1)S(1)} %get-tuple-element.41), channel_id=1, source_target_pairs={{0,3},{1,0},{2,1},{3,2},{4,7},{5,4},{6,5},{7,6},{8,11},{9,8},{10,9... | collective-permute-start | bytes 589832 | tf_op jit(solution)/shard_map/ppermute | solution.py:372
  30.2 10.9 %copy-start.5 = (f32[4,576]{1,0:T(4,128)S(1)}, f32[4,576]{1,0:T(4,128)}, u32[]{:S(2)}) copy-start(f32[4,576]{1,0:T(4,128)} %copy-done.4) | copy-start | bytes 27652
  30.8 14.0 %collective-permute-start.13 = (bf16[1,4,16,768]{3,2,1,0:T(8,128)(2,1)S(1)}, bf16[1,4,16,768]{3,2,1,0:T(8,128)(2,1)S(1)}, u32[]{:S(2)}, u32[]{:S(2)}) collective-permute-start(bf16[1,4,16,768]{3,2,1,0:T(8,128)(2,1)S(1)} %get-tuple-element.50), channel_id=1, source_target_pairs={{0,2},{1,3},{2,0},{3,1},{4,6},{5,7},{6,4},{7,5},{8,10},{9,11},{10,... | collective-permute-start | bytes 294920 | tf_op jit(solution)/shard_map/ppermute | solution.py:372
  31.4 9.7 %copy-start.8 = (s32[16]{0:T(128)S(1)}, s32[16]{0:T(128)}, u32[]{:S(2)}) copy-start(s32[16]{0:T(128)} %tokens_ref.7) | copy-start | bytes 196
  31.4 15.3 %collective-permute-start.12 = (bf16[2,4,16,768]{3,2,1,0:T(8,128)(2,1)S(1)}, bf16[2,4,16,768]{3,2,1,0:T(8,128)(2,1)S(1)}, u32[]{:S(2)}, u32[]{:S(2)}) collective-permute-start(bf16[2,4,16,768]{3,2,1,0:T(8,128)(2,1)S(1)} %get-tuple-element.49), channel_id=1, source_target_pairs={{0,1},{1,2},{2,3},{3,0},{4,5},{5,6},{6,7},{7,4},{8,9},{9,10},{10,1... | collective-permute-start | bytes 589832 | tf_op jit(solution)/shard_map/ppermute | solution.py:372
  31.5 15.3 %collective-permute-start.14 = (bf16[2,4,16,768]{3,2,1,0:T(8,128)(2,1)S(1)}, bf16[2,4,16,768]{3,2,1,0:T(8,128)(2,1)S(1)}, u32[]{:S(2)}, u32[]{:S(2)}) collective-permute-start(bf16[2,4,16,768]{3,2,1,0:T(8,128)(2,1)S(1)} %get-tuple-element.51), channel_id=1, source_target_pairs={{0,3},{1,0},{2,1},{3,2},{4,7},{5,4},{6,5},{7,6},{8,11},{9,8},{10,9... | collective-permute-start | bytes 589832 | tf_op jit(solution)/shard_map/ppermute | solution.py:372
  42.8 6.7 %collective-permute-start.7 = (bf16[4,16,384]{2,1,0:T(8,128)(2,1)S(1)}, bf16[4,16,384]{2,1,0:T(8,128)(2,1)S(1)}, u32[]{:S(2)}, u32[]{:S(2)}) collective-permute-start(bf16[4,16,384]{2,1,0:T(8,128)(2,1)S(1)} %get-tuple-element.43), channel_id=1, source_target_pairs={{0,8},{4,12},{8,0},{12,4},{1,9},{5,13},{9,1},{13,5},{2,10},{6,14},... | collective-permute-start | bytes 147464 | tf_op jit(solution)/shard_map/ppermute | solution.py:372
  42.8 12.2 %collective-permute-start.8 = (bf16[4,16,384]{2,1,0:T(8,128)(2,1)S(1)}, bf16[4,16,384]{2,1,0:T(8,128)(2,1)S(1)}, u32[]{:S(2)}, u32[]{:S(2)}) collective-permute-start(bf16[4,16,384]{2,1,0:T(8,128)(2,1)S(1)} %get-tuple-element.44), channel_id=1, source_target_pairs={{0,4},{4,8},{8,12},{12,0},{1,5},{5,9},{9,13},{13,1},{2,6},{6,10},{... | collective-permute-start | bytes 147464 | tf_op jit(solution)/shard_map/ppermute | solution.py:372
  44.9 10.2 %collective-permute-start.6 = (bf16[4,16,384]{2,1,0:T(8,128)(2,1)S(1)}, bf16[4,16,384]{2,1,0:T(8,128)(2,1)S(1)}, u32[]{:S(2)}, u32[]{:S(2)}) collective-permute-start(bf16[4,16,384]{2,1,0:T(8,128)(2,1)S(1)} %get-tuple-element.42.refs_7_), channel_id=1, source_target_pairs={{0,12},{4,0},{8,4},{12,8},{1,13},{5,1},{9,5},{13,9},{2,14},{6,2},{... | collective-permute-start | bytes 147464 | tf_op jit(solution)/shard_map/ppermute | solution.py:372
  48.3 6.7 %collective-permute-start.16 = (bf16[4,16,384]{2,1,0:T(8,128)(2,1)S(1)}, bf16[4,16,384]{2,1,0:T(8,128)(2,1)S(1)}, u32[]{:S(2)}, u32[]{:S(2)}) collective-permute-start(bf16[4,16,384]{2,1,0:T(8,128)(2,1)S(1)} %get-tuple-element.53), channel_id=1, source_target_pairs={{0,8},{4,12},{8,0},{12,4},{1,9},{5,13},{9,1},{13,5},{2,10},{6,14},... | collective-permute-start | bytes 147464 | tf_op jit(solution)/shard_map/ppermute | solution.py:372
  49.5 5.9 %collective-permute-start.17 = (bf16[4,16,384]{2,1,0:T(8,128)(2,1)S(1)}, bf16[4,16,384]{2,1,0:T(8,128)(2,1)S(1)}, u32[]{:S(2)}, u32[]{:S(2)}) collective-permute-start(bf16[4,16,384]{2,1,0:T(8,128)(2,1)S(1)} %get-tuple-element.54), channel_id=1, source_target_pairs={{0,4},{4,8},{8,12},{12,0},{1,5},{5,9},{9,13},{13,1},{2,6},{6,10},{... | collective-permute-start | bytes 147464 | tf_op jit(solution)/shard_map/ppermute | solution.py:372
  49.5 5.9 %collective-permute-start.15 = (bf16[4,16,384]{2,1,0:T(8,128)(2,1)S(1)}, bf16[4,16,384]{2,1,0:T(8,128)(2,1)S(1)}, u32[]{:S(2)}, u32[]{:S(2)}) collective-permute-start(bf16[4,16,384]{2,1,0:T(8,128)(2,1)S(1)} %get-tuple-element.52.refs_14_), channel_id=1, source_target_pairs={{0,12},{4,0},{8,4},{12,8},{1,13},{5,1},{9,5},{13,9},{2,14},{6,2},{... | collective-permute-start | bytes 147464 | tf_op jit(solution)/shard_map/ppermute | solution.py:372

commit v11 on v9

--- a/solution.py
+++ b/solution.py
@@ -50,7 +50,7 @@
 
 
 def by_distance(refs, count, direction):
-    if len(refs) > 1:
+    if len(refs[0].shape) == 3:
         return list(refs)
     me = lax.axis_index("head")
     return [refs[0].at[lax.rem(me + direction * s + count, count)] for s in range(count)]
@@ -118,8 +118,10 @@
     return NEAR_CAP if distance in (1, count_tm - 1) else FAR_CAP
 
 
-def pick_kernel(count_head, count_tm, lanes, skipped, picks_ref, *refs):
-    pieces, outs = refs[:count_head], refs[count_head + skipped :]
+def pick_kernel(counts, lanes, picks_ref, *refs):
+    count_head, count_tm, own_count, skipped = counts
+    pieces = by_distance(refs[:own_count], count_head, -1)
+    outs = refs[own_count + skipped :]
     shard = lax.axis_index("tm")
     for distance, out in enumerate(outs, 1):
         goal = lax.rem(shard + distance, count_tm)
@@ -129,14 +131,15 @@
                 out[k, s] = pieces[s][pick, :, lanes[0] : lanes[1]]
 
 
-def pick_blocks(picks, pieces, lanes, count_tm, after):
-    count_head = len(pieces)
-    one = (count_head, pieces[0].shape[1], lanes[1] - lanes[0])
+def pick_blocks(picks, pieces, lanes, count_head, count_tm, after):
+    one = (count_head, pieces[0].shape[-2], lanes[1] - lanes[0])
     vmem = pl.BlockSpec(memory_space=pltpu.VMEM)
     return pl.pallas_call(
-        functools.partial(pick_kernel, count_head, count_tm, lanes, len(after)),
+        functools.partial(
+            pick_kernel, (count_head, count_tm, len(pieces), len(after)), lanes
+        ),
         in_specs=[pl.BlockSpec(memory_space=pltpu.SMEM)]
-        + [vmem] * count_head
+        + [vmem] * len(pieces)
         + [pl.BlockSpec(memory_space=pl.ANY)] * len(after),
         out_specs=[vmem] * (count_tm - 1),
         out_shape=[
@@ -257,11 +260,14 @@
 
 
 def attend_kernel(counts, heads_of, distances, tokens_ref, bias_ref, query_ref, *refs):
-    count_head, count_tm = counts
+    count_head, count_tm, own_counts = counts
     queries = by_distance([query_ref], count_head, -1)
-    per_part = count_head + count_tm - 1
-    parts = [refs[p * per_part : (p + 1) * per_part] for p in range(len(heads_of))]
-    outs = refs[len(heads_of) * per_part :][-len(distances) :]
+    parts, at = [], 0
+    for count in own_counts:
+        owns = by_distance(refs[at : at + count], count_head, -1)
+        parts.append((owns, refs[at + count : at + count + count_tm - 1]))
+        at += count + count_tm - 1
+    outs = refs[-len(distances) :]
     blocks, tokens, _ = outs[0].shape
     rows = len(distances) * tokens
     shard = lax.axis_index("tm")
@@ -273,9 +279,10 @@
         p, h = place_of[head]
         first = kind * heads_of[p][1] + h * HD
         lanes = slice(first, first + HD)
-        pieces = [rows_of(own[:, :, lanes]) for own in parts[p][:count_head]]
+        owns, slots = parts[p]
+        pieces = [rows_of(own[:, :, lanes]) for own in owns]
         pieces += [
-            rows_of(parts[p][count_head + distance - 1][k, :, :, lanes])
+            rows_of(slots[distance - 1][k, :, :, lanes])
             for distance, k in remote_rows(count_tm)
         ]
         return jnp.concatenate(pieces, axis=0)
@@ -323,10 +330,11 @@
 def attend(block_tokens, bias, query, parts, heads_of, distances, after=(), cost=NO_COST):
     count_head, count_tm = query.shape[0], len(parts[0][1]) + 1
     operands = [ref for owns, slots in parts for ref in owns + slots]
+    counts = (count_head, count_tm, [len(owns) for owns, _ in parts])
     shape = query.shape[1:3] + (sum(size for _, size in heads_of),)
     vmem = pl.BlockSpec(memory_space=pltpu.VMEM)
     return pl.pallas_call(
-        functools.partial(attend_kernel, (count_head, count_tm), heads_of, distances),
+        functools.partial(attend_kernel, counts, heads_of, distances),
         in_specs=[pl.BlockSpec(memory_space=pltpu.SMEM)]
         + [vmem] * (2 + len(operands))
         + [pl.BlockSpec(memory_space=pl.ANY)] * len(after),
@@ -389,18 +397,19 @@
     parts = [(0, cut), (cut, width_here - cut)] if heads > 1 else [(0, width_here)]
     arrays = [query_rows, key_rows, value_rows]
     messages = [[(1,) + part, (2,) + part] for part in parts]
-    pieces, token = rotate_pieces(arrays, messages[0], count_head, limit=WIDE_VMEM)
-    packed = [pieces]
+    stacked, token = rotate_pieces(
+        arrays, messages[0], count_head, limit=WIDE_VMEM, stacked=True
+    )
+    received = [[lax.all_to_all(stacked[0], "head", split_axis=0, concat_axis=0, tiled=True)]]
     picks, bias = plan(pair_list, block_tokens, token, blocks, count_head, count_tm)
     after = (bias,)
     for message in messages[1:]:
         pieces, token = rotate_pieces(arrays, message, count_head, after)
-        packed.append(pieces)
+        received.append(pieces[:1] + exchange(pieces[1:], 1))
         after = (token,)
-    received = [pieces[:1] + exchange(pieces[1:], 1) for pieces in packed]
     sent, after = [], ()
     for owns, (_, size) in zip(received, parts):
-        sent.append(pick_blocks(picks, owns, (0, 2 * size), count_tm, after))
+        sent.append(pick_blocks(picks, owns, (0, 2 * size), count_head, count_tm, after))
         after = (sent[-1][0],)
     message = [(0, 0, width_here)]
     (query,), _ = rotate_pieces(arrays, message, count_head, (sent[0][0],), stacked=True)

time: 54 us -> 61.8 us (1.14)
  waiting for transfers between devices: 8.35 us -> 13.8 us
  starting transfers between devices: 28.9 us -> 30.4 us
  local copies, waits for them, and re-layouts: 0.74 us -> 1.37 us
    all_to_all x0 -> x1, starting transfers between devices: none -> 6.46 us  [shards(): lax.all_to_all(stacked[0], 'head', split_axis=0, concat_axis=0, tiled=True)]
    all_to_all x0 -> x1, waiting for transfers between devices: none -> 5.49 us  [shards(): lax.all_to_all(stacked[0], 'head', split_axis=0, concat_axis=0, tiled=True)]
    ppermute x18 -> x15, starting transfers between devices: 25.5 us -> 20.5 us  [shifted(): lax.ppermute(array, axis, [(i, (i + distance) % count) for i in range(cou...]
    unnamed x20 -> x18, local copies, waits for them, and re-layouts: 0.74 us -> 1.37 us
    ppermute x18 -> x15, waiting for transfers between devices: 2.58 us -> 2.54 us  [shifted(): lax.ppermute(array, axis, [(i, (i + distance) % count) for i in range(cou...]
  transfers between devices with their start and end apart: 19 -> 17, of which waited for: 3 -> 4; matrix products, arithmetic and copies ran while one was open for 0% -> 0% of each run, Pallas kernels for 22% -> 19%
where the time goes in v11:
time: 61.8 us; the launch traced here: 61.4 us
  starting transfers between devices  30.4 us (49%)
  Pallas kernels  15.6 us (25%)
  waiting for transfers between devices  13.8 us (22%)
  local copies, waits for them, and re-layouts  1.37 us (2%)
    ppermute x15, starting transfers between devices, shifted(): lax.ppermute(array, axis, [(i, (i + distance) % count) for i in range(cou...  20.5 us
    all_to_all x1, starting transfers between devices, shards(): lax.all_to_all(stacked[0], 'head', split_axis=0, concat_axis=0, tiled=True)  6.46 us
    pallas_call x3, Pallas kernels, rotate_pieces(): pl.pallas_call(functools.partial(rotate_kernel, message, sources, count_h...  6.44 us
    all_to_all x1, waiting for transfers between devices, shards(): lax.all_to_all(query, 'head', split_axis=0, concat_axis=0, tiled=True)  5.77 us
    all_to_all x1, waiting for transfers between devices, shards(): lax.all_to_all(stacked[0], 'head', split_axis=0, concat_axis=0, tiled=True)  5.49 us
    pallas_call x3, Pallas kernels, attend(): pl.pallas_call(functools.partial(attend_kernel, counts, heads_of, distanc...  4.95 us
    all_to_all x1, starting transfers between devices, shards(): lax.all_to_all(query, 'head', split_axis=0, concat_axis=0, tiled=True)  3.47 us
    ppermute x15, waiting for transfers between devices, shifted(): lax.ppermute(array, axis, [(i, (i + distance) % count) for i in range(cou...  2.54 us
  transfers between devices with their start and end apart: 17, of which 4 were waited for; matrix products, arithmetic and copies ran while one was open for 0% of the time, Pallas kernels for 19%

profile of v11, /device:TPU:0, one launch (start us, length us, event | category | flops | bytes accessed | tf_op | source)
XLA Modules:
  0.0 61.4 jit_solution(7021377966617214504)
XLA Ops:
  0.0 0.0 copy-start.5
  0.0 2.9 %shard_map.55 = (bf16[4,4,16,768]{3,2,1,0:T(8,128)(2,1)}, f32[8,128]{1,0:T(8,128)}) custom-call(bf16[4,16,3072]{2,1,0:T(8,128)(2,1)} %refs_0_.5, bf16[4,16,3072]{2,1,0:T(8,128)(2,1)} %refs_1_.3), custom_call_target="tpu_custom_call" | custom-call | tf_op jit(solution)/shard_map/pallas_call | solution.py:101
  2.9 0.0 copy-start
  2.9 0.0 copy-start.1
  2.9 6.5 %all-to-all-start = ((bf16[4,4,16,768]{3,2,1,0:T(8,128)(2,1)}), bf16[4,4,16,768]{3,2,1,0:T(8,128)(2,1)S(1)}, u32[]{:S(2)}, u32[]{:S(2)}) async-start(bf16[4,4,16,768]{3,2,1,0:T(8,128)(2,1)} %get-tuple-element.29), calls=%async_computation | async-start | bytes 786432 | tf_op jit(solution)/shard_map/all_to_all | solution.py:403
  9.4 0.0 copy-start.6
  9.4 0.0 copy-done.5
  9.4 0.7 %copy-done.6 = s32[16]{0:T(128)S(1)} copy-done((s32[16]{0:T(128)S(1)}, s32[16]{0:T(128)}, u32[]{:S(2)}) %copy-start.6) | copy-done | bytes 88
  10.0 0.0 copy-start.8
  10.1 0.7 %copy-done.8 = f32[8,128]{1,0:T(8,128)S(1)} copy-done((f32[8,128]{1,0:T(8,128)S(1)}, f32[8,128]{1,0:T(8,128)}, u32[]{:S(2)}) %copy-start.8) | copy-done | bytes 4120
  10.7 2.3 %shard_map.56 = (s32[8]{0:T(128)S(1)}, f32[4,576]{1,0:T(4,128)S(1)}) custom-call(s32[16,32]{1,0:T(8,128)S(1)} %copy-done.5, s32[16]{0:T(128)S(1)} %copy-done.6, f32[8,128]{1,0:T(8,128)S(1)} %copy-done.8), custom_call_target="tpu_custom_call" | custom-call | tf_op jit(solution)/shard_map/pallas_call | solution.py:240
  13.0 0.0 copy-start.3
  13.0 0.0 copy-done
  13.0 0.0 copy-done.1
  13.0 1.9 %shard_map.60 = (bf16[4,16,768]{2,1,0:T(8,128)(2,1)S(1)}, bf16[4,16,768]{2,1,0:T(8,128)(2,1)S(1)}, bf16[4,16,768]{2,1,0:T(8,128)(2,1)S(1)}, bf16[4,16,768]{2,1,0:T(8,128)(2,1)S(1)}, f32[8,128]{1,0:T(8,128)}) custom-call(bf16[4,16,3072]{2,1,0:T(8,128)(2,1)S(1)} %copy-done, bf16[4,16,3072]{2,1,0:T(8,128)(2,1)S(1)} %copy-done.1, ...), custom_call_target="tpu_custom_call" | custom-call | tf_op jit(solution)/shard_map/pallas_call | solution.py:101
  14.9 0.0 copy-done.3
  15.0 2.1 %collective-permute-start.6 = (bf16[4,16,768]{2,1,0:T(8,128)(2,1)S(1)}, bf16[4,16,768]{2,1,0:T(8,128)(2,1)S(1)}, u32[]{:S(2)}, u32[]{:S(2)}) collective-permute-start(bf16[4,16,768]{2,1,0:T(8,128)(2,1)S(1)} %get-tuple-element.38), channel_id=1, source_target_pairs={{0,4},{4,8},{8,12},{12,0},{1,5},{5,9},{9,13},{13,1},{2,6},{6,10},{... | collective-permute-start | bytes 294920 | tf_op jit(solution)/shard_map/ppermute | solution.py:379
  17.0 2.4 %collective-permute-start.7 = (bf16[4,16,768]{2,1,0:T(8,128)(2,1)S(1)}, bf16[4,16,768]{2,1,0:T(8,128)(2,1)S(1)}, u32[]{:S(2)}, u32[]{:S(2)}) collective-permute-start(bf16[4,16,768]{2,1,0:T(8,128)(2,1)S(1)} %get-tuple-element.39), channel_id=1, source_target_pairs={{0,8},{4,12},{8,0},{12,4},{1,9},{5,13},{9,1},{13,5},{2,10},{6,14},... | collective-permute-start | bytes 294920 | tf_op jit(solution)/shard_map/ppermute | solution.py:379
  19.4 1.5 %collective-permute-start.8 = (bf16[4,16,768]{2,1,0:T(8,128)(2,1)S(1)}, bf16[4,16,768]{2,1,0:T(8,128)(2,1)S(1)}, u32[]{:S(2)}, u32[]{:S(2)}) collective-permute-start(bf16[4,16,768]{2,1,0:T(8,128)(2,1)S(1)} %get-tuple-element.40), channel_id=1, source_target_pairs={{0,12},{4,0},{8,4},{12,8},{1,13},{5,1},{9,5},{13,9},{2,14},{6,2},{... | collective-permute-start | bytes 294920 | tf_op jit(solution)/shard_map/ppermute | solution.py:379
  20.9 5.5 %all-to-all-done.refs_0_ = bf16[4,4,16,768]{3,2,1,0:T(8,128)(2,1)S(1)} async-done(((bf16[4,4,16,768]{3,2,1,0:T(8,128)(2,1)}), bf16[4,4,16,768]{3,2,1,0:T(8,128)(2,1)S(1)}, u32[]{:S(2)}, u32[]{:S(2)}) %all-to-all-start) | async-done | bytes 393248 | tf_op jit(solution)/shard_map/all_to_all | solution.py:403
  26.3 0.0 copy-start.2
  26.3 0.6 shard_map.57
  26.9 1.6 %collective-permute-start.1 = (bf16[1,4,16,768]{3,2,1,0:T(8,128)(2,1)S(1)}, bf16[1,4,16,768]{3,2,1,0:T(8,128)(2,1)S(1)}, u32[]{:S(2)}, u32[]{:S(2)}) collective-permute-start(bf16[1,4,16,768]{3,2,1,0:T(8,128)(2,1)S(1)} %get-tuple-element.32), channel_id=1, source_target_pairs={{0,2},{1,3},{2,0},{3,1},{4,6},{5,7},{6,4},{7,5},{8,10},{9,11},{10,... | collective-permute-start | bytes 294920 | tf_op jit(solution)/shard_map/ppermute | solution.py:379
  28.5 0.0 collective-permute-start
  28.5 0.0 copy-done.2
  28.5 1.6 %shard_map.58 = (bf16[4,4,16,768]{3,2,1,0:T(8,128)(2,1)}, f32[8,128]{1,0:T(8,128)}) custom-call(bf16[4,16,3072]{2,1,0:T(8,128)(2,1)S(1)} %copy-done.2, bf16[2,4,16,768]{3,2,1,0:T(8,128)(2,1)S(1)} %get-tuple-element.30.refs_1_.refs_4_), custom_call_target="tpu_custom_call" | custom-call | tf_op jit(solution)/shard_map/pallas_call | solution.py:101
  30.1 3.5 %all-to-all-start.1 = ((bf16[4,4,16,768]{3,2,1,0:T(8,128)(2,1)}), bf16[4,4,16,768]{3,2,1,0:T(8,128)(2,1)S(1)}, u32[]{:S(2)}, u32[]{:S(2)}) async-start(bf16[4,4,16,768]{3,2,1,0:T(8,128)(2,1)} %get-tuple-element.31), calls=%async_computation.1 | async-start | bytes 786432 | tf_op jit(solution)/shard_map/all_to_all | solution.py:416
  33.6 0.0 collective-permute-done.6.refs_1_.refs_5_
  33.6 1.8 %collective-permute-start.2 = (bf16[2,4,16,768]{3,2,1,0:T(8,128)(2,1)S(1)}, bf16[2,4,16,768]{3,2,1,0:T(8,128)(2,1)S(1)}, u32[]{:S(2)}, u32[]{:S(2)}) collective-permute-start(bf16[2,4,16,768]{3,2,1,0:T(8,128)(2,1)S(1)} %get-tuple-element.33), channel_id=1, source_target_pairs={{0,3},{1,0},{2,1},{3,2},{4,7},{5,4},{6,5},{7,6},{8,11},{9,8},{10,9... | collective-permute-start | bytes 589832 | tf_op jit(solution)/shard_map/ppermute | solution.py:379
  35.4 0.0 collective-permute-done.7.refs_2_.refs_6_
  35.4 0.0 collective-permute-done.8.refs_3_.refs_7_
  35.4 0.0 copy-start.4
  35.4 0.6 shard_map.61
  36.0 0.6 collective-permute-start.10
  36.6 0.0 copy-start.7
  36.6 0.0 collective-permute-start.9
  36.6 0.0 collective-permute-done.1.refs_2_
  36.6 1.7 %collective-permute-start.11 = (bf16[2,4,16,768]{3,2,1,0:T(8,128)(2,1)S(1)}, bf16[2,4,16,768]{3,2,1,0:T(8,128)(2,1)S(1)}, u32[]{:S(2)}, u32[]{:S(2)}) collective-permute-start(bf16[2,4,16,768]{3,2,1,0:T(8,128)(2,1)S(1)} %get-tuple-element.43), channel_id=1, source_target_pairs={{0,3},{1,0},{2,1},{3,2},{4,7},{5,4},{6,5},{7,6},{8,11},{9,8},{10,9... | collective-permute-start | bytes 589832 | tf_op jit(solution)/shard_map/ppermute | solution.py:379
  38.4 2.2 %collective-permute-done.2.refs_3_ = bf16[2,4,16,768]{3,2,1,0:T(8,128)(2,1)S(1)} collective-permute-done((bf16[2,4,16,768]{3,2,1,0:T(8,128)(2,1)S(1)}, bf16[2,4,16,768]{3,2,1,0:T(8,128)(2,1)S(1)}, u32[]{:S(2)}, u32[]{:S(2)}) %collective-permute-start.2) | collective-permute-done | bytes 196640 | tf_op jit(solution)/shard_map/ppermute | solution.py:379
  40.6 0.0 collective-permute-done.refs_1_
  40.6 5.8 %all-to-all-done.1.query_ref = bf16[4,4,16,768]{3,2,1,0:T(8,128)(2,1)S(1)} async-done(((bf16[4,4,16,768]{3,2,1,0:T(8,128)(2,1)}), bf16[4,4,16,768]{3,2,1,0:T(8,128)(2,1)S(1)}, u32[]{:S(2)}, u32[]{:S(2)}) %all-to-all-start.1) | async-done | bytes 393248 | tf_op jit(solution)/shard_map/all_to_all | solution.py:416
  46.4 0.0 copy-done.4
  46.4 0.0 copy-done.7
  46.4 1.6 %shard_map.59 = (bf16[4,16,384]{2,1,0:T(8,128)(2,1)S(1)}, bf16[4,16,384]{2,1,0:T(8,128)(2,1)S(1)}, bf16[4,16,384]{2,1,0:T(8,128)(2,1)S(1)}) custom-call(s32[16]{0:T(128)S(1)} %copy-done.7, f32[4,576]{1,0:T(4,128)S(1)} %copy-done.4, bf16[4,4,16,768]{3,2,1,0:T(8,128)(2,1)S(1)} %all-to-all-done.1.query_ref, bf16[4,4,16,768]{3,2,1,0:T(8,128)(2,1)S(1)} %all-to-all-done.refs_0_, ...), custom_call_target="tpu_custom_call" | custom-call | flops 99999997952 | tf_op jit(solution)/shard_map/pallas_call | solution.py:336
  48.0 0.1 collective-permute-start.4
  48.1 2.0 %collective-permute-start.5 = (bf16[4,16,384]{2,1,0:T(8,128)(2,1)S(1)}, bf16[4,16,384]{2,1,0:T(8,128)(2,1)S(1)}, u32[]{:S(2)}, u32[]{:S(2)}) collective-permute-start(bf16[4,16,384]{2,1,0:T(8,128)(2,1)S(1)} %get-tuple-element.36), channel_id=1, source_target_pairs={{0,4},{4,8},{8,12},{12,0},{1,5},{5,9},{9,13},{13,1},{2,6},{6,10},{... | collective-permute-start | bytes 147464 | tf_op jit(solution)/shard_map/ppermute | solution.py:379
  50.1 0.0 collective-permute-done.10.refs_5_.refs_9_
  50.1 1.9 %collective-permute-start.3 = (bf16[4,16,384]{2,1,0:T(8,128)(2,1)S(1)}, bf16[4,16,384]{2,1,0:T(8,128)(2,1)S(1)}, u32[]{:S(2)}, u32[]{:S(2)}) collective-permute-start(bf16[4,16,384]{2,1,0:T(8,128)(2,1)S(1)} %get-tuple-element.34.refs_7_), channel_id=1, source_target_pairs={{0,12},{4,0},{8,4},{12,8},{1,13},{5,1},{9,5},{13,9},{2,14},{6,2},{... | collective-permute-start | bytes 147464 | tf_op jit(solution)/shard_map/ppermute | solution.py:379
  51.9 0.0 collective-permute-done.9.refs_4_.refs_8_
  51.9 0.0 collective-permute-done.11.refs_6_.refs_10_
  51.9 1.6 %shard_map.62 = (bf16[4,16,384]{2,1,0:T(8,128)(2,1)S(1)}, bf16[4,16,384]{2,1,0:T(8,128)(2,1)S(1)}, bf16[4,16,384]{2,1,0:T(8,128)(2,1)S(1)}) custom-call(s32[16]{0:T(128)S(1)} %copy-done.7, f32[4,576]{1,0:T(4,128)S(1)} %copy-done.4, bf16[4,4,16,768]{3,2,1,0:T(8,128)(2,1)S(1)} %all-to-all-done.1.query_ref, ...), custom_call_target="tpu_custom_call" | custom-call | tf_op jit(solution)/shard_map/pallas_call | solution.py:336
  53.5 1.1 %collective-permute-start.13 = (bf16[4,16,384]{2,1,0:T(8,128)(2,1)S(1)}, bf16[4,16,384]{2,1,0:T(8,128)(2,1)S(1)}, u32[]{:S(2)}, u32[]{:S(2)}) collective-permute-start(bf16[4,16,384]{2,1,0:T(8,128)(2,1)S(1)} %get-tuple-element.45), channel_id=1, source_target_pairs={{0,8},{4,12},{8,0},{12,4},{1,9},{5,13},{9,1},{13,5},{2,10},{6,14},... | collective-permute-start | bytes 147464 | tf_op jit(solution)/shard_map/ppermute | solution.py:379
  54.7 0.0 collective-permute-start.14
  54.7 0.0 collective-permute-done.4.refs_1_
  54.7 3.8 %collective-permute-start.12 = (bf16[4,16,384]{2,1,0:T(8,128)(2,1)S(1)}, bf16[4,16,384]{2,1,0:T(8,128)(2,1)S(1)}, u32[]{:S(2)}, u32[]{:S(2)}) collective-permute-start(bf16[4,16,384]{2,1,0:T(8,128)(2,1)S(1)} %get-tuple-element.44.refs_11_), channel_id=1, source_target_pairs={{0,12},{4,0},{8,4},{12,8},{1,13},{5,1},{9,5},{13,9},{2,14},{6,2},{... | collective-permute-start | bytes 147464 | tf_op jit(solution)/shard_map/ppermute | solution.py:379
  58.5 1.7 %shard_map.63.refs_6_ = bf16[4,16,768]{2,1,0:T(8,128)(2,1)S(1)} custom-call(s32[16]{0:T(128)S(1)} %copy-done.7, f32[4,576]{1,0:T(4,128)S(1)} %copy-done.4, bf16[4,4,16,768]{3,2,1,0:T(8,128)(2,1)S(1)} %all-to-all-done.1.query_ref, bf16[4,4,16,768]{3,2,1,0:T(8,128)(2,1)S(1)} %all-to-all-done.refs_0_, bf16[2,4,16,768]{3,2,1,0:T(8,128)(2,1)S(1)} %collective-permute-done.refs_1_, ...), custom_call_target="tpu_custom_call" | custom-call | tf_op jit(solution)/shard_map/pallas_call | solution.py:336
  60.3 0.0 collective-permute-done.5.refs_2_
  60.3 0.0 collective-permute-done.3.refs_0_
  60.3 0.0 collective-permute-done.13.refs_4_
  60.3 0.3 collective-permute-done.14.refs_5_
  60.6 0.0 collective-permute-done.12.refs_3_
  60.6 0.8 %shard_map.64 = bf16[4,16,3072]{2,1,0:T(8,128)(2,1)} custom-call(bf16[4,16,384]{2,1,0:T(8,128)(2,1)S(1)} %collective-permute-done.3.refs_0_, bf16[4,16,384]{2,1,0:T(8,128)(2,1)S(1)} %collective-permute-done.4.refs_1_, bf16[4,16,384]{2,1,0:T(8,128)(2,1)S(1)} %collective-permute-done.5.refs_2_, bf16[4,16,384]{2,1,0:T(8,128)(2,1)S(1)} %collective-permute-done.12.refs_3_, ...), custom_call_target="tpu_custom_call" | custom-call | tf_op jit(solution)/shard_map/pallas_call | solution.py:367
Async XLA Ops:
  0.0 9.4 %copy-start.5 = (s32[16,32]{1,0:T(8,128)S(1)}, s32[16,32]{1,0:T(8,128)}, u32[]{:S(2)}) copy-start(s32[16,32]{1,0:T(8,128)} %pair_ref.1) | copy-start | bytes 6148
  2.9 10.1 %copy-start = (bf16[4,16,3072]{2,1,0:T(8,128)(2,1)S(1)}, bf16[4,16,3072]{2,1,0:T(8,128)(2,1)}, u32[]{:S(2)}) copy-start(bf16[4,16,3072]{2,1,0:T(8,128)(2,1)} %refs_0_.5) | copy-start | bytes 1179652
  2.9 10.1 %copy-start.1 = (bf16[4,16,3072]{2,1,0:T(8,128)(2,1)S(1)}, bf16[4,16,3072]{2,1,0:T(8,128)(2,1)}, u32[]{:S(2)}) copy-start(bf16[4,16,3072]{2,1,0:T(8,128)(2,1)} %refs_1_.3) | copy-start | bytes 1179652
  2.9 23.4 %all-to-all-start = ((bf16[4,4,16,768]{3,2,1,0:T(8,128)(2,1)}), bf16[4,4,16,768]{3,2,1,0:T(8,128)(2,1)S(1)}, u32[]{:S(2)}, u32[]{:S(2)}) async-start(bf16[4,4,16,768]{3,2,1,0:T(8,128)(2,1)} %get-tuple-element.29), calls=%async_computation | async-start | bytes 786432 | tf_op jit(solution)/shard_map/all_to_all | solution.py:403
  9.4 0.7 %copy-start.6 = (s32[16]{0:T(128)S(1)}, s32[16]{0:T(128)}, u32[]{:S(2)}) copy-start(s32[16]{0:T(128)} %tokens_ref.7) | copy-start | bytes 196
  10.0 0.7 %copy-start.8 = (f32[8,128]{1,0:T(8,128)S(1)}, f32[8,128]{1,0:T(8,128)}, u32[]{:S(2)}) copy-start(f32[8,128]{1,0:T(8,128)} %get-tuple-element.26._) | copy-start | bytes 12292
  13.0 1.9 %copy-start.3 = (f32[4,576]{1,0:T(4,128)}, f32[4,576]{1,0:T(4,128)S(1)}, u32[]{:S(2)}) copy-start(f32[4,576]{1,0:T(4,128)S(1)} %get-tuple-element.27.bias_ref.refs_2_) | copy-start | bytes 27652
  15.0 18.7 %collective-permute-start.6 = (bf16[4,16,768]{2,1,0:T(8,128)(2,1)S(1)}, bf16[4,16,768]{2,1,0:T(8,128)(2,1)S(1)}, u32[]{:S(2)}, u32[]{:S(2)}) collective-permute-start(bf16[4,16,768]{2,1,0:T(8,128)(2,1)S(1)} %get-tuple-element.38), channel_id=1, source_target_pairs={{0,4},{4,8},{8,12},{12,0},{1,5},{5,9},{9,13},{13,1},{2,6},{6,10},{... | collective-permute-start | bytes 294920 | tf_op jit(solution)/shard_map/ppermute | solution.py:379
  17.0 18.4 %collective-permute-start.7 = (bf16[4,16,768]{2,1,0:T(8,128)(2,1)S(1)}, bf16[4,16,768]{2,1,0:T(8,128)(2,1)S(1)}, u32[]{:S(2)}, u32[]{:S(2)}) collective-permute-start(bf16[4,16,768]{2,1,0:T(8,128)(2,1)S(1)} %get-tuple-element.39), channel_id=1, source_target_pairs={{0,8},{4,12},{8,0},{12,4},{1,9},{5,13},{9,1},{13,5},{2,10},{6,14},... | collective-permute-start | bytes 294920 | tf_op jit(solution)/shard_map/ppermute | solution.py:379
  19.4 16.0 %collective-permute-start.8 = (bf16[4,16,768]{2,1,0:T(8,128)(2,1)S(1)}, bf16[4,16,768]{2,1,0:T(8,128)(2,1)S(1)}, u32[]{:S(2)}, u32[]{:S(2)}) collective-permute-start(bf16[4,16,768]{2,1,0:T(8,128)(2,1)S(1)} %get-tuple-element.40), channel_id=1, source_target_pairs={{0,12},{4,0},{8,4},{12,8},{1,13},{5,1},{9,5},{13,9},{2,14},{6,2},{... | collective-permute-start | bytes 294920 | tf_op jit(solution)/shard_map/ppermute | solution.py:379
  26.3 2.2 %copy-start.2 = (bf16[4,16,3072]{2,1,0:T(8,128)(2,1)S(1)}, bf16[4,16,3072]{2,1,0:T(8,128)(2,1)}, u32[]{:S(2)}) copy-start(bf16[4,16,3072]{2,1,0:T(8,128)(2,1)} %refs_0_.4) | copy-start | bytes 1179652
  26.9 9.7 %collective-permute-start.1 = (bf16[1,4,16,768]{3,2,1,0:T(8,128)(2,1)S(1)}, bf16[1,4,16,768]{3,2,1,0:T(8,128)(2,1)S(1)}, u32[]{:S(2)}, u32[]{:S(2)}) collective-permute-start(bf16[1,4,16,768]{3,2,1,0:T(8,128)(2,1)S(1)} %get-tuple-element.32), channel_id=1, source_target_pairs={{0,2},{1,3},{2,0},{3,1},{4,6},{5,7},{6,4},{7,5},{8,10},{9,11},{10,... | collective-permute-start | bytes 294920 | tf_op jit(solution)/shard_map/ppermute | solution.py:379
  28.5 12.1 %collective-permute-start = (bf16[2,4,16,768]{3,2,1,0:T(8,128)(2,1)S(1)}, bf16[2,4,16,768]{3,2,1,0:T(8,128)(2,1)S(1)}, u32[]{:S(2)}, u32[]{:S(2)}) collective-permute-start(bf16[2,4,16,768]{3,2,1,0:T(8,128)(2,1)S(1)} %get-tuple-element.30.refs_1_.refs_4_), channel_id=1, source_target_pairs={{0,1},{1,2},{2,3},{3,0},{4,5},{5,6},{6,7},{7,4},{8,9},{9,10},{10,1... | collective-permute-start | bytes 589832 | tf_op jit(solution)/shard_map/ppermute | solution.py:379
  30.1 16.2 %all-to-all-start.1 = ((bf16[4,4,16,768]{3,2,1,0:T(8,128)(2,1)}), bf16[4,4,16,768]{3,2,1,0:T(8,128)(2,1)S(1)}, u32[]{:S(2)}, u32[]{:S(2)}) async-start(bf16[4,4,16,768]{3,2,1,0:T(8,128)(2,1)} %get-tuple-element.31), calls=%async_computation.1 | async-start | bytes 786432 | tf_op jit(solution)/shard_map/all_to_all | solution.py:416
  33.6 7.0 %collective-permute-start.2 = (bf16[2,4,16,768]{3,2,1,0:T(8,128)(2,1)S(1)}, bf16[2,4,16,768]{3,2,1,0:T(8,128)(2,1)S(1)}, u32[]{:S(2)}, u32[]{:S(2)}) collective-permute-start(bf16[2,4,16,768]{3,2,1,0:T(8,128)(2,1)S(1)} %get-tuple-element.33), channel_id=1, source_target_pairs={{0,3},{1,0},{2,1},{3,2},{4,7},{5,4},{6,5},{7,6},{8,11},{9,8},{10,9... | collective-permute-start | bytes 589832 | tf_op jit(solution)/shard_map/ppermute | solution.py:379
  35.4 10.9 %copy-start.4 = (f32[4,576]{1,0:T(4,128)S(1)}, f32[4,576]{1,0:T(4,128)}, u32[]{:S(2)}) copy-start(f32[4,576]{1,0:T(4,128)} %copy-done.3) | copy-start | bytes 27652
  36.0 14.0 %collective-permute-start.10 = (bf16[1,4,16,768]{3,2,1,0:T(8,128)(2,1)S(1)}, bf16[1,4,16,768]{3,2,1,0:T(8,128)(2,1)S(1)}, u32[]{:S(2)}, u32[]{:S(2)}) collective-permute-start(bf16[1,4,16,768]{3,2,1,0:T(8,128)(2,1)S(1)} %get-tuple-element.42), channel_id=1, source_target_pairs={{0,2},{1,3},{2,0},{3,1},{4,6},{5,7},{6,4},{7,5},{8,10},{9,11},{10,... | collective-permute-start | bytes 294920 | tf_op jit(solution)/shard_map/ppermute | solution.py:379
  36.6 9.7 %copy-start.7 = (s32[16]{0:T(128)S(1)}, s32[16]{0:T(128)}, u32[]{:S(2)}) copy-start(s32[16]{0:T(128)} %tokens_ref.7) | copy-start | bytes 196
  36.6 15.3 %collective-permute-start.9 = (bf16[2,4,16,768]{3,2,1,0:T(8,128)(2,1)S(1)}, bf16[2,4,16,768]{3,2,1,0:T(8,128)(2,1)S(1)}, u32[]{:S(2)}, u32[]{:S(2)}) collective-permute-start(bf16[2,4,16,768]{3,2,1,0:T(8,128)(2,1)S(1)} %get-tuple-element.41), channel_id=1, source_target_pairs={{0,1},{1,2},{2,3},{3,0},{4,5},{5,6},{6,7},{7,4},{8,9},{9,10},{10,1... | collective-permute-start | bytes 589832 | tf_op jit(solution)/shard_map/ppermute | solution.py:379
  36.6 15.3 %collective-permute-start.11 = (bf16[2,4,16,768]{3,2,1,0:T(8,128)(2,1)S(1)}, bf16[2,4,16,768]{3,2,1,0:T(8,128)(2,1)S(1)}, u32[]{:S(2)}, u32[]{:S(2)}) collective-permute-start(bf16[2,4,16,768]{3,2,1,0:T(8,128)(2,1)S(1)} %get-tuple-element.43), channel_id=1, source_target_pairs={{0,3},{1,0},{2,1},{3,2},{4,7},{5,4},{6,5},{7,6},{8,11},{9,8},{10,9... | collective-permute-start | bytes 589832 | tf_op jit(solution)/shard_map/ppermute | solution.py:379
  48.0 6.7 %collective-permute-start.4 = (bf16[4,16,384]{2,1,0:T(8,128)(2,1)S(1)}, bf16[4,16,384]{2,1,0:T(8,128)(2,1)S(1)}, u32[]{:S(2)}, u32[]{:S(2)}) collective-permute-start(bf16[4,16,384]{2,1,0:T(8,128)(2,1)S(1)} %get-tuple-element.35), channel_id=1, source_target_pairs={{0,8},{4,12},{8,0},{12,4},{1,9},{5,13},{9,1},{13,5},{2,10},{6,14},... | collective-permute-start | bytes 147464 | tf_op jit(solution)/shard_map/ppermute | solution.py:379
  48.1 12.2 %collective-permute-start.5 = (bf16[4,16,384]{2,1,0:T(8,128)(2,1)S(1)}, bf16[4,16,384]{2,1,0:T(8,128)(2,1)S(1)}, u32[]{:S(2)}, u32[]{:S(2)}) collective-permute-start(bf16[4,16,384]{2,1,0:T(8,128)(2,1)S(1)} %get-tuple-element.36), channel_id=1, source_target_pairs={{0,4},{4,8},{8,12},{12,0},{1,5},{5,9},{9,13},{13,1},{2,6},{6,10},{... | collective-permute-start | bytes 147464 | tf_op jit(solution)/shard_map/ppermute | solution.py:379
  50.1 10.2 %collective-permute-start.3 = (bf16[4,16,384]{2,1,0:T(8,128)(2,1)S(1)}, bf16[4,16,384]{2,1,0:T(8,128)(2,1)S(1)}, u32[]{:S(2)}, u32[]{:S(2)}) collective-permute-start(bf16[4,16,384]{2,1,0:T(8,128)(2,1)S(1)} %get-tuple-element.34.refs_7_), channel_id=1, source_target_pairs={{0,12},{4,0},{8,4},{12,8},{1,13},{5,1},{9,5},{13,9},{2,14},{6,2},{... | collective-permute-start | bytes 147464 | tf_op jit(solution)/shard_map/ppermute | solution.py:379
  53.5 6.7 %collective-permute-start.13 = (bf16[4,16,384]{2,1,0:T(8,128)(2,1)S(1)}, bf16[4,16,384]{2,1,0:T(8,128)(2,1)S(1)}, u32[]{:S(2)}, u32[]{:S(2)}) collective-permute-start(bf16[4,16,384]{2,1,0:T(8,128)(2,1)S(1)} %get-tuple-element.45), channel_id=1, source_target_pairs={{0,8},{4,12},{8,0},{12,4},{1,9},{5,13},{9,1},{13,5},{2,10},{6,14},... | collective-permute-start | bytes 147464 | tf_op jit(solution)/shard_map/ppermute | solution.py:379
  54.7 5.9 %collective-permute-start.14 = (bf16[4,16,384]{2,1,0:T(8,128)(2,1)S(1)}, bf16[4,16,384]{2,1,0:T(8,128)(2,1)S(1)}, u32[]{:S(2)}, u32[]{:S(2)}) collective-permute-start(bf16[4,16,384]{2,1,0:T(8,128)(2,1)S(1)} %get-tuple-element.46), channel_id=1, source_target_pairs={{0,4},{4,8},{8,12},{12,0},{1,5},{5,9},{9,13},{13,1},{2,6},{6,10},{... | collective-permute-start | bytes 147464 | tf_op jit(solution)/shard_map/ppermute | solution.py:379
  54.7 5.9 %collective-permute-start.12 = (bf16[4,16,384]{2,1,0:T(8,128)(2,1)S(1)}, bf16[4,16,384]{2,1,0:T(8,128)(2,1)S(1)}, u32[]{:S(2)}, u32[]{:S(2)}) collective-permute-start(bf16[4,16,384]{2,1,0:T(8,128)(2,1)S(1)} %get-tuple-element.44.refs_11_), channel_id=1, source_target_pairs={{0,12},{4,0},{8,4},{12,8},{1,13},{5,1},{9,5},{13,9},{2,14},{6,2},{... | collective-permute-start | bytes 147464 | tf_op jit(solution)/shard_map/ppermute | solution.py:379

commit v12 on v9

--- a/solution.py
+++ b/solution.py
@@ -50,20 +50,32 @@
 
 
 def by_distance(refs, count, direction):
-    if len(refs) > 1:
+    if len(refs[0].shape) == 3:
         return list(refs)
     me = lax.axis_index("head")
     return [refs[0].at[lax.rem(me + direction * s + count, count)] for s in range(count)]
 
 
-def rotate_kernel(message, sources, count_head, skipped, *refs):
+def rotated(block, sign):
+    blocks, tokens, size = block.shape
+    flat = rows_of(block)
+    heads = [flat[:, at : at + HD] for at in range(0, size, HD)]
+    turned = jnp.dot(jnp.concatenate(heads, axis=0), sign, preferred_element_type=jnp.float32)
+    return (turned * ROTATE_SCALE).reshape(size // HD, blocks, tokens, HD).astype(jnp.bfloat16)
+
+
+def store_heads(out, start, turned):
+    for h in range(turned.shape[0]):
+        at = start + h * HD
+        out[:, :, at : at + HD] = turned[h]
+
+
+def rotate_kernel(message, sources, count_head, *refs):
     fields, total = fields_of(message)
     ins = dict(zip(sources, refs))
-    outs = by_distance(refs[len(sources) + skipped : -3], count_head, 1)
-    token, buffer, sems = refs[-3:]
+    outs, (token, buffer, sems) = refs[len(sources) : -3], refs[-3:]
     token[...] = jnp.zeros_like(token)
-    blocks, tokens, width = refs[0].shape
-    width_here = width // count_head
+    width_here = refs[0].shape[2] // count_head
     me = lax.axis_index("head")
     order = list(range(1, count_head)) + [0]
     copies = {}
@@ -81,36 +93,57 @@
     for s in order:
         for f, (_, _, size, start) in enumerate(fields):
             copies[s, f].wait()
-            flat = rows_of(buffer[s, :, :, start : start + size])
-            heads = [flat[:, at : at + HD] for at in range(0, size, HD)]
-            turned = jnp.dot(
-                jnp.concatenate(heads, axis=0), sign, preferred_element_type=jnp.float32
-            )
-            turned = (turned * ROTATE_SCALE).reshape(size // HD, blocks, tokens, HD)
-            for h in range(size // HD):
-                at = start + h * HD
-                outs[s][:, :, at : at + HD] = turned[h].astype(jnp.bfloat16)
-
-
-def rotate_pieces(arrays, message, count_head, after=(), limit=VMEM, stacked=False):
+            store_heads(outs[s], start, rotated(buffer[s, :, :, start : start + size], sign))
+
+
+def rotate_here(fields, ins, outs, distances, count_head, sign):
+    width_here = next(iter(ins.values())).shape[2] // count_head
+    me = lax.axis_index("head")
+    for s in distances:
+        goal = lax.rem(me + s, count_head)
+        for source, start, size, at in fields:
+            column = pl.multiple_of(goal * width_here + start, HD)
+            store_heads(outs[s], at, rotated(ins[source][:, :, pl.ds(column, size)], sign))
+
+
+def stack_kernel(message, source, count_head, source_ref, _, out_ref):
+    outs = by_distance([out_ref], count_head, 1)
+    fields, _ = fields_of(message)
+    places = range(count_head)
+    rotate_here(fields, {source: source_ref}, outs, places, count_head, sign_matrix())
+
+
+def rotate_stacked(arrays, message, count_head, after):
+    blocks, tokens, _ = arrays[0].shape
+    source, total = message[0][0], fields_of(message)[1]
+    vmem = pl.BlockSpec(memory_space=pltpu.VMEM)
+    return pl.pallas_call(
+        functools.partial(stack_kernel, message, source, count_head),
+        in_specs=[vmem, pl.BlockSpec(memory_space=pl.ANY)],
+        out_specs=vmem,
+        out_shape=jax.ShapeDtypeStruct((count_head, blocks, tokens, total), jnp.bfloat16),
+        cost_estimate=NO_COST,
+        compiler_params=pltpu.CompilerParams(vmem_limit_bytes=VMEM),
+    )(arrays[source], after)
+
+
+def rotate_pieces(arrays, message, count_head):
     blocks, tokens, _ = arrays[0].shape
     fields, total = fields_of(message)
     sources = sorted({source for source, _, _ in message})
     one = (blocks, tokens, total)
-    shapes = [(count_head,) + one] if stacked else [one] * count_head
     *pieces, token = pl.pallas_call(
-        functools.partial(rotate_kernel, message, sources, count_head, len(after)),
-        in_specs=[pl.BlockSpec(memory_space=pltpu.HBM)] * len(sources)
-        + [pl.BlockSpec(memory_space=pl.ANY)] * len(after),
-        out_specs=[pl.BlockSpec(memory_space=pltpu.VMEM)] * (len(shapes) + 1),
-        out_shape=[jax.ShapeDtypeStruct(shape, jnp.bfloat16) for shape in shapes] + [TOKEN],
+        functools.partial(rotate_kernel, message, sources, count_head),
+        in_specs=[pl.BlockSpec(memory_space=pltpu.HBM)] * len(sources),
+        out_specs=[pl.BlockSpec(memory_space=pltpu.VMEM)] * (count_head + 1),
+        out_shape=[jax.ShapeDtypeStruct(one, jnp.bfloat16)] * count_head + [TOKEN],
         scratch_shapes=[
             pltpu.VMEM((count_head,) + one, jnp.bfloat16),
             pltpu.SemaphoreType.DMA((count_head, len(fields))),
         ],
         cost_estimate=NO_COST,
-        compiler_params=pltpu.CompilerParams(vmem_limit_bytes=limit),
-    )(*[arrays[source] for source in sources], *after)
+        compiler_params=pltpu.CompilerParams(vmem_limit_bytes=WIDE_VMEM),
+    )(*[arrays[source] for source in sources])
     return pieces, token
 
 
@@ -162,7 +195,25 @@
     return lax.div(value, by), lax.rem(value, by)
 
 
-def plan_kernel(count_head, count_tm, blocks, pair_ref, tokens_ref, _, picks_ref, bias_ref, named_ref, table_ref, sem):
+def plan_kernel(messages, count_head, count_tm, blocks, *refs):
+    key_ref, value_ref, pair_hbm, tokens_ref, _ = refs[:5]
+    picks_ref, bias_ref = refs[5:7]
+    pair_ref, named_ref, table_ref, pair_sem, table_sem = refs[-5:]
+    outs = refs[7:-5]
+    ins = {1: key_ref, 2: value_ref}
+    pair_copy = pltpu.make_async_copy(pair_hbm, pair_ref, pair_sem)
+    pair_copy.start()
+    sign = sign_matrix()
+    places = list(range(1, count_head)) + [0]
+    jobs = [
+        (fields_of(message)[0], outs[m * count_head : (m + 1) * count_head], s)
+        for m, message in enumerate(messages)
+        for s in places
+    ]
+    half = len(jobs) // 2
+    for fields, pieces, s in jobs[:half]:
+        rotate_here(fields, ins, pieces, [s], count_head, sign)
+    pair_copy.wait()
     total_blocks, columns = pair_ref.shape
     pairs = pair_ref[...]
     lane = lax.broadcasted_iota(jnp.int32, named_ref.shape, 1)
@@ -170,8 +221,10 @@
     for c in range(columns):
         named = jnp.where(pairs[:, c : c + 1] == lane, 1, named)
     named_ref[...] = named
-    copy = pltpu.make_async_copy(named_ref, table_ref, sem)
+    copy = pltpu.make_async_copy(named_ref, table_ref, table_sem)
     copy.start()
+    for fields, pieces, s in jobs[half:]:
+        rotate_here(fields, ins, pieces, [s], count_head, sign)
     copy.wait()
     shard = lax.axis_index("tm")
     place = lax.axis_index("head")
@@ -230,30 +283,39 @@
     bias_ref[...] = jnp.where(position < limit, 0.0, NEG)
 
 
-def plan(pair_list, block_tokens, after, blocks, count_head, count_tm):
-    total_blocks = pair_list.shape[0]
+def plan(arrays, messages, pair_list, block_tokens, after, count_head, count_tm):
+    blocks, tokens, _ = arrays[0].shape
+    total_blocks, columns = pair_list.shape
     lanes = -(-total_blocks // 128) * 128
     total = (blocks + len(remote_rows(count_tm))) * BLK
-    return pl.pallas_call(
-        functools.partial(plan_kernel, count_head, count_tm, blocks),
-        in_specs=[
-            pl.BlockSpec(memory_space=pltpu.VMEM),
-            pl.BlockSpec(memory_space=pltpu.SMEM),
-            pl.BlockSpec(memory_space=pl.ANY),
-        ],
-        out_specs=[pl.BlockSpec(memory_space=pltpu.SMEM), pl.BlockSpec(memory_space=pltpu.VMEM)],
+    vmem = pl.BlockSpec(memory_space=pltpu.VMEM)
+    smem = pl.BlockSpec(memory_space=pltpu.SMEM)
+    shapes = [
+        jax.ShapeDtypeStruct((blocks, tokens, fields_of(message)[1]), jnp.bfloat16)
+        for message in messages
+        for _ in range(count_head)
+    ]
+    picks, bias, *pieces = pl.pallas_call(
+        functools.partial(plan_kernel, messages, count_head, count_tm, blocks),
+        in_specs=[vmem, vmem, pl.BlockSpec(memory_space=pl.ANY), smem]
+        + [pl.BlockSpec(memory_space=pl.ANY)],
+        out_specs=[smem, vmem] + [vmem] * len(shapes),
         out_shape=[
             jax.ShapeDtypeStruct((NEAR_CAP * count_tm,), jnp.int32),
             jax.ShapeDtypeStruct((blocks, total), jnp.float32),
-        ],
+        ]
+        + shapes,
         scratch_shapes=[
+            pltpu.VMEM((total_blocks, columns), jnp.int32),
             pltpu.VMEM((total_blocks, lanes), jnp.int32),
             pltpu.SMEM((total_blocks, lanes), jnp.int32),
+            pltpu.SemaphoreType.DMA,
             pltpu.SemaphoreType.DMA,
         ],
         cost_estimate=NO_COST,
         compiler_params=pltpu.CompilerParams(vmem_limit_bytes=VMEM),
-    )(pair_list, block_tokens, after)
+    )(arrays[1], arrays[2], pair_list, block_tokens, after)
+    return picks, bias, [pieces[at : at + count_head] for at in range(0, len(pieces), count_head)]
 
 
 def attend_kernel(counts, heads_of, distances, tokens_ref, bias_ref, query_ref, *refs):
@@ -389,21 +451,17 @@
     parts = [(0, cut), (cut, width_here - cut)] if heads > 1 else [(0, width_here)]
     arrays = [query_rows, key_rows, value_rows]
     messages = [[(1,) + part, (2,) + part] for part in parts]
-    pieces, token = rotate_pieces(arrays, messages[0], count_head, limit=WIDE_VMEM)
-    packed = [pieces]
-    picks, bias = plan(pair_list, block_tokens, token, blocks, count_head, count_tm)
-    after = (bias,)
-    for message in messages[1:]:
-        pieces, token = rotate_pieces(arrays, message, count_head, after)
-        packed.append(pieces)
-        after = (token,)
-    received = [pieces[:1] + exchange(pieces[1:], 1) for pieces in packed]
+    pieces, token = rotate_pieces(arrays, messages[0], count_head)
+    picks, bias, later = plan(
+        arrays, messages[1:], pair_list, block_tokens, token, count_head, count_tm
+    )
+    received = [piece[:1] + exchange(piece[1:], 1) for piece in [pieces] + later]
     sent, after = [], ()
     for owns, (_, size) in zip(received, parts):
         sent.append(pick_blocks(picks, owns, (0, 2 * size), count_tm, after))
         after = (sent[-1][0],)
     message = [(0, 0, width_here)]
-    (query,), _ = rotate_pieces(arrays, message, count_head, (sent[0][0],), stacked=True)
+    query = rotate_stacked(arrays, message, count_head, sent[0][0])
     query = lax.all_to_all(query, "head", split_axis=0, concat_axis=0, tiled=True)
     inputs = [(owns, forward(picked)) for owns, picked in zip(received, sent)]
     distances, after = list(range(1, count_head)), ()

time: 54 us -> 56.6 us (1.048)
  starting transfers between devices: 28.9 us -> 33.7 us
  Pallas kernels: 15.5 us -> 13.3 us
    all_to_all x1, starting transfers between devices: 3.47 us -> 8.56 us  [shards(): lax.all_to_all(query, 'head', split_axis=0, concat_axis=0, tiled=True)]
    pallas_call x3 -> x1, Pallas kernels: 6.4 us -> 2.86 us  [rotate_pieces(): pl.pallas_call(functools.partial(rotate_kernel, message, sources, count_h...]
    pallas_call x1 -> x2, Pallas kernels: 2.25 us -> 3.55 us  [the longest x1 2.52 us: plan(): pl.pallas_call(functools.partial(plan_kernel, messages, count_head, count...]
  transfers between devices with their start and end apart: 19 -> 19, of which waited for: 3 -> 3; matrix products, arithmetic and copies ran while one was open for 0% -> 0% of each run, Pallas kernels for 22% -> 17%
where the time goes in v12:
time: 56.6 us; the launch traced here: 56.3 us
  starting transfers between devices  33.7 us (60%)
  Pallas kernels  13.3 us (23%)
  waiting for transfers between devices  8.45 us (15%)
  local copies, waits for them, and re-layouts  0.72 us (1%)
    ppermute x18, starting transfers between devices, shifted(): lax.ppermute(array, axis, [(i, (i + distance) % count) for i in range(cou...  25.1 us
    all_to_all x1, starting transfers between devices, shards(): lax.all_to_all(query, 'head', split_axis=0, concat_axis=0, tiled=True)  8.56 us
    all_to_all x1, waiting for transfers between devices, shards(): lax.all_to_all(query, 'head', split_axis=0, concat_axis=0, tiled=True)  5.84 us
    pallas_call x3, Pallas kernels, attend(): pl.pallas_call(functools.partial(attend_kernel, (count_head, count_tm), h...  4.91 us
    pallas_call x1, Pallas kernels, rotate_pieces(): pl.pallas_call(functools.partial(rotate_kernel, message, sources, count_h...  2.86 us
    ppermute x18, waiting for transfers between devices, shifted(): lax.ppermute(array, axis, [(i, (i + distance) % count) for i in range(cou...  2.61 us
    pallas_call x1, Pallas kernels, plan(): pl.pallas_call(functools.partial(plan_kernel, messages, count_head, count...  2.52 us
    pallas_call x2, Pallas kernels, pick_blocks(): pl.pallas_call(functools.partial(pick_kernel, count_head, count_tm, lanes...  1.18 us
  transfers between devices with their start and end apart: 19, of which 3 were waited for; matrix products, arithmetic and copies ran while one was open for 0% of the time, Pallas kernels for 17%

profile of v12, /device:TPU:0, one launch (start us, length us, event | category | flops | bytes accessed | tf_op | source)
XLA Modules:
  0.0 56.3 jit_solution(14519445486930831269)
XLA Ops:
  0.0 0.0 copy-start.1
  0.0 0.0 copy-start
  0.0 2.9 %shard_map.55 = (bf16[4,16,768]{2,1,0:T(8,128)(2,1)}, bf16[4,16,768]{2,1,0:T(8,128)(2,1)}, bf16[4,16,768]{2,1,0:T(8,128)(2,1)}, bf16[4,16,768]{2,1,0:T(8,128)(2,1)}, f32[8,128]{1,0:T(8,128)}) custom-call(bf16[4,16,3072]{2,1,0:T(8,128)(2,1)} %refs_0_.3, bf16[4,16,3072]{2,1,0:T(8,128)(2,1)} %refs_1_.3), custom_call_target="tpu_custom_call" | custom-call | tf_op jit(solution)/shard_map/pallas_call | solution.py:135
  2.9 0.0 copy-start.7
  2.9 3.1 %collective-permute-start = (bf16[4,16,768]{2,1,0:T(8,128)(2,1)}, bf16[4,16,768]{2,1,0:T(8,128)(2,1)S(1)}, u32[]{:S(2)}, u32[]{:S(2)}) collective-permute-start(bf16[4,16,768]{2,1,0:T(8,128)(2,1)} %get-tuple-element.32), channel_id=1, source_target_pairs={{0,4},{4,8},{8,12},{12,0},{1,5},{5,9},{9,13},{13,1},{2,6},{6,10},{... | collective-permute-start | bytes 294920 | tf_op jit(solution)/shard_map/ppermute | solution.py:433
  6.0 2.6 %collective-permute-start.1 = (bf16[4,16,768]{2,1,0:T(8,128)(2,1)}, bf16[4,16,768]{2,1,0:T(8,128)(2,1)S(1)}, u32[]{:S(2)}, u32[]{:S(2)}) collective-permute-start(bf16[4,16,768]{2,1,0:T(8,128)(2,1)} %get-tuple-element.33), channel_id=1, source_target_pairs={{0,8},{4,12},{8,0},{12,4},{1,9},{5,13},{9,1},{13,5},{2,10},{6,14},... | collective-permute-start | bytes 294920 | tf_op jit(solution)/shard_map/ppermute | solution.py:433
  8.5 0.0 copy-start.5
  8.6 1.3 %collective-permute-start.2 = (bf16[4,16,768]{2,1,0:T(8,128)(2,1)}, bf16[4,16,768]{2,1,0:T(8,128)(2,1)S(1)}, u32[]{:S(2)}, u32[]{:S(2)}) collective-permute-start(bf16[4,16,768]{2,1,0:T(8,128)(2,1)} %get-tuple-element.34), channel_id=1, source_target_pairs={{0,12},{4,0},{8,4},{12,8},{1,13},{5,1},{9,5},{13,9},{2,14},{6,2},{... | collective-permute-start | bytes 294920 | tf_op jit(solution)/shard_map/ppermute | solution.py:433
  9.9 0.0 copy-done.1
  9.9 0.0 copy-done
  9.9 0.0 copy-done.7
  9.9 0.0 copy-done.5
  9.9 0.0 copy-start.4
  9.9 0.7 %copy-done.4 = s32[16,32]{1,0:T(8,128)S(1)} copy-done((s32[16,32]{1,0:T(8,128)S(1)}, s32[16,32]{1,0:T(8,128)}, u32[]{:S(2)}) %copy-start.4) | copy-done | bytes 2072
  10.6 0.0 copy-start.3
  10.6 2.5 %shard_map.56 = (s32[8]{0:T(128)S(1)}, f32[4,576]{1,0:T(4,128)S(1)}, bf16[4,16,768]{2,1,0:T(8,128)(2,1)S(1)}, bf16[4,16,768]{2,1,0:T(8,128)(2,1)S(1)}, bf16[4,16...) custom-call(bf16[4,16,3072]{2,1,0:T(8,128)(2,1)S(1)} %copy-done, bf16[4,16,3072]{2,1,0:T(8,128)(2,1)S(1)} %copy-done.1, ...), custom_call_target="tpu_custom_call" | custom-call | tf_op jit(solution)/shard_map/pallas_call | solution.py:298
  13.1 0.7 %collective-permute-start.9 = (bf16[4,16,768]{2,1,0:T(8,128)(2,1)S(1)}, bf16[4,16,768]{2,1,0:T(8,128)(2,1)S(1)}, u32[]{:S(2)}, u32[]{:S(2)}) collective-permute-start(bf16[4,16,768]{2,1,0:T(8,128)(2,1)S(1)} %get-tuple-element.42), channel_id=1, source_target_pairs={{0,4},{4,8},{8,12},{12,0},{1,5},{5,9},{9,13},{13,1},{2,6},{6,10},{... | collective-permute-start | bytes 294920 | tf_op jit(solution)/shard_map/ppermute | solution.py:433
  13.9 0.5 collective-permute-start.10
  14.4 0.0 collective-permute-done.refs_1_
  14.4 2.6 %collective-permute-start.11 = (bf16[4,16,768]{2,1,0:T(8,128)(2,1)S(1)}, bf16[4,16,768]{2,1,0:T(8,128)(2,1)S(1)}, u32[]{:S(2)}, u32[]{:S(2)}) collective-permute-start(bf16[4,16,768]{2,1,0:T(8,128)(2,1)S(1)} %get-tuple-element.44), channel_id=1, source_target_pairs={{0,12},{4,0},{8,4},{12,8},{1,13},{5,1},{9,5},{13,9},{2,14},{6,2},{... | collective-permute-start | bytes 294920 | tf_op jit(solution)/shard_map/ppermute | solution.py:433
  17.0 0.0 collective-permute-done.1.refs_2_
  17.0 0.0 collective-permute-done.2.refs_3_
  17.0 0.0 copy-done.3
  17.0 0.0 copy-start.2
  17.1 0.6 %shard_map.57 = (bf16[2,4,16,768]{3,2,1,0:T(8,128)(2,1)S(1)}, bf16[1,4,16,768]{3,2,1,0:T(8,128)(2,1)S(1)}, bf16[2,4,16,768]{3,2,1,0:T(8,128)(2,1)S(1)}) custom-call(s32[8]{0:T(128)S(1)} %get-tuple-element.30.picks_ref, bf16[4,16,768]{2,1,0:T(8,128)(2,1)S(1)} %copy-done.3, bf16[4,16,768]{2,1,0:T(8,128)(2,1)S(1)} %collective-permute-done.refs_1_, ...), custom_call_target="tpu_custom_call" | custom-call | flops 99999997952 | tf_op jit(solution)/shard_map/pallas_call | solution.py:169
  17.7 1.6 %collective-permute-start.4 = (bf16[1,4,16,768]{3,2,1,0:T(8,128)(2,1)S(1)}, bf16[1,4,16,768]{3,2,1,0:T(8,128)(2,1)S(1)}, u32[]{:S(2)}, u32[]{:S(2)}) collective-permute-start(bf16[1,4,16,768]{3,2,1,0:T(8,128)(2,1)S(1)} %get-tuple-element.36), channel_id=1, source_target_pairs={{0,2},{1,3},{2,0},{3,1},{4,6},{5,7},{6,4},{7,5},{8,10},{9,11},{10,... | collective-permute-start | bytes 294920 | tf_op jit(solution)/shard_map/ppermute | solution.py:433
  19.2 0.0 collective-permute-start.3
  19.2 0.0 copy-done.2
  19.2 1.0 %shard_map.58 = bf16[4,4,16,768]{3,2,1,0:T(8,128)(2,1)} custom-call(bf16[4,16,3072]{2,1,0:T(8,128)(2,1)S(1)} %copy-done.2, bf16[2,4,16,768]{3,2,1,0:T(8,128)(2,1)S(1)} %get-tuple-element.35._.refs_4_), custom_call_target="tpu_custom_call" | custom-call | tf_op jit(solution)/shard_map/pallas_call | solution.py:120
  20.2 8.6 %all-to-all-start = ((bf16[4,4,16,768]{3,2,1,0:T(8,128)(2,1)}), bf16[4,4,16,768]{3,2,1,0:T(8,128)(2,1)S(1)}, u32[]{:S(2)}, u32[]{:S(2)}) async-start(bf16[4,4,16,768]{3,2,1,0:T(8,128)(2,1)} %shard_map.58), calls=%async_computation | async-start | bytes 786432 | tf_op jit(solution)/shard_map/all_to_all | solution.py:465
  28.8 0.0 collective-permute-done.9.refs_1_.refs_8_
  28.8 1.5 %collective-permute-start.5 = (bf16[2,4,16,768]{3,2,1,0:T(8,128)(2,1)S(1)}, bf16[2,4,16,768]{3,2,1,0:T(8,128)(2,1)S(1)}, u32[]{:S(2)}, u32[]{:S(2)}) collective-permute-start(bf16[2,4,16,768]{3,2,1,0:T(8,128)(2,1)S(1)} %get-tuple-element.37), channel_id=1, source_target_pairs={{0,3},{1,0},{2,1},{3,2},{4,7},{5,4},{6,5},{7,6},{8,11},{9,8},{10,9... | collective-permute-start | bytes 589832 | tf_op jit(solution)/shard_map/ppermute | solution.py:433
  30.3 0.0 collective-permute-done.10.refs_2_.refs_9_
  30.3 0.0 collective-permute-done.11.refs_3_.refs_10_
  30.3 0.6 %shard_map.60 = (bf16[2,4,16,768]{3,2,1,0:T(8,128)(2,1)S(1)}, bf16[1,4,16,768]{3,2,1,0:T(8,128)(2,1)S(1)}, bf16[2,4,16,768]{3,2,1,0:T(8,128)(2,1)S(1)}) custom-call(s32[8]{0:T(128)S(1)} %get-tuple-element.30.picks_ref, bf16[4,16,768]{2,1,0:T(8,128)(2,1)S(1)} %get-tuple-element.41.refs_0_.refs_7_, ...), custom_call_target="tpu_custom_call" | custom-call | flops 99999997952 | tf_op jit(solution)/shard_map/pallas_call | solution.py:169
  30.9 0.6 %collective-permute-start.13 = (bf16[1,4,16,768]{3,2,1,0:T(8,128)(2,1)S(1)}, bf16[1,4,16,768]{3,2,1,0:T(8,128)(2,1)S(1)}, u32[]{:S(2)}, u32[]{:S(2)}) collective-permute-start(bf16[1,4,16,768]{3,2,1,0:T(8,128)(2,1)S(1)} %get-tuple-element.46), channel_id=1, source_target_pairs={{0,2},{1,3},{2,0},{3,1},{4,6},{5,7},{6,4},{7,5},{8,10},{9,11},{10,... | collective-permute-start | bytes 294920 | tf_op jit(solution)/shard_map/ppermute | solution.py:433
  31.5 0.0 collective-permute-start.12
  31.5 0.0 collective-permute-done.4.refs_5_
  31.5 0.0 copy-start.6
  31.5 1.7 %collective-permute-start.14 = (bf16[2,4,16,768]{3,2,1,0:T(8,128)(2,1)S(1)}, bf16[2,4,16,768]{3,2,1,0:T(8,128)(2,1)S(1)}, u32[]{:S(2)}, u32[]{:S(2)}) collective-permute-start(bf16[2,4,16,768]{3,2,1,0:T(8,128)(2,1)S(1)} %get-tuple-element.47), channel_id=1, source_target_pairs={{0,3},{1,0},{2,1},{3,2},{4,7},{5,4},{6,5},{7,6},{8,11},{9,8},{10,9... | collective-permute-start | bytes 589832 | tf_op jit(solution)/shard_map/ppermute | solution.py:433
  33.2 2.2 %collective-permute-done.5.refs_6_ = bf16[2,4,16,768]{3,2,1,0:T(8,128)(2,1)S(1)} collective-permute-done((bf16[2,4,16,768]{3,2,1,0:T(8,128)(2,1)S(1)}, bf16[2,4,16,768]{3,2,1,0:T(8,128)(2,1)S(1)}, u32[]{:S(2)}, u32[]{:S(2)}) %collective-permute-start.5) | collective-permute-done | bytes 196640 | tf_op jit(solution)/shard_map/ppermute | solution.py:433
  35.4 0.0 collective-permute-done.3.refs_4_
  35.5 5.8 %all-to-all-done.query_ref = bf16[4,4,16,768]{3,2,1,0:T(8,128)(2,1)S(1)} async-done(((bf16[4,4,16,768]{3,2,1,0:T(8,128)(2,1)}), bf16[4,4,16,768]{3,2,1,0:T(8,128)(2,1)S(1)}, u32[]{:S(2)}, u32[]{:S(2)}) %all-to-all-start) | async-done | bytes 393248 | tf_op jit(solution)/shard_map/all_to_all | solution.py:465
  41.3 0.0 copy-done.6
  41.3 1.6 %shard_map.59 = (bf16[4,16,384]{2,1,0:T(8,128)(2,1)S(1)}, bf16[4,16,384]{2,1,0:T(8,128)(2,1)S(1)}, bf16[4,16,384]{2,1,0:T(8,128)(2,1)S(1)}) custom-call(s32[16]{0:T(128)S(1)} %copy-done.6, f32[4,576]{1,0:T(4,128)S(1)} %get-tuple-element.29.bias_ref, bf16[4,4,16,768]{3,2,1,0:T(8,128)(2,1)S(1)} %all-to-all-done.query_ref, bf16[4,16,768]{2,1,0:T(8,128)(2,1)S(1)} %copy-done.3, ...), custom_call_target="tpu_custom_call" | custom-call | flops 99999997952 | tf_op jit(solution)/shard_map/pallas_call | solution.py:390
  42.9 0.1 collective-permute-start.7
  43.0 2.0 %collective-permute-start.8 = (bf16[4,16,384]{2,1,0:T(8,128)(2,1)S(1)}, bf16[4,16,384]{2,1,0:T(8,128)(2,1)S(1)}, u32[]{:S(2)}, u32[]{:S(2)}) collective-permute-start(bf16[4,16,384]{2,1,0:T(8,128)(2,1)S(1)} %get-tuple-element.40), channel_id=1, source_target_pairs={{0,4},{4,8},{8,12},{12,0},{1,5},{5,9},{9,13},{13,1},{2,6},{6,10},{... | collective-permute-start | bytes 147464 | tf_op jit(solution)/shard_map/ppermute | solution.py:433
  45.0 0.0 collective-permute-done.13.refs_5_.refs_12_
  45.0 1.8 %collective-permute-start.6 = (bf16[4,16,384]{2,1,0:T(8,128)(2,1)S(1)}, bf16[4,16,384]{2,1,0:T(8,128)(2,1)S(1)}, u32[]{:S(2)}, u32[]{:S(2)}) collective-permute-start(bf16[4,16,384]{2,1,0:T(8,128)(2,1)S(1)} %get-tuple-element.38.refs_7_), channel_id=1, source_target_pairs={{0,12},{4,0},{8,4},{12,8},{1,13},{5,1},{9,5},{13,9},{2,14},{6,2},{... | collective-permute-start | bytes 147464 | tf_op jit(solution)/shard_map/ppermute | solution.py:433
  46.8 0.0 collective-permute-done.12.refs_4_.refs_11_
  46.9 0.0 collective-permute-done.14.refs_6_.refs_13_
  46.9 1.6 %shard_map.61 = (bf16[4,16,384]{2,1,0:T(8,128)(2,1)S(1)}, bf16[4,16,384]{2,1,0:T(8,128)(2,1)S(1)}, bf16[4,16,384]{2,1,0:T(8,128)(2,1)S(1)}) custom-call(s32[16]{0:T(128)S(1)} %copy-done.6, f32[4,576]{1,0:T(4,128)S(1)} %get-tuple-element.29.bias_ref, bf16[4,4,16,768]{3,2,1,0:T(8,128)(2,1)S(1)} %all-to-all-done.query_ref, ...), custom_call_target="tpu_custom_call" | custom-call | tf_op jit(solution)/shard_map/pallas_call | solution.py:390
  48.5 1.1 %collective-permute-start.16 = (bf16[4,16,384]{2,1,0:T(8,128)(2,1)S(1)}, bf16[4,16,384]{2,1,0:T(8,128)(2,1)S(1)}, u32[]{:S(2)}, u32[]{:S(2)}) collective-permute-start(bf16[4,16,384]{2,1,0:T(8,128)(2,1)S(1)} %get-tuple-element.49), channel_id=1, source_target_pairs={{0,8},{4,12},{8,0},{12,4},{1,9},{5,13},{9,1},{13,5},{2,10},{6,14},... | collective-permute-start | bytes 147464 | tf_op jit(solution)/shard_map/ppermute | solution.py:433
  49.6 0.0 collective-permute-start.17
  49.6 0.0 collective-permute-done.7.refs_1_
  49.6 3.8 %collective-permute-start.15 = (bf16[4,16,384]{2,1,0:T(8,128)(2,1)S(1)}, bf16[4,16,384]{2,1,0:T(8,128)(2,1)S(1)}, u32[]{:S(2)}, u32[]{:S(2)}) collective-permute-start(bf16[4,16,384]{2,1,0:T(8,128)(2,1)S(1)} %get-tuple-element.48.refs_14_), channel_id=1, source_target_pairs={{0,12},{4,0},{8,4},{12,8},{1,13},{5,1},{9,5},{13,9},{2,14},{6,2},{... | collective-permute-start | bytes 147464 | tf_op jit(solution)/shard_map/ppermute | solution.py:433
  53.4 1.7 %shard_map.62.refs_6_ = bf16[4,16,768]{2,1,0:T(8,128)(2,1)S(1)} custom-call(s32[16]{0:T(128)S(1)} %copy-done.6, f32[4,576]{1,0:T(4,128)S(1)} %get-tuple-element.29.bias_ref, bf16[4,4,16,768]{3,2,1,0:T(8,128)(2,1)S(1)} %all-to-all-done.query_ref, bf16[4,16,768]{2,1,0:T(8,128)(2,1)S(1)} %copy-done.3, bf16[4,16,768]{2,1,0:T(8,128)(2,1)S(1)} %collective-permute-done.refs_1_, ...), custom_call_target="tpu_custom_call" | custom-call | tf_op jit(solution)/shard_map/pallas_call | solution.py:390
  55.1 0.0 collective-permute-done.8.refs_2_
  55.1 0.0 collective-permute-done.6.refs_0_
  55.2 0.0 collective-permute-done.16.refs_4_
  55.2 0.3 collective-permute-done.17.refs_5_
  55.5 0.0 collective-permute-done.15.refs_3_
  55.5 0.8 %shard_map.63 = bf16[4,16,3072]{2,1,0:T(8,128)(2,1)} custom-call(bf16[4,16,384]{2,1,0:T(8,128)(2,1)S(1)} %collective-permute-done.6.refs_0_, bf16[4,16,384]{2,1,0:T(8,128)(2,1)S(1)} %collective-permute-done.7.refs_1_, bf16[4,16,384]{2,1,0:T(8,128)(2,1)S(1)} %collective-permute-done.8.refs_2_, bf16[4,16,384]{2,1,0:T(8,128)(2,1)S(1)} %collective-permute-done.15.refs_3_, ...), custom_call_target="tpu_custom_call" | custom-call | tf_op jit(solution)/shard_map/pallas_call | solution.py:421
Async XLA Ops:
  0.0 9.9 %copy-start.1 = (bf16[4,16,3072]{2,1,0:T(8,128)(2,1)S(1)}, bf16[4,16,3072]{2,1,0:T(8,128)(2,1)}, u32[]{:S(2)}) copy-start(bf16[4,16,3072]{2,1,0:T(8,128)(2,1)} %refs_1_.3) | copy-start | bytes 1179652
  0.0 9.9 %copy-start = (bf16[4,16,3072]{2,1,0:T(8,128)(2,1)S(1)}, bf16[4,16,3072]{2,1,0:T(8,128)(2,1)}, u32[]{:S(2)}) copy-start(bf16[4,16,3072]{2,1,0:T(8,128)(2,1)} %refs_0_.3) | copy-start | bytes 1179652
  2.9 7.0 %copy-start.7 = (f32[8,128]{1,0:T(8,128)S(1)}, f32[8,128]{1,0:T(8,128)}, u32[]{:S(2)}) copy-start(f32[8,128]{1,0:T(8,128)} %get-tuple-element.28.refs_4_) | copy-start | bytes 12292
  2.9 11.5 %collective-permute-start = (bf16[4,16,768]{2,1,0:T(8,128)(2,1)}, bf16[4,16,768]{2,1,0:T(8,128)(2,1)S(1)}, u32[]{:S(2)}, u32[]{:S(2)}) collective-permute-start(bf16[4,16,768]{2,1,0:T(8,128)(2,1)} %get-tuple-element.32), channel_id=1, source_target_pairs={{0,4},{4,8},{8,12},{12,0},{1,5},{5,9},{9,13},{13,1},{2,6},{6,10},{... | collective-permute-start | bytes 294920 | tf_op jit(solution)/shard_map/ppermute | solution.py:433
  6.0 11.1 %collective-permute-start.1 = (bf16[4,16,768]{2,1,0:T(8,128)(2,1)}, bf16[4,16,768]{2,1,0:T(8,128)(2,1)S(1)}, u32[]{:S(2)}, u32[]{:S(2)}) collective-permute-start(bf16[4,16,768]{2,1,0:T(8,128)(2,1)} %get-tuple-element.33), channel_id=1, source_target_pairs={{0,8},{4,12},{8,0},{12,4},{1,9},{5,13},{9,1},{13,5},{2,10},{6,14},... | collective-permute-start | bytes 294920 | tf_op jit(solution)/shard_map/ppermute | solution.py:433
  8.5 1.4 %copy-start.5 = (s32[16]{0:T(128)S(1)}, s32[16]{0:T(128)}, u32[]{:S(2)}) copy-start(s32[16]{0:T(128)} %tokens_ref.5) | copy-start | bytes 196
  8.6 8.5 %collective-permute-start.2 = (bf16[4,16,768]{2,1,0:T(8,128)(2,1)}, bf16[4,16,768]{2,1,0:T(8,128)(2,1)S(1)}, u32[]{:S(2)}, u32[]{:S(2)}) collective-permute-start(bf16[4,16,768]{2,1,0:T(8,128)(2,1)} %get-tuple-element.34), channel_id=1, source_target_pairs={{0,12},{4,0},{8,4},{12,8},{1,13},{5,1},{9,5},{13,9},{2,14},{6,2},{... | collective-permute-start | bytes 294920 | tf_op jit(solution)/shard_map/ppermute | solution.py:433
  9.9 0.7 %copy-start.4 = (s32[16,32]{1,0:T(8,128)S(1)}, s32[16,32]{1,0:T(8,128)}, u32[]{:S(2)}) copy-start(s32[16,32]{1,0:T(8,128)} %refs_2_.1) | copy-start | bytes 6148
  10.6 6.4 %copy-start.3 = (bf16[4,16,768]{2,1,0:T(8,128)(2,1)S(1)}, bf16[4,16,768]{2,1,0:T(8,128)(2,1)}, u32[]{:S(2)}) copy-start(bf16[4,16,768]{2,1,0:T(8,128)(2,1)} %get-tuple-element.31.refs_0_) | copy-start | bytes 294916
  13.1 15.7 %collective-permute-start.9 = (bf16[4,16,768]{2,1,0:T(8,128)(2,1)S(1)}, bf16[4,16,768]{2,1,0:T(8,128)(2,1)S(1)}, u32[]{:S(2)}, u32[]{:S(2)}) collective-permute-start(bf16[4,16,768]{2,1,0:T(8,128)(2,1)S(1)} %get-tuple-element.42), channel_id=1, source_target_pairs={{0,4},{4,8},{8,12},{12,0},{1,5},{5,9},{9,13},{13,1},{2,6},{6,10},{... | collective-permute-start | bytes 294920 | tf_op jit(solution)/shard_map/ppermute | solution.py:433
  13.9 16.4 %collective-permute-start.10 = (bf16[4,16,768]{2,1,0:T(8,128)(2,1)S(1)}, bf16[4,16,768]{2,1,0:T(8,128)(2,1)S(1)}, u32[]{:S(2)}, u32[]{:S(2)}) collective-permute-start(bf16[4,16,768]{2,1,0:T(8,128)(2,1)S(1)} %get-tuple-element.43), channel_id=1, source_target_pairs={{0,8},{4,12},{8,0},{12,4},{1,9},{5,13},{9,1},{13,5},{2,10},{6,14},... | collective-permute-start | bytes 294920 | tf_op jit(solution)/shard_map/ppermute | solution.py:433
  14.4 15.9 %collective-permute-start.11 = (bf16[4,16,768]{2,1,0:T(8,128)(2,1)S(1)}, bf16[4,16,768]{2,1,0:T(8,128)(2,1)S(1)}, u32[]{:S(2)}, u32[]{:S(2)}) collective-permute-start(bf16[4,16,768]{2,1,0:T(8,128)(2,1)S(1)} %get-tuple-element.44), channel_id=1, source_target_pairs={{0,12},{4,0},{8,4},{12,8},{1,13},{5,1},{9,5},{13,9},{2,14},{6,2},{... | collective-permute-start | bytes 294920 | tf_op jit(solution)/shard_map/ppermute | solution.py:433
  17.0 2.2 %copy-start.2 = (bf16[4,16,3072]{2,1,0:T(8,128)(2,1)S(1)}, bf16[4,16,3072]{2,1,0:T(8,128)(2,1)}, u32[]{:S(2)}) copy-start(bf16[4,16,3072]{2,1,0:T(8,128)(2,1)} %source_ref.1) | copy-start | bytes 1179652
  17.7 13.8 %collective-permute-start.4 = (bf16[1,4,16,768]{3,2,1,0:T(8,128)(2,1)S(1)}, bf16[1,4,16,768]{3,2,1,0:T(8,128)(2,1)S(1)}, u32[]{:S(2)}, u32[]{:S(2)}) collective-permute-start(bf16[1,4,16,768]{3,2,1,0:T(8,128)(2,1)S(1)} %get-tuple-element.36), channel_id=1, source_target_pairs={{0,2},{1,3},{2,0},{3,1},{4,6},{5,7},{6,4},{7,5},{8,10},{9,11},{10,... | collective-permute-start | bytes 294920 | tf_op jit(solution)/shard_map/ppermute | solution.py:433
  19.2 16.2 %collective-permute-start.3 = (bf16[2,4,16,768]{3,2,1,0:T(8,128)(2,1)S(1)}, bf16[2,4,16,768]{3,2,1,0:T(8,128)(2,1)S(1)}, u32[]{:S(2)}, u32[]{:S(2)}) collective-permute-start(bf16[2,4,16,768]{3,2,1,0:T(8,128)(2,1)S(1)} %get-tuple-element.35._.refs_4_), channel_id=1, source_target_pairs={{0,1},{1,2},{2,3},{3,0},{4,5},{5,6},{6,7},{7,4},{8,9},{9,10},{10,1... | collective-permute-start | bytes 589832 | tf_op jit(solution)/shard_map/ppermute | solution.py:433
  20.2 21.0 %all-to-all-start = ((bf16[4,4,16,768]{3,2,1,0:T(8,128)(2,1)}), bf16[4,4,16,768]{3,2,1,0:T(8,128)(2,1)S(1)}, u32[]{:S(2)}, u32[]{:S(2)}) async-start(bf16[4,4,16,768]{3,2,1,0:T(8,128)(2,1)} %shard_map.58), calls=%async_computation | async-start | bytes 786432 | tf_op jit(solution)/shard_map/all_to_all | solution.py:465
  28.8 6.6 %collective-permute-start.5 = (bf16[2,4,16,768]{3,2,1,0:T(8,128)(2,1)S(1)}, bf16[2,4,16,768]{3,2,1,0:T(8,128)(2,1)S(1)}, u32[]{:S(2)}, u32[]{:S(2)}) collective-permute-start(bf16[2,4,16,768]{3,2,1,0:T(8,128)(2,1)S(1)} %get-tuple-element.37), channel_id=1, source_target_pairs={{0,3},{1,0},{2,1},{3,2},{4,7},{5,4},{6,5},{7,6},{8,11},{9,8},{10,9... | collective-permute-start | bytes 589832 | tf_op jit(solution)/shard_map/ppermute | solution.py:433
  30.9 14.1 %collective-permute-start.13 = (bf16[1,4,16,768]{3,2,1,0:T(8,128)(2,1)S(1)}, bf16[1,4,16,768]{3,2,1,0:T(8,128)(2,1)S(1)}, u32[]{:S(2)}, u32[]{:S(2)}) collective-permute-start(bf16[1,4,16,768]{3,2,1,0:T(8,128)(2,1)S(1)} %get-tuple-element.46), channel_id=1, source_target_pairs={{0,2},{1,3},{2,0},{3,1},{4,6},{5,7},{6,4},{7,5},{8,10},{9,11},{10,... | collective-permute-start | bytes 294920 | tf_op jit(solution)/shard_map/ppermute | solution.py:433
  31.5 15.4 %collective-permute-start.12 = (bf16[2,4,16,768]{3,2,1,0:T(8,128)(2,1)S(1)}, bf16[2,4,16,768]{3,2,1,0:T(8,128)(2,1)S(1)}, u32[]{:S(2)}, u32[]{:S(2)}) collective-permute-start(bf16[2,4,16,768]{3,2,1,0:T(8,128)(2,1)S(1)} %get-tuple-element.45), channel_id=1, source_target_pairs={{0,1},{1,2},{2,3},{3,0},{4,5},{5,6},{6,7},{7,4},{8,9},{9,10},{10,1... | collective-permute-start | bytes 589832 | tf_op jit(solution)/shard_map/ppermute | solution.py:433
  31.5 9.8 %copy-start.6 = (s32[16]{0:T(128)S(1)}, s32[16]{0:T(128)}, u32[]{:S(2)}) copy-start(s32[16]{0:T(128)} %tokens_ref.5) | copy-start | bytes 196
  31.5 15.4 %collective-permute-start.14 = (bf16[2,4,16,768]{3,2,1,0:T(8,128)(2,1)S(1)}, bf16[2,4,16,768]{3,2,1,0:T(8,128)(2,1)S(1)}, u32[]{:S(2)}, u32[]{:S(2)}) collective-permute-start(bf16[2,4,16,768]{3,2,1,0:T(8,128)(2,1)S(1)} %get-tuple-element.47), channel_id=1, source_target_pairs={{0,3},{1,0},{2,1},{3,2},{4,7},{5,4},{6,5},{7,6},{8,11},{9,8},{10,9... | collective-permute-start | bytes 589832 | tf_op jit(solution)/shard_map/ppermute | solution.py:433
  42.9 6.7 %collective-permute-start.7 = (bf16[4,16,384]{2,1,0:T(8,128)(2,1)S(1)}, bf16[4,16,384]{2,1,0:T(8,128)(2,1)S(1)}, u32[]{:S(2)}, u32[]{:S(2)}) collective-permute-start(bf16[4,16,384]{2,1,0:T(8,128)(2,1)S(1)} %get-tuple-element.39), channel_id=1, source_target_pairs={{0,8},{4,12},{8,0},{12,4},{1,9},{5,13},{9,1},{13,5},{2,10},{6,14},... | collective-permute-start | bytes 147464 | tf_op jit(solution)/shard_map/ppermute | solution.py:433
  43.0 12.2 %collective-permute-start.8 = (bf16[4,16,384]{2,1,0:T(8,128)(2,1)S(1)}, bf16[4,16,384]{2,1,0:T(8,128)(2,1)S(1)}, u32[]{:S(2)}, u32[]{:S(2)}) collective-permute-start(bf16[4,16,384]{2,1,0:T(8,128)(2,1)S(1)} %get-tuple-element.40), channel_id=1, source_target_pairs={{0,4},{4,8},{8,12},{12,0},{1,5},{5,9},{9,13},{13,1},{2,6},{6,10},{... | collective-permute-start | bytes 147464 | tf_op jit(solution)/shard_map/ppermute | solution.py:433
  45.0 10.1 %collective-permute-start.6 = (bf16[4,16,384]{2,1,0:T(8,128)(2,1)S(1)}, bf16[4,16,384]{2,1,0:T(8,128)(2,1)S(1)}, u32[]{:S(2)}, u32[]{:S(2)}) collective-permute-start(bf16[4,16,384]{2,1,0:T(8,128)(2,1)S(1)} %get-tuple-element.38.refs_7_), channel_id=1, source_target_pairs={{0,12},{4,0},{8,4},{12,8},{1,13},{5,1},{9,5},{13,9},{2,14},{6,2},{... | collective-permute-start | bytes 147464 | tf_op jit(solution)/shard_map/ppermute | solution.py:433
  48.5 6.7 %collective-permute-start.16 = (bf16[4,16,384]{2,1,0:T(8,128)(2,1)S(1)}, bf16[4,16,384]{2,1,0:T(8,128)(2,1)S(1)}, u32[]{:S(2)}, u32[]{:S(2)}) collective-permute-start(bf16[4,16,384]{2,1,0:T(8,128)(2,1)S(1)} %get-tuple-element.49), channel_id=1, source_target_pairs={{0,8},{4,12},{8,0},{12,4},{1,9},{5,13},{9,1},{13,5},{2,10},{6,14},... | collective-permute-start | bytes 147464 | tf_op jit(solution)/shard_map/ppermute | solution.py:433
  49.6 5.9 %collective-permute-start.17 = (bf16[4,16,384]{2,1,0:T(8,128)(2,1)S(1)}, bf16[4,16,384]{2,1,0:T(8,128)(2,1)S(1)}, u32[]{:S(2)}, u32[]{:S(2)}) collective-permute-start(bf16[4,16,384]{2,1,0:T(8,128)(2,1)S(1)} %get-tuple-element.50), channel_id=1, source_target_pairs={{0,4},{4,8},{8,12},{12,0},{1,5},{5,9},{9,13},{13,1},{2,6},{6,10},{... | collective-permute-start | bytes 147464 | tf_op jit(solution)/shard_map/ppermute | solution.py:433
  49.6 5.9 %collective-permute-start.15 = (bf16[4,16,384]{2,1,0:T(8,128)(2,1)S(1)}, bf16[4,16,384]{2,1,0:T(8,128)(2,1)S(1)}, u32[]{:S(2)}, u32[]{:S(2)}) collective-permute-start(bf16[4,16,384]{2,1,0:T(8,128)(2,1)S(1)} %get-tuple-element.48.refs_14_), channel_id=1, source_target_pairs={{0,12},{4,0},{8,4},{12,8},{1,13},{5,1},{9,5},{13,9},{2,14},{6,2},{... | collective-permute-start | bytes 147464 | tf_op jit(solution)/shard_map/ppermute | solution.py:433
